TPU v7x, 256 devices: a whole 4x4x8 slice. The times are simulated.
256 devices in a mesh: dp: 8 (over z_lo, x), seq: 32 (over y, z_hi, core).
Axes of the slice: x: 4, y: 4, z: 8 (z_hi: 4, z_lo: 2; z = z_hi * 2 + z_lo), core: 2. Of those that a mesh axis runs over, the one named last changes fastest.
Arguments:
- q_coarse: bfloat16 [8, 256, 1024], P('dp'), may hold values from -6 to 6
- k_coarse: bfloat16 [8, 256, 1024], P('dp'), may hold values from -6 to 6
- v_coarse: bfloat16 [8, 256, 1024], P('dp'), may hold values from -18 to 18
- cot_coarse: bfloat16 [8, 256, 1024], P('dp'), may hold values from -6 to 6
- coarse_ids: int32 [8, 256], P('dp'), may hold values from 0 to 5, never falling along the last dimension, each value on 1 to 64 neighbouring positions
- q_fine: bfloat16 [8, 3072, 1024], P('dp', 'seq'), may hold values from -6 to 6
- k_fine: bfloat16 [8, 3072, 1024], P('dp', 'seq'), may hold values from -6 to 6
- v_fine: bfloat16 [8, 3072, 1024], P('dp', 'seq'), may hold values from -18 to 18
- cot_fine: bfloat16 [8, 3072, 1024], P('dp', 'seq'), may hold values from -6 to 6
- fine_ids: int32 [8, 3072], P('dp', 'seq'), may hold values from 0 to 2, never falling along the last dimension, each value on 1 to 1536 neighbouring positions
- log_scale: float32 [8], replicated, may hold values from 3 to 3.7
Outputs:
- out_coarse: bfloat16 [8, 256, 1024], P('dp')
- dq_coarse: bfloat16 [8, 256, 1024], P('dp')
- dk_coarse: bfloat16 [8, 256, 1024], P('dp')
- dv_coarse: bfloat16 [8, 256, 1024], P('dp')
- out_fine: bfloat16 [8, 3072, 1024], P('dp', 'seq')
- dq_fine: bfloat16 [8, 3072, 1024], P('dp', 'seq')
- dk_fine: bfloat16 [8, 3072, 1024], P('dp', 'seq')
- dv_fine: bfloat16 [8, 3072, 1024], P('dp', 'seq')
- grad_scale: float32 [8], replicated
Inputs may be any that keep to these rules, and one draw needn't show every extreme that they name: `coarse_ids`: along each image the coarse scale index never falls; every index is used; the largest scale holds exactly 64 tokens (more than one scale may) and no scale holds more. `fine_ids`: along each image the fine scale index never falls; every index is used; the largest scale holds exactly 1536 tokens (more than one scale may) and no scale holds more.
All inputs are finite; a program needn't handle non-finite values.
Results may differ from a plain program's by a relative error of at most 0.022.
Values may be sent and summed in bfloat16 or wider, within the bound.
No kernel may reach another device: no remote copies, remote signals or barrier semaphores. Data moves between devices by JAX's collectives and lax.ppermute only.
A program may use at most 128 MiB of HBM per device.

v0:
```python
from functools import partial
import math

import jax
import jax.numpy as jnp
from jax import lax
from jax.sharding import PartitionSpec as P

norm_eps = 1e-06


def add_trees(first_tree, second_tree):
    return jax.tree.map(jnp.add, first_tree, second_tree)


def join_halves(first_tree, second_tree):
    return jax.tree.map(
        lambda upper, lower: jnp.concatenate([upper, lower], axis=0), first_tree, second_tree
    )


def maybe_add(condition, running, compute):

    def with_terms(current):
        return add_trees(current, compute())

    def without_terms(current):
        return current

    return lax.cond(condition, with_terms, without_terms, running)


def unit_heads(matrix, head_count):
    by_head = matrix.astype(jnp.float32).reshape(matrix.shape[0], head_count, -1)
    inv_norm = lax.rsqrt(jnp.sum(by_head * by_head, axis=-1, keepdims=True) + norm_eps)
    return (by_head * inv_norm, inv_norm)


def unit_back(unit_dir, inv_norm, grad_unit):
    along_dir = jnp.sum(unit_dir * grad_unit, axis=-1, keepdims=True)
    return (inv_norm * (grad_unit - unit_dir * along_dir)).reshape(unit_dir.shape[0], -1)


def score_block(sharpness, query_unit, query_level, key_unit, key_level):
    cosine = jnp.einsum("qhd,khd->hqk", query_unit, key_unit, preferred_element_type=jnp.float32)
    score = sharpness[:, None, None] * cosine
    visible = (key_level[None, :] <= query_level[:, None])[None]
    prob = jnp.where(visible, jnp.exp(score - sharpness[:, None, None]), 0.0)
    return (score, prob)


def query_terms(sharpness, query_unit, cotangent, query_level, key_unit, values, key_level):
    score, prob = score_block(sharpness, query_unit, query_level, key_unit, key_level)
    dprob = jnp.einsum("qhd,khd->hqk", cotangent, values, preferred_element_type=jnp.float32)
    weighted = prob * dprob
    prob_low = prob.astype(jnp.bfloat16)
    weight_low = weighted.astype(jnp.bfloat16)
    numerator = jnp.einsum("hqk,khd->qhd", prob_low, values, preferred_element_type=jnp.float32)
    along_keys = jnp.einsum("hqk,khd->qhd", prob_low, key_unit, preferred_element_type=jnp.float32)
    weighted_keys = jnp.einsum(
        "hqk,khd->qhd", weight_low, key_unit, preferred_element_type=jnp.float32
    )
    return (
        jnp.sum(prob, axis=-1).T,
        numerator,
        jnp.sum(weighted, axis=-1).T,
        weighted_keys,
        along_keys,
        jnp.sum(prob * score, axis=-1).T,
        jnp.sum(weighted * score, axis=-1).T,
    )


def finish_queries(sharpness, sums, unit_dir, inv_norm):
    denominator, numerator, weighted_sum, weighted_keys, along_keys, prob_score, weighted_score = (
        sums
    )
    mean_dprob = weighted_sum / denominator
    outputs = (
        (numerator / denominator[:, :, None]).reshape(numerator.shape[0], -1).astype(jnp.bfloat16)
    )
    grad_unit = (
        sharpness[None, :, None]
        * (weighted_keys - mean_dprob[:, :, None] * along_keys)
        / denominator[:, :, None]
    )
    scale_term = jnp.sum((weighted_score - mean_dprob * prob_score) / denominator, axis=0)
    grads = unit_back(unit_dir, inv_norm, grad_unit).astype(jnp.bfloat16)
    return (outputs, grads, scale_term, denominator, mean_dprob)


def key_terms(
    sharpness,
    query_unit,
    cotangent,
    query_level,
    denominator,
    mean_dprob,
    key_unit,
    values,
    key_level,
):
    prob = score_block(sharpness, query_unit, query_level, key_unit, key_level)[1]
    dprob = jnp.einsum("qhd,khd->hqk", cotangent, values, preferred_element_type=jnp.float32)
    norm_prob = prob / denominator.T[:, :, None]
    dscore = norm_prob * (dprob - mean_dprob.T[:, :, None])
    grad_keys = sharpness[None, :, None] * jnp.einsum(
        "hqk,qhd->khd", dscore.astype(jnp.bfloat16), query_unit, preferred_element_type=jnp.float32
    )
    grad_values = jnp.einsum(
        "hqk,qhd->khd",
        norm_prob.astype(jnp.bfloat16),
        cotangent,
        preferred_element_type=jnp.float32,
    )
    return (grad_keys, grad_values)


def body(
    q_coarse,
    k_coarse,
    v_coarse,
    cot_coarse,
    coarse_ids,
    q_fine,
    k_fine,
    v_fine,
    cot_fine,
    fine_ids,
    log_scale,
):
    sharpness = jnp.exp(log_scale)
    head_count = log_scale.shape[0]
    coarse_count = q_coarse.shape[1]
    seq_count = lax.axis_size("seq")
    query_rows = q_fine[0]
    key_rows = k_fine[0]
    value_rows = v_fine[0]
    cot_rows = cot_fine[0]
    levels = fine_ids[0] + coarse_count
    row_count = query_rows.shape[0]
    half_rows = row_count // 2
    query_dir, query_inv = unit_heads(query_rows, head_count)
    key_dir, key_inv = unit_heads(key_rows, head_count)
    query_unit = query_dir.astype(jnp.bfloat16)
    key_unit = key_dir.astype(jnp.bfloat16)
    values = value_rows.reshape(row_count, head_count, -1)
    cotangent = cot_rows.reshape(row_count, head_count, -1)
    coarse_query_dir, coarse_query_inv = unit_heads(q_coarse[0], head_count)
    coarse_key_dir, coarse_key_inv = unit_heads(k_coarse[0], head_count)
    coarse_query_unit = coarse_query_dir.astype(jnp.bfloat16)
    coarse_key_unit = coarse_key_dir.astype(jnp.bfloat16)
    coarse_values = v_coarse[0].reshape(coarse_count, head_count, -1)
    coarse_cot = cot_coarse[0].reshape(coarse_count, head_count, -1)
    coarse_levels = coarse_ids[0]
    windows = [slice(0, half_rows), slice(half_rows, row_count)]

    def slot_view(matrix, shards, slot):
        shaped = matrix.reshape((shards, 2, half_rows) + matrix.shape[1:])
        return shaped[:, slot].reshape((shards * half_rows,) + matrix.shape[1:])

    start_sums = tuple(
        (
            query_terms(
                sharpness,
                query_unit[window],
                cotangent[window],
                levels[window],
                coarse_key_unit,
                coarse_values,
                coarse_levels,
            )
            for window in windows
        )
    )
    units_in = lax.all_gather(key_unit.reshape(row_count, -1), "seq", axis=0, tiled=True)
    values_in = lax.all_gather(value_rows, "seq", axis=0, tiled=True)
    levels_in = lax.all_gather(levels, "seq", axis=0, tiled=True)
    shards = units_in.shape[0] // row_count
    updated = []
    for member in range(2):
        window = windows[member]
        current = start_sums[member]
        reach = jnp.max(levels[window])
        for slot in range(2):
            slot_levels = slot_view(levels_in, shards, slot)
            terms = partial(
                query_terms,
                sharpness,
                query_unit[window],
                cotangent[window],
                levels[window],
                slot_view(units_in, shards, slot).reshape(shards * half_rows, head_count, -1),
                slot_view(values_in, shards, slot).reshape(shards * half_rows, head_count, -1),
                slot_levels,
            )
            current = maybe_add(jnp.min(slot_levels) <= reach, current, terms)
        updated.append(current)
    fine_sums = tuple(updated)
    fine_out, fine_dq, fine_scale, denominator, mean_dprob = finish_queries(
        sharpness, join_halves(fine_sums[0], fine_sums[1]), query_dir, query_inv
    )
    denominator_all, mean_all = (
        lax.all_gather(denominator, "seq", axis=0, tiled=True),
        lax.all_gather(mean_dprob, "seq", axis=0, tiled=True),
    )
    empty_half = jnp.zeros((half_rows,) + values.shape[1:], jnp.float32)
    running = ((empty_half, empty_half), (empty_half, empty_half))
    units_in = lax.all_gather(query_unit.reshape(row_count, -1), "seq", axis=0, tiled=True)
    cots_in = lax.all_gather(cot_rows, "seq", axis=0, tiled=True)
    levels_in = lax.all_gather(levels, "seq", axis=0, tiled=True)
    span = units_in.shape[0]
    shards = span // row_count
    updated = []
    for member in range(2):
        window = windows[member]
        current = running[member]
        floor_level = jnp.min(levels[window])
        for slot in range(2):
            slot_levels = slot_view(levels_in, shards, slot)
            terms = partial(
                key_terms,
                sharpness,
                slot_view(units_in, shards, slot).reshape(shards * half_rows, head_count, -1),
                slot_view(cots_in, shards, slot).reshape(shards * half_rows, head_count, -1),
                slot_levels,
                slot_view(denominator_all, shards, slot),
                slot_view(mean_all, shards, slot),
                key_unit[window],
                values[window],
                levels[window],
            )
            current = maybe_add(jnp.max(slot_levels) >= floor_level, current, terms)
        updated.append(current)
    key_sums = tuple(updated)
    grad_keys, grad_values = join_halves(key_sums[0], key_sums[1])
    fine_dk = unit_back(key_dir, key_inv, grad_keys).astype(jnp.bfloat16)
    fine_dv = grad_values.reshape(row_count, -1).astype(jnp.bfloat16)
    coarse_part = key_terms(
        sharpness,
        query_unit,
        cotangent,
        levels,
        denominator,
        mean_dprob,
        coarse_key_unit,
        coarse_values,
        coarse_levels,
    )
    coarse_sums = query_terms(
        sharpness,
        coarse_query_unit,
        coarse_cot,
        coarse_levels,
        coarse_key_unit,
        coarse_values,
        coarse_levels,
    )
    coarse_out, coarse_dq, coarse_scale, coarse_denom, coarse_mean = finish_queries(
        sharpness, coarse_sums, coarse_query_dir, coarse_query_inv
    )
    coarse_own = key_terms(
        sharpness,
        coarse_query_unit,
        coarse_cot,
        coarse_levels,
        coarse_denom,
        coarse_mean,
        coarse_key_unit,
        coarse_values,
        coarse_levels,
    )
    leading = (lax.axis_index("seq") == 0).astype(jnp.float32)
    scale_part = fine_scale + leading * coarse_scale
    key_sum, value_sum = (
        lax.psum(coarse_part[0].astype(jnp.bfloat16), "seq").astype(jnp.float32),
        lax.psum(coarse_part[1].astype(jnp.bfloat16), "seq").astype(jnp.float32),
    )
    scale_total = lax.psum(scale_part, ("dp", "seq"))
    key_sum = key_sum + coarse_own[0]
    value_sum = value_sum + coarse_own[1]
    coarse_dk = unit_back(coarse_key_dir, coarse_key_inv, key_sum).astype(jnp.bfloat16)
    coarse_dv = value_sum.reshape(coarse_count, -1).astype(jnp.bfloat16)
    grad_scale = scale_total / math.sqrt(
        lax.axis_size("dp") * (coarse_count + row_count * seq_count)
    )
    return (
        coarse_out[None],
        coarse_dq[None],
        coarse_dk[None],
        coarse_dv[None],
        fine_out[None],
        fine_dq[None],
        fine_dk[None],
        fine_dv[None],
        grad_scale,
    )


def solution(mesh):
    placed = (
        P("dp", None, None),
        P("dp", None, None),
        P("dp", None, None),
        P("dp", None, None),
        P("dp", None),
        P("dp", "seq", None),
        P("dp", "seq", None),
        P("dp", "seq", None),
        P("dp", "seq", None),
        P("dp", "seq"),
        P(),
    )
    return jax.shard_map(
        body,
        mesh=mesh,
        in_specs=placed,
        out_specs=(
            P("dp", None, None),
            P("dp", None, None),
            P("dp", None, None),
            P("dp", None, None),
            P("dp", "seq", None),
            P("dp", "seq", None),
            P("dp", "seq", None),
            P("dp", "seq", None),
            P(),
        ),
        check_vma=False,
    )
```

profile of v0, /device:TPU:1, one launch (start us, length us, event | category | flops | bytes accessed | tf_op | source)
XLA Modules:
  0.0 920.4 jit_solution(12808820629384005146)
XLA Ops:
  14.8 146.6 %all-reduce = s32[3072]{0:T(1024)S(1)} all-reduce(s32[3072]{0:T(1024)S(1)} %bitcast_dynamic-update-slice_fusion), channel_id=2, replica_groups=mesh['dp'=8,'seq'=32] {'seq'}, use_global_device_ids=true, to_apply=%add | all-reduce | flops 3072 | bytes 24576
  181.2 2.1 copy.493
  192.7 2.1 copy.448
  194.8 3.0 fusion.297
  197.8 2.0 copy.447
  214.0 5.7 fusion.388
  219.7 2.5 copy.499
  222.3 3.7 fusion.387
  226.0 2.5 copy.500
  228.6 2.9 copy.501
  231.5 2.5 copy.502
  233.9 20.0 %conditional.8 = ((f32[48,8]{0,1:T(8,128)}, f32[48,8,128]{2,0,1:T(8,128)}, f32[48,8]{0,1:T(8,128)}, f32[48,8,128]{2,0,1:T(8,128)}, f32[48,8,128]{2,0,1:T(8,128)}, /*index=5*/f32[48,8]{0,1:T(8,128)}, f32[48,8]{0,1:T(8,128)})) conditional(s32[]{:T(128)} %convert_element_type.310, (f32[48,8]{0,1:T(8,128)}, f32[48,8,128]{2,0,1:T(8,128)}, ...), branch_computations={%region_14.15_spmd, %region_15.20_spmd} | conditional | flops 765222912 | bytes 68623384 | solution.py:30
  233.9 4.6 convolution_multiply_fusion.1
  239.1 2.0 reduce.32
  243.3 5.0 multiply_reduce_fusion.1
  253.9 20.8 %conditional.10 = ((f32[48,8]{0,1:T(8,128)}, f32[48,8,128]{2,0,1:T(8,128)}, f32[48,8]{0,1:T(8,128)}, f32[48,8,128]{2,0,1:T(8,128)}, f32[48,8,128]{2,0,1:T(8,128)}, /*index=5*/f32[48,8]{0,1:T(8,128)}, f32[48,8]{0,1:T(8,128)})) conditional(s32[]{:T(128)} %convert_element_type.319, (f32[48,8]{0,1:T(8,128)}, f32[48,8,128]{2,0,1:T(8,128)}, ...), branch_computations={%region_31.32_spmd, %region_32.37_spmd} | conditional | flops 765222912 | bytes 68623384 | solution.py:30
  253.9 4.6 convolution_multiply_fusion.5
  259.0 2.0 reduce.34
  263.3 4.9 multiply_reduce_fusion.5
  274.7 19.5 %conditional.9 = ((f32[48,8]{0,1:T(8,128)}, f32[48,8]{0,1:T(8,128)}, f32[48,8,128]{2,0,1:T(8,128)}, f32[48,8,128]{2,0,1:T(8,128)}, f32[48,8]{0,1:T(8,128)}, /*index=5*/f32[48,8]{0,1:T(8,128)}, f32[48,8,128]{2,0,1:T(8,128)})) conditional(s32[]{:T(128)} %convert_element_type.309, (f32[48,8]{0,1:T(8,128)}, f32[48,8]{0,1:T(8,128)}, ...), branch_computations={%region_20.21_spmd, %region_21.26_spmd} | conditional | flops 765222912 | bytes 68623368 | solution.py:30
  274.7 4.7 convolution_multiply_fusion.3
  283.4 5.1 multiply_reduce_fusion.3
  294.1 19.9 %conditional.11 = ((f32[48,8]{0,1:T(8,128)}, f32[48,8]{0,1:T(8,128)}, f32[48,8,128]{2,0,1:T(8,128)}, f32[48,8,128]{2,0,1:T(8,128)}, f32[48,8]{0,1:T(8,128)}, /*index=5*/f32[48,8]{0,1:T(8,128)}, f32[48,8,128]{2,0,1:T(8,128)})) conditional(s32[]{:T(128)} %convert_element_type.318, (f32[48,8]{0,1:T(8,128)}, f32[48,8]{0,1:T(8,128)}, ...), branch_computations={%region_37.38_spmd, %region_38.43_spmd} | conditional | flops 765222912 | bytes 68623368 | solution.py:30
  294.3 4.5 convolution_multiply_fusion.7
  302.9 4.9 multiply_reduce_fusion.7
  314.0 2.1 fusion.371
  317.5 48.2 %all-gather.3 = f32[32,96,8]{1,2,0:T(8,128)} all-gather(f32[1,96,8]{1,2,0:T(8,128)} %bitcast.426), channel_id=1, replica_groups=mesh['dp'=8,'seq'=32] {'seq'}, dimensions={0}, use_global_device_ids=true | all-gather | bytes 101376 | tf_op jit(solution)/shard_map/all_gather | solution.py:204
  365.7 1.8 reshape.868
  367.5 1.9 fusion.390
  373.1 45.1 %all-gather.4 = f32[32,96,8]{1,2,0:T(8,128)} all-gather(f32[1,96,8]{1,2,0:T(8,128)} %bitcast.417), channel_id=1, replica_groups=mesh['dp'=8,'seq'=32] {'seq'}, dimensions={0}, use_global_device_ids=true | all-gather | bytes 101376 | tf_op jit(solution)/shard_map/all_gather | solution.py:205
  418.2 1.8 reshape.870
  420.0 1.9 fusion.389
  424.2 5.5 fusion.386
  429.7 2.5 copy.506
  432.3 5.6 fusion.385
  437.8 2.5 copy.507
  445.9 4.5 copy.509
  450.4 2.5 copy.510
  452.9 20.4 %conditional.12 = (f32[48,8,128]{2,0,1:T(8,128)}, f32[48,8,128]{2,0,1:T(8,128)}) conditional(s32[]{:T(128)} %convert_element_type.340, () %tuple.118, (f32[8]{0:T(128)}, s32[48]{0:T(128)}, s32[32,1,48]{2,1,0:T(1,128)}, bf16[1536,8,128]{2,1,0:T(8,128)(2,1)}, bf16[48,8,128]{2,0,1:T(8,128)(2,1)}, /*index=5*/f32[1536,8]{0,1:T(8,128)}, ...), branch_computations={%region_50.51_spmd, %region_51.52_spmd} | conditional | flops 608821248 | bytes 20527388 | solution.py:30
  453.4 2.0 reduce.36
  457.6 4.8 fusion.155
  462.4 6.6 fusion.162
  469.0 4.3 fusion.165
  473.3 20.3 %conditional.13 = ((f32[48,8,128]{2,0,1:T(8,128)}, f32[48,8,128]{2,0,1:T(8,128)})) conditional(s32[]{:T(128)} %convert_element_type.339, (f32[48,8,128]{2,0,1:T(8,128)}, f32[48,8,128]{2,0,1:T(8,128)}) %conditional.12, (f32[8]{0:T(128)}, s32[48]{0:T(128)}, s32[32,1,48]{2,1,0:T(1,128)S(1)}, bf16[1536,8,128]{2,1,0:T(8,128)(2,1)}, ...), branch_computations={%region_52.53_spmd, %region_53.54_spmd} | conditional | flops 608919552 | bytes 20920612 | solution.py:30
  477.8 4.8 fusion.185
  482.6 6.7 fusion.195
  489.3 4.4 fusion.203
  495.2 20.5 %conditional.14 = (f32[48,8,128]{2,0,1:T(8,128)}, f32[48,8,128]{2,0,1:T(8,128)}) conditional(s32[]{:T(128)} %convert_element_type.346, () %tuple.121, (f32[8]{0:T(128)}, s32[48]{0:T(128)}, s32[32,1,48]{2,1,0:T(1,128)}, bf16[1536,8,128]{2,1,0:T(8,128)(2,1)}, bf16[48,8,128]{2,0,1:T(8,128)(2,1)}, /*index=5*/f32[1536,8]{0,1:T(8,128)}, ...), branch_computations={%region_55.56_spmd, %region_56.57_spmd} | conditional | flops 608821248 | bytes 20527388 | solution.py:30
  495.8 2.0 reduce.38
  500.0 4.8 fusion.223
  504.7 6.6 fusion.230
  511.3 4.3 fusion.233
  515.7 19.3 %conditional.15 = ((f32[48,8,128]{2,0,1:T(8,128)}, f32[48,8,128]{2,0,1:T(8,128)})) conditional(s32[]{:T(128)} %convert_element_type.345, (f32[48,8,128]{2,0,1:T(8,128)}, f32[48,8,128]{2,0,1:T(8,128)}) %conditional.14, (f32[8]{0:T(128)}, s32[48]{0:T(128)}, s32[32,1,48]{2,1,0:T(1,128)S(1)}, bf16[1536,8,128]{2,1,0:T(8,128)(2,1)}, ...), branch_computations={%region_57.58_spmd, %region_58.59_spmd} | conditional | flops 608919552 | bytes 20920768 | solution.py:30
  519.2 4.9 fusion.253
  524.0 6.6 fusion.263
  530.6 4.4 fusion.271
  543.3 74.4 %psum.23 = f32[8]{0:T(128)S(1)} all-reduce(f32[8]{0:T(128)S(1)} %multiply_add_fusion), channel_id=1, replica_groups=mesh['dp'=8,'seq'=32] {'dp','seq'}, use_global_device_ids=true, to_apply=%region_64.65 | all-reduce | flops 8 | bytes 64 | tf_op jit(solution)/shard_map/psum | solution.py:279
  621.1 2.6 fusion.308
  626.3 1.8 mul.568
  649.6 2.1 fusion.333
  651.6 2.6 fusion.325
  654.3 251.0 %all-reduce.4.cloned.1.call-done = (bf16[256,8,128]{0,2,1:T(8,128)(2,1)}, bf16[256,8,128]{2,0,1:T(8,128)(2,1)}) async-done(((bf16[256,8,128]{0,2,1:T(8,128)(2,1)}, bf16[256,8,128]{2,0,1:T(8,128)(2,1)}), (bf16[256,8,128]{0,2,1:T(8,128)(2,1)}, bf16[256,8,128]{2,0,1:T(8,128)(2,1)})) %all-reduce.4.cloned.1.call-update) | async-done | bytes 1048592 | tf_op jit(solution)/shard_map/psum | solution.py:276
  905.3 2.5 fusion.296
  909.1 3.3 fusion.289
  (432 shorter events, 141.3 us)
Async XLA Ops:
  7.2 206.8 %all-gather.10.cloned.1.call-start = ((), (), s32[]{:S(2)}) async-start(), calls=%async_computation | async-start | bytes 6488064 | tf_op jit(solution)/shard_map/all_gather | solution.py:176
  8.9 4.5 copy-start.126
  8.9 5.7 copy-start.124
  9.7 212.6 %all-gather.14.cloned.1.call-start = ((), (), s32[]{:S(2)}) async-start(), calls=%async_computation.2 | async-start | bytes 6488064 | tf_op jit(solution)/shard_map/all_gather | solution.py:177
  10.5 413.7 %all-gather.12.cloned.1.call-start = ((), (), s32[]{:S(2)}) async-start(), calls=%async_computation.1 | async-start | bytes 6488064 | tf_op jit(solution)/shard_map/all_gather | solution.py:209
  10.6 166.1 %copy-start.125 = (f32[8]{0:T(128)S(1)}, f32[8]{0:T(128)}, u32[]{:S(2)}) copy-start(f32[8]{0:T(128)} %param.37) | copy-start | bytes 100
  10.6 166.6 %copy-start.58 = (bf16[1,256,1024]{2,1,0:T(8,128)(2,1)S(1)}, bf16[1,256,1024]{2,1,0:T(8,128)(2,1)}, u32[]{:S(2)}) copy-start(bf16[1,256,1024]{2,1,0:T(8,128)(2,1)} %param.28) | copy-start | bytes 1572868
  11.7 165.7 %copy-start.80 = (f32[96,8]{0,1:T(8,128)}, f32[96,8]{0,1:T(8,128)S(1)}, u32[]{:S(2)}) copy-start(f32[96,8]{0,1:T(8,128)S(1)} %add_rsqrt_fusion.3) | copy-start | bytes 9220
  12.7 165.8 %copy-start.21 = (bf16[1,96,1024]{2,1,0:T(8,128)(2,1)S(1)}, bf16[1,96,1024]{2,1,0:T(8,128)(2,1)}, u32[]{:S(2)}) copy-start(bf16[1,96,1024]{2,1,0:T(8,128)(2,1)} %param.35) | copy-start | bytes 589828
  12.8 419.5 %all-gather.16.cloned.1.call-start = ((), (), s32[]{:S(2)}) async-start(), calls=%async_computation.3 | async-start | bytes 6488064 | tf_op jit(solution)/shard_map/all_gather | solution.py:210
  13.3 892.0 %all-reduce.4.cloned.1.call-start = ((), (), s32[]{:S(2)}) async-start(), calls=%async_computation.4 | async-start | bytes 2097152 | tf_op jit(solution)/shard_map/psum | solution.py:276
  175.0 4.9 copy-start.49
  178.5 6.0 copy-start.22
  181.2 4.3 copy-start.120
  185.4 6.2 copy-start.115
  185.6 5.3 copy-start.61
  199.8 3.8 copy-start.60
  199.8 3.8 copy-start.66
  201.8 10.6 %copy-start.14 = (bf16[96,8,128]{2,0,1:T(8,128)(2,1)}, bf16[96,8,128]{2,0,1:T(8,128)(2,1)S(1)}, u32[]{:S(2)}) copy-start(bf16[96,8,128]{2,0,1:T(8,128)(2,1)S(1)} %fusion.348) | copy-start | bytes 589828
  206.9 4.9 copy-start.121
  206.9 4.9 copy-start.123
  208.2 5.0 copy-start.78
  243.2 5.0 copy-start.107
  243.2 5.0 copy-start.111
  243.3 5.1 copy-start.99
  243.3 5.1 copy-start.103
  243.3 5.1 copy-start.2
  243.3 5.1 copy-start.43
  263.2 5.0 copy-start.91
  263.2 5.0 copy-start.95
  263.2 5.0 copy-start.83
  263.2 5.0 copy-start.87
  263.2 5.7 copy-start.3
  263.2 5.7 copy-start.28
  283.3 5.1 copy-start.109
  283.4 5.1 copy-start.113
  283.4 5.2 copy-start.101
  283.4 5.2 copy-start.105
  283.4 5.2 copy-start
  283.4 5.2 copy-start.45
  302.8 5.0 copy-start.93
  302.9 5.0 copy-start.97
  302.9 5.0 copy-start.85
  302.9 5.0 copy-start.89
  302.9 5.7 copy-start.1
  302.9 5.7 copy-start.30
  445.9 4.5 copy-start.4
  519.2 4.9 copy-start.72
  619.9 3.8 copy-start.79
  623.7 7.7 copy-start.42
  623.7 10.1 %copy-start.37 = (f32[48,8,128]{2,0,1:T(8,128)S(1)}, f32[48,8,128]{2,0,1:T(8,128)}, u32[]{:S(2)}) copy-start(f32[48,8,128]{2,0,1:T(8,128)} %get-tuple-element.1028) | copy-start | bytes 589828
  623.7 10.9 %copy-start.32 = (f32[48,8,128]{2,0,1:T(8,128)S(1)}, f32[48,8,128]{2,0,1:T(8,128)}, u32[]{:S(2)}) copy-start(f32[48,8,128]{2,0,1:T(8,128)} %get-tuple-element.1027) | copy-start | bytes 589828
  623.8 11.6 %copy-start.8 = (f32[12,8,8,128]{3,2,1,0:T(8,128)S(1)}, f32[12,8,8,128]{3,2,1,0:T(8,128)}, u32[]{:S(2)}) copy-start(f32[12,8,8,128]{3,2,1,0:T(8,128)} %copy-done.7) | copy-start | bytes 1179652
  623.8 11.6 %copy-start.81 = (f32[96,8]{0,1:T(8,128)S(1)}, f32[96,8]{0,1:T(8,128)}, u32[]{:S(2)}) copy-start(f32[96,8]{0,1:T(8,128)} %copy-done.80) | copy-start | bytes 9220
  623.8 11.6 %copy-start.82 = (f32[96,8]{0,1:T(8,128)S(1)}, f32[96,8]{0,1:T(8,128)}, u32[]{:S(2)}) copy-start(f32[96,8]{0,1:T(8,128)} %get-tuple-element.1073) | copy-start | bytes 9220
  625.3 10.1 %copy-start.47 = (f32[48,8,128]{2,0,1:T(8,128)S(1)}, f32[48,8,128]{2,0,1:T(8,128)}, u32[]{:S(2)}) copy-start(f32[48,8,128]{2,0,1:T(8,128)} %get-tuple-element.1020) | copy-start | bytes 589828
  628.1 8.9 copy-start.63
  632.2 5.9 copy-start.64
  638.0 11.6 %copy-start.24 = (bf16[1,96,1024]{2,1,0:T(8,128)(2,1)S(1)}, bf16[1,96,1024]{2,1,0:T(8,128)(2,1)}, u32[]{:S(2)}) copy-start(bf16[1,96,1024]{2,1,0:T(8,128)(2,1)} %param.33) | copy-start | bytes 589828
  639.0 12.6 %copy-start.26 = (bf16[1,96,1024]{2,1,0:T(8,128)(2,1)S(1)}, bf16[1,96,1024]{2,1,0:T(8,128)(2,1)}, u32[]{:S(2)}) copy-start(bf16[1,96,1024]{2,1,0:T(8,128)(2,1)} %param.32) | copy-start | bytes 589828
  639.0 12.6 %copy-start.48 = (f32[1,96,1024]{2,1,0:T(8,128)S(1)}, f32[1,96,1024]{2,1,0:T(8,128)}, u32[]{:S(2)}) copy-start(f32[1,96,1024]{2,1,0:T(8,128)} %mul.544) | copy-start | bytes 1179652
  639.0 12.6 %copy-start.119 = (f32[1024]{0:T(1024)S(1)}, f32[1024]{0:T(1024)}, u32[]{:S(2)}) copy-start(f32[1024]{0:T(1024)} %broadcast_bitcast_fusion) | copy-start | bytes 12292
  649.6 255.7 %copy-start.20 = (bf16[1,256,1024]{1,2,0:T(8,128)(2,1)S(1)}, bf16[1,256,1024]{1,2,0:T(8,128)(2,1)}, u32[]{:S(2)}) copy-start(bf16[1,256,1024]{1,2,0:T(8,128)(2,1)} %copy.493) | copy-start | bytes 1572868
  649.6 255.7 %copy-start.118 = (f32[8,256]{1,0:T(8,128)S(1)}, f32[8,256]{1,0:T(8,128)}, u32[]{:S(2)}) copy-start(f32[8,256]{1,0:T(8,128)} %copy-done.117) | copy-start | bytes 24580
  (68 other events, 117.0 us)
Sparse Core Ops, SparseCore 0:
  11.1 73.8 all-gather.9
  87.6 67.6 all-gather.13
  157.8 66.7 all-gather.11
  227.1 66.8 all-gather.15
  623.9 281.3 all-reduce.3
where the time goes:
time: 933 us; the launch traced here: 920 us
  blocking collectives  314 us (34%)
  waiting for transfers between devices  252 us (27%)
  matrix products  142 us (15%)
  local copies, waits for them, and re-layouts  138 us (15%)
  other arithmetic  45.1 us (5%)
  between operations  25.8 us (3%)
    psum x1, waiting for transfers between devices, body(): lax.psum(coarse_part[0].astype(jnp.bfloat16), 'seq').astype(jnp.float32)  251 us
    unnamed x1, blocking collectives  147 us
    psum x1, blocking collectives, body(): scale_total = lax.psum(scale_part, ('dp', 'seq'))  74.4 us
    all_gather x1, blocking collectives, body(): lax.all_gather(denominator, 'seq', axis=0, tiled=True)  48.2 us
    unnamed x142, local copies, waits for them, and re-layouts  46.2 us
    all_gather x1, blocking collectives, body(): lax.all_gather(mean_dprob, 'seq', axis=0, tiled=True)  45.1 us
    dot_general x12, matrix products, score_block(): jnp.einsum('qhd,khd->hqk', query_unit, key_unit, preferred_element_type=j...  41.9 us
    dot_general x6, matrix products, key_terms(): jnp.einsum('hqk,qhd->khd', dscore.astype(jnp.bfloat16), query_unit, prefe...  32.3 us
  transfers between devices with their start and end apart: 5, of which 1 were waited for; matrix products, arithmetic and copies ran while one was open for 20% of the time, Pallas kernels for 0%

commit v1 on v0

v1 whole, which is shorter than its diff:
```python
import math

import jax
import jax.numpy as jnp
from jax import lax
from jax.experimental import pallas as pl
from jax.experimental.pallas import tpu as pltpu
from jax.sharding import PartitionSpec as P

norm_eps = 1e-06
log2_e = 1.4426950408889634
k_tile = 256
note_rows = 16

planes = 4


def dot_nt(left, right):
    return lax.dot_general(
        left, right, (((1,), (1,)), ((), ())), preferred_element_type=jnp.float32
    )


def dot_nn(left, right):
    return jnp.dot(left, right, preferred_element_type=jnp.float32)


def unit_rows(rows):
    wide = rows.astype(jnp.float32)
    inv_norm = lax.rsqrt(jnp.sum(wide * wide, axis=-1, keepdims=True) + norm_eps)
    return wide * inv_norm, inv_norm


def project(key_rows, grad):
    key_dir, key_inv = unit_rows(key_rows)
    along = jnp.sum(key_dir * grad, axis=-1, keepdims=True)
    return key_inv * (grad - key_dir * along)


def fold_rows(terms):
    rows, width = terms.shape
    return jnp.sum(terms.reshape(rows // 8, 8, width), axis=0)


def seq_place():
    here = lax.axis_index("seq")
    plane = lax.shift_right_logical(here, 3)
    head = lax.bitwise_and(here, 7)
    group = lax.bitwise_and(plane - lax.shift_right_logical(head, 1), 3)
    return plane, head, group


def params(mebibytes):
    return pltpu.CompilerParams(vmem_limit_bytes=mebibytes * 1024 * 1024)


def pack_kernel(ids_ref, k_ref, v_ref, q_ref, cot_ref, all_ref):
    heads, _, width = all_ref.shape
    rows = k_ref.shape[0]
    ids = ids_ref[...]
    row = lax.broadcasted_iota(jnp.int32, (note_rows, width), 0)
    lane = lax.broadcasted_iota(jnp.int32, (note_rows, width), 1)
    note = jnp.zeros((note_rows, width), jnp.float32)
    for level in range(2):
        count = jnp.sum(jnp.where(ids <= level, 1.0, 0.0), axis=-1, keepdims=True)
        note = jnp.where((row == level) & (lane == 0), count, note)
    note = note.astype(jnp.bfloat16)
    first_query = 2 * rows + note_rows
    for head in range(heads):
        lanes = slice(head * width, (head + 1) * width)
        all_ref[head, 0:rows] = k_ref[:, lanes]
        all_ref[head, rows : 2 * rows] = v_ref[:, lanes]
        all_ref[head, 2 * rows : first_query] = note
        all_ref[head, first_query : first_query + rows] = q_ref[:, lanes]
        all_ref[head, first_query + rows :] = cot_ref[:, lanes]


def run_pack(heads, ids, keys, values, queries, cots):
    rows, features = keys.shape
    shape = (heads, 4 * rows + note_rows, features // heads)
    return pl.pallas_call(
        pack_kernel,
        out_shape=jax.ShapeDtypeStruct(shape, jnp.bfloat16),
        compiler_params=params(56),
        name="pack_heads",
    )(ids, keys, values, queries, cots)


def fine_kernel(
    log_ref,
    own_ref,
    kv1_ref,
    kv2_ref,
    kv3_ref,
    kc_ref,
    vc_ref,
    coarse_scale_ref,
    od_ref,
    dkv0_ref,
    dkv1_ref,
    dkv2_ref,
    dkv3_ref,
    scale_ref,
    key_scr,
    val_scr,
    query_scr,
    cot_scr,
    limit_scr,
    sum_scr,
    mean_scr,
    grad_scr,
    query_turn,
    cot_turn,
    prob_scr,
    turn_scr,
):
    plane, head, group = seq_place()
    members, _, width = own_ref.shape
    rows = od_ref.shape[1] // 2
    coarse = kc_ref.shape[0]
    queries = members * rows
    fine = planes * queries
    total = coarse + fine
    block = 2 * rows
    blocks = members // 2
    first_query = 2 * rows + note_rows
    half = queries // 2

    def block_start(owner, part):
        return (lax.bitwise_and(owner + part, 3) * members + 2 * part) * rows

    notes = jnp.zeros((note_rows, width), jnp.float32)
    for step, ref in enumerate((own_ref, kv1_ref, kv2_ref, kv3_ref)):
        owner = lax.bitwise_and(group - step, 3)
        notes = notes + jnp.sum(ref[:, 2 * rows : first_query].astype(jnp.float32), axis=0)
        for part in range(blocks):
            pick = slice(2 * part, 2 * part + 2)
            spot = pl.ds(pl.multiple_of(coarse + block_start(owner, part), 64), block)
            key_scr[spot, :] = unit_rows(ref[pick, 0:rows].reshape(block, width))[0].astype(
                jnp.bfloat16
            )
            val_scr[spot, 0:width] = ref[pick, rows : 2 * rows].reshape(block, width)
    val_scr[:, width:] = jnp.ones((total, width), jnp.bfloat16)
    key_scr[0:coarse, :] = kc_ref[...]
    val_scr[0:coarse, 0:width] = vc_ref[...]
    ends = [jnp.sum(notes[level : level + 1]).astype(jnp.int32) for level in range(2)]

    def limit_of(place):
        return jnp.where(place < ends[0], ends[0], jnp.where(place < ends[1], ends[1], fine))

    def rows_of(part):
        spot = lax.bitwise_and(group + part, 3) * block
        return pl.ds(pl.multiple_of(spot, 64), block)

    def own_query(part):
        pick = own_ref[2 * part : 2 * part + 2, first_query : first_query + rows]
        return unit_rows(pick.reshape(block, width))

    for part in range(blocks):
        pick = slice(2 * part, 2 * part + 2)
        spot = rows_of(part)
        query_scr[spot, :] = own_query(part)[0].astype(jnp.bfloat16)
        cot_scr[spot, :] = own_ref[pick, first_query + rows :].reshape(block, width)
        place = block_start(group, part) + lax.broadcasted_iota(jnp.int32, (block, width), 0)
        limit_scr[spot, :] = limit_of(place) + coarse

    sharp = jnp.exp(jnp.full((1, width), log_ref[head], jnp.float32))[:, 0:1]
    slope = sharp * log2_e
    sum_scr[...] = jnp.zeros_like(sum_scr)
    grad_scr[...] = jnp.zeros_like(grad_scr)

    def twice(column):
        return jnp.concatenate([column, column], axis=1)

    def keys_of(chunk):
        return pl.ds(pl.multiple_of(chunk * k_tile, k_tile), k_tile)

    def probs(chunk, first):
        cosine = dot_nt(query_scr[first:, :], key_scr[keys_of(chunk), :])
        prob = jnp.exp2(cosine * slope - slope)
        place = chunk * k_tile + lax.broadcasted_iota(jnp.int32, (1, k_tile), 1)
        prob = jnp.where(place < twice(limit_scr[first:, :]), prob, 0.0).astype(jnp.bfloat16)
        prob_scr[chunk, first:, :] = prob
        sum_scr[first:, :] += dot_nn(prob, val_scr[keys_of(chunk), :])

    def grads(chunk, first):
        prob = prob_scr[chunk, first:, :]
        dprob = dot_nt(cot_scr[first:, :], val_scr[keys_of(chunk), 0:width])
        dscore = prob.astype(jnp.float32) * (dprob - twice(mean_scr[first:, :]))
        dscore = dscore.astype(jnp.bfloat16)
        grad_scr[first:, :] += dot_nn(dscore, key_scr[keys_of(chunk), :])
        dk = dot_nn(query_turn[:, first:], dscore)
        dv = dot_nn(cot_turn[:, first:], prob)
        turn_scr[keys_of(chunk), 0:width] = jnp.transpose(dk).astype(jnp.bfloat16)
        turn_scr[keys_of(chunk), width:] = jnp.transpose(dv).astype(jnp.bfloat16)

    def all_chunks(work):
        last = (members + 2 * lax.bitwise_and(1 - group, 3)) * rows + block - 1
        shared = (limit_of(last) + coarse + k_tile - 1) // k_tile

        def both(chunk, carry):
            work(chunk, 0)
            return carry

        def upper(chunk, carry):
            work(chunk, half)
            return carry

        lax.fori_loop(0, shared, both, 0)
        lax.fori_loop(shared, total // k_tile, upper, 0)

    all_chunks(probs)

    r_den = 1.0 / sum_scr[:, width:]
    outs = sum_scr[:, :width] * r_den
    cot = cot_scr[...].astype(jnp.float32)
    mean_scr[...] = jnp.broadcast_to(
        jnp.sum(outs * cot, axis=-1, keepdims=True), mean_scr.shape
    )
    sum_scr[:, :width] = outs
    query_turn[...] = jnp.transpose(
        query_scr[...].astype(jnp.float32) * (r_den * sharp)
    ).astype(jnp.bfloat16)
    cot_turn[...] = jnp.transpose(cot * r_den).astype(jnp.bfloat16)

    all_chunks(grads)

    leading = jnp.where(plane == 0, 1.0, 0.0)
    scale = coarse_scale_ref[pl.ds(pl.multiple_of(head * 8, 8), 8), :] * leading
    for part in range(blocks):
        pick = slice(2 * part, 2 * part + 2)
        spot = rows_of(part)
        q_dir, q_inv = own_query(part)
        grad = grad_scr[spot, :] * (sharp / sum_scr[spot, width:])
        along = jnp.sum(q_dir * grad, axis=-1, keepdims=True)
        scale = scale + fold_rows(query_scr[spot, :].astype(jnp.float32) * grad)
        dq = (q_inv * (grad - q_dir * along)).astype(jnp.bfloat16)
        od_ref[pick, 0:rows] = sum_scr[spot, :width].astype(jnp.bfloat16).reshape(2, rows, width)
        od_ref[pick, rows:] = dq.reshape(2, rows, width)
    scale_ref[...] = scale

    small = coarse // planes
    for step, ref in enumerate((dkv0_ref, dkv1_ref, dkv2_ref, dkv3_ref)):
        owner = lax.bitwise_and(group + step, 3)
        target = lax.bitwise_and(plane + step, 3)
        for part in range(blocks):
            spot = pl.ds(pl.multiple_of(coarse + block_start(owner, part), 64), block)
            ref[part * block : (part + 1) * block, :] = turn_scr[spot, :]
        ref[queries:, :] = turn_scr[pl.ds(pl.multiple_of(target * small, 64), small), :]


def run_fine(log_scale, own_rows, kv_parts, key_coarse, val_coarse, coarse_scale):
    members, tall, width = own_rows.shape
    rows = (tall - note_rows) // 4
    coarse = key_coarse.shape[0]
    queries = members * rows
    total = coarse + planes * queries
    vmem = pl.BlockSpec(memory_space=pltpu.VMEM)
    low = jnp.bfloat16
    wide = jnp.float32
    return pl.pallas_call(
        fine_kernel,
        out_shape=(jax.ShapeDtypeStruct((members, 2 * rows, width), low),)
        + (jax.ShapeDtypeStruct((total // planes, 2 * width), low),) * 4
        + (jax.ShapeDtypeStruct((8, width), wide),),
        in_specs=[pl.BlockSpec(memory_space=pltpu.SMEM)] + [vmem] * 7,
        out_specs=(vmem,) * 6,
        scratch_shapes=[
            pltpu.VMEM((total, width), low),
            pltpu.VMEM((total, 2 * width), low),
            pltpu.VMEM((queries, width), low),
            pltpu.VMEM((queries, width), low),
            pltpu.VMEM((queries, width), jnp.int32),
            pltpu.VMEM((queries, 2 * width), wide),
            pltpu.VMEM((queries, width), wide),
            pltpu.VMEM((queries, width), wide),
            pltpu.VMEM((width, queries), low),
            pltpu.VMEM((width, queries), low),
            pltpu.VMEM((total // k_tile, queries, k_tile), low),
            pltpu.VMEM((total, 2 * width), low),
        ],
        compiler_params=params(28),
        cost_estimate=pl.CostEstimate(
            flops=12 * queries * total * width,
            bytes_accessed=8 * total * width,
            transcendentals=queries * total,
        ),
        name="fine_attention",
    )(log_scale, own_rows, *kv_parts, key_coarse, val_coarse, coarse_scale)


def coarse_kernel(
    log_ref,
    row_level_ref,
    col_level_ref,
    q_ref,
    k_ref,
    v_ref,
    cot_ref,
    out_ref,
    dq_ref,
    dk_ref,
    dv_ref,
    scale_ref,
    key_low_ref,
    value_ref,
):
    _, own, _ = seq_place()
    count, features = q_ref.shape
    heads = log_ref.shape[0]
    width = features // heads
    visible = col_level_ref[...] <= row_level_ref[...]
    for head in range(heads):
        lanes = slice(head * width, (head + 1) * width)
        sharp = jnp.exp(jnp.full((1, width), log_ref[head], jnp.float32))[:, 0:1]
        slope = sharp * log2_e
        q_dir, q_inv = unit_rows(q_ref[:, lanes])
        q_low = q_dir.astype(jnp.bfloat16)
        key_low = unit_rows(k_ref[:, lanes])[0].astype(jnp.bfloat16)
        values = v_ref[:, lanes]
        cot = cot_ref[:, lanes]
        prob = jnp.exp2(dot_nt(q_low, key_low) * slope - slope)
        prob = jnp.where(visible, prob, 0.0)
        r_den = 1.0 / jnp.sum(prob, axis=-1, keepdims=True)
        norm_prob = prob * r_den
        dprob = dot_nt(cot, values)
        mean = jnp.sum(norm_prob * dprob, axis=-1, keepdims=True)
        dscore = (norm_prob * (dprob - mean)).astype(jnp.bfloat16)
        norm_low = norm_prob.astype(jnp.bfloat16)
        out_ref[:, lanes] = dot_nn(norm_low, values).astype(jnp.bfloat16)
        grad = sharp * dot_nn(dscore, key_low)
        along = jnp.sum(q_dir * grad, axis=-1, keepdims=True)
        dq_ref[:, lanes] = (q_inv * (grad - q_dir * along)).astype(jnp.bfloat16)
        scale_ref[head * 8 : head * 8 + 8, :] = fold_rows(q_low.astype(jnp.float32) * grad)
        q_turned = jnp.transpose(q_dir).astype(jnp.bfloat16)
        cot_turned = jnp.transpose(cot.astype(jnp.float32)).astype(jnp.bfloat16)
        dk_ref[:, lanes] = sharp * jnp.transpose(dot_nn(q_turned, dscore))
        dv_ref[:, lanes] = jnp.transpose(dot_nn(cot_turned, norm_low))

        @pl.when(own == head)
        def _():
            key_low_ref[...] = key_low
            value_ref[...] = values


def run_coarse(log_scale, levels, queries, keys, values, cots):
    count, features = queries.shape
    heads = log_scale.shape[0]
    width = features // heads
    vmem = pl.BlockSpec(memory_space=pltpu.VMEM)
    wide = jax.ShapeDtypeStruct((count, features), jnp.float32)
    low = jax.ShapeDtypeStruct((count, features), jnp.bfloat16)
    return pl.pallas_call(
        coarse_kernel,
        out_shape=(low, low, wide, wide, jax.ShapeDtypeStruct((heads * 8, width), jnp.float32))
        + (jax.ShapeDtypeStruct((count, width), jnp.bfloat16),) * 2,
        in_specs=[pl.BlockSpec(memory_space=pltpu.SMEM)] + [vmem] * 6,
        compiler_params=params(16),
        cost_estimate=pl.CostEstimate(
            flops=12 * count * count * features,
            bytes_accessed=24 * count * features,
            transcendentals=heads * count * count,
        ),
        name="coarse_attention",
    )(log_scale, levels[:, None], levels[None, :], queries, keys, values, cots)


def sum_kernel(term0_ref, term1_ref, term2_ref, term3_ref, own_ref, scale_in_ref, dkv_ref, small_ref):
    members, pair, width = dkv_ref.shape
    rows = pair // 2
    fine = members * rows
    summed = term0_ref[...].astype(jnp.float32)
    for ref in (term1_ref, term2_ref, term3_ref):
        summed = summed + ref[...].astype(jnp.float32)
    grad = project(own_ref[:, 0:rows].reshape(fine, width), summed[:fine, :width])
    dkv_ref[:, 0:rows] = grad.astype(jnp.bfloat16).reshape(members, rows, width)
    dkv_ref[:, rows:] = summed[:fine, width:].astype(jnp.bfloat16).reshape(members, rows, width)
    small = summed.shape[0] - fine
    small_ref[0:small, :] = summed[fine:].astype(jnp.bfloat16)
    left = jnp.sum(scale_in_ref[...], axis=0, keepdims=True)
    left = jnp.sum(left, axis=-1, keepdims=True)
    row = lax.broadcasted_iota(jnp.int32, (note_rows, 2 * width), 0)
    note = jnp.zeros((note_rows, 2 * width), jnp.float32)
    for part in range(3):
        piece = left.astype(jnp.bfloat16).astype(jnp.float32)
        note = jnp.where(row == part, piece, note)
        left = left - piece
    small_ref[small:, :] = note.astype(jnp.bfloat16)


def run_sum(terms, own_rows, scales):
    count, both = terms[0].shape
    members, tall, width = own_rows.shape
    pair = (tall - note_rows) // 2
    small = count - members * pair // 2
    return pl.pallas_call(
        sum_kernel,
        out_shape=(
            jax.ShapeDtypeStruct((members, pair, width), jnp.bfloat16),
            jax.ShapeDtypeStruct((small + note_rows, both), jnp.bfloat16),
        ),
        compiler_params=params(12),
        name="sum_key_terms",
    )(*terms, own_rows, scales)


def join_kernel(terms_ref, dk_own_ref, dv_own_ref, k_ref, dk_ref, dv_ref, scale_ref):
    _, heads, tall, both = terms_ref.shape
    width = both // 2
    small = tall - note_rows
    for head in range(heads):
        lanes = slice(head * width, (head + 1) * width)
        terms = terms_ref[:, head].astype(jnp.float32)
        scale_ref[head : head + 1, :] = jnp.sum(
            jnp.sum(terms[:, small:, :width], axis=0), axis=0, keepdims=True
        )
        terms = terms[:, :small].reshape(planes * small, both)
        grad = terms[:, :width] + dk_own_ref[:, lanes]
        dk_ref[:, lanes] = project(k_ref[:, lanes], grad).astype(jnp.bfloat16)
        dv_ref[:, lanes] = (terms[:, width:] + dv_own_ref[:, lanes]).astype(jnp.bfloat16)


def run_join(terms, dk_own, dv_own, keys):
    _, heads, _, both = terms.shape
    count, features = keys.shape
    low = jax.ShapeDtypeStruct((count, features), jnp.bfloat16)
    return pl.pallas_call(
        join_kernel,
        out_shape=(low, low, jax.ShapeDtypeStruct((heads, both // 2), jnp.float32)),
        compiler_params=params(14),
        name="join_coarse",
    )(terms, dk_own, dv_own, keys)


def unpack_kernel(od_ref, dkv_ref, out_ref, dq_ref, dk_ref, dv_ref):
    heads, pair, width = od_ref.shape
    rows = pair // 2
    for head in range(heads):
        lanes = slice(head * width, (head + 1) * width)
        out_ref[:, lanes] = od_ref[head, 0:rows]
        dq_ref[:, lanes] = od_ref[head, rows:]
        dk_ref[:, lanes] = dkv_ref[head, 0:rows]
        dv_ref[:, lanes] = dkv_ref[head, rows:]


def run_unpack(od_back, dkv_back):
    heads, pair, width = od_back.shape
    flat = jax.ShapeDtypeStruct((pair // 2, heads * width), jnp.bfloat16)
    return pl.pallas_call(
        unpack_kernel,
        out_shape=(flat,) * 4,
        compiler_params=params(4),
        name="unpack_heads",
    )(od_back, dkv_back)


def body(
    q_coarse,
    k_coarse,
    v_coarse,
    cot_coarse,
    coarse_ids,
    q_fine,
    k_fine,
    v_fine,
    cot_fine,
    fine_ids,
    log_scale,
):
    heads = log_scale.shape[0]
    coarse = q_coarse.shape[1]
    rows = q_fine.shape[1]
    seq = lax.axis_size("seq")
    images = lax.axis_size("dp")
    groups = [
        [((g + h // 2) % planes) * heads + h for h in range(heads)] for g in range(planes)
    ]

    def exchange(parts):
        return lax.all_to_all(parts, "seq", 0, 0, axis_index_groups=groups, tiled=True)

    def to_plane(array, step):
        return lax.ppermute(
            array, "seq", [(i, (i + step * heads) % seq) for i in range(seq)]
        )

    own_rows = exchange(run_pack(heads, fine_ids, k_fine[0], v_fine[0], q_fine[0], cot_fine[0]))
    kv_own = own_rows[:, : 2 * rows + note_rows]
    kv_rows = [to_plane(kv_own, step) for step in range(1, planes)]

    out_c, dq_c, dk_own, dv_own, scale_c, key_c, val_c = run_coarse(
        log_scale, coarse_ids[0], q_coarse[0], k_coarse[0], v_coarse[0], cot_coarse[0]
    )
    od, *dkv, scale = run_fine(log_scale, own_rows, kv_rows, key_c, val_c, scale_c)

    terms = [dkv[0]] + [to_plane(dkv[step], step) for step in range(1, planes)]
    scales = lax.all_gather(scale, "dp", axis=0, tiled=True)
    od_back = exchange(od)
    dkv_parts, small_terms = run_sum(terms, own_rows, scales)
    dkv_back = exchange(dkv_parts)
    of_image = lax.all_gather(small_terms, "seq", axis=0)
    of_image = of_image.reshape((planes, heads) + small_terms.shape)
    dk_c, dv_c, scale_rows = run_join(of_image, dk_own, dv_own, k_coarse[0])
    fine_out, fine_dq, fine_dk, fine_dv = run_unpack(od_back, dkv_back)
    grad_scale = scale_rows[:, 0] / math.sqrt(images * (coarse + seq * rows))
    return (
        out_c[None],
        dq_c[None],
        dk_c[None],
        dv_c[None],
        fine_out[None],
        fine_dq[None],
        fine_dk[None],
        fine_dv[None],
        grad_scale,
    )


def solution(mesh):
    whole = P("dp", None, None)
    split = P("dp", "seq", None)
    return jax.shard_map(
        body,
        mesh=mesh,
        in_specs=(whole,) * 4 + (P("dp", None),) + (split,) * 4 + (P("dp", "seq"), P()),
        out_specs=(whole,) * 4 + (split,) * 4 + (P(),),
        check_vma=False,
    )
```

time: 933 us -> 186 us (0.20); the launches traced: 920 us -> 184 us
  waiting for transfers between devices: 252 us -> 15 us
  blocking collectives: 314 us -> 113 us
  matrix products: 142 us -> 0 us
  local copies, waits for them, and re-layouts: 138 us -> 7.69 us
  other arithmetic: 45.1 us -> 0.63 us
  Pallas kernels: 0 us -> 30.3 us
  between operations: 25.8 us -> 14.1 us
    psum x1 -> x0, waiting for transfers between devices: 251 us -> none  [body(): lax.psum(coarse_part[0].astype(jnp.bfloat16), 'seq').astype(jnp.float32)]
    unnamed x1 -> x0, blocking collectives: 147 us -> none
    dot_general x52 -> x0, matrix products: 142 us -> none  [the longest x12 41.9 us: score_block(): jnp.einsum('qhd,khd->hqk', query_unit, key_unit, preferred_element_type=j...]
    all_to_all x0 -> x3, blocking collectives: none -> 89.8 us  [exchange(): lax.all_to_all(parts, 'seq', 0, 0, axis_index_groups=groups, tiled=True)]
    psum x1 -> x0, blocking collectives: 74.4 us -> none  [body(): scale_total = lax.psum(scale_part, ('dp', 'seq'))]
    all_gather x2 -> x1, blocking collectives: 93.3 us -> 22.8 us  [body(): scales = lax.all_gather(scale, 'dp', axis=0, tiled=True)]
    unnamed x142 -> x20, local copies, waits for them, and re-layouts: 46.2 us -> 6.11 us
    pallas_call x0 -> x6, Pallas kernels: none -> 30.3 us  [the longest x1 16.4 us: run_fine(): pl.pallas_call(fine_kernel, out_shape=(jax.ShapeDtypeStruct((members, 2 *...]
  transfers between devices with their start and end apart: 5 -> 7, of which waited for: 1 -> 2; matrix products, arithmetic and copies ran while one was open for 20% -> 0% of each run, Pallas kernels for 0% -> 5%
where the time goes in v1:
time: 186 us; the launch traced here: 184 us
  blocking collectives  113 us (61%)
  Pallas kernels  30.3 us (16%)
  waiting for transfers between devices  15 us (8%)
  between operations  14.1 us (8%)
  local copies, waits for them, and re-layouts  7.69 us (4%)
  starting transfers between devices  4.26 us (2%)
    all_to_all x3, blocking collectives, exchange(): lax.all_to_all(parts, 'seq', 0, 0, axis_index_groups=groups, tiled=True)  89.8 us
    all_gather x1, blocking collectives, body(): scales = lax.all_gather(scale, 'dp', axis=0, tiled=True)  22.8 us
    pallas_call x1, Pallas kernels, run_fine(): pl.pallas_call(fine_kernel, out_shape=(jax.ShapeDtypeStruct((members, 2 *...  16.4 us
    ppermute x6, waiting for transfers between devices, to_plane(): lax.ppermute(array, 'seq', [(i, (i + step * heads) % seq) for i in range(...  9.35 us
    pallas_call x1, Pallas kernels, run_coarse(): pl.pallas_call(coarse_kernel, out_shape=(low, low, wide, wide, jax.ShapeD...  7.79 us
    unnamed x20, local copies, waits for them, and re-layouts  6.11 us
    all_gather x1, waiting for transfers between devices, body(): of_image = lax.all_gather(small_terms, 'seq', axis=0)  5.62 us
    ppermute x6, starting transfers between devices, to_plane(): lax.ppermute(array, 'seq', [(i, (i + step * heads) % seq) for i in range(...  4.22 us
  transfers between devices with their start and end apart: 7, of which 2 were waited for; matrix products, arithmetic and copies ran while one was open for 0% of the time, Pallas kernels for 5%

profile of v1, /device:TPU:1, one launch (start us, length us, event | category | flops | bytes accessed | tf_op | source)
XLA Modules:
  0.0 184.5 jit_solution(11889209802064598594)
XLA Ops:
  7.2 0.0 all-gather.3.cloned.1.call-start
  7.2 2.3 %pack_heads.1 = bf16[8,400,128]{2,1,0:T(8,128)(2,1)} custom-call(s32[1,96]{1,0:T(1,128)} %ids_ref.1, bf16[96,1024]{1,0:T(8,128)(2,1)} %bitcast.25, bf16[96,1024]{1,0:T(8,128)(2,1)} %bitcast.26, bf16[96,1024]{1,0:T(8,128)(2,1)} %bitcast.27, bf16[96,1024]{1,0:T(8,128)(2,1)} %bitcast.28), custom_call_target="tpu_custom_call" | custom-call | tf_op jit(solution)/shard_map/pack_heads/pallas_call | solution.py:81
  9.5 0.0 copy-start.5
  9.5 0.0 copy-start.1
  9.5 0.0 copy-start.9
  9.5 38.9 %all_to_all.15.own_ref = bf16[8,400,128]{2,1,0:T(8,128)(2,1)S(1)} all-to-all(bf16[8,400,128]{2,1,0:T(8,128)(2,1)} %pack_heads.1), channel_id=1, replica_groups={{0,1,10,11,20,21,30,31},{8,9,18,19,28,29,6,7},{16,17,26,27,4,5,14,15},{..., dimensions={0} | all-to-all | bytes 1638400 | tf_op jit(solution)/shard_map/all_to_all | solution.py:480
  48.4 0.8 slice.8
  49.1 0.8 collective-permute-start.2
  49.9 0.6 collective-permute-start.1
  50.5 0.1 collective-permute-start
  50.6 0.0 copy-done.5
  50.6 0.8 copy.20.row_level_ref
  51.4 0.0 copy-done.1
  51.4 0.0 copy-done.9
  51.4 0.0 copy-start.4
  51.4 0.9 copy-done.4
  52.3 0.0 copy-start.6
  52.3 1.0 copy-done.6
  53.4 0.0 copy-start.7
  53.4 1.0 copy-done.7
  54.4 0.0 copy-start.8
  54.4 1.0 copy-done.8
  55.4 7.8 %coarse_attention.1 = (bf16[256,1024]{1,0:T(8,128)(2,1)}, bf16[256,1024]{1,0:T(8,128)(2,1)}, f32[256,1024]{1,0:T(8,128)S(1)}, f32[256,1024]{1,0:T(8,128)S(1)}, f...) custom-call(f32[8]{0:T(128)S(1)} %copy-done.9, s32[256,1]{1,0:T(8,128)S(1)} %copy-done.4, ...), custom_call_target="tpu_custom_call" | custom-call | flops 805306368 | bytes 6291456 | tf_op jit(solution)/shard_map/coarse_attention/pallas_call | solution.py:353
  63.2 0.0 collective-permute-done.2.kv3_ref
  63.2 0.0 collective-permute-done.1.kv2_ref
  63.2 9.3 %collective-permute-done.kv1_ref = bf16[8,208,128]{2,1,0:T(8,128)(2,1)} collective-permute-done((bf16[8,208,128]{2,1,0:T(8,128)(2,1)}, bf16[8,208,128]{2,1,0:T(8,128)(2,1)}, u32[]{:S(2)}, u32[]{:S(2)}) %collective-permute-start) | collective-permute-done | bytes 426016 | tf_op jit(solution)/shard_map/ppermute | solution.py:483
  72.6 16.4 %fine_attention.1 = (bf16[8,192,128]{2,1,0:T(8,128)(2,1)S(1)}, bf16[832,256]{1,0:T(8,128)(2,1)S(1)}, bf16[832,256]{1,0:T(8,128)(2,1)S(1)}, bf16[832,256]{1,0:T(8...) custom-call(f32[8]{0:T(128)S(1)} %copy-done.9, bf16[8,400,128]{2,1,0:T(8,128)(2,1)S(1)} %all_to_all.15.own_ref, ...), custom_call_target="tpu_custom_call" | custom-call | flops 3925868544 | bytes 3407872 | tf_op jit(solution)/shard_map/fine_attention/pallas_call | solution.py:261
  89.0 0.0 copy-start.2
  89.0 0.1 collective-permute-start.3
  89.1 0.9 collective-permute-start.4
  90.0 1.8 collective-permute-start.5
  91.8 22.8 %all_gather.9.scale_in_ref = f32[64,128]{1,0:T(8,128)S(1)} all-gather(f32[8,128]{1,0:T(8,128)S(1)} %get-tuple-element.40), channel_id=1, replica_groups=mesh['dp'=8,'seq'=32] {'dp'}, dimensions={0}, use_global_device_ids=true | all-gather | bytes 36864 | tf_op jit(solution)/shard_map/all_gather | solution.py:497
  114.5 0.0 collective-permute-done.3.term1_ref
  114.5 0.0 collective-permute-done.4.term2_ref
  114.5 0.0 collective-permute-done.5.term3_ref
  114.5 0.9 sum_key_terms.1
  115.5 0.0 copy-done.2
  115.5 0.0 copy-start.3
  115.5 0.7 copy-done.3
  116.2 0.0 all-gather.3.cloned.1.call-update
  116.3 28.3 %all_to_all.16.od_ref = bf16[8,192,128]{2,1,0:T(8,128)(2,1)S(1)} all-to-all(bf16[8,192,128]{2,1,0:T(8,128)(2,1)} %copy-done.2), channel_id=1, replica_groups={{0,1,10,11,20,21,30,31},{8,9,18,19,28,29,6,7},{16,17,26,27,4,5,14,15},{..., dimensions={0} | all-to-all | bytes 786432 | tf_op jit(solution)/shard_map/all_to_all | solution.py:480
  144.6 22.6 %all_to_all.17.dkv_ref = bf16[8,192,128]{2,1,0:T(8,128)(2,1)S(1)} all-to-all(bf16[8,192,128]{2,1,0:T(8,128)(2,1)} %copy-done.3), channel_id=1, replica_groups={{0,1,10,11,20,21,30,31},{8,9,18,19,28,29,6,7},{16,17,26,27,4,5,14,15},{..., dimensions={0} | all-to-all | bytes 786432 | tf_op jit(solution)/shard_map/all_to_all | solution.py:480
  167.2 1.1 unpack_heads.1
  168.3 5.6 %all-gather.3.cloned.1.call-done = bf16[2560,256]{1,0:T(8,128)(2,1)} async-done(((bf16[80,256]{1,0:T(8,128)(2,1)}), bf16[2560,256]{1,0:T(8,128)(2,1)}) %all-gather.3.cloned.1.call-update) | async-done | bytes 1310736 | tf_op jit(solution)/shard_map/all_gather | solution.py:501
  173.9 0.0 copy-start
  173.9 1.3 copy-done
  175.2 1.8 join_coarse.1
  177.0 0.6 multiply_reduce_fusion
Async XLA Ops:
  7.2 166.7 %all-gather.3.cloned.1.call-start = ((), (), s32[]{:S(2)}) async-start(), calls=%async_computation.3 | async-start | bytes 1351680 | tf_op jit(solution)/shard_map/all_gather | solution.py:501
  9.5 41.1 %copy-start.5 = (s32[1,256]{1,0:T(1,128)S(1)}, s32[1,256]{1,0:T(1,128)}, u32[]{:S(2)}) copy-start(s32[1,256]{1,0:T(1,128)} %col_level_ref.1) | copy-start | bytes 3076
  9.5 41.9 %copy-start.1 = (bf16[1,256,1024]{2,1,0:T(8,128)(2,1)S(1)}, bf16[1,256,1024]{2,1,0:T(8,128)(2,1)}, u32[]{:S(2)}) copy-start(bf16[1,256,1024]{2,1,0:T(8,128)(2,1)} %param.12) | copy-start | bytes 1572868
  9.5 41.9 %copy-start.9 = (f32[8]{0:T(128)S(1)}, f32[8]{0:T(128)}, u32[]{:S(2)}) copy-start(f32[8]{0:T(128)} %log_ref.3) | copy-start | bytes 100
  49.1 14.1 %collective-permute-start.2 = (bf16[8,208,128]{2,1,0:T(8,128)(2,1)}, bf16[8,208,128]{2,1,0:T(8,128)(2,1)}, u32[]{:S(2)}, u32[]{:S(2)}) collective-permute-start(bf16[8,208,128]{2,1,0:T(8,128)(2,1)} %slice.8), channel_id=1, source_target_pairs={{0,24},{1,25},{2,26},{3,27},{4,28},{5,29},{6,30},{7,31},{8,0},{9,1... | collective-permute-start | bytes 1277960 | tf_op jit(solution)/shard_map/ppermute | solution.py:483
  49.9 13.3 %collective-permute-start.1 = (bf16[8,208,128]{2,1,0:T(8,128)(2,1)}, bf16[8,208,128]{2,1,0:T(8,128)(2,1)}, u32[]{:S(2)}, u32[]{:S(2)}) collective-permute-start(bf16[8,208,128]{2,1,0:T(8,128)(2,1)} %slice.8), channel_id=1, source_target_pairs={{0,16},{1,17},{2,18},{3,19},{4,20},{5,21},{6,22},{7,23},{8,24},{9,... | collective-permute-start | bytes 1277960 | tf_op jit(solution)/shard_map/ppermute | solution.py:483
  50.5 22.1 %collective-permute-start = (bf16[8,208,128]{2,1,0:T(8,128)(2,1)}, bf16[8,208,128]{2,1,0:T(8,128)(2,1)}, u32[]{:S(2)}, u32[]{:S(2)}) collective-permute-start(bf16[8,208,128]{2,1,0:T(8,128)(2,1)} %slice.8), channel_id=1, source_target_pairs={{0,8},{1,9},{2,10},{3,11},{4,12},{5,13},{6,14},{7,15},{8,16},{9,17... | collective-permute-start | bytes 1277960 | tf_op jit(solution)/shard_map/ppermute | solution.py:483
  51.4 0.9 copy-start.4
  52.3 1.0 copy-start.6
  53.4 1.0 copy-start.7
  54.4 1.0 copy-start.8
  89.0 26.5 %copy-start.2 = (bf16[8,192,128]{2,1,0:T(8,128)(2,1)}, bf16[8,192,128]{2,1,0:T(8,128)(2,1)S(1)}, u32[]{:S(2)}) copy-start(bf16[8,192,128]{2,1,0:T(8,128)(2,1)S(1)} %get-tuple-element.46) | copy-start | bytes 1179652
  89.0 25.5 %collective-permute-start.3 = (bf16[832,256]{1,0:T(8,128)(2,1)S(1)}, bf16[832,256]{1,0:T(8,128)(2,1)S(1)}, u32[]{:S(2)}, u32[]{:S(2)}) collective-permute-start(bf16[832,256]{1,0:T(8,128)(2,1)S(1)} %get-tuple-element.37), channel_id=1, source_target_pairs={{0,8},{1,9},{2,10},{3,11},{4,12},{5,13},{6,14},{7,15},{8,16},{9,17... | collective-permute-start | bytes 1277960 | tf_op jit(solution)/shard_map/ppermute | solution.py:483
  89.1 25.4 %collective-permute-start.4 = (bf16[832,256]{1,0:T(8,128)(2,1)S(1)}, bf16[832,256]{1,0:T(8,128)(2,1)S(1)}, u32[]{:S(2)}, u32[]{:S(2)}) collective-permute-start(bf16[832,256]{1,0:T(8,128)(2,1)S(1)} %get-tuple-element.38), channel_id=1, source_target_pairs={{0,16},{1,17},{2,18},{3,19},{4,20},{5,21},{6,22},{7,23},{8,24},{9,... | collective-permute-start | bytes 1277960 | tf_op jit(solution)/shard_map/ppermute | solution.py:483
  90.0 24.6 %collective-permute-start.5 = (bf16[832,256]{1,0:T(8,128)(2,1)S(1)}, bf16[832,256]{1,0:T(8,128)(2,1)S(1)}, u32[]{:S(2)}, u32[]{:S(2)}) collective-permute-start(bf16[832,256]{1,0:T(8,128)(2,1)S(1)} %get-tuple-element.39), channel_id=1, source_target_pairs={{0,24},{1,25},{2,26},{3,27},{4,28},{5,29},{6,30},{7,31},{8,0},{9,1... | collective-permute-start | bytes 1277960 | tf_op jit(solution)/shard_map/ppermute | solution.py:483
  115.5 0.7 copy-start.3
  173.9 1.3 copy-start
Sparse Core Ops, SparseCore 0:
  116.4 57.4 all-gather.2

commit v2 on v1

v2 whole, which is shorter than its diff:
```python
import math

import jax
import jax.numpy as jnp
from jax import lax
from jax.experimental import pallas as pl
from jax.experimental.pallas import tpu as pltpu
from jax.sharding import PartitionSpec as P

norm_eps = 1e-06
log2_e = 1.4426950408889634
k_tile = 256
note_rows = 16

planes = 4


def dot_nt(left, right):
    return lax.dot_general(
        left, right, (((1,), (1,)), ((), ())), preferred_element_type=jnp.float32
    )


def dot_nn(left, right):
    return jnp.dot(left, right, preferred_element_type=jnp.float32)


def unit_rows(rows):
    wide = rows.astype(jnp.float32)
    inv_norm = lax.rsqrt(jnp.sum(wide * wide, axis=-1, keepdims=True) + norm_eps)
    return wide * inv_norm, inv_norm


def project(key_rows, grad):
    key_dir, key_inv = unit_rows(key_rows)
    along = jnp.sum(key_dir * grad, axis=-1, keepdims=True)
    return key_inv * (grad - key_dir * along)


def fold_rows(terms):
    rows, width = terms.shape
    return jnp.sum(terms.reshape(rows // 8, 8, width), axis=0)


def in_pieces(value, width):
    row = lax.broadcasted_iota(jnp.int32, (note_rows, width), 0)
    note = jnp.zeros((note_rows, width), jnp.float32)
    for part in range(3):
        piece = value.astype(jnp.bfloat16).astype(jnp.float32)
        note = jnp.where(row == part, piece, note)
        value = value - piece
    return note.astype(jnp.bfloat16)


def sum_all(terms):
    return jnp.sum(jnp.sum(terms, axis=0, keepdims=True), axis=-1, keepdims=True)


def seq_place():
    here = lax.axis_index("seq")
    plane = lax.bitwise_and(lax.shift_right_logical(here, 1), 3)
    head = 2 * lax.shift_right_logical(here, 3) + lax.bitwise_and(here, 1)
    return plane, head


def key_slot(plane):
    return lax.bitwise_and(plane, 1)


def query_slot(plane):
    return lax.shift_right_logical(plane, 1)


def params(mebibytes):
    return pltpu.CompilerParams(vmem_limit_bytes=mebibytes * 1024 * 1024)


def pack_kernel(ids_ref, k_ref, v_ref, q_ref, cot_ref, all_ref):
    heads, _, width = all_ref.shape
    rows = k_ref.shape[0]
    ids = ids_ref[...]
    row = lax.broadcasted_iota(jnp.int32, (note_rows, width), 0)
    lane = lax.broadcasted_iota(jnp.int32, (note_rows, width), 1)
    note = jnp.zeros((note_rows, width), jnp.float32)
    for level in range(2):
        count = jnp.sum(jnp.where(ids <= level, 1.0, 0.0), axis=-1, keepdims=True)
        note = jnp.where((row == level) & (lane == 0), count, note)
    note = note.astype(jnp.bfloat16)
    first_query = 2 * rows + note_rows
    for head in range(heads):
        lanes = slice(head * width, (head + 1) * width)
        all_ref[head, 0:rows] = k_ref[:, lanes]
        all_ref[head, rows : 2 * rows] = v_ref[:, lanes]
        all_ref[head, 2 * rows : first_query] = note
        all_ref[head, first_query : first_query + rows] = q_ref[:, lanes]
        all_ref[head, first_query + rows :] = cot_ref[:, lanes]


def run_pack(heads, ids, keys, values, queries, cots):
    rows, features = keys.shape
    shape = (heads, 4 * rows + note_rows, features // heads)
    return pl.pallas_call(
        pack_kernel,
        out_shape=jax.ShapeDtypeStruct(shape, jnp.bfloat16),
        compiler_params=params(56),
        name="pack_heads",
    )(ids, keys, values, queries, cots)


def twice(column):
    return jnp.concatenate([column, column], axis=1)


def wide_as(column, size):
    return column if size == column.shape[1] else twice(column)


def place_of(run, slot, block):
    return pl.multiple_of((2 * run + slot) * block, 64)


def key_spot(first, size):
    return pl.ds(first if isinstance(first, int) else pl.multiple_of(first, 128), size)


def all_chunks(work, some_keys, shared, chunks):
    work(0, some_keys, 0)

    def both(chunk, carry):
        work(some_keys + chunk * k_tile, k_tile, 0)
        return carry

    def upper(chunk, carry):
        work(some_keys + chunk * k_tile, k_tile, 1)
        return carry

    lax.fori_loop(0, shared, both, 0)
    lax.fori_loop(shared, chunks, upper, 0)


def forward_kernel(
    log_ref,
    own_ref,
    kv_ref,
    qc_ref,
    kc_ref,
    vc_ref,
    prob_ref,
    key_ref,
    val_ref,
    query_ref,
    cot_ref,
    num_ref,
    stat_ref,
    shared_ref,
    wide_scr,
    limit_scr,
    sum_scr,
):
    plane, head = seq_place()
    members, tall, width = own_ref.shape
    rows = (tall - note_rows) // 4
    block = 2 * rows
    runs = members // 2
    queries = query_ref.shape[0]
    some_keys = kc_ref.shape[0] // 2
    fine = key_ref.shape[0] - some_keys
    first_query = 2 * rows + note_rows

    def count(notes):
        total = jnp.sum(notes.astype(jnp.float32), axis=0)
        return [jnp.sum(total[level : level + 1]).astype(jnp.int32) for level in range(2)]

    own_counts = count(own_ref[:, 2 * rows : first_query])
    key_counts = [a + b for a, b in zip(own_counts, count(kv_ref[:, 2 * rows :]))]
    query_counts = [a + b for a, b in zip(own_counts, count(qc_ref[:, :note_rows]))]

    def limit_of(place):
        return jnp.where(
            place < query_counts[0],
            key_counts[0],
            jnp.where(place < query_counts[1], key_counts[1], fine),
        )

    own_slot = key_slot(plane)
    for ref, slot in ((own_ref, own_slot), (kv_ref, 1 - own_slot)):
        for run in range(runs):
            pick = slice(2 * run, 2 * run + 2)
            spot = pl.ds(pl.multiple_of(some_keys + place_of(run, slot, block), 64), block)
            key_ref[spot, :] = unit_rows(ref[pick, 0:rows].reshape(block, width))[0].astype(
                jnp.bfloat16
            )
            values = ref[pick, rows : 2 * rows].reshape(block, width)
            val_ref[spot, :] = values
            wide_scr[spot, 0:width] = values
    half = pl.ds(pl.multiple_of(query_slot(plane) * some_keys, some_keys), some_keys)
    key_ref[0:some_keys, :] = kc_ref[half, :]
    val_ref[0:some_keys, :] = vc_ref[half, :]
    wide_scr[0:some_keys, 0:width] = vc_ref[half, :]
    wide_scr[:, width:] = jnp.ones((some_keys + fine, width), jnp.bfloat16)

    own_slot = query_slot(plane)
    for ref, slot, start in ((own_ref, own_slot, first_query), (qc_ref, 1 - own_slot, note_rows)):
        for run in range(runs):
            pick = slice(2 * run, 2 * run + 2)
            spot = pl.ds(place_of(run, slot, block), block)
            query_ref[spot, :] = unit_rows(
                ref[pick, start : start + rows].reshape(block, width)
            )[0].astype(jnp.bfloat16)
            cot_ref[spot, :] = ref[pick, start + rows : start + 2 * rows].reshape(block, width)
    limit_scr[...] = some_keys + limit_of(
        lax.broadcasted_iota(jnp.int32, (queries, width), 0)
    )

    sharp = jnp.exp(jnp.full((1, width), log_ref[head], jnp.float32))[:, 0:1]
    slope = sharp * log2_e
    sum_scr[...] = jnp.zeros_like(sum_scr)

    def probs(start, size, part):
        first = part * queries // 2
        spot = key_spot(start, size)
        cosine = dot_nt(query_ref[first:, :], key_ref[spot, :])
        prob = jnp.exp2(cosine * slope - slope)
        place = start + lax.broadcasted_iota(jnp.int32, (1, size), 1)
        seen = place < wide_as(limit_scr[first:, :], size)
        prob = jnp.where(seen, prob, 0.0).astype(jnp.bfloat16)
        prob_ref[first:, spot] = prob
        sum_scr[first:, :] += dot_nn(prob, wide_scr[spot, :])

    shared = (limit_of(queries // 2 - 1) + k_tile - 1) // k_tile
    shared_ref[0] = shared
    all_chunks(probs, some_keys, shared, fine // k_tile)

    num = sum_scr[:, :width]
    num_ref[...] = num
    weighted = jnp.sum(num * cot_ref[...].astype(jnp.float32), axis=-1, keepdims=True)
    row = lax.broadcasted_iota(jnp.int32, (width, width), 0)
    lane = lax.broadcasted_iota(jnp.int32, (width, width), 1)
    parts = queries // width
    for part in range(parts):
        spot = slice(part * width, (part + 1) * width)
        for index, value in ((part, sum_scr[spot, width:]), (parts + part, weighted[spot])):
            stat_ref[index : index + 1, :] = jnp.sum(
                jnp.where(row == lane, value, 0.0), axis=0, keepdims=True
            )


def backward_kernel(
    log_ref,
    shared_ref,
    own_ref,
    qc_ref,
    stat_ref,
    other_stat_ref,
    prob_ref,
    key_ref,
    val_ref,
    query_ref,
    cot_ref,
    num_ref,
    coarse_scale_ref,
    od_ref,
    od_send_ref,
    dkv_ref,
    dkv_send_ref,
    small_ref,
    den_scr,
    mean_scr,
    grad_scr,
    query_turn,
    cot_turn,
    turn_scr,
):
    plane, head = seq_place()
    members, tall, width = own_ref.shape
    rows = (tall - note_rows) // 4
    block = 2 * rows
    runs = members // 2
    queries = query_ref.shape[0]
    first_query = 2 * rows + note_rows
    some_keys = small_ref.shape[0] - note_rows
    fine = key_ref.shape[0] - some_keys
    sharp = jnp.exp(jnp.full((1, width), log_ref[head], jnp.float32))[:, 0:1]

    row = lax.broadcasted_iota(jnp.int32, (width, width), 0)
    lane = lax.broadcasted_iota(jnp.int32, (width, width), 1)
    parts = queries // width

    def column(index):
        values = stat_ref[index : index + 1, :] + other_stat_ref[index : index + 1, :]
        return jnp.sum(jnp.where(row == lane, values, 0.0), axis=1, keepdims=True)

    for part in range(parts):
        spot = slice(part * width, (part + 1) * width)
        r_den = 1.0 / column(part)
        den_scr[spot, :] = jnp.broadcast_to(r_den, (width, width))
        mean_scr[spot, :] = jnp.broadcast_to(column(parts + part) * r_den, (width, width))

    grad_scr[...] = jnp.zeros_like(grad_scr)
    query_turn[...] = jnp.transpose(
        query_ref[...].astype(jnp.float32) * (den_scr[...] * sharp)
    ).astype(jnp.bfloat16)
    cot_turn[...] = jnp.transpose(cot_ref[...].astype(jnp.float32) * den_scr[...]).astype(
        jnp.bfloat16
    )

    def grads(start, size, part):
        first = part * queries // 2
        spot = key_spot(start, size)
        prob = prob_ref[first:, spot]
        dprob = dot_nt(cot_ref[first:, :], val_ref[spot, :])
        dscore = prob.astype(jnp.float32) * (dprob - wide_as(mean_scr[first:, :], size))
        dscore = dscore.astype(jnp.bfloat16)
        grad_scr[first:, :] += dot_nn(dscore, key_ref[spot, :])
        dk = dot_nn(query_turn[:, first:], dscore)
        dv = dot_nn(cot_turn[:, first:], prob)
        turn_scr[spot, 0:width] = jnp.transpose(dk).astype(jnp.bfloat16)
        turn_scr[spot, width:] = jnp.transpose(dv).astype(jnp.bfloat16)

    all_chunks(grads, some_keys, shared_ref[0], fine // k_tile)

    own_slot = query_slot(plane)
    scale = coarse_scale_ref[pl.ds(pl.multiple_of(head * 8, 8), 8), :]
    scale = scale * jnp.where(plane == 0, 1.0, 0.0)
    for ref, slot, start, target in (
        (own_ref, own_slot, first_query, od_ref),
        (qc_ref, 1 - own_slot, note_rows, od_send_ref),
    ):
        for run in range(runs):
            spot = pl.ds(place_of(run, slot, block), block)
            pick = ref[2 * run : 2 * run + 2, start : start + rows]
            q_dir, q_inv = unit_rows(pick.reshape(block, width))
            r_den = den_scr[spot, :]
            grad = grad_scr[spot, :] * (r_den * sharp)
            along = jnp.sum(q_dir * grad, axis=-1, keepdims=True)
            scale = scale + fold_rows(query_ref[spot, :].astype(jnp.float32) * grad)
            to = slice(run * block, (run + 1) * block)
            target[to, 0:width] = (num_ref[spot, :] * r_den).astype(jnp.bfloat16)
            target[to, width:] = (q_inv * (grad - q_dir * along)).astype(jnp.bfloat16)

    own_slot = key_slot(plane)
    for slot, target in ((own_slot, dkv_ref), (1 - own_slot, dkv_send_ref)):
        for run in range(runs):
            spot = pl.ds(pl.multiple_of(some_keys + place_of(run, slot, block), 64), block)
            target[run * block : (run + 1) * block, :] = turn_scr[spot, :]
    small_ref[0:some_keys, :] = turn_scr[0:some_keys, :]
    small_ref[some_keys:, :] = in_pieces(sum_all(scale), 2 * width)


def run_fine(log_scale, own_rows, kv_rows, qc_rows, key_coarse, val_coarse, coarse_scale, swap):
    members, tall, width = own_rows.shape
    rows = (tall - note_rows) // 4
    some_keys = key_coarse.shape[0] // 2
    queries = 2 * members * rows
    total = some_keys + queries
    vmem = pl.BlockSpec(memory_space=pltpu.VMEM)
    smem = pl.BlockSpec(memory_space=pltpu.SMEM)

    def low(*shape):
        return jax.ShapeDtypeStruct(shape, jnp.bfloat16)

    def wide(*shape):
        return jax.ShapeDtypeStruct(shape, jnp.float32)

    prob, keys, values, query, cot, num, stat, shared = pl.pallas_call(
        forward_kernel,
        out_shape=(
            low(queries, total),
            low(total, width),
            low(total, width),
            low(queries, width),
            low(queries, width),
            wide(queries, width),
            wide(2 * queries // width, width),
            jax.ShapeDtypeStruct((1,), jnp.int32),
        ),
        in_specs=[smem] + [vmem] * 5,
        out_specs=(vmem,) * 7 + (smem,),
        scratch_shapes=[
            pltpu.VMEM((total, 2 * width), jnp.bfloat16),
            pltpu.VMEM((queries, width), jnp.int32),
            pltpu.VMEM((queries, 2 * width), jnp.float32),
        ],
        compiler_params=params(20),
        cost_estimate=pl.CostEstimate(
            flops=4 * queries * total * width,
            bytes_accessed=4 * queries * total,
            transcendentals=queries * total,
        ),
        name="fine_forward",
    )(log_scale, own_rows, kv_rows, qc_rows, key_coarse, val_coarse)
    other_stat = swap(stat)
    half = low(queries // 2, 2 * width)
    return pl.pallas_call(
        backward_kernel,
        out_shape=(half, half, half, half, low(some_keys + note_rows, 2 * width)),
        in_specs=[smem, smem] + [vmem] * 11,
        out_specs=(vmem,) * 5,
        scratch_shapes=[
            pltpu.VMEM((queries, width), jnp.float32),
            pltpu.VMEM((queries, width), jnp.float32),
            pltpu.VMEM((queries, width), jnp.float32),
            pltpu.VMEM((width, queries), jnp.bfloat16),
            pltpu.VMEM((width, queries), jnp.bfloat16),
            pltpu.VMEM((total, 2 * width), jnp.bfloat16),
        ],
        compiler_params=params(20),
        cost_estimate=pl.CostEstimate(
            flops=8 * queries * total * width,
            bytes_accessed=4 * queries * total,
            transcendentals=0,
        ),
        name="fine_backward",
    )(
        log_scale,
        shared,
        own_rows,
        qc_rows,
        stat,
        other_stat,
        prob,
        keys,
        values,
        query,
        cot,
        num,
        coarse_scale,
    )


def coarse_kernel(
    log_ref,
    row_level_ref,
    col_level_ref,
    q_ref,
    k_ref,
    v_ref,
    cot_ref,
    out_ref,
    dq_ref,
    dk_ref,
    dv_ref,
    scale_ref,
    key_low_ref,
    value_ref,
):
    _, own = seq_place()
    count, features = q_ref.shape
    heads = log_ref.shape[0]
    width = features // heads
    visible = col_level_ref[...] <= row_level_ref[...]
    for head in range(heads):
        lanes = slice(head * width, (head + 1) * width)
        sharp = jnp.exp(jnp.full((1, width), log_ref[head], jnp.float32))[:, 0:1]
        slope = sharp * log2_e
        q_dir, q_inv = unit_rows(q_ref[:, lanes])
        q_low = q_dir.astype(jnp.bfloat16)
        key_low = unit_rows(k_ref[:, lanes])[0].astype(jnp.bfloat16)
        values = v_ref[:, lanes]
        cot = cot_ref[:, lanes]
        prob = jnp.exp2(dot_nt(q_low, key_low) * slope - slope)
        prob = jnp.where(visible, prob, 0.0)
        r_den = 1.0 / jnp.sum(prob, axis=-1, keepdims=True)
        norm_prob = prob * r_den
        dprob = dot_nt(cot, values)
        mean = jnp.sum(norm_prob * dprob, axis=-1, keepdims=True)
        dscore = (norm_prob * (dprob - mean)).astype(jnp.bfloat16)
        norm_low = norm_prob.astype(jnp.bfloat16)
        out_ref[:, lanes] = dot_nn(norm_low, values).astype(jnp.bfloat16)
        grad = sharp * dot_nn(dscore, key_low)
        along = jnp.sum(q_dir * grad, axis=-1, keepdims=True)
        dq_ref[:, lanes] = (q_inv * (grad - q_dir * along)).astype(jnp.bfloat16)
        scale_ref[head * 8 : head * 8 + 8, :] = fold_rows(q_low.astype(jnp.float32) * grad)
        q_turned = jnp.transpose(q_dir).astype(jnp.bfloat16)
        cot_turned = jnp.transpose(cot.astype(jnp.float32)).astype(jnp.bfloat16)
        dk_ref[:, lanes] = sharp * jnp.transpose(dot_nn(q_turned, dscore))
        dv_ref[:, lanes] = jnp.transpose(dot_nn(cot_turned, norm_low))

        @pl.when(own == head)
        def _():
            key_low_ref[...] = key_low
            value_ref[...] = values


def run_coarse(log_scale, levels, queries, keys, values, cots):
    count, features = queries.shape
    heads = log_scale.shape[0]
    width = features // heads
    vmem = pl.BlockSpec(memory_space=pltpu.VMEM)
    wide = jax.ShapeDtypeStruct((count, features), jnp.float32)
    low = jax.ShapeDtypeStruct((count, features), jnp.bfloat16)
    return pl.pallas_call(
        coarse_kernel,
        out_shape=(low, low, wide, wide, jax.ShapeDtypeStruct((heads * 8, width), jnp.float32))
        + (jax.ShapeDtypeStruct((count, width), jnp.bfloat16),) * 2,
        in_specs=[pl.BlockSpec(memory_space=pltpu.SMEM)] + [vmem] * 6,
        compiler_params=params(16),
        cost_estimate=pl.CostEstimate(
            flops=12 * count * count * features,
            bytes_accessed=24 * count * features,
            transcendentals=heads * count * count,
        ),
        name="coarse_attention",
    )(log_scale, levels[:, None], levels[None, :], queries, keys, values, cots)


def small_kernel(own_ref, near_ref, across_ref, far_ref, sum_ref, scale_ref):
    plane, _ = seq_place()
    some_keys = own_ref.shape[0] - note_rows
    terms = [ref[...].astype(jnp.float32) for ref in (own_ref, near_ref, across_ref, far_ref)]
    half = query_slot(plane)
    for place, pair in ((half, terms[:2]), (1 - half, terms[2:])):
        spot = pl.ds(pl.multiple_of(place * some_keys, some_keys), some_keys)
        sum_ref[spot, :] = (pair[0][:some_keys] + pair[1][:some_keys]).astype(jnp.bfloat16)
    scale = terms[0][some_keys:] + terms[1][some_keys:] + terms[2][some_keys:] + terms[3][some_keys:]
    scale = jnp.sum(scale[:, : scale_ref.shape[2]], axis=0, keepdims=True)
    scale_ref[...] = jnp.broadcast_to(scale[None], scale_ref.shape)


def run_small(images, terms):
    tall, both = terms[0].shape
    return pl.pallas_call(
        small_kernel,
        out_shape=(
            jax.ShapeDtypeStruct((2 * (tall - note_rows), both), jnp.bfloat16),
            jax.ShapeDtypeStruct((images, 8, both // 2), jnp.float32),
        ),
        compiler_params=params(4),
        name="sum_coarse_terms",
    )(*terms)


def sum_kernel(od_ref, other_od_ref, dkv_ref, other_dkv_ref, own_ref, scale_ref, all_ref):
    members, tall, width = all_ref.shape
    rows = (tall - note_rows) // 4
    fine = members * rows

    def put(place, value):
        all_ref[:, place * rows : (place + 1) * rows] = value.astype(jnp.bfloat16).reshape(
            members, rows, width
        )

    summed = od_ref[...].astype(jnp.float32) + other_od_ref[...].astype(jnp.float32)
    put(0, summed[:, :width])
    put(1, summed[:, width:])
    summed = dkv_ref[...].astype(jnp.float32) + other_dkv_ref[...].astype(jnp.float32)
    put(2, project(own_ref[:, 0:rows].reshape(fine, width), summed[:, :width]))
    put(3, summed[:, width:])
    scale = jnp.sum(scale_ref[:, 0, 0:1], axis=0, keepdims=True)
    note = in_pieces(scale, width)
    for member in range(members):
        all_ref[member, 4 * rows :] = note


def run_sum(od, other_od, dkv, other_dkv, own_rows, scale):
    return pl.pallas_call(
        sum_kernel,
        out_shape=jax.ShapeDtypeStruct(own_rows.shape, jnp.bfloat16),
        compiler_params=params(10),
        name="sum_pairs",
    )(od, other_od, dkv, other_dkv, own_rows, scale)


def join_kernel(terms_ref, dk_own_ref, dv_own_ref, k_ref, dk_ref, dv_ref):
    heads, _, both = terms_ref.shape
    width = both // 2
    for head in range(heads):
        lanes = slice(head * width, (head + 1) * width)
        terms = terms_ref[head].astype(jnp.float32)
        grad = terms[:, :width] + dk_own_ref[:, lanes]
        dk_ref[:, lanes] = project(k_ref[:, lanes], grad).astype(jnp.bfloat16)
        dv_ref[:, lanes] = (terms[:, width:] + dv_own_ref[:, lanes]).astype(jnp.bfloat16)


def run_join(terms, dk_own, dv_own, keys):
    low = jax.ShapeDtypeStruct(keys.shape, jnp.bfloat16)
    return pl.pallas_call(
        join_kernel,
        out_shape=(low, low),
        compiler_params=params(14),
        name="join_coarse",
    )(terms, dk_own, dv_own, keys)


def unpack_kernel(all_ref, out_ref, dq_ref, dk_ref, dv_ref, scale_ref):
    heads, tall, width = all_ref.shape
    rows = (tall - note_rows) // 4
    for head in range(heads):
        lanes = slice(head * width, (head + 1) * width)
        for place, ref in enumerate((out_ref, dq_ref, dk_ref, dv_ref)):
            ref[:, lanes] = all_ref[head, place * rows : (place + 1) * rows]
    scale_ref[...] = jnp.sum(all_ref[:, 4 * rows :].astype(jnp.float32), axis=1)


def run_unpack(all_back):
    heads, tall, width = all_back.shape
    flat = jax.ShapeDtypeStruct(((tall - note_rows) // 4, heads * width), jnp.bfloat16)
    return pl.pallas_call(
        unpack_kernel,
        out_shape=(flat,) * 4 + (jax.ShapeDtypeStruct((heads, width), jnp.float32),),
        compiler_params=params(4),
        name="unpack_heads",
    )(all_back)


def body(
    q_coarse,
    k_coarse,
    v_coarse,
    cot_coarse,
    coarse_ids,
    q_fine,
    k_fine,
    v_fine,
    cot_fine,
    fine_ids,
    log_scale,
):
    heads = log_scale.shape[0]
    coarse = q_coarse.shape[1]
    rows = q_fine.shape[1]
    seq = lax.axis_size("seq")
    images = lax.axis_size("dp")
    groups = [
        [8 * (h // 2) + 2 * plane + h % 2 for h in range(heads)] for plane in range(planes)
    ]

    def exchange(parts):
        return lax.all_to_all(parts, "seq", 0, 0, axis_index_groups=groups, tiled=True)

    def to_plane(array, flip):
        return lax.ppermute(array, "seq", [(i, i ^ (2 * flip)) for i in range(seq)])

    own_rows = exchange(run_pack(heads, fine_ids, k_fine[0], v_fine[0], q_fine[0], cot_fine[0]))
    kv_rows = to_plane(own_rows[:, : 2 * rows + note_rows], 1)
    qc_rows = to_plane(own_rows[:, 2 * rows :], 3)

    out_c, dq_c, dk_own, dv_own, scale_c, key_c, val_c = run_coarse(
        log_scale, coarse_ids[0], q_coarse[0], k_coarse[0], v_coarse[0], cot_coarse[0]
    )
    od, od_send, dkv, dkv_send, small = run_fine(
        log_scale, own_rows, kv_rows, qc_rows, key_c, val_c, scale_c, lambda stat: to_plane(stat, 3)
    )

    small_sum, scale = run_small(images, [small] + [to_plane(small, flip) for flip in (1, 2, 3)])
    of_image = lax.all_gather(small_sum, "seq", axis=0, axis_index_groups=groups)

    other_dkv = to_plane(dkv_send, 1)
    other_od = to_plane(od_send, 3)
    scale = lax.all_to_all(scale, "dp", 0, 0, tiled=True)
    all_back = exchange(run_sum(od, other_od, dkv, other_dkv, own_rows, scale))
    fine_out, fine_dq, fine_dk, fine_dv, scale = run_unpack(all_back)
    dk_c, dv_c = run_join(of_image, dk_own, dv_own, k_coarse[0])
    grad_scale = scale[:, 0] / math.sqrt(images * (coarse + seq * rows))
    return (
        out_c[None],
        dq_c[None],
        dk_c[None],
        dv_c[None],
        fine_out[None],
        fine_dq[None],
        fine_dk[None],
        fine_dv[None],
        grad_scale,
    )


def solution(mesh):
    whole = P("dp", None, None)
    split = P("dp", "seq", None)
    return jax.shard_map(
        body,
        mesh=mesh,
        in_specs=(whole,) * 4 + (P("dp", None),) + (split,) * 4 + (P("dp", "seq"), P()),
        out_specs=(whole,) * 4 + (split,) * 4 + (P(),),
        check_vma=False,
    )
```

time: 186 us -> 145 us (0.78)
  blocking collectives: 113 us -> 56.5 us
  starting transfers between devices: 4.26 us -> 17.4 us
  local copies, waits for them, and re-layouts: 7.69 us -> 15.7 us
  waiting for transfers between devices: 15 us -> 11.3 us
    all_to_all x3 -> x2, blocking collectives: 89.8 us -> 37 us  [exchange(): lax.all_to_all(parts, 'seq', 0, 0, axis_index_groups=groups, tiled=True)]
    all_gather x1 -> x0, blocking collectives: 22.8 us -> none  [body(): scales = lax.all_gather(scale, 'dp', axis=0, tiled=True)]
    all_to_all x0 -> x1, blocking collectives: none -> 19.5 us  [body(): scale = lax.all_to_all(scale, 'dp', 0, 0, tiled=True)]
    ppermute x6 -> x8, starting transfers between devices: 4.22 us -> 17.4 us  [to_plane(): return lax.ppermute(array, 'seq', [(i, i ^ 2 * flip) for i in range(seq)])]
    unnamed x20 -> x34, local copies, waits for them, and re-layouts: 6.11 us -> 13.3 us
    all_gather x1, waiting for transfers between devices: 5.62 us -> 0.01 us  [body(): lax.all_gather(small_sum, 'seq', axis=0, axis_index_groups=groups)]
    ppermute x6 -> x8, waiting for transfers between devices: 9.35 us -> 11.3 us  [to_plane(): return lax.ppermute(array, 'seq', [(i, i ^ 2 * flip) for i in range(seq)])]
    pallas_call x4 -> x6, Pallas kernels: 20.2 us -> 18.4 us  [the longest x1 8.62 us: run_fine(): pl.pallas_call(backward_kernel, out_shape=(half, half, half, half, low(so...]
  transfers between devices with their start and end apart: 7 -> 9, of which waited for: 2 -> 5; matrix products, arithmetic and copies ran while one was open for 0% -> 1% of each run, Pallas kernels for 5% -> 6%
where the time goes in v2:
time: 145 us; the launch traced here: 144 us
  blocking collectives  56.5 us (39%)
  Pallas kernels  28.5 us (20%)
  starting transfers between devices  17.4 us (12%)
  local copies, waits for them, and re-layouts  15.7 us (11%)
  between operations  14.1 us (10%)
  waiting for transfers between devices  11.3 us (8%)
    all_to_all x2, blocking collectives, exchange(): lax.all_to_all(parts, 'seq', 0, 0, axis_index_groups=groups, tiled=True)  37 us
    all_to_all x1, blocking collectives, body(): scale = lax.all_to_all(scale, 'dp', 0, 0, tiled=True)  19.5 us
    ppermute x8, starting transfers between devices, to_plane(): return lax.ppermute(array, 'seq', [(i, i ^ 2 * flip) for i in range(seq)])  17.4 us
    unnamed x34, local copies, waits for them, and re-layouts  13.3 us
    ppermute x8, waiting for transfers between devices, to_plane(): return lax.ppermute(array, 'seq', [(i, i ^ 2 * flip) for i in range(seq)])  11.3 us
    pallas_call x1, Pallas kernels, run_fine(): pl.pallas_call(backward_kernel, out_shape=(half, half, half, half, low(so...  8.62 us
    pallas_call x1, Pallas kernels, run_coarse(): pl.pallas_call(coarse_kernel, out_shape=(low, low, wide, wide, jax.ShapeD...  7.79 us
    pallas_call x1, Pallas kernels, run_fine(): pl.pallas_call(forward_kernel, out_shape=(low(queries, total), low(total,...  6.37 us
  transfers between devices with their start and end apart: 9, of which 5 were waited for; matrix products, arithmetic and copies ran while one was open for 1% of the time, Pallas kernels for 6%

profile of v2, /device:TPU:1, one launch (start us, length us, event | category | flops | bytes accessed | tf_op | source)
XLA Modules:
  0.0 144.2 jit_solution(10363991116088400114)
XLA Ops:
  7.2 0.0 copy-start.16
  7.2 0.0 all-gather.3.cloned.1.call-start
  7.2 2.3 %pack_heads.1 = bf16[8,400,128]{2,1,0:T(8,128)(2,1)} custom-call(s32[1,96]{1,0:T(1,128)} %ids_ref.1, bf16[96,1024]{1,0:T(8,128)(2,1)} %bitcast.25, bf16[96,1024]{1,0:T(8,128)(2,1)} %bitcast.26, bf16[96,1024]{1,0:T(8,128)(2,1)} %bitcast.27, bf16[96,1024]{1,0:T(8,128)(2,1)} %bitcast.28), custom_call_target="tpu_custom_call" | custom-call | tf_op jit(solution)/shard_map/pack_heads/pallas_call | solution.py:102
  9.5 19.7 %all_to_all.15.own_ref = bf16[8,400,128]{2,1,0:T(8,128)(2,1)S(1)} all-to-all(bf16[8,400,128]{2,1,0:T(8,128)(2,1)} %pack_heads.1), channel_id=1, replica_groups={{0,1,8,9,16,17,24,25},{2,3,10,11,18,19,26,27},{4,5,12,13,20,21,28,29},{..., dimensions={0} | all-to-all | bytes 1638400 | tf_op jit(solution)/shard_map/all_to_all | solution.py:629
  29.2 1.0 fusion
  30.2 5.3 %collective-permute-start.1 = (bf16[8,208,128]{2,1,0:T(8,128)(2,1)}, bf16[8,208,128]{2,1,0:T(8,128)(2,1)}, u32[]{:S(2)}, u32[]{:S(2)}) collective-permute-start(bf16[8,208,128]{2,1,0:T(8,128)(2,1)} %get-tuple-element.67), channel_id=1, source_target_pairs={{0,6},{1,7},{2,4},{3,5},{4,2},{5,3},{6,0},{7,1},{8,14},{9,15},{10,... | collective-permute-start | bytes 1277960 | tf_op jit(solution)/shard_map/ppermute | solution.py:632
  35.5 1.2 collective-permute-start
  36.7 1.5 %copy.20.row_level_ref = s32[256,1]{1,0:T(8,128)} copy(s32[256,1]{0,1:T(1,128)} %bitcast.21) | data formatting | bytes 2048 | tf_op jit(solution)/shard_map/broadcast_in_dim;squeeze | solution.py:504
  38.1 0.0 copy-start.1
  38.2 1.0 copy-done.1
  39.2 0.0 copy-start.8
  39.2 0.9 copy-done.8
  40.1 0.0 copy-start.9
  40.1 0.7 copy-done.9
  40.8 0.0 copy-start.10
  40.8 1.0 copy-done.10
  41.8 0.0 copy-start.11
  41.8 1.0 copy-done.11
  42.9 0.0 copy-start.12
  42.9 1.0 copy-done.12
  43.9 0.0 copy-start.15
  43.9 0.7 copy-done.15
  44.6 7.8 %coarse_attention.1 = (bf16[256,1024]{1,0:T(8,128)(2,1)}, bf16[256,1024]{1,0:T(8,128)(2,1)}, f32[256,1024]{1,0:T(8,128)S(1)}, f32[256,1024]{1,0:T(8,128)S(1)}, f...) custom-call(f32[8]{0:T(128)S(1)} %copy-done.15, s32[256,1]{1,0:T(8,128)S(1)} %copy-done.8, ...), custom_call_target="tpu_custom_call" | custom-call | flops 805306368 | bytes 6291456 | tf_op jit(solution)/shard_map/coarse_attention/pallas_call | solution.py:492
  52.3 1.7 %collective-permute-done.1.qc_ref = bf16[8,208,128]{2,1,0:T(8,128)(2,1)} collective-permute-done((bf16[8,208,128]{2,1,0:T(8,128)(2,1)}, bf16[8,208,128]{2,1,0:T(8,128)(2,1)}, u32[]{:S(2)}, u32[]{:S(2)}) %collective-permute-start.1) | collective-permute-done | bytes 426016 | tf_op jit(solution)/shard_map/ppermute | solution.py:632
  54.0 1.5 %collective-permute-done.kv_ref = bf16[8,208,128]{2,1,0:T(8,128)(2,1)} collective-permute-done((bf16[8,208,128]{2,1,0:T(8,128)(2,1)}, bf16[8,208,128]{2,1,0:T(8,128)(2,1)}, u32[]{:S(2)}, u32[]{:S(2)}) %collective-permute-start) | collective-permute-done | bytes 426016 | tf_op jit(solution)/shard_map/ppermute | solution.py:632
  55.6 0.0 copy-done.16
  55.6 6.4 %fine_forward.1 = (bf16[1536,1664]{1,0:T(8,128)(2,1)S(1)}, bf16[1664,128]{1,0:T(8,128)(2,1)S(1)}, bf16[1664,128]{1,0:T(8,128)(2,1)S(1)}, bf16[1536,128]{1,0:T(8,...) custom-call(f32[8]{0:T(128)S(1)} %copy-done.16, ...), custom_call_target="tpu_custom_call" | custom-call | flops 1308622848 | bytes 10223616 | tf_op jit(solution)/shard_map/fine_forward/pallas_call | solution.py:365
  61.9 2.9 %collective-permute-start.2 = (f32[24,128]{1,0:T(8,128)S(1)}, f32[24,128]{1,0:T(8,128)S(1)}, u32[]{:S(2)}, u32[]{:S(2)}) collective-permute-start(f32[24,128]{1,0:T(8,128)S(1)} %get-tuple-element.43.stat_ref), channel_id=1, source_target_pairs={{0,6},{1,7},{2,4},{3,5},{4,2},{5,3},{6,0},{7,1},{8,14},{9,15},{10,... | collective-permute-start | bytes 36872 | tf_op jit(solution)/shard_map/ppermute | solution.py:632
  64.8 1.9 %collective-permute-done.2.other_stat_ref = f32[24,128]{1,0:T(8,128)S(1)} collective-permute-done((f32[24,128]{1,0:T(8,128)S(1)}, f32[24,128]{1,0:T(8,128)S(1)}, u32[]{:S(2)}, u32[]{:S(2)}) %collective-permute-start.2) | collective-permute-done | bytes 12320 | tf_op jit(solution)/shard_map/ppermute | solution.py:632
  66.7 8.6 %fine_backward.1 = (bf16[768,256]{1,0:T(8,128)(2,1)S(1)}, bf16[768,256]{1,0:T(8,128)(2,1)S(1)}, bf16[768,256]{1,0:T(8,128)(2,1)S(1)}, bf16[768,256]{1,0:T(8,128)(2,1)S(1)}, bf16[144,256]{1,0:T(8,128)(2,1)S(1)}) custom-call(f32[8]{0:T(128)S(1)} %copy-done.16, s32[1]{0:T(128)} %get-tuple-element.42.shared_ref, bf16[8,400,128]{2,1,0:T(8,128)(2,1)S(1)} %all_to_all.15.own_ref, ...), custom_call_target="tpu_custom_call" | custom-call | flops 2617245696 | bytes 10223616 | tf_op jit(solution)/shard_map/fine_backward/pallas_call | solution.py:394
  75.3 0.0 copy-start.3
  75.3 0.7 copy-done.3
  76.1 0.0 copy-start.5
  76.1 0.7 copy-done.5
  76.8 0.0 copy-start.13
  76.8 0.8 copy-done.13
  77.6 0.0 copy-start.14
  77.6 0.7 copy-done.14
  78.3 0.0 copy-start.2
  78.3 2.8 %collective-permute-start.5 = (bf16[144,256]{1,0:T(8,128)(2,1)S(1)}, bf16[144,256]{1,0:T(8,128)(2,1)S(1)}, u32[]{:S(2)}, u32[]{:S(2)}) collective-permute-start(bf16[144,256]{1,0:T(8,128)(2,1)S(1)} %get-tuple-element.51.own_ref), channel_id=1, source_target_pairs={{0,6},{1,7},{2,4},{3,5},{4,2},{5,3},{6,0},{7,1},{8,14},{9,15},{10,... | collective-permute-start | bytes 221192 | tf_op jit(solution)/shard_map/ppermute | solution.py:632
  81.1 2.4 %collective-permute-start.4 = (bf16[144,256]{1,0:T(8,128)(2,1)S(1)}, bf16[144,256]{1,0:T(8,128)(2,1)S(1)}, u32[]{:S(2)}, u32[]{:S(2)}) collective-permute-start(bf16[144,256]{1,0:T(8,128)(2,1)S(1)} %get-tuple-element.51.own_ref), channel_id=1, source_target_pairs={{0,4},{1,5},{2,6},{3,7},{4,0},{5,1},{6,2},{7,3},{8,12},{9,13},{10,... | collective-permute-start | bytes 221192 | tf_op jit(solution)/shard_map/ppermute | solution.py:632
  83.5 0.4 collective-permute-start.3
  84.0 0.0 collective-permute-done.5.far_ref
  84.0 4.5 %collective-permute-done.4.across_ref = bf16[144,256]{1,0:T(8,128)(2,1)S(1)} collective-permute-done((bf16[144,256]{1,0:T(8,128)(2,1)S(1)}, bf16[144,256]{1,0:T(8,128)(2,1)S(1)}, u32[]{:S(2)}, u32[]{:S(2)}) %collective-permute-start.4) | collective-permute-done | bytes 73760 | tf_op jit(solution)/shard_map/ppermute | solution.py:632
  88.5 1.7 %collective-permute-done.3.near_ref = bf16[144,256]{1,0:T(8,128)(2,1)S(1)} collective-permute-done((bf16[144,256]{1,0:T(8,128)(2,1)S(1)}, bf16[144,256]{1,0:T(8,128)(2,1)S(1)}, u32[]{:S(2)}, u32[]{:S(2)}) %collective-permute-start.3) | collective-permute-done | bytes 73760 | tf_op jit(solution)/shard_map/ppermute | solution.py:632
  90.3 0.0 copy-start.7
  90.3 0.6 copy-done.7
  90.9 0.0 all-gather.3.cloned.1.call-update
  90.9 0.9 collective-permute-start.6
  91.8 1.5 %collective-permute-start.7 = (bf16[768,256]{1,0:T(8,128)(2,1)}, bf16[768,256]{1,0:T(8,128)(2,1)S(1)}, u32[]{:S(2)}, u32[]{:S(2)}) collective-permute-start(bf16[768,256]{1,0:T(8,128)(2,1)} %copy-done.13), channel_id=1, source_target_pairs={{0,2},{1,3},{2,0},{3,1},{4,6},{5,7},{6,4},{7,5},{8,10},{9,11},{10,... | collective-permute-start | bytes 1179656 | tf_op jit(solution)/shard_map/ppermute | solution.py:632
  93.3 19.5 %all_to_all.16.scale_ref = f32[8,8,128]{2,1,0:T(8,128)S(1)} all-to-all(f32[8,8,128]{2,1,0:T(8,128)S(1)} %get-tuple-element.61), channel_id=1, replica_groups=mesh['dp'=8,'seq'=32] {'dp'}, dimensions={0} | all-to-all | bytes 65536 | tf_op jit(solution)/shard_map/all_to_all | solution.py:650
  112.8 0.0 collective-permute-done.6.other_od_ref
  112.8 0.0 collective-permute-done.7.other_dkv_ref
  112.8 0.0 copy-start.4
  112.8 1.0 copy-done.4
  113.8 0.0 copy-start.6
  113.8 1.0 copy-done.6
  114.8 0.4 sum_pairs.1
  115.3 17.3 %all_to_all.17.all_ref = bf16[8,400,128]{2,1,0:T(8,128)(2,1)S(1)} all-to-all(bf16[8,400,128]{2,1,0:T(8,128)(2,1)S(1)} %sum_pairs.1), channel_id=1, replica_groups={{0,1,8,9,16,17,24,25},{2,3,10,11,18,19,26,27},{4,5,12,13,20,21,28,29},{..., dimensions={0} | all-to-all | bytes 1638400 | tf_op jit(solution)/shard_map/all_to_all | solution.py:629
  132.5 1.1 unpack_heads.1
  133.6 0.6 multiply_reduce_fusion
  134.3 0.0 copy-done.2
  134.3 1.2 copy-done
  135.5 1.9 %join_coarse.1 = (bf16[256,1024]{1,0:T(8,128)(2,1)}, bf16[256,1024]{1,0:T(8,128)(2,1)}) custom-call(bf16[8,256,256]{2,1,0:T(8,128)(2,1)S(1)} %bitcast.18, f32[256,1024]{1,0:T(8,128)S(1)} %get-tuple-element.53.dk_own_ref, f32[256,1024]{1,0:T(8,128)S(1)} %get-tuple-element.54.dv_own_ref, bf16[256,1024]{1,0:T(8,128)(2,1)S(1)} %bitcast.20), custom_call_target="tpu_custom_call" | custom-call | tf_op jit(solution)/shard_map/join_coarse/pallas_call | solution.py:577
  (3 shorter events, 0.0 us)
Async XLA Ops:
  7.2 48.4 %copy-start.16 = (f32[8]{0:T(128)S(1)}, f32[8]{0:T(128)}, u32[]{:S(2)}) copy-start(f32[8]{0:T(128)} %log_ref.5) | copy-start | bytes 100
  7.2 127.1 %all-gather.3.cloned.1.call-start = ((), (), s32[]{:S(2)}) async-start(), calls=%async_computation.3 | async-start | bytes 1179648 | tf_op jit(solution)/shard_map/all_gather | solution.py:646
  30.2 23.8 %collective-permute-start.1 = (bf16[8,208,128]{2,1,0:T(8,128)(2,1)}, bf16[8,208,128]{2,1,0:T(8,128)(2,1)}, u32[]{:S(2)}, u32[]{:S(2)}) collective-permute-start(bf16[8,208,128]{2,1,0:T(8,128)(2,1)} %get-tuple-element.67), channel_id=1, source_target_pairs={{0,6},{1,7},{2,4},{3,5},{4,2},{5,3},{6,0},{7,1},{8,14},{9,15},{10,... | collective-permute-start | bytes 1277960 | tf_op jit(solution)/shard_map/ppermute | solution.py:632
  35.5 20.1 %collective-permute-start = (bf16[8,208,128]{2,1,0:T(8,128)(2,1)}, bf16[8,208,128]{2,1,0:T(8,128)(2,1)}, u32[]{:S(2)}, u32[]{:S(2)}) collective-permute-start(bf16[8,208,128]{2,1,0:T(8,128)(2,1)} %get-tuple-element.68), channel_id=1, source_target_pairs={{0,2},{1,3},{2,0},{3,1},{4,6},{5,7},{6,4},{7,5},{8,10},{9,11},{10,... | collective-permute-start | bytes 1277960 | tf_op jit(solution)/shard_map/ppermute | solution.py:632
  38.1 1.0 copy-start.1
  39.2 0.9 copy-start.8
  40.1 0.7 copy-start.9
  40.8 1.0 copy-start.10
  41.8 1.0 copy-start.11
  42.9 1.0 copy-start.12
  43.9 0.7 copy-start.15
  61.9 4.7 %collective-permute-start.2 = (f32[24,128]{1,0:T(8,128)S(1)}, f32[24,128]{1,0:T(8,128)S(1)}, u32[]{:S(2)}, u32[]{:S(2)}) collective-permute-start(f32[24,128]{1,0:T(8,128)S(1)} %get-tuple-element.43.stat_ref), channel_id=1, source_target_pairs={{0,6},{1,7},{2,4},{3,5},{4,2},{5,3},{6,0},{7,1},{8,14},{9,15},{10,... | collective-permute-start | bytes 36872 | tf_op jit(solution)/shard_map/ppermute | solution.py:632
  75.3 0.7 copy-start.3
  76.1 0.7 copy-start.5
  76.8 0.8 copy-start.13
  77.6 0.7 copy-start.14
  78.3 55.9 %copy-start.2 = (bf16[1,256,1024]{2,1,0:T(8,128)(2,1)S(1)}, bf16[1,256,1024]{2,1,0:T(8,128)(2,1)}, u32[]{:S(2)}) copy-start(bf16[1,256,1024]{2,1,0:T(8,128)(2,1)} %param.12) | copy-start | bytes 1572868
  78.3 5.7 %collective-permute-start.5 = (bf16[144,256]{1,0:T(8,128)(2,1)S(1)}, bf16[144,256]{1,0:T(8,128)(2,1)S(1)}, u32[]{:S(2)}, u32[]{:S(2)}) collective-permute-start(bf16[144,256]{1,0:T(8,128)(2,1)S(1)} %get-tuple-element.51.own_ref), channel_id=1, source_target_pairs={{0,6},{1,7},{2,4},{3,5},{4,2},{5,3},{6,0},{7,1},{8,14},{9,15},{10,... | collective-permute-start | bytes 221192 | tf_op jit(solution)/shard_map/ppermute | solution.py:632
  81.1 7.4 %collective-permute-start.4 = (bf16[144,256]{1,0:T(8,128)(2,1)S(1)}, bf16[144,256]{1,0:T(8,128)(2,1)S(1)}, u32[]{:S(2)}, u32[]{:S(2)}) collective-permute-start(bf16[144,256]{1,0:T(8,128)(2,1)S(1)} %get-tuple-element.51.own_ref), channel_id=1, source_target_pairs={{0,4},{1,5},{2,6},{3,7},{4,0},{5,1},{6,2},{7,3},{8,12},{9,13},{10,... | collective-permute-start | bytes 221192 | tf_op jit(solution)/shard_map/ppermute | solution.py:632
  83.5 6.7 %collective-permute-start.3 = (bf16[144,256]{1,0:T(8,128)(2,1)S(1)}, bf16[144,256]{1,0:T(8,128)(2,1)S(1)}, u32[]{:S(2)}, u32[]{:S(2)}) collective-permute-start(bf16[144,256]{1,0:T(8,128)(2,1)S(1)} %get-tuple-element.51.own_ref), channel_id=1, source_target_pairs={{0,2},{1,3},{2,0},{3,1},{4,6},{5,7},{6,4},{7,5},{8,10},{9,11},{10,... | collective-permute-start | bytes 221192 | tf_op jit(solution)/shard_map/ppermute | solution.py:632
  90.3 0.7 copy-start.7
  90.9 21.9 %collective-permute-start.6 = (bf16[768,256]{1,0:T(8,128)(2,1)}, bf16[768,256]{1,0:T(8,128)(2,1)S(1)}, u32[]{:S(2)}, u32[]{:S(2)}) collective-permute-start(bf16[768,256]{1,0:T(8,128)(2,1)} %copy-done.14), channel_id=1, source_target_pairs={{0,6},{1,7},{2,4},{3,5},{4,2},{5,3},{6,0},{7,1},{8,14},{9,15},{10,... | collective-permute-start | bytes 1179656 | tf_op jit(solution)/shard_map/ppermute | solution.py:632
  91.8 21.0 %collective-permute-start.7 = (bf16[768,256]{1,0:T(8,128)(2,1)}, bf16[768,256]{1,0:T(8,128)(2,1)S(1)}, u32[]{:S(2)}, u32[]{:S(2)}) collective-permute-start(bf16[768,256]{1,0:T(8,128)(2,1)} %copy-done.13), channel_id=1, source_target_pairs={{0,2},{1,3},{2,0},{3,1},{4,6},{5,7},{6,4},{7,5},{8,10},{9,11},{10,... | collective-permute-start | bytes 1179656 | tf_op jit(solution)/shard_map/ppermute | solution.py:632
  112.8 1.0 copy-start.4
  113.8 1.0 copy-start.6
  134.3 1.2 copy-start
Sparse Core Ops, SparseCore 0:
  91.1 26.5 all-gather.2

commit v3 on v2

--- a/solution.py
+++ b/solution.py
@@ -1,4 +1,5 @@
 import math
+from functools import partial
 
 import jax
 import jax.numpy as jnp
@@ -381,7 +382,7 @@
             pltpu.VMEM((queries, width), jnp.int32),
             pltpu.VMEM((queries, 2 * width), jnp.float32),
         ],
-        compiler_params=params(20),
+        compiler_params=params(16),
         cost_estimate=pl.CostEstimate(
             flops=4 * queries * total * width,
             bytes_accessed=4 * queries * total,
@@ -404,7 +405,7 @@
             pltpu.VMEM((width, queries), jnp.bfloat16),
             pltpu.VMEM((total, 2 * width), jnp.bfloat16),
         ],
-        compiler_params=params(20),
+        compiler_params=params(16),
         cost_estimate=pl.CostEstimate(
             flops=8 * queries * total * width,
             bytes_accessed=4 * queries * total,
@@ -494,7 +495,7 @@
         out_shape=(low, low, wide, wide, jax.ShapeDtypeStruct((heads * 8, width), jnp.float32))
         + (jax.ShapeDtypeStruct((count, width), jnp.bfloat16),) * 2,
         in_specs=[pl.BlockSpec(memory_space=pltpu.SMEM)] + [vmem] * 6,
-        compiler_params=params(16),
+        compiler_params=params(14),
         cost_estimate=pl.CostEstimate(
             flops=12 * count * count * features,
             bytes_accessed=24 * count * features,
@@ -513,24 +514,26 @@
         spot = pl.ds(pl.multiple_of(place * some_keys, some_keys), some_keys)
         sum_ref[spot, :] = (pair[0][:some_keys] + pair[1][:some_keys]).astype(jnp.bfloat16)
     scale = terms[0][some_keys:] + terms[1][some_keys:] + terms[2][some_keys:] + terms[3][some_keys:]
-    scale = jnp.sum(scale[:, : scale_ref.shape[2]], axis=0, keepdims=True)
-    scale_ref[...] = jnp.broadcast_to(scale[None], scale_ref.shape)
-
-
-def run_small(images, terms):
+    scale = jnp.sum(scale[:, : scale_ref.shape[1]], axis=0, keepdims=True)
+    scale_ref[...] = jnp.broadcast_to(scale, scale_ref.shape)
+
+
+def run_small(terms):
     tall, both = terms[0].shape
     return pl.pallas_call(
         small_kernel,
         out_shape=(
             jax.ShapeDtypeStruct((2 * (tall - note_rows), both), jnp.bfloat16),
-            jax.ShapeDtypeStruct((images, 8, both // 2), jnp.float32),
+            jax.ShapeDtypeStruct((8, both // 2), jnp.float32),
         ),
-        compiler_params=params(4),
+        compiler_params=params(2),
         name="sum_coarse_terms",
     )(*terms)
 
 
-def sum_kernel(od_ref, other_od_ref, dkv_ref, other_dkv_ref, own_ref, scale_ref, all_ref):
+def sum_kernel(
+    od_ref, other_od_ref, dkv_ref, other_dkv_ref, own_ref, scale_ref, other_scale_ref, all_ref
+):
     members, tall, width = all_ref.shape
     rows = (tall - note_rows) // 4
     fine = members * rows
@@ -546,22 +549,21 @@
     summed = dkv_ref[...].astype(jnp.float32) + other_dkv_ref[...].astype(jnp.float32)
     put(2, project(own_ref[:, 0:rows].reshape(fine, width), summed[:, :width]))
     put(3, summed[:, width:])
-    scale = jnp.sum(scale_ref[:, 0, 0:1], axis=0, keepdims=True)
-    note = in_pieces(scale, width)
+    note = in_pieces(scale_ref[0:1, 0:1] + other_scale_ref[0:1, 0:1], width)
     for member in range(members):
         all_ref[member, 4 * rows :] = note
 
 
-def run_sum(od, other_od, dkv, other_dkv, own_rows, scale):
+def run_sum(od, other_od, dkv, other_dkv, own_rows, scale, other_scale):
     return pl.pallas_call(
         sum_kernel,
         out_shape=jax.ShapeDtypeStruct(own_rows.shape, jnp.bfloat16),
-        compiler_params=params(10),
+        compiler_params=params(6),
         name="sum_pairs",
-    )(od, other_od, dkv, other_dkv, own_rows, scale)
-
-
-def join_kernel(terms_ref, dk_own_ref, dv_own_ref, k_ref, dk_ref, dv_ref):
+    )(od, other_od, dkv, other_dkv, own_rows, scale, other_scale)
+
+
+def join_kernel(terms_ref, dk_own_ref, dv_own_ref, k_ref, dk_ref, dv_ref, last_ref):
     heads, _, both = terms_ref.shape
     width = both // 2
     for head in range(heads):
@@ -570,37 +572,42 @@
         grad = terms[:, :width] + dk_own_ref[:, lanes]
         dk_ref[:, lanes] = project(k_ref[:, lanes], grad).astype(jnp.bfloat16)
         dv_ref[:, lanes] = (terms[:, width:] + dv_own_ref[:, lanes]).astype(jnp.bfloat16)
+    last_ref[...] = jnp.zeros_like(last_ref)
 
 
 def run_join(terms, dk_own, dv_own, keys):
     low = jax.ShapeDtypeStruct(keys.shape, jnp.bfloat16)
     return pl.pallas_call(
         join_kernel,
-        out_shape=(low, low),
-        compiler_params=params(14),
+        out_shape=(low, low, jax.ShapeDtypeStruct((8, 128), jnp.float32)),
+        compiler_params=params(8),
         name="join_coarse",
     )(terms, dk_own, dv_own, keys)
 
 
-def unpack_kernel(all_ref, out_ref, dq_ref, dk_ref, dv_ref, scale_ref):
+def unpack_kernel(factor, all_ref, _, out_ref, dq_ref, dk_ref, dv_ref, scale_ref):
     heads, tall, width = all_ref.shape
     rows = (tall - note_rows) // 4
     for head in range(heads):
         lanes = slice(head * width, (head + 1) * width)
         for place, ref in enumerate((out_ref, dq_ref, dk_ref, dv_ref)):
             ref[:, lanes] = all_ref[head, place * rows : (place + 1) * rows]
-    scale_ref[...] = jnp.sum(all_ref[:, 4 * rows :].astype(jnp.float32), axis=1)
-
-
-def run_unpack(all_back):
+        note = all_ref[head, 4 * rows :].astype(jnp.float32)
+        scale_ref[head] = jnp.sum(note[:, 0:1]) * factor
+
+
+def run_unpack(factor, all_back, after):
     heads, tall, width = all_back.shape
     flat = jax.ShapeDtypeStruct(((tall - note_rows) // 4, heads * width), jnp.bfloat16)
+    vmem = pl.BlockSpec(memory_space=pltpu.VMEM)
     return pl.pallas_call(
-        unpack_kernel,
-        out_shape=(flat,) * 4 + (jax.ShapeDtypeStruct((heads, width), jnp.float32),),
-        compiler_params=params(4),
+        partial(unpack_kernel, factor),
+        out_shape=(flat,) * 4 + (jax.ShapeDtypeStruct((heads,), jnp.float32),),
+        in_specs=[vmem, vmem],
+        out_specs=(vmem,) * 4 + (pl.BlockSpec(memory_space=pltpu.SMEM),),
+        compiler_params=params(3),
         name="unpack_heads",
-    )(all_back)
+    )(all_back, after)
 
 
 def body(
@@ -631,6 +638,9 @@
     def to_plane(array, flip):
         return lax.ppermute(array, "seq", [(i, i ^ (2 * flip)) for i in range(seq)])
 
+    def to_image(array, flip):
+        return lax.ppermute(array, "dp", [(i, i ^ flip) for i in range(images)])
+
     own_rows = exchange(run_pack(heads, fine_ids, k_fine[0], v_fine[0], q_fine[0], cot_fine[0]))
     kv_rows = to_plane(own_rows[:, : 2 * rows + note_rows], 1)
     qc_rows = to_plane(own_rows[:, 2 * rows :], 3)
@@ -642,16 +652,18 @@
         log_scale, own_rows, kv_rows, qc_rows, key_c, val_c, scale_c, lambda stat: to_plane(stat, 3)
     )
 
-    small_sum, scale = run_small(images, [small] + [to_plane(small, flip) for flip in (1, 2, 3)])
+    small_sum, scale = run_small([small] + [to_plane(small, flip) for flip in (1, 2, 3)])
     of_image = lax.all_gather(small_sum, "seq", axis=0, axis_index_groups=groups)
 
     other_dkv = to_plane(dkv_send, 1)
     other_od = to_plane(od_send, 3)
-    scale = lax.all_to_all(scale, "dp", 0, 0, tiled=True)
-    all_back = exchange(run_sum(od, other_od, dkv, other_dkv, own_rows, scale))
-    fine_out, fine_dq, fine_dk, fine_dv, scale = run_unpack(all_back)
-    dk_c, dv_c = run_join(of_image, dk_own, dv_own, k_coarse[0])
-    grad_scale = scale[:, 0] / math.sqrt(images * (coarse + seq * rows))
+    for flip in (1, 2):
+        scale = scale + to_image(scale, flip)
+    all_parts = run_sum(od, other_od, dkv, other_dkv, own_rows, scale, to_image(scale, 4))
+    all_back = exchange(all_parts)
+    dk_c, dv_c, after = run_join(of_image, dk_own, dv_own, k_coarse[0])
+    factor = 1.0 / math.sqrt(images * (coarse + seq * rows))
+    fine_out, fine_dq, fine_dk, fine_dv, grad_scale = run_unpack(factor, all_back, after)
     return (
         out_c[None],
         dq_c[None],

time: 145 us -> 142 us (0.979)
  blocking collectives: 56.5 us -> 19.7 us
  waiting for transfers between devices: 11.3 us -> 34.2 us
  starting transfers between devices: 17.4 us -> 27.7 us
    all_to_all x1 -> x0, blocking collectives: 19.5 us -> none  [body(): scale = lax.all_to_all(scale, 'dp', 0, 0, tiled=True)]
    all_to_all x2 -> x1, blocking collectives: 37 us -> 19.7 us  [exchange(): lax.all_to_all(parts, 'seq', 0, 0, axis_index_groups=groups, tiled=True)]
    ppermute x0 -> x3, waiting for transfers between devices: none -> 10.1 us  [to_image(): return lax.ppermute(array, 'dp', [(i, i ^ flip) for i in range(images)])]
    all_to_all x0 -> x1, waiting for transfers between devices: none -> 9.55 us  [exchange(): lax.all_to_all(parts, 'seq', 0, 0, axis_index_groups=groups, tiled=True)]
    ppermute x0 -> x3, starting transfers between devices: none -> 5.31 us  [to_image(): return lax.ppermute(array, 'dp', [(i, i ^ flip) for i in range(images)])]
    all_to_all x0 -> x1, starting transfers between devices: none -> 5.06 us  [exchange(): lax.all_to_all(parts, 'seq', 0, 0, axis_index_groups=groups, tiled=True)]
    ppermute x8, waiting for transfers between devices: 11.3 us -> 14.6 us  [to_plane(): return lax.ppermute(array, 'seq', [(i, i ^ 2 * flip) for i in range(seq)])]
  transfers between devices with their start and end apart: 9 -> 13, of which waited for: 5 -> 10; matrix products, arithmetic and copies ran while one was open for 1% -> 1% of each run, Pallas kernels for 6% -> 8%
where the time goes in v3:
time: 142 us; the launch traced here: 141 us
  waiting for transfers between devices  34.2 us (24%)
  Pallas kernels  29.4 us (21%)
  starting transfers between devices  27.7 us (20%)
  blocking collectives  19.7 us (14%)
  local copies, waits for them, and re-layouts  15.7 us (11%)
  between operations  14.1 us (10%)
    all_to_all x1, blocking collectives, exchange(): lax.all_to_all(parts, 'seq', 0, 0, axis_index_groups=groups, tiled=True)  19.7 us
    ppermute x8, starting transfers between devices, to_plane(): return lax.ppermute(array, 'seq', [(i, i ^ 2 * flip) for i in range(seq)])  17.3 us
    ppermute x8, waiting for transfers between devices, to_plane(): return lax.ppermute(array, 'seq', [(i, i ^ 2 * flip) for i in range(seq)])  14.6 us
    unnamed x34, local copies, waits for them, and re-layouts  13.3 us
    ppermute x3, waiting for transfers between devices, to_image(): return lax.ppermute(array, 'dp', [(i, i ^ flip) for i in range(images)])  10.1 us
    all_to_all x1, waiting for transfers between devices, exchange(): lax.all_to_all(parts, 'seq', 0, 0, axis_index_groups=groups, tiled=True)  9.55 us
    pallas_call x1, Pallas kernels, run_fine(): pl.pallas_call(backward_kernel, out_shape=(half, half, half, half, low(so...  8.74 us
    pallas_call x1, Pallas kernels, run_coarse(): pl.pallas_call(coarse_kernel, out_shape=(low, low, wide, wide, jax.ShapeD...  7.81 us
  transfers between devices with their start and end apart: 13, of which 10 were waited for; matrix products, arithmetic and copies ran while one was open for 1% of the time, Pallas kernels for 8%

profile of v3, /device:TPU:1, one launch (start us, length us, event | category | flops | bytes accessed | tf_op | source)
XLA Modules:
  0.0 140.8 jit_solution(6557812588291379863)
XLA Ops:
  7.2 0.0 copy-start.16
  7.2 0.0 all-gather.3.cloned.1.call-start
  7.2 2.3 %pack_heads.1 = bf16[8,400,128]{2,1,0:T(8,128)(2,1)} custom-call(s32[1,96]{1,0:T(1,128)} %ids_ref.1, bf16[96,1024]{1,0:T(8,128)(2,1)} %bitcast.25, bf16[96,1024]{1,0:T(8,128)(2,1)} %bitcast.26, bf16[96,1024]{1,0:T(8,128)(2,1)} %bitcast.27, bf16[96,1024]{1,0:T(8,128)(2,1)} %bitcast.28), custom_call_target="tpu_custom_call" | custom-call | tf_op jit(solution)/shard_map/pack_heads/pallas_call | solution.py:103
  9.5 19.7 %all_to_all.10.own_ref = bf16[8,400,128]{2,1,0:T(8,128)(2,1)S(1)} all-to-all(bf16[8,400,128]{2,1,0:T(8,128)(2,1)} %pack_heads.1), channel_id=1, replica_groups={{0,1,8,9,16,17,24,25},{2,3,10,11,18,19,26,27},{4,5,12,13,20,21,28,29},{..., dimensions={0} | all-to-all | bytes 1638400 | tf_op jit(solution)/shard_map/all_to_all | solution.py:636
  29.2 1.0 fusion
  30.2 5.3 %collective-permute-start.1 = (bf16[8,208,128]{2,1,0:T(8,128)(2,1)}, bf16[8,208,128]{2,1,0:T(8,128)(2,1)}, u32[]{:S(2)}, u32[]{:S(2)}) collective-permute-start(bf16[8,208,128]{2,1,0:T(8,128)(2,1)} %get-tuple-element.69), channel_id=1, source_target_pairs={{0,6},{1,7},{2,4},{3,5},{4,2},{5,3},{6,0},{7,1},{8,14},{9,15},{10,... | collective-permute-start | bytes 1277960 | tf_op jit(solution)/shard_map/ppermute | solution.py:639
  35.5 1.2 collective-permute-start
  36.7 1.5 %copy.20.row_level_ref = s32[256,1]{1,0:T(8,128)} copy(s32[256,1]{0,1:T(1,128)} %bitcast.21) | data formatting | bytes 2048 | tf_op jit(solution)/shard_map/broadcast_in_dim;squeeze | solution.py:505
  38.1 0.0 copy-start.1
  38.1 1.0 copy-done.1
  39.2 0.0 copy-start.8
  39.2 0.9 copy-done.8
  40.1 0.0 copy-start.9
  40.1 0.7 copy-done.9
  40.8 0.0 copy-start.10
  40.8 1.0 copy-done.10
  41.8 0.0 copy-start.11
  41.8 1.0 copy-done.11
  42.8 0.0 copy-start.12
  42.8 1.0 copy-done.12
  43.9 0.0 copy-start.15
  43.9 0.7 copy-done.15
  44.5 7.8 %coarse_attention.1 = (bf16[256,1024]{1,0:T(8,128)(2,1)}, bf16[256,1024]{1,0:T(8,128)(2,1)}, f32[256,1024]{1,0:T(8,128)S(1)}, f32[256,1024]{1,0:T(8,128)S(1)}, f...) custom-call(f32[8]{0:T(128)S(1)} %copy-done.15, s32[256,1]{1,0:T(8,128)S(1)} %copy-done.8, ...), custom_call_target="tpu_custom_call" | custom-call | flops 805306368 | bytes 6291456 | tf_op jit(solution)/shard_map/coarse_attention/pallas_call | solution.py:493
  52.3 1.7 %collective-permute-done.1.qc_ref = bf16[8,208,128]{2,1,0:T(8,128)(2,1)} collective-permute-done((bf16[8,208,128]{2,1,0:T(8,128)(2,1)}, bf16[8,208,128]{2,1,0:T(8,128)(2,1)}, u32[]{:S(2)}, u32[]{:S(2)}) %collective-permute-start.1) | collective-permute-done | bytes 426016 | tf_op jit(solution)/shard_map/ppermute | solution.py:639
  54.0 1.5 %collective-permute-done.kv_ref = bf16[8,208,128]{2,1,0:T(8,128)(2,1)} collective-permute-done((bf16[8,208,128]{2,1,0:T(8,128)(2,1)}, bf16[8,208,128]{2,1,0:T(8,128)(2,1)}, u32[]{:S(2)}, u32[]{:S(2)}) %collective-permute-start) | collective-permute-done | bytes 426016 | tf_op jit(solution)/shard_map/ppermute | solution.py:639
  55.5 0.0 copy-done.16
  55.5 6.4 %fine_forward.1 = (bf16[1536,1664]{1,0:T(8,128)(2,1)S(1)}, bf16[1664,128]{1,0:T(8,128)(2,1)S(1)}, bf16[1664,128]{1,0:T(8,128)(2,1)S(1)}, bf16[1536,128]{1,0:T(8,...) custom-call(f32[8]{0:T(128)S(1)} %copy-done.16, ...), custom_call_target="tpu_custom_call" | custom-call | flops 1308622848 | bytes 10223616 | tf_op jit(solution)/shard_map/fine_forward/pallas_call | solution.py:366
  61.9 2.9 %collective-permute-start.2 = (f32[24,128]{1,0:T(8,128)S(1)}, f32[24,128]{1,0:T(8,128)S(1)}, u32[]{:S(2)}, u32[]{:S(2)}) collective-permute-start(f32[24,128]{1,0:T(8,128)S(1)} %get-tuple-element.44.stat_ref), channel_id=1, source_target_pairs={{0,6},{1,7},{2,4},{3,5},{4,2},{5,3},{6,0},{7,1},{8,14},{9,15},{10,... | collective-permute-start | bytes 36872 | tf_op jit(solution)/shard_map/ppermute | solution.py:639
  64.8 1.8 %collective-permute-done.2.other_stat_ref = f32[24,128]{1,0:T(8,128)S(1)} collective-permute-done((f32[24,128]{1,0:T(8,128)S(1)}, f32[24,128]{1,0:T(8,128)S(1)}, u32[]{:S(2)}, u32[]{:S(2)}) %collective-permute-start.2) | collective-permute-done | bytes 12320 | tf_op jit(solution)/shard_map/ppermute | solution.py:639
  66.7 0.0 copy-start.2
  66.7 8.7 %fine_backward.1 = (bf16[768,256]{1,0:T(8,128)(2,1)S(1)}, bf16[768,256]{1,0:T(8,128)(2,1)S(1)}, bf16[768,256]{1,0:T(8,128)(2,1)S(1)}, bf16[768,256]{1,0:T(8,128)(2,1)S(1)}, bf16[144,256]{1,0:T(8,128)(2,1)S(1)}) custom-call(f32[8]{0:T(128)S(1)} %copy-done.16, s32[1]{0:T(128)} %get-tuple-element.43.shared_ref, bf16[8,400,128]{2,1,0:T(8,128)(2,1)S(1)} %all_to_all.10.own_ref, ...), custom_call_target="tpu_custom_call" | custom-call | flops 2617245696 | bytes 10223616 | tf_op jit(solution)/shard_map/fine_backward/pallas_call | solution.py:395
  75.4 0.0 copy-start.3
  75.4 0.7 copy-done.3
  76.2 0.8 copy-done.5
  76.9 0.8 copy-done.13
  77.7 0.7 copy-done.14
  78.4 2.8 %collective-permute-start.5 = (bf16[144,256]{1,0:T(8,128)(2,1)S(1)}, bf16[144,256]{1,0:T(8,128)(2,1)S(1)}, u32[]{:S(2)}, u32[]{:S(2)}) collective-permute-start(bf16[144,256]{1,0:T(8,128)(2,1)S(1)} %get-tuple-element.52.own_ref), channel_id=1, source_target_pairs={{0,6},{1,7},{2,4},{3,5},{4,2},{5,3},{6,0},{7,1},{8,14},{9,15},{10,... | collective-permute-start | bytes 221192 | tf_op jit(solution)/shard_map/ppermute | solution.py:639
  81.2 2.4 %collective-permute-start.4 = (bf16[144,256]{1,0:T(8,128)(2,1)S(1)}, bf16[144,256]{1,0:T(8,128)(2,1)S(1)}, u32[]{:S(2)}, u32[]{:S(2)}) collective-permute-start(bf16[144,256]{1,0:T(8,128)(2,1)S(1)} %get-tuple-element.52.own_ref), channel_id=1, source_target_pairs={{0,4},{1,5},{2,6},{3,7},{4,0},{5,1},{6,2},{7,3},{8,12},{9,13},{10,... | collective-permute-start | bytes 221192 | tf_op jit(solution)/shard_map/ppermute | solution.py:639
  83.7 0.4 collective-permute-start.3
  84.1 0.0 collective-permute-done.5.far_ref
  84.1 4.6 %collective-permute-done.4.across_ref = bf16[144,256]{1,0:T(8,128)(2,1)S(1)} collective-permute-done((bf16[144,256]{1,0:T(8,128)(2,1)S(1)}, bf16[144,256]{1,0:T(8,128)(2,1)S(1)}, u32[]{:S(2)}, u32[]{:S(2)}) %collective-permute-start.4) | collective-permute-done | bytes 73760 | tf_op jit(solution)/shard_map/ppermute | solution.py:639
  88.6 1.9 %collective-permute-done.3.near_ref = bf16[144,256]{1,0:T(8,128)(2,1)S(1)} collective-permute-done((bf16[144,256]{1,0:T(8,128)(2,1)S(1)}, bf16[144,256]{1,0:T(8,128)(2,1)S(1)}, u32[]{:S(2)}, u32[]{:S(2)}) %collective-permute-start.3) | collective-permute-done | bytes 73760 | tf_op jit(solution)/shard_map/ppermute | solution.py:639
  90.5 0.0 copy-start.7
  90.6 0.6 copy-done.7
  91.2 0.0 all-gather.3.cloned.1.call-update
  91.2 0.8 collective-permute-start.6
  92.0 1.5 %collective-permute-start.7 = (bf16[768,256]{1,0:T(8,128)(2,1)}, bf16[768,256]{1,0:T(8,128)(2,1)S(1)}, u32[]{:S(2)}, u32[]{:S(2)}) collective-permute-start(bf16[768,256]{1,0:T(8,128)(2,1)} %copy-done.13), channel_id=1, source_target_pairs={{0,2},{1,3},{2,0},{3,1},{4,6},{5,7},{6,4},{7,5},{8,10},{9,11},{10,... | collective-permute-start | bytes 1179656 | tf_op jit(solution)/shard_map/ppermute | solution.py:639
  93.5 1.5 %collective-permute-start.8 = (f32[8,128]{1,0:T(8,128)S(1)}, f32[8,128]{1,0:T(8,128)S(1)}, u32[]{:S(2)}, u32[]{:S(2)}) collective-permute-start(f32[8,128]{1,0:T(8,128)S(1)} %get-tuple-element.62), channel_id=1, source_target_pairs={{0,32},{32,0},{64,96},{96,64},{128,160},{160,128},{192,224},{224,1... | collective-permute-start | bytes 12296 | tf_op jit(solution)/shard_map/ppermute | solution.py:642
  95.0 1.0 collective-permute-done.8
  96.0 2.7 %collective-permute-start.9 = (f32[8,128]{1,0:T(8,128)S(1)}, f32[8,128]{1,0:T(8,128)S(1)}, u32[]{:S(2)}, u32[]{:S(2)}) collective-permute-start(f32[8,128]{1,0:T(8,128)S(1)} %add.6), channel_id=1, source_target_pairs={{0,64},{32,96},{64,0},{96,32},{128,192},{160,224},{192,128},{224,1... | collective-permute-start | bytes 12296 | tf_op jit(solution)/shard_map/ppermute | solution.py:642
  98.7 1.6 %collective-permute-done.9 = f32[8,128]{1,0:T(8,128)S(1)} collective-permute-done((f32[8,128]{1,0:T(8,128)S(1)}, f32[8,128]{1,0:T(8,128)S(1)}, u32[]{:S(2)}, u32[]{:S(2)}) %collective-permute-start.9) | collective-permute-done | bytes 4128 | tf_op jit(solution)/shard_map/ppermute | solution.py:642
  100.3 1.1 collective-permute-start.10
  101.3 7.5 %collective-permute-done.10.other_scale_ref = f32[8,128]{1,0:T(8,128)S(1)} collective-permute-done((f32[8,128]{1,0:T(8,128)S(1)}, f32[8,128]{1,0:T(8,128)S(1)}, u32[]{:S(2)}, u32[]{:S(2)}) %collective-permute-start.10) | collective-permute-done | bytes 4128 | tf_op jit(solution)/shard_map/ppermute | solution.py:642
  108.9 3.1 %collective-permute-done.6.other_od_ref = bf16[768,256]{1,0:T(8,128)(2,1)S(1)} collective-permute-done((bf16[768,256]{1,0:T(8,128)(2,1)}, bf16[768,256]{1,0:T(8,128)(2,1)S(1)}, u32[]{:S(2)}, u32[]{:S(2)}) %collective-permute-start.6) | collective-permute-done | bytes 393248 | tf_op jit(solution)/shard_map/ppermute | solution.py:639
  112.0 0.0 collective-permute-done.7.other_dkv_ref
  112.0 1.0 copy-done.4
  113.0 1.0 copy-done.6
  114.0 1.3 sum_pairs.1
  115.3 5.1 %all-to-all-start.1 = ((bf16[8,400,128]{2,1,0:T(8,128)(2,1)}), bf16[8,400,128]{2,1,0:T(8,128)(2,1)S(1)}, u32[]{:S(2)}, u32[]{:S(2)}) async-start(bf16[8,400,128]{2,1,0:T(8,128)(2,1)} %sum_pairs.1), calls=%async_computation.1 | async-start | bytes 1638400 | tf_op jit(solution)/shard_map/all_to_all | solution.py:636
  120.4 0.0 copy-done.2
  120.4 1.2 copy-done
  121.6 1.9 %join_coarse.1 = (bf16[256,1024]{1,0:T(8,128)(2,1)}, bf16[256,1024]{1,0:T(8,128)(2,1)}, f32[8,128]{1,0:T(8,128)S(1)}) custom-call(bf16[8,256,256]{2,1,0:T(8,128)(2,1)S(1)} %bitcast.18, f32[256,1024]{1,0:T(8,128)S(1)} %get-tuple-element.54.dk_own_ref, f32[256,1024]{1,0:T(8,128)S(1)} %get-tuple-element.55.dv_own_ref, bf16[256,1024]{1,0:T(8,128)(2,1)S(1)} %bitcast.20), custom_call_target="tpu_custom_call" | custom-call | tf_op jit(solution)/shard_map/join_coarse/pallas_call | solution.py:580
  123.5 9.5 %all-to-all-done.1.all_ref = bf16[8,400,128]{2,1,0:T(8,128)(2,1)S(1)} async-done(((bf16[8,400,128]{2,1,0:T(8,128)(2,1)}), bf16[8,400,128]{2,1,0:T(8,128)(2,1)S(1)}, u32[]{:S(2)}, u32[]{:S(2)}) %all-to-all-start.1) | async-done | bytes 819232 | tf_op jit(solution)/shard_map/all_to_all | solution.py:636
  133.0 0.9 unpack_heads.1
  (10 shorter events, 0.1 us)
Async XLA Ops:
  7.2 48.4 %copy-start.16 = (f32[8]{0:T(128)S(1)}, f32[8]{0:T(128)}, u32[]{:S(2)}) copy-start(f32[8]{0:T(128)} %log_ref.5) | copy-start | bytes 100
  7.2 113.2 %all-gather.3.cloned.1.call-start = ((), (), s32[]{:S(2)}) async-start(), calls=%async_computation.2 | async-start | bytes 1179648 | tf_op jit(solution)/shard_map/all_gather | solution.py:656
  30.2 23.8 %collective-permute-start.1 = (bf16[8,208,128]{2,1,0:T(8,128)(2,1)}, bf16[8,208,128]{2,1,0:T(8,128)(2,1)}, u32[]{:S(2)}, u32[]{:S(2)}) collective-permute-start(bf16[8,208,128]{2,1,0:T(8,128)(2,1)} %get-tuple-element.69), channel_id=1, source_target_pairs={{0,6},{1,7},{2,4},{3,5},{4,2},{5,3},{6,0},{7,1},{8,14},{9,15},{10,... | collective-permute-start | bytes 1277960 | tf_op jit(solution)/shard_map/ppermute | solution.py:639
  35.5 20.1 %collective-permute-start = (bf16[8,208,128]{2,1,0:T(8,128)(2,1)}, bf16[8,208,128]{2,1,0:T(8,128)(2,1)}, u32[]{:S(2)}, u32[]{:S(2)}) collective-permute-start(bf16[8,208,128]{2,1,0:T(8,128)(2,1)} %get-tuple-element.70), channel_id=1, source_target_pairs={{0,2},{1,3},{2,0},{3,1},{4,6},{5,7},{6,4},{7,5},{8,10},{9,11},{10,... | collective-permute-start | bytes 1277960 | tf_op jit(solution)/shard_map/ppermute | solution.py:639
  38.1 1.0 copy-start.1
  39.2 0.9 copy-start.8
  40.1 0.7 copy-start.9
  40.8 1.0 copy-start.10
  41.8 1.0 copy-start.11
  42.8 1.0 copy-start.12
  43.9 0.7 copy-start.15
  61.9 4.7 %collective-permute-start.2 = (f32[24,128]{1,0:T(8,128)S(1)}, f32[24,128]{1,0:T(8,128)S(1)}, u32[]{:S(2)}, u32[]{:S(2)}) collective-permute-start(f32[24,128]{1,0:T(8,128)S(1)} %get-tuple-element.44.stat_ref), channel_id=1, source_target_pairs={{0,6},{1,7},{2,4},{3,5},{4,2},{5,3},{6,0},{7,1},{8,14},{9,15},{10,... | collective-permute-start | bytes 36872 | tf_op jit(solution)/shard_map/ppermute | solution.py:639
  66.7 53.7 %copy-start.2 = (bf16[1,256,1024]{2,1,0:T(8,128)(2,1)S(1)}, bf16[1,256,1024]{2,1,0:T(8,128)(2,1)}, u32[]{:S(2)}) copy-start(bf16[1,256,1024]{2,1,0:T(8,128)(2,1)} %param.12) | copy-start | bytes 1572868
  75.4 0.7 copy-start.3
  76.2 0.8 copy-start.5
  76.9 0.8 copy-start.13
  77.7 0.7 copy-start.14
  78.4 5.7 %collective-permute-start.5 = (bf16[144,256]{1,0:T(8,128)(2,1)S(1)}, bf16[144,256]{1,0:T(8,128)(2,1)S(1)}, u32[]{:S(2)}, u32[]{:S(2)}) collective-permute-start(bf16[144,256]{1,0:T(8,128)(2,1)S(1)} %get-tuple-element.52.own_ref), channel_id=1, source_target_pairs={{0,6},{1,7},{2,4},{3,5},{4,2},{5,3},{6,0},{7,1},{8,14},{9,15},{10,... | collective-permute-start | bytes 221192 | tf_op jit(solution)/shard_map/ppermute | solution.py:639
  81.2 7.4 %collective-permute-start.4 = (bf16[144,256]{1,0:T(8,128)(2,1)S(1)}, bf16[144,256]{1,0:T(8,128)(2,1)S(1)}, u32[]{:S(2)}, u32[]{:S(2)}) collective-permute-start(bf16[144,256]{1,0:T(8,128)(2,1)S(1)} %get-tuple-element.52.own_ref), channel_id=1, source_target_pairs={{0,4},{1,5},{2,6},{3,7},{4,0},{5,1},{6,2},{7,3},{8,12},{9,13},{10,... | collective-permute-start | bytes 221192 | tf_op jit(solution)/shard_map/ppermute | solution.py:639
  83.7 6.8 %collective-permute-start.3 = (bf16[144,256]{1,0:T(8,128)(2,1)S(1)}, bf16[144,256]{1,0:T(8,128)(2,1)S(1)}, u32[]{:S(2)}, u32[]{:S(2)}) collective-permute-start(bf16[144,256]{1,0:T(8,128)(2,1)S(1)} %get-tuple-element.52.own_ref), channel_id=1, source_target_pairs={{0,2},{1,3},{2,0},{3,1},{4,6},{5,7},{6,4},{7,5},{8,10},{9,11},{10,... | collective-permute-start | bytes 221192 | tf_op jit(solution)/shard_map/ppermute | solution.py:639
  90.5 0.7 copy-start.7
  91.2 20.7 %collective-permute-start.6 = (bf16[768,256]{1,0:T(8,128)(2,1)}, bf16[768,256]{1,0:T(8,128)(2,1)S(1)}, u32[]{:S(2)}, u32[]{:S(2)}) collective-permute-start(bf16[768,256]{1,0:T(8,128)(2,1)} %copy-done.14), channel_id=1, source_target_pairs={{0,6},{1,7},{2,4},{3,5},{4,2},{5,3},{6,0},{7,1},{8,14},{9,15},{10,... | collective-permute-start | bytes 1179656 | tf_op jit(solution)/shard_map/ppermute | solution.py:639
  92.0 20.0 %collective-permute-start.7 = (bf16[768,256]{1,0:T(8,128)(2,1)}, bf16[768,256]{1,0:T(8,128)(2,1)S(1)}, u32[]{:S(2)}, u32[]{:S(2)}) collective-permute-start(bf16[768,256]{1,0:T(8,128)(2,1)} %copy-done.13), channel_id=1, source_target_pairs={{0,2},{1,3},{2,0},{3,1},{4,6},{5,7},{6,4},{7,5},{8,10},{9,11},{10,... | collective-permute-start | bytes 1179656 | tf_op jit(solution)/shard_map/ppermute | solution.py:639
  93.5 2.5 %collective-permute-start.8 = (f32[8,128]{1,0:T(8,128)S(1)}, f32[8,128]{1,0:T(8,128)S(1)}, u32[]{:S(2)}, u32[]{:S(2)}) collective-permute-start(f32[8,128]{1,0:T(8,128)S(1)} %get-tuple-element.62), channel_id=1, source_target_pairs={{0,32},{32,0},{64,96},{96,64},{128,160},{160,128},{192,224},{224,1... | collective-permute-start | bytes 12296 | tf_op jit(solution)/shard_map/ppermute | solution.py:642
  96.0 4.3 %collective-permute-start.9 = (f32[8,128]{1,0:T(8,128)S(1)}, f32[8,128]{1,0:T(8,128)S(1)}, u32[]{:S(2)}, u32[]{:S(2)}) collective-permute-start(f32[8,128]{1,0:T(8,128)S(1)} %add.6), channel_id=1, source_target_pairs={{0,64},{32,96},{64,0},{96,32},{128,192},{160,224},{192,128},{224,1... | collective-permute-start | bytes 12296 | tf_op jit(solution)/shard_map/ppermute | solution.py:642
  100.3 8.6 %collective-permute-start.10 = (f32[8,128]{1,0:T(8,128)S(1)}, f32[8,128]{1,0:T(8,128)S(1)}, u32[]{:S(2)}, u32[]{:S(2)}) collective-permute-start(f32[8,128]{1,0:T(8,128)S(1)} %add.7.scale_ref), channel_id=1, source_target_pairs={{0,128},{32,160},{64,192},{96,224},{128,0},{160,32},{192,64},{224,... | collective-permute-start | bytes 12296 | tf_op jit(solution)/shard_map/ppermute | solution.py:642
  112.0 1.0 copy-start.4
  113.0 1.0 copy-start.6
  115.3 17.7 %all-to-all-start.1 = ((bf16[8,400,128]{2,1,0:T(8,128)(2,1)}), bf16[8,400,128]{2,1,0:T(8,128)(2,1)S(1)}, u32[]{:S(2)}, u32[]{:S(2)}) async-start(bf16[8,400,128]{2,1,0:T(8,128)(2,1)} %sum_pairs.1), calls=%async_computation.1 | async-start | bytes 1638400 | tf_op jit(solution)/shard_map/all_to_all | solution.py:636
  120.4 1.2 copy-start
Sparse Core Ops, SparseCore 0:
  91.3 26.3 all-gather.2

commit v4 on v3

--- a/solution.py
+++ b/solution.py
@@ -271,6 +271,8 @@
     query_turn,
     cot_turn,
     turn_scr,
+    od_scr,
+    sems,
 ):
     plane, head = seq_place()
     members, tall, width = own_ref.shape
@@ -320,12 +322,26 @@
 
     all_chunks(grads, some_keys, shared_ref[0], fine // k_tile)
 
+    copies = []
+
+    def send(source, target):
+        copies.append(pltpu.make_async_copy(source, target, sems.at[len(copies)]))
+        copies[-1].start()
+
+    own_slot = key_slot(plane)
+    for slot, target in ((1 - own_slot, dkv_send_ref), (own_slot, dkv_ref)):
+        for run in range(runs):
+            spot = pl.ds(pl.multiple_of(some_keys + place_of(run, slot, block), 64), block)
+            send(turn_scr.at[spot, :], target.at[run * block : (run + 1) * block, :])
+
     own_slot = query_slot(plane)
     scale = coarse_scale_ref[pl.ds(pl.multiple_of(head * 8, 8), 8), :]
     scale = scale * jnp.where(plane == 0, 1.0, 0.0)
-    for ref, slot, start, target in (
-        (own_ref, own_slot, first_query, od_ref),
-        (qc_ref, 1 - own_slot, note_rows, od_send_ref),
+    for index, (ref, slot, start, target) in enumerate(
+        (
+            (qc_ref, 1 - own_slot, note_rows, od_send_ref),
+            (own_ref, own_slot, first_query, od_ref),
+        )
     ):
         for run in range(runs):
             spot = pl.ds(place_of(run, slot, block), block)
@@ -336,16 +352,13 @@
             along = jnp.sum(q_dir * grad, axis=-1, keepdims=True)
             scale = scale + fold_rows(query_ref[spot, :].astype(jnp.float32) * grad)
             to = slice(run * block, (run + 1) * block)
-            target[to, 0:width] = (num_ref[spot, :] * r_den).astype(jnp.bfloat16)
-            target[to, width:] = (q_inv * (grad - q_dir * along)).astype(jnp.bfloat16)
-
-    own_slot = key_slot(plane)
-    for slot, target in ((own_slot, dkv_ref), (1 - own_slot, dkv_send_ref)):
-        for run in range(runs):
-            spot = pl.ds(pl.multiple_of(some_keys + place_of(run, slot, block), 64), block)
-            target[run * block : (run + 1) * block, :] = turn_scr[spot, :]
+            od_scr[index, to, 0:width] = (num_ref[spot, :] * r_den).astype(jnp.bfloat16)
+            od_scr[index, to, width:] = (q_inv * (grad - q_dir * along)).astype(jnp.bfloat16)
+        send(od_scr.at[index], target)
     small_ref[0:some_keys, :] = turn_scr[0:some_keys, :]
     small_ref[some_keys:, :] = in_pieces(sum_all(scale), 2 * width)
+    for copy in copies:
+        copy.wait()
 
 
 def run_fine(log_scale, own_rows, kv_rows, qc_rows, key_coarse, val_coarse, coarse_scale, swap):
@@ -396,7 +409,7 @@
         backward_kernel,
         out_shape=(half, half, half, half, low(some_keys + note_rows, 2 * width)),
         in_specs=[smem, smem] + [vmem] * 11,
-        out_specs=(vmem,) * 5,
+        out_specs=(pl.BlockSpec(memory_space=pltpu.HBM),) * 4 + (vmem,),
         scratch_shapes=[
             pltpu.VMEM((queries, width), jnp.float32),
             pltpu.VMEM((queries, width), jnp.float32),
@@ -404,6 +417,8 @@
             pltpu.VMEM((width, queries), jnp.bfloat16),
             pltpu.VMEM((width, queries), jnp.bfloat16),
             pltpu.VMEM((total, 2 * width), jnp.bfloat16),
+            pltpu.VMEM((2, queries // 2, 2 * width), jnp.bfloat16),
+            pltpu.SemaphoreType.DMA((members + 2,)),
         ],
         compiler_params=params(16),
         cost_estimate=pl.CostEstimate(
@@ -532,8 +547,24 @@
 
 
 def sum_kernel(
-    od_ref, other_od_ref, dkv_ref, other_dkv_ref, own_ref, scale_ref, other_scale_ref, all_ref
+    od_hbm,
+    other_od_ref,
+    dkv_hbm,
+    other_dkv_ref,
+    own_ref,
+    scale_ref,
+    other_scale_ref,
+    all_ref,
+    od_ref,
+    dkv_ref,
+    sems,
 ):
+    copies = [
+        pltpu.make_async_copy(od_hbm, od_ref, sems.at[0]),
+        pltpu.make_async_copy(dkv_hbm, dkv_ref, sems.at[1]),
+    ]
+    for copy in copies:
+        copy.start()
     members, tall, width = all_ref.shape
     rows = (tall - note_rows) // 4
     fine = members * rows
@@ -543,9 +574,11 @@
             members, rows, width
         )
 
+    copies[0].wait()
     summed = od_ref[...].astype(jnp.float32) + other_od_ref[...].astype(jnp.float32)
     put(0, summed[:, :width])
     put(1, summed[:, width:])
+    copies[1].wait()
     summed = dkv_ref[...].astype(jnp.float32) + other_dkv_ref[...].astype(jnp.float32)
     put(2, project(own_ref[:, 0:rows].reshape(fine, width), summed[:, :width]))
     put(3, summed[:, width:])
@@ -555,9 +588,18 @@
 
 
 def run_sum(od, other_od, dkv, other_dkv, own_rows, scale, other_scale):
+    vmem = pl.BlockSpec(memory_space=pltpu.VMEM)
+    hbm = pl.BlockSpec(memory_space=pltpu.HBM)
     return pl.pallas_call(
         sum_kernel,
         out_shape=jax.ShapeDtypeStruct(own_rows.shape, jnp.bfloat16),
+        in_specs=[hbm, vmem, hbm, vmem, vmem, vmem, vmem],
+        out_specs=vmem,
+        scratch_shapes=[
+            pltpu.VMEM(od.shape, jnp.bfloat16),
+            pltpu.VMEM(dkv.shape, jnp.bfloat16),
+            pltpu.SemaphoreType.DMA((2,)),
+        ],
         compiler_params=params(6),
         name="sum_pairs",
     )(od, other_od, dkv, other_dkv, own_rows, scale, other_scale)
@@ -657,8 +699,7 @@
 
     other_dkv = to_plane(dkv_send, 1)
     other_od = to_plane(od_send, 3)
-    for flip in (1, 2):
-        scale = scale + to_image(scale, flip)
+    scale = scale + to_image(scale, 1) + to_image(scale, 2) + to_image(scale, 3)
     all_parts = run_sum(od, other_od, dkv, other_dkv, own_rows, scale, to_image(scale, 4))
     all_back = exchange(all_parts)
     dk_c, dv_c, after = run_join(of_image, dk_own, dv_own, k_coarse[0])

time: 142 us -> 144 us (1.014)
  Pallas kernels: 29.4 us -> 32.9 us
  starting transfers between devices: 27.7 us -> 24.5 us
  waiting for transfers between devices: 34.2 us -> 36.4 us
    ppermute x3 -> x4, waiting for transfers between devices: 10.1 us -> 12.7 us  [to_image(): return lax.ppermute(array, 'dp', [(i, i ^ flip) for i in range(images)])]
    pallas_call x1, Pallas kernels: 8.74 us -> 11.2 us  [run_fine(): pl.pallas_call(backward_kernel, out_shape=(half, half, half, half, low(so...]
    ppermute x3 -> x4, starting transfers between devices: 5.31 us -> 3.35 us  [to_image(): return lax.ppermute(array, 'dp', [(i, i ^ flip) for i in range(images)])]
  transfers between devices with their start and end apart: 13 -> 14, of which waited for: 10 -> 10; matrix products, arithmetic and copies ran while one was open for 1% -> 1% of each run, Pallas kernels for 8% -> 8%
where the time goes in v4:
time: 144 us; the launch traced here: 143 us
  waiting for transfers between devices  36.4 us (25%)
  Pallas kernels  32.9 us (23%)
  starting transfers between devices  24.5 us (17%)
  blocking collectives  19.7 us (14%)
  local copies, waits for them, and re-layouts  15.7 us (11%)
  between operations  14.2 us (10%)
    all_to_all x1, blocking collectives, exchange(): lax.all_to_all(parts, 'seq', 0, 0, axis_index_groups=groups, tiled=True)  19.7 us
    ppermute x8, starting transfers between devices, to_plane(): return lax.ppermute(array, 'seq', [(i, i ^ 2 * flip) for i in range(seq)])  16.7 us
    ppermute x8, waiting for transfers between devices, to_plane(): return lax.ppermute(array, 'seq', [(i, i ^ 2 * flip) for i in range(seq)])  14.1 us
    unnamed x34, local copies, waits for them, and re-layouts  13.3 us
    ppermute x4, waiting for transfers between devices, to_image(): return lax.ppermute(array, 'dp', [(i, i ^ flip) for i in range(images)])  12.7 us
    pallas_call x1, Pallas kernels, run_fine(): pl.pallas_call(backward_kernel, out_shape=(half, half, half, half, low(so...  11.2 us
    all_to_all x1, waiting for transfers between devices, exchange(): lax.all_to_all(parts, 'seq', 0, 0, axis_index_groups=groups, tiled=True)  9.55 us
    pallas_call x1, Pallas kernels, run_coarse(): pl.pallas_call(coarse_kernel, out_shape=(low, low, wide, wide, jax.ShapeD...  7.81 us
  transfers between devices with their start and end apart: 14, of which 10 were waited for; matrix products, arithmetic and copies ran while one was open for 1% of the time, Pallas kernels for 8%

profile of v4, /device:TPU:1, one launch (start us, length us, event | category | flops | bytes accessed | tf_op | source)
XLA Modules:
  0.0 143.4 jit_solution(10659479925369661831)
XLA Ops:
  7.2 0.0 copy-start.16
  7.2 0.0 all-gather.3.cloned.1.call-start
  7.2 2.3 %pack_heads.1 = bf16[8,400,128]{2,1,0:T(8,128)(2,1)} custom-call(s32[1,96]{1,0:T(1,128)} %ids_ref.1, bf16[96,1024]{1,0:T(8,128)(2,1)} %bitcast.25, bf16[96,1024]{1,0:T(8,128)(2,1)} %bitcast.26, bf16[96,1024]{1,0:T(8,128)(2,1)} %bitcast.27, bf16[96,1024]{1,0:T(8,128)(2,1)} %bitcast.28), custom_call_target="tpu_custom_call" | custom-call | tf_op jit(solution)/shard_map/pack_heads/pallas_call | solution.py:103
  9.5 19.7 %all_to_all.10.own_ref = bf16[8,400,128]{2,1,0:T(8,128)(2,1)S(1)} all-to-all(bf16[8,400,128]{2,1,0:T(8,128)(2,1)} %pack_heads.1), channel_id=1, replica_groups={{0,1,8,9,16,17,24,25},{2,3,10,11,18,19,26,27},{4,5,12,13,20,21,28,29},{..., dimensions={0} | all-to-all | bytes 1638400 | tf_op jit(solution)/shard_map/all_to_all | solution.py:678
  29.2 1.0 fusion
  30.2 5.3 %collective-permute-start.1 = (bf16[8,208,128]{2,1,0:T(8,128)(2,1)}, bf16[8,208,128]{2,1,0:T(8,128)(2,1)}, u32[]{:S(2)}, u32[]{:S(2)}) collective-permute-start(bf16[8,208,128]{2,1,0:T(8,128)(2,1)} %get-tuple-element.69), channel_id=1, source_target_pairs={{0,6},{1,7},{2,4},{3,5},{4,2},{5,3},{6,0},{7,1},{8,14},{9,15},{10,... | collective-permute-start | bytes 1277960 | tf_op jit(solution)/shard_map/ppermute | solution.py:681
  35.5 1.2 collective-permute-start
  36.7 1.5 %copy.20.row_level_ref = s32[256,1]{1,0:T(8,128)} copy(s32[256,1]{0,1:T(1,128)} %bitcast.21) | data formatting | bytes 2048 | tf_op jit(solution)/shard_map/broadcast_in_dim;squeeze | solution.py:520
  38.1 0.0 copy-start.1
  38.1 1.0 copy-done.1
  39.2 0.0 copy-start.8
  39.2 0.9 copy-done.8
  40.1 0.7 copy-done.9
  40.8 0.0 copy-start.10
  40.8 1.0 copy-done.10
  41.8 0.0 copy-start.11
  41.8 1.0 copy-done.11
  42.9 0.0 copy-start.12
  42.9 1.0 copy-done.12
  43.9 0.0 copy-start.15
  43.9 0.7 copy-done.15
  44.6 7.8 %coarse_attention.1 = (bf16[256,1024]{1,0:T(8,128)(2,1)}, bf16[256,1024]{1,0:T(8,128)(2,1)}, f32[256,1024]{1,0:T(8,128)S(1)}, f32[256,1024]{1,0:T(8,128)S(1)}, f...) custom-call(f32[8]{0:T(128)S(1)} %copy-done.15, s32[256,1]{1,0:T(8,128)S(1)} %copy-done.8, ...), custom_call_target="tpu_custom_call" | custom-call | flops 805306368 | bytes 6291456 | tf_op jit(solution)/shard_map/coarse_attention/pallas_call | solution.py:508
  52.4 1.7 %collective-permute-done.1.qc_ref = bf16[8,208,128]{2,1,0:T(8,128)(2,1)} collective-permute-done((bf16[8,208,128]{2,1,0:T(8,128)(2,1)}, bf16[8,208,128]{2,1,0:T(8,128)(2,1)}, u32[]{:S(2)}, u32[]{:S(2)}) %collective-permute-start.1) | collective-permute-done | bytes 426016 | tf_op jit(solution)/shard_map/ppermute | solution.py:681
  54.0 1.5 %collective-permute-done.kv_ref = bf16[8,208,128]{2,1,0:T(8,128)(2,1)} collective-permute-done((bf16[8,208,128]{2,1,0:T(8,128)(2,1)}, bf16[8,208,128]{2,1,0:T(8,128)(2,1)}, u32[]{:S(2)}, u32[]{:S(2)}) %collective-permute-start) | collective-permute-done | bytes 426016 | tf_op jit(solution)/shard_map/ppermute | solution.py:681
  55.6 0.0 copy-done.16
  55.6 7.0 %fine_forward.1 = (bf16[1536,1664]{1,0:T(8,128)(2,1)S(1)}, bf16[1664,128]{1,0:T(8,128)(2,1)S(1)}, bf16[1664,128]{1,0:T(8,128)(2,1)S(1)}, bf16[1536,128]{1,0:T(8,...) custom-call(f32[8]{0:T(128)S(1)} %copy-done.16, ...), custom_call_target="tpu_custom_call" | custom-call | flops 1308622848 | bytes 10223616 | tf_op jit(solution)/shard_map/fine_forward/pallas_call | solution.py:379
  62.6 2.7 %collective-permute-start.2 = (f32[24,128]{1,0:T(8,128)S(1)}, f32[24,128]{1,0:T(8,128)S(1)}, u32[]{:S(2)}, u32[]{:S(2)}) collective-permute-start(f32[24,128]{1,0:T(8,128)S(1)} %get-tuple-element.44.stat_ref), channel_id=1, source_target_pairs={{0,6},{1,7},{2,4},{3,5},{4,2},{5,3},{6,0},{7,1},{8,14},{9,15},{10,... | collective-permute-start | bytes 36872 | tf_op jit(solution)/shard_map/ppermute | solution.py:681
  65.3 2.1 %collective-permute-done.2.other_stat_ref = f32[24,128]{1,0:T(8,128)S(1)} collective-permute-done((f32[24,128]{1,0:T(8,128)S(1)}, f32[24,128]{1,0:T(8,128)S(1)}, u32[]{:S(2)}, u32[]{:S(2)}) %collective-permute-start.2) | collective-permute-done | bytes 12320 | tf_op jit(solution)/shard_map/ppermute | solution.py:681
  67.4 11.2 %fine_backward.1 = (bf16[768,256]{1,0:T(8,128)(2,1)S(1)}, bf16[768,256]{1,0:T(8,128)(2,1)S(1)}, bf16[768,256]{1,0:T(8,128)(2,1)S(1)}, bf16[768,256]{1,0:T(8,128)(2,1)S(1)}, bf16[144,256]{1,0:T(8,128)(2,1)S(1)}) custom-call(f32[8]{0:T(128)S(1)} %copy-done.16, s32[1]{0:T(128)} %get-tuple-element.43.shared_ref, bf16[8,400,128]{2,1,0:T(8,128)(2,1)S(1)} %all_to_all.10.own_ref, ...), custom_call_target="tpu_custom_call" | custom-call | flops 2617245696 | bytes 10223616 | tf_op jit(solution)/shard_map/fine_backward/pallas_call | solution.py:408
  78.6 0.0 copy-start.3
  78.6 0.7 copy-done.3
  79.3 0.7 copy-done.5
  80.1 0.8 copy-done.13
  80.8 0.7 copy-done.14
  81.6 2.2 %collective-permute-start.5 = (bf16[144,256]{1,0:T(8,128)(2,1)S(1)}, bf16[144,256]{1,0:T(8,128)(2,1)S(1)}, u32[]{:S(2)}, u32[]{:S(2)}) collective-permute-start(bf16[144,256]{1,0:T(8,128)(2,1)S(1)} %get-tuple-element.52.own_ref), channel_id=1, source_target_pairs={{0,6},{1,7},{2,4},{3,5},{4,2},{5,3},{6,0},{7,1},{8,14},{9,15},{10,... | collective-permute-start | bytes 221192 | tf_op jit(solution)/shard_map/ppermute | solution.py:681
  83.8 3.0 %collective-permute-start.4 = (bf16[144,256]{1,0:T(8,128)(2,1)S(1)}, bf16[144,256]{1,0:T(8,128)(2,1)S(1)}, u32[]{:S(2)}, u32[]{:S(2)}) collective-permute-start(bf16[144,256]{1,0:T(8,128)(2,1)S(1)} %get-tuple-element.52.own_ref), channel_id=1, source_target_pairs={{0,4},{1,5},{2,6},{3,7},{4,0},{5,1},{6,2},{7,3},{8,12},{9,13},{10,... | collective-permute-start | bytes 221192 | tf_op jit(solution)/shard_map/ppermute | solution.py:681
  86.8 0.4 collective-permute-start.3
  87.2 0.0 collective-permute-done.5.far_ref
  87.3 4.2 %collective-permute-done.4.across_ref = bf16[144,256]{1,0:T(8,128)(2,1)S(1)} collective-permute-done((bf16[144,256]{1,0:T(8,128)(2,1)S(1)}, bf16[144,256]{1,0:T(8,128)(2,1)S(1)}, u32[]{:S(2)}, u32[]{:S(2)}) %collective-permute-start.4) | collective-permute-done | bytes 73760 | tf_op jit(solution)/shard_map/ppermute | solution.py:681
  91.4 2.0 %collective-permute-done.3.near_ref = bf16[144,256]{1,0:T(8,128)(2,1)S(1)} collective-permute-done((bf16[144,256]{1,0:T(8,128)(2,1)S(1)}, bf16[144,256]{1,0:T(8,128)(2,1)S(1)}, u32[]{:S(2)}, u32[]{:S(2)}) %collective-permute-start.3) | collective-permute-done | bytes 73760 | tf_op jit(solution)/shard_map/ppermute | solution.py:681
  93.5 0.0 copy-start.7
  93.5 0.6 copy-done.7
  94.1 0.0 all-gather.3.cloned.1.call-update
  94.1 0.2 collective-permute-start.6
  94.3 1.7 %collective-permute-start.7 = (bf16[768,256]{1,0:T(8,128)(2,1)}, bf16[768,256]{1,0:T(8,128)(2,1)S(1)}, u32[]{:S(2)}, u32[]{:S(2)}) collective-permute-start(bf16[768,256]{1,0:T(8,128)(2,1)} %copy-done.13), channel_id=1, source_target_pairs={{0,2},{1,3},{2,0},{3,1},{4,6},{5,7},{6,4},{7,5},{8,10},{9,11},{10,... | collective-permute-start | bytes 1179656 | tf_op jit(solution)/shard_map/ppermute | solution.py:681
  96.1 2.1 %collective-permute-start.10 = (f32[8,128]{1,0:T(8,128)S(1)}, f32[8,128]{1,0:T(8,128)S(1)}, u32[]{:S(2)}, u32[]{:S(2)}) collective-permute-start(f32[8,128]{1,0:T(8,128)S(1)} %get-tuple-element.62), channel_id=1, source_target_pairs={{0,96},{32,64},{64,32},{96,0},{128,224},{160,192},{192,160},{224,1... | collective-permute-start | bytes 12296 | tf_op jit(solution)/shard_map/ppermute | solution.py:684
  98.1 0.0 collective-permute-start.9
  98.1 1.2 collective-permute-start.8
  99.3 0.4 collective-permute-done.10
  99.7 2.6 %collective-permute-done.9 = f32[8,128]{1,0:T(8,128)S(1)} collective-permute-done((f32[8,128]{1,0:T(8,128)S(1)}, f32[8,128]{1,0:T(8,128)S(1)}, u32[]{:S(2)}, u32[]{:S(2)}) %collective-permute-start.9) | collective-permute-done | bytes 4128 | tf_op jit(solution)/shard_map/ppermute | solution.py:684
  102.4 0.0 collective-permute-done.8
  102.4 0.1 collective-permute-start.11
  102.5 9.7 %collective-permute-done.11.other_scale_ref = f32[8,128]{1,0:T(8,128)S(1)} collective-permute-done((f32[8,128]{1,0:T(8,128)S(1)}, f32[8,128]{1,0:T(8,128)S(1)}, u32[]{:S(2)}, u32[]{:S(2)}) %collective-permute-start.11) | collective-permute-done | bytes 4128 | tf_op jit(solution)/shard_map/ppermute | solution.py:684
  112.1 2.7 %collective-permute-done.6.other_od_ref = bf16[768,256]{1,0:T(8,128)(2,1)S(1)} collective-permute-done((bf16[768,256]{1,0:T(8,128)(2,1)}, bf16[768,256]{1,0:T(8,128)(2,1)S(1)}, u32[]{:S(2)}, u32[]{:S(2)}) %collective-permute-start.6) | collective-permute-done | bytes 393248 | tf_op jit(solution)/shard_map/ppermute | solution.py:681
  114.8 0.0 collective-permute-done.7.other_dkv_ref
  114.8 1.0 copy-done.4
  115.8 1.0 copy-done.6
  116.8 1.7 %sum_pairs.1 = bf16[8,400,128]{2,1,0:T(8,128)(2,1)} custom-call(bf16[768,256]{1,0:T(8,128)(2,1)S(1)} %copy-done.4, bf16[768,256]{1,0:T(8,128)(2,1)S(1)} %collective-permute-done.6.other_od_ref, bf16[768,256]{1,0:T(8,128)(2,1)S(1)} %copy-done.6, bf16[768,256]{1,0:T(8,128)(2,1)S(1)} %collective-permute-done.7.other_dkv_ref, ...), custom_call_target="tpu_custom_call" | custom-call | tf_op jit(solution)/shard_map/sum_pairs/pallas_call | solution.py:593
  118.5 4.5 %all-to-all-start.1 = ((bf16[8,400,128]{2,1,0:T(8,128)(2,1)}), bf16[8,400,128]{2,1,0:T(8,128)(2,1)S(1)}, u32[]{:S(2)}, u32[]{:S(2)}) async-start(bf16[8,400,128]{2,1,0:T(8,128)(2,1)} %sum_pairs.1), calls=%async_computation.1 | async-start | bytes 1638400 | tf_op jit(solution)/shard_map/all_to_all | solution.py:678
  123.0 0.0 copy-done.2
  123.0 1.2 copy-done
  124.2 1.9 %join_coarse.1 = (bf16[256,1024]{1,0:T(8,128)(2,1)}, bf16[256,1024]{1,0:T(8,128)(2,1)}, f32[8,128]{1,0:T(8,128)S(1)}) custom-call(bf16[8,256,256]{2,1,0:T(8,128)(2,1)S(1)} %bitcast.18, f32[256,1024]{1,0:T(8,128)S(1)} %get-tuple-element.54.dk_own_ref, f32[256,1024]{1,0:T(8,128)S(1)} %get-tuple-element.55.dv_own_ref, bf16[256,1024]{1,0:T(8,128)(2,1)S(1)} %bitcast.20), custom_call_target="tpu_custom_call" | custom-call | tf_op jit(solution)/shard_map/join_coarse/pallas_call | solution.py:622
  126.1 9.5 %all-to-all-done.1.all_ref = bf16[8,400,128]{2,1,0:T(8,128)(2,1)S(1)} async-done(((bf16[8,400,128]{2,1,0:T(8,128)(2,1)}), bf16[8,400,128]{2,1,0:T(8,128)(2,1)S(1)}, u32[]{:S(2)}, u32[]{:S(2)}) %all-to-all-start.1) | async-done | bytes 819232 | tf_op jit(solution)/shard_map/all_to_all | solution.py:678
  135.6 0.9 unpack_heads.1
  (11 shorter events, 0.1 us)
Async XLA Ops:
  7.2 48.4 %copy-start.16 = (f32[8]{0:T(128)S(1)}, f32[8]{0:T(128)}, u32[]{:S(2)}) copy-start(f32[8]{0:T(128)} %log_ref.5) | copy-start | bytes 100
  7.2 115.8 %all-gather.3.cloned.1.call-start = ((), (), s32[]{:S(2)}) async-start(), calls=%async_computation.2 | async-start | bytes 1179648 | tf_op jit(solution)/shard_map/all_gather | solution.py:698
  30.2 23.8 %collective-permute-start.1 = (bf16[8,208,128]{2,1,0:T(8,128)(2,1)}, bf16[8,208,128]{2,1,0:T(8,128)(2,1)}, u32[]{:S(2)}, u32[]{:S(2)}) collective-permute-start(bf16[8,208,128]{2,1,0:T(8,128)(2,1)} %get-tuple-element.69), channel_id=1, source_target_pairs={{0,6},{1,7},{2,4},{3,5},{4,2},{5,3},{6,0},{7,1},{8,14},{9,15},{10,... | collective-permute-start | bytes 1277960 | tf_op jit(solution)/shard_map/ppermute | solution.py:681
  35.5 20.1 %collective-permute-start = (bf16[8,208,128]{2,1,0:T(8,128)(2,1)}, bf16[8,208,128]{2,1,0:T(8,128)(2,1)}, u32[]{:S(2)}, u32[]{:S(2)}) collective-permute-start(bf16[8,208,128]{2,1,0:T(8,128)(2,1)} %get-tuple-element.70), channel_id=1, source_target_pairs={{0,2},{1,3},{2,0},{3,1},{4,6},{5,7},{6,4},{7,5},{8,10},{9,11},{10,... | collective-permute-start | bytes 1277960 | tf_op jit(solution)/shard_map/ppermute | solution.py:681
  38.1 1.0 copy-start.1
  39.2 0.9 copy-start.8
  40.1 0.7 copy-start.9
  40.8 1.0 copy-start.10
  41.8 1.0 copy-start.11
  42.9 1.0 copy-start.12
  43.9 0.7 copy-start.15
  62.6 4.7 %collective-permute-start.2 = (f32[24,128]{1,0:T(8,128)S(1)}, f32[24,128]{1,0:T(8,128)S(1)}, u32[]{:S(2)}, u32[]{:S(2)}) collective-permute-start(f32[24,128]{1,0:T(8,128)S(1)} %get-tuple-element.44.stat_ref), channel_id=1, source_target_pairs={{0,6},{1,7},{2,4},{3,5},{4,2},{5,3},{6,0},{7,1},{8,14},{9,15},{10,... | collective-permute-start | bytes 36872 | tf_op jit(solution)/shard_map/ppermute | solution.py:681
  67.4 55.6 %copy-start.2 = (bf16[1,256,1024]{2,1,0:T(8,128)(2,1)S(1)}, bf16[1,256,1024]{2,1,0:T(8,128)(2,1)}, u32[]{:S(2)}) copy-start(bf16[1,256,1024]{2,1,0:T(8,128)(2,1)} %param.12) | copy-start | bytes 1572868
  78.6 0.7 copy-start.3
  79.3 0.8 copy-start.5
  80.1 0.8 copy-start.13
  80.8 0.7 copy-start.14
  81.6 5.7 %collective-permute-start.5 = (bf16[144,256]{1,0:T(8,128)(2,1)S(1)}, bf16[144,256]{1,0:T(8,128)(2,1)S(1)}, u32[]{:S(2)}, u32[]{:S(2)}) collective-permute-start(bf16[144,256]{1,0:T(8,128)(2,1)S(1)} %get-tuple-element.52.own_ref), channel_id=1, source_target_pairs={{0,6},{1,7},{2,4},{3,5},{4,2},{5,3},{6,0},{7,1},{8,14},{9,15},{10,... | collective-permute-start | bytes 221192 | tf_op jit(solution)/shard_map/ppermute | solution.py:681
  83.8 7.6 %collective-permute-start.4 = (bf16[144,256]{1,0:T(8,128)(2,1)S(1)}, bf16[144,256]{1,0:T(8,128)(2,1)S(1)}, u32[]{:S(2)}, u32[]{:S(2)}) collective-permute-start(bf16[144,256]{1,0:T(8,128)(2,1)S(1)} %get-tuple-element.52.own_ref), channel_id=1, source_target_pairs={{0,4},{1,5},{2,6},{3,7},{4,0},{5,1},{6,2},{7,3},{8,12},{9,13},{10,... | collective-permute-start | bytes 221192 | tf_op jit(solution)/shard_map/ppermute | solution.py:681
  86.8 6.6 %collective-permute-start.3 = (bf16[144,256]{1,0:T(8,128)(2,1)S(1)}, bf16[144,256]{1,0:T(8,128)(2,1)S(1)}, u32[]{:S(2)}, u32[]{:S(2)}) collective-permute-start(bf16[144,256]{1,0:T(8,128)(2,1)S(1)} %get-tuple-element.52.own_ref), channel_id=1, source_target_pairs={{0,2},{1,3},{2,0},{3,1},{4,6},{5,7},{6,4},{7,5},{8,10},{9,11},{10,... | collective-permute-start | bytes 221192 | tf_op jit(solution)/shard_map/ppermute | solution.py:681
  93.5 0.7 copy-start.7
  94.1 20.7 %collective-permute-start.6 = (bf16[768,256]{1,0:T(8,128)(2,1)}, bf16[768,256]{1,0:T(8,128)(2,1)S(1)}, u32[]{:S(2)}, u32[]{:S(2)}) collective-permute-start(bf16[768,256]{1,0:T(8,128)(2,1)} %copy-done.14), channel_id=1, source_target_pairs={{0,6},{1,7},{2,4},{3,5},{4,2},{5,3},{6,0},{7,1},{8,14},{9,15},{10,... | collective-permute-start | bytes 1179656 | tf_op jit(solution)/shard_map/ppermute | solution.py:681
  94.3 20.5 %collective-permute-start.7 = (bf16[768,256]{1,0:T(8,128)(2,1)}, bf16[768,256]{1,0:T(8,128)(2,1)S(1)}, u32[]{:S(2)}, u32[]{:S(2)}) collective-permute-start(bf16[768,256]{1,0:T(8,128)(2,1)} %copy-done.13), channel_id=1, source_target_pairs={{0,2},{1,3},{2,0},{3,1},{4,6},{5,7},{6,4},{7,5},{8,10},{9,11},{10,... | collective-permute-start | bytes 1179656 | tf_op jit(solution)/shard_map/ppermute | solution.py:681
  96.1 3.7 %collective-permute-start.10 = (f32[8,128]{1,0:T(8,128)S(1)}, f32[8,128]{1,0:T(8,128)S(1)}, u32[]{:S(2)}, u32[]{:S(2)}) collective-permute-start(f32[8,128]{1,0:T(8,128)S(1)} %get-tuple-element.62), channel_id=1, source_target_pairs={{0,96},{32,64},{64,32},{96,0},{128,224},{160,192},{192,160},{224,1... | collective-permute-start | bytes 12296 | tf_op jit(solution)/shard_map/ppermute | solution.py:684
  98.1 4.3 %collective-permute-start.9 = (f32[8,128]{1,0:T(8,128)S(1)}, f32[8,128]{1,0:T(8,128)S(1)}, u32[]{:S(2)}, u32[]{:S(2)}) collective-permute-start(f32[8,128]{1,0:T(8,128)S(1)} %get-tuple-element.62), channel_id=1, source_target_pairs={{0,64},{32,96},{64,0},{96,32},{128,192},{160,224},{192,128},{224,1... | collective-permute-start | bytes 12296 | tf_op jit(solution)/shard_map/ppermute | solution.py:684
  98.1 4.3 %collective-permute-start.8 = (f32[8,128]{1,0:T(8,128)S(1)}, f32[8,128]{1,0:T(8,128)S(1)}, u32[]{:S(2)}, u32[]{:S(2)}) collective-permute-start(f32[8,128]{1,0:T(8,128)S(1)} %get-tuple-element.62), channel_id=1, source_target_pairs={{0,32},{32,0},{64,96},{96,64},{128,160},{160,128},{192,224},{224,1... | collective-permute-start | bytes 12296 | tf_op jit(solution)/shard_map/ppermute | solution.py:684
  102.4 9.8 %collective-permute-start.11 = (f32[8,128]{1,0:T(8,128)S(1)}, f32[8,128]{1,0:T(8,128)S(1)}, u32[]{:S(2)}, u32[]{:S(2)}) collective-permute-start(f32[8,128]{1,0:T(8,128)S(1)} %add_add_fusion.scale_ref), channel_id=1, source_target_pairs={{0,128},{32,160},{64,192},{96,224},{128,0},{160,32},{192,64},{224,... | collective-permute-start | bytes 12296 | tf_op jit(solution)/shard_map/ppermute | solution.py:684
  114.8 1.0 copy-start.4
  115.8 1.0 copy-start.6
  118.5 17.1 %all-to-all-start.1 = ((bf16[8,400,128]{2,1,0:T(8,128)(2,1)}), bf16[8,400,128]{2,1,0:T(8,128)(2,1)S(1)}, u32[]{:S(2)}, u32[]{:S(2)}) async-start(bf16[8,400,128]{2,1,0:T(8,128)(2,1)} %sum_pairs.1), calls=%async_computation.1 | async-start | bytes 1638400 | tf_op jit(solution)/shard_map/all_to_all | solution.py:678
  123.0 1.2 copy-start
Sparse Core Ops, SparseCore 0:
  94.3 24.2 all-gather.2

commit v5 on v3

--- a/solution.py
+++ b/solution.py
@@ -70,6 +70,9 @@
 
 def query_slot(plane):
     return lax.shift_right_logical(plane, 1)
+
+
+late_chain = pl.CostEstimate(flops=60_000_000_000, bytes_accessed=0, transcendentals=0)
 
 
 def params(mebibytes):
@@ -559,6 +562,7 @@
         sum_kernel,
         out_shape=jax.ShapeDtypeStruct(own_rows.shape, jnp.bfloat16),
         compiler_params=params(6),
+        cost_estimate=late_chain,
         name="sum_pairs",
     )(od, other_od, dkv, other_dkv, own_rows, scale, other_scale)
 
@@ -606,6 +610,7 @@
         in_specs=[vmem, vmem],
         out_specs=(vmem,) * 4 + (pl.BlockSpec(memory_space=pltpu.SMEM),),
         compiler_params=params(3),
+        cost_estimate=late_chain,
         name="unpack_heads",
     )(all_back, after)
 
@@ -657,8 +662,7 @@
 
     other_dkv = to_plane(dkv_send, 1)
     other_od = to_plane(od_send, 3)
-    for flip in (1, 2):
-        scale = scale + to_image(scale, flip)
+    scale = scale + to_image(scale, 1) + to_image(scale, 2) + to_image(scale, 3)
     all_parts = run_sum(od, other_od, dkv, other_dkv, own_rows, scale, to_image(scale, 4))
     all_back = exchange(all_parts)
     dk_c, dv_c, after = run_join(of_image, dk_own, dv_own, k_coarse[0])

time: 142 us -> 152 us (1.070)
  waiting for transfers between devices: 34.2 us -> 44.1 us
    ppermute x8, waiting for transfers between devices: 14.6 us -> 27.3 us  [to_plane(): return lax.ppermute(array, 'seq', [(i, i ^ 2 * flip) for i in range(seq)])]
    all_gather x1, waiting for transfers between devices: 0.01 us -> 11.4 us  [body(): lax.all_gather(small_sum, 'seq', axis=0, axis_index_groups=groups)]
    all_to_all x1, waiting for transfers between devices: 9.55 us -> 0.01 us  [exchange(): lax.all_to_all(parts, 'seq', 0, 0, axis_index_groups=groups, tiled=True)]
    ppermute x3 -> x4, waiting for transfers between devices: 10.1 us -> 5.25 us  [to_image(): return lax.ppermute(array, 'dp', [(i, i ^ flip) for i in range(images)])]
    ppermute x3 -> x4, starting transfers between devices: 5.31 us -> 3.7 us  [to_image(): return lax.ppermute(array, 'dp', [(i, i ^ flip) for i in range(images)])]
    unnamed x34 -> x32, local copies, waits for them, and re-layouts: 13.3 us -> 12.9 us
  transfers between devices with their start and end apart: 13 -> 14, of which waited for: 10 -> 9; matrix products, arithmetic and copies ran while one was open for 1% -> 1% of each run, Pallas kernels for 8% -> 8%
where the time goes in v5:
time: 152 us; the launch traced here: 151 us
  waiting for transfers between devices  44.1 us (29%)
  Pallas kernels  30.3 us (20%)
  starting transfers between devices  27.9 us (18%)
  blocking collectives  19.7 us (13%)
  local copies, waits for them, and re-layouts  14.6 us (10%)
  between operations  14.1 us (9%)
    ppermute x8, waiting for transfers between devices, to_plane(): return lax.ppermute(array, 'seq', [(i, i ^ 2 * flip) for i in range(seq)])  27.3 us
    all_to_all x1, blocking collectives, exchange(): lax.all_to_all(parts, 'seq', 0, 0, axis_index_groups=groups, tiled=True)  19.7 us
    ppermute x8, starting transfers between devices, to_plane(): return lax.ppermute(array, 'seq', [(i, i ^ 2 * flip) for i in range(seq)])  17.6 us
    unnamed x32, local copies, waits for them, and re-layouts  12.9 us
    all_gather x1, waiting for transfers between devices, body(): lax.all_gather(small_sum, 'seq', axis=0, axis_index_groups=groups)  11.4 us
    pallas_call x1, Pallas kernels, run_fine(): pl.pallas_call(backward_kernel, out_shape=(half, half, half, half, low(so...  8.98 us
    pallas_call x1, Pallas kernels, run_coarse(): pl.pallas_call(coarse_kernel, out_shape=(low, low, wide, wide, jax.ShapeD...  7.79 us
    all_to_all x1, starting transfers between devices, exchange(): lax.all_to_all(parts, 'seq', 0, 0, axis_index_groups=groups, tiled=True)  6.53 us
  transfers between devices with their start and end apart: 14, of which 9 were waited for; matrix products, arithmetic and copies ran while one was open for 1% of the time, Pallas kernels for 8%

profile of v5, /device:TPU:1, one launch (start us, length us, event | category | flops | bytes accessed | tf_op | source)
XLA Modules:
  0.0 150.7 jit_solution(12764019203507598745)
XLA Ops:
  7.2 0.0 copy-start.11
  7.2 0.0 all-gather.3.cloned.1.call-start
  7.2 2.3 %pack_heads.1 = bf16[8,400,128]{2,1,0:T(8,128)(2,1)} custom-call(s32[1,96]{1,0:T(1,128)} %ids_ref.1, bf16[96,1024]{1,0:T(8,128)(2,1)} %bitcast.25, bf16[96,1024]{1,0:T(8,128)(2,1)} %bitcast.26, bf16[96,1024]{1,0:T(8,128)(2,1)} %bitcast.27, bf16[96,1024]{1,0:T(8,128)(2,1)} %bitcast.28), custom_call_target="tpu_custom_call" | custom-call | tf_op jit(solution)/shard_map/pack_heads/pallas_call | solution.py:106
  9.5 19.7 %all_to_all.10.own_ref = bf16[8,400,128]{2,1,0:T(8,128)(2,1)S(1)} all-to-all(bf16[8,400,128]{2,1,0:T(8,128)(2,1)} %pack_heads.1), channel_id=1, replica_groups={{0,1,8,9,16,17,24,25},{2,3,10,11,18,19,26,27},{4,5,12,13,20,21,28,29},{..., dimensions={0} | all-to-all | bytes 1638400 | tf_op jit(solution)/shard_map/all_to_all | solution.py:641
  29.2 1.0 fusion
  30.2 5.3 %collective-permute-start.1 = (bf16[8,208,128]{2,1,0:T(8,128)(2,1)}, bf16[8,208,128]{2,1,0:T(8,128)(2,1)S(1)}, u32[]{:S(2)}, u32[]{:S(2)}) collective-permute-start(bf16[8,208,128]{2,1,0:T(8,128)(2,1)} %get-tuple-element.69), channel_id=1, source_target_pairs={{0,6},{1,7},{2,4},{3,5},{4,2},{5,3},{6,0},{7,1},{8,14},{9,15},{10,... | collective-permute-start | bytes 1277960 | tf_op jit(solution)/shard_map/ppermute | solution.py:644
  35.5 1.2 collective-permute-start
  36.7 0.8 copy.20.row_level_ref
  37.5 0.0 copy-start.2
  37.5 1.0 copy-done.2
  38.5 0.7 copy-done.4
  39.2 0.0 copy-start.5
  39.2 1.0 copy-done.5
  40.2 0.0 copy-start.6
  40.2 1.0 copy-done.6
  41.3 0.0 copy-start.7
  41.3 1.0 copy-done.7
  42.3 0.0 copy-start.10
  42.3 0.7 copy-done.10
  43.0 7.8 %coarse_attention.1 = (bf16[256,1024]{1,0:T(8,128)(2,1)}, bf16[256,1024]{1,0:T(8,128)(2,1)}, f32[256,1024]{1,0:T(8,128)S(1)}, f32[256,1024]{1,0:T(8,128)S(1)}, f...) custom-call(f32[8]{0:T(128)S(1)} %copy-done.10, ...), custom_call_target="tpu_custom_call" | custom-call | flops 805306368 | bytes 6291456 | tf_op jit(solution)/shard_map/coarse_attention/pallas_call | solution.py:496
  50.8 3.2 %collective-permute-done.1.qc_ref = bf16[8,208,128]{2,1,0:T(8,128)(2,1)S(1)} collective-permute-done((bf16[8,208,128]{2,1,0:T(8,128)(2,1)}, bf16[8,208,128]{2,1,0:T(8,128)(2,1)S(1)}, u32[]{:S(2)}, u32[]{:S(2)}) %collective-permute-start.1) | collective-permute-done | bytes 426016 | tf_op jit(solution)/shard_map/ppermute | solution.py:644
  54.0 1.5 %collective-permute-done.kv_ref = bf16[8,208,128]{2,1,0:T(8,128)(2,1)} collective-permute-done((bf16[8,208,128]{2,1,0:T(8,128)(2,1)}, bf16[8,208,128]{2,1,0:T(8,128)(2,1)}, u32[]{:S(2)}, u32[]{:S(2)}) %collective-permute-start) | collective-permute-done | bytes 426016 | tf_op jit(solution)/shard_map/ppermute | solution.py:644
  55.5 0.0 copy-done.11
  55.5 6.2 %fine_forward.1 = (bf16[1536,1664]{1,0:T(8,128)(2,1)S(1)}, bf16[1664,128]{1,0:T(8,128)(2,1)S(1)}, bf16[1664,128]{1,0:T(8,128)(2,1)S(1)}, bf16[1536,128]{1,0:T(8,...) custom-call(f32[8]{0:T(128)S(1)} %copy-done.11, ...), custom_call_target="tpu_custom_call" | custom-call | flops 1308622848 | bytes 10223616 | tf_op jit(solution)/shard_map/fine_forward/pallas_call | solution.py:369
  61.8 2.8 %collective-permute-start.2 = (f32[24,128]{1,0:T(8,128)S(1)}, f32[24,128]{1,0:T(8,128)S(1)}, u32[]{:S(2)}, u32[]{:S(2)}) collective-permute-start(f32[24,128]{1,0:T(8,128)S(1)} %get-tuple-element.44.stat_ref), channel_id=1, source_target_pairs={{0,6},{1,7},{2,4},{3,5},{4,2},{5,3},{6,0},{7,1},{8,14},{9,15},{10,... | collective-permute-start | bytes 36872 | tf_op jit(solution)/shard_map/ppermute | solution.py:644
  64.6 2.0 %collective-permute-done.2.other_stat_ref = f32[24,128]{1,0:T(8,128)S(1)} collective-permute-done((f32[24,128]{1,0:T(8,128)S(1)}, f32[24,128]{1,0:T(8,128)S(1)}, u32[]{:S(2)}, u32[]{:S(2)}) %collective-permute-start.2) | collective-permute-done | bytes 12320 | tf_op jit(solution)/shard_map/ppermute | solution.py:644
  66.5 9.0 %fine_backward.1 = (bf16[768,256]{1,0:T(8,128)(2,1)S(1)}, bf16[768,256]{1,0:T(8,128)(2,1)}, bf16[768,256]{1,0:T(8,128)(2,1)S(1)}, bf16[768,256]{1,0:T(8,128)(2,1)}, bf16[144,256]{1,0:T(8,128)(2,1)S(1)}) custom-call(f32[8]{0:T(128)S(1)} %copy-done.11, s32[1]{0:T(128)} %get-tuple-element.43.shared_ref, bf16[8,400,128]{2,1,0:T(8,128)(2,1)S(1)} %all_to_all.10.own_ref, ...), custom_call_target="tpu_custom_call" | custom-call | flops 2617245696 | bytes 10223616 | tf_op jit(solution)/shard_map/fine_backward/pallas_call | solution.py:398
  75.5 0.8 copy-done.12
  76.3 0.0 copy-start.14
  76.3 0.8 copy-done.14
  77.0 2.7 %collective-permute-start.6 = (bf16[768,256]{1,0:T(8,128)(2,1)}, bf16[768,256]{1,0:T(8,128)(2,1)S(1)}, u32[]{:S(2)}, u32[]{:S(2)}) collective-permute-start(bf16[768,256]{1,0:T(8,128)(2,1)} %get-tuple-element.59), channel_id=1, source_target_pairs={{0,6},{1,7},{2,4},{3,5},{4,2},{5,3},{6,0},{7,1},{8,14},{9,15},{10,... | collective-permute-start | bytes 1179656 | tf_op jit(solution)/shard_map/ppermute | solution.py:644
  79.7 0.0 collective-permute-start.7
  79.7 2.8 %collective-permute-start.5 = (bf16[144,256]{1,0:T(8,128)(2,1)S(1)}, bf16[144,256]{1,0:T(8,128)(2,1)S(1)}, u32[]{:S(2)}, u32[]{:S(2)}) collective-permute-start(bf16[144,256]{1,0:T(8,128)(2,1)S(1)} %get-tuple-element.52.own_ref), channel_id=1, source_target_pairs={{0,6},{1,7},{2,4},{3,5},{4,2},{5,3},{6,0},{7,1},{8,14},{9,15},{10,... | collective-permute-start | bytes 221192 | tf_op jit(solution)/shard_map/ppermute | solution.py:644
  82.5 2.8 %collective-permute-start.4 = (bf16[144,256]{1,0:T(8,128)(2,1)S(1)}, bf16[144,256]{1,0:T(8,128)(2,1)S(1)}, u32[]{:S(2)}, u32[]{:S(2)}) collective-permute-start(bf16[144,256]{1,0:T(8,128)(2,1)S(1)} %get-tuple-element.52.own_ref), channel_id=1, source_target_pairs={{0,4},{1,5},{2,6},{3,7},{4,0},{5,1},{6,2},{7,3},{8,12},{9,13},{10,... | collective-permute-start | bytes 221192 | tf_op jit(solution)/shard_map/ppermute | solution.py:644
  85.4 0.0 collective-permute-start.3
  85.4 17.5 %collective-permute-done.5.far_ref = bf16[144,256]{1,0:T(8,128)(2,1)S(1)} collective-permute-done((bf16[144,256]{1,0:T(8,128)(2,1)S(1)}, bf16[144,256]{1,0:T(8,128)(2,1)S(1)}, u32[]{:S(2)}, u32[]{:S(2)}) %collective-permute-start.5) | collective-permute-done | bytes 73760 | tf_op jit(solution)/shard_map/ppermute | solution.py:644
  102.9 0.0 collective-permute-done.4.across_ref
  102.9 3.1 %collective-permute-done.3.near_ref = bf16[144,256]{1,0:T(8,128)(2,1)S(1)} collective-permute-done((bf16[144,256]{1,0:T(8,128)(2,1)S(1)}, bf16[144,256]{1,0:T(8,128)(2,1)S(1)}, u32[]{:S(2)}, u32[]{:S(2)}) %collective-permute-start.3) | collective-permute-done | bytes 73760 | tf_op jit(solution)/shard_map/ppermute | solution.py:644
  106.0 0.7 sum_coarse_terms.1
  106.7 2.5 %collective-permute-start.10 = (f32[8,128]{1,0:T(8,128)S(1)}, f32[8,128]{1,0:T(8,128)S(1)}, u32[]{:S(2)}, u32[]{:S(2)}) collective-permute-start(f32[8,128]{1,0:T(8,128)S(1)} %get-tuple-element.62), channel_id=1, source_target_pairs={{0,96},{32,64},{64,32},{96,0},{128,224},{160,192},{192,160},{224,1... | collective-permute-start | bytes 12296 | tf_op jit(solution)/shard_map/ppermute | solution.py:647
  109.1 0.3 collective-permute-start.9
  109.4 0.5 collective-permute-start.8
  109.9 0.4 collective-permute-done.10
  110.3 2.8 %collective-permute-done.9 = f32[8,128]{1,0:T(8,128)S(1)} collective-permute-done((f32[8,128]{1,0:T(8,128)S(1)}, f32[8,128]{1,0:T(8,128)S(1)}, u32[]{:S(2)}, u32[]{:S(2)}) %collective-permute-start.9) | collective-permute-done | bytes 4128 | tf_op jit(solution)/shard_map/ppermute | solution.py:647
  113.1 0.0 collective-permute-done.8
  113.1 0.4 collective-permute-start.11
  113.5 0.0 all-gather.3.cloned.1.call-update
  113.6 2.1 %collective-permute-done.11.other_scale_ref = f32[8,128]{1,0:T(8,128)S(1)} collective-permute-done((f32[8,128]{1,0:T(8,128)S(1)}, f32[8,128]{1,0:T(8,128)S(1)}, u32[]{:S(2)}, u32[]{:S(2)}) %collective-permute-start.11) | collective-permute-done | bytes 4128 | tf_op jit(solution)/shard_map/ppermute | solution.py:647
  115.6 0.0 collective-permute-done.6.other_od_ref
  115.7 0.7 copy-done.8
  116.4 0.0 collective-permute-done.7.other_dkv_ref
  116.4 1.0 copy-done.9
  117.4 1.0 copy-done.13
  118.4 1.0 copy-done.15
  119.4 1.5 sum_pairs.1
  120.9 0.0 copy-start.1
  120.9 0.9 copy-done.1
  121.8 6.5 %all-to-all-start.1 = ((bf16[8,400,128]{2,1,0:T(8,128)(2,1)}), bf16[8,400,128]{2,1,0:T(8,128)(2,1)S(1)}, u32[]{:S(2)}, u32[]{:S(2)}) async-start(bf16[8,400,128]{2,1,0:T(8,128)(2,1)} %copy-done.1), calls=%async_computation.1 | async-start | bytes 1638400 | tf_op jit(solution)/shard_map/all_to_all | solution.py:641
  128.3 11.4 %all-gather.3.cloned.1.call-done = bf16[2048,256]{1,0:T(8,128)(2,1)} async-done(((bf16[256,256]{1,0:T(8,128)(2,1)}), bf16[2048,256]{1,0:T(8,128)(2,1)}) %all-gather.3.cloned.1.call-update) | async-done | bytes 1048592 | tf_op jit(solution)/shard_map/all_gather | solution.py:661
  139.8 0.0 copy-done.3
  139.8 1.2 copy-done
  141.0 1.9 %join_coarse.1 = (bf16[256,1024]{1,0:T(8,128)(2,1)}, bf16[256,1024]{1,0:T(8,128)(2,1)}, f32[8,128]{1,0:T(8,128)S(1)}) custom-call(bf16[8,256,256]{2,1,0:T(8,128)(2,1)S(1)} %bitcast.18, f32[256,1024]{1,0:T(8,128)S(1)} %get-tuple-element.54.dk_own_ref, f32[256,1024]{1,0:T(8,128)S(1)} %get-tuple-element.55.dv_own_ref, bf16[256,1024]{1,0:T(8,128)(2,1)S(1)} %bitcast.20), custom_call_target="tpu_custom_call" | custom-call | tf_op jit(solution)/shard_map/join_coarse/pallas_call | solution.py:584
  142.9 0.0 all-to-all-done.1.all_ref
  142.9 0.9 unpack_heads.1
  (9 shorter events, 0.0 us)
Async XLA Ops:
  7.2 48.4 %copy-start.11 = (f32[8]{0:T(128)S(1)}, f32[8]{0:T(128)}, u32[]{:S(2)}) copy-start(f32[8]{0:T(128)} %log_ref.5) | copy-start | bytes 100
  7.2 132.6 %all-gather.3.cloned.1.call-start = ((), (), s32[]{:S(2)}) async-start(), calls=%async_computation.2 | async-start | bytes 1179648 | tf_op jit(solution)/shard_map/all_gather | solution.py:661
  30.2 23.8 %collective-permute-start.1 = (bf16[8,208,128]{2,1,0:T(8,128)(2,1)}, bf16[8,208,128]{2,1,0:T(8,128)(2,1)S(1)}, u32[]{:S(2)}, u32[]{:S(2)}) collective-permute-start(bf16[8,208,128]{2,1,0:T(8,128)(2,1)} %get-tuple-element.69), channel_id=1, source_target_pairs={{0,6},{1,7},{2,4},{3,5},{4,2},{5,3},{6,0},{7,1},{8,14},{9,15},{10,... | collective-permute-start | bytes 1277960 | tf_op jit(solution)/shard_map/ppermute | solution.py:644
  35.5 20.1 %collective-permute-start = (bf16[8,208,128]{2,1,0:T(8,128)(2,1)}, bf16[8,208,128]{2,1,0:T(8,128)(2,1)}, u32[]{:S(2)}, u32[]{:S(2)}) collective-permute-start(bf16[8,208,128]{2,1,0:T(8,128)(2,1)} %get-tuple-element.70), channel_id=1, source_target_pairs={{0,2},{1,3},{2,0},{3,1},{4,6},{5,7},{6,4},{7,5},{8,10},{9,11},{10,... | collective-permute-start | bytes 1277960 | tf_op jit(solution)/shard_map/ppermute | solution.py:644
  37.5 1.0 copy-start.2
  38.5 0.7 copy-start.4
  39.2 1.0 copy-start.5
  40.2 1.0 copy-start.6
  41.3 1.0 copy-start.7
  42.3 0.7 copy-start.10
  61.8 4.7 %collective-permute-start.2 = (f32[24,128]{1,0:T(8,128)S(1)}, f32[24,128]{1,0:T(8,128)S(1)}, u32[]{:S(2)}, u32[]{:S(2)}) collective-permute-start(f32[24,128]{1,0:T(8,128)S(1)} %get-tuple-element.44.stat_ref), channel_id=1, source_target_pairs={{0,6},{1,7},{2,4},{3,5},{4,2},{5,3},{6,0},{7,1},{8,14},{9,15},{10,... | collective-permute-start | bytes 36872 | tf_op jit(solution)/shard_map/ppermute | solution.py:644
  75.5 0.8 copy-start.12
  76.3 0.8 copy-start.14
  77.0 38.6 %collective-permute-start.6 = (bf16[768,256]{1,0:T(8,128)(2,1)}, bf16[768,256]{1,0:T(8,128)(2,1)S(1)}, u32[]{:S(2)}, u32[]{:S(2)}) collective-permute-start(bf16[768,256]{1,0:T(8,128)(2,1)} %get-tuple-element.59), channel_id=1, source_target_pairs={{0,6},{1,7},{2,4},{3,5},{4,2},{5,3},{6,0},{7,1},{8,14},{9,15},{10,... | collective-permute-start | bytes 1179656 | tf_op jit(solution)/shard_map/ppermute | solution.py:644
  79.7 36.7 %collective-permute-start.7 = (bf16[768,256]{1,0:T(8,128)(2,1)}, bf16[768,256]{1,0:T(8,128)(2,1)}, u32[]{:S(2)}, u32[]{:S(2)}) collective-permute-start(bf16[768,256]{1,0:T(8,128)(2,1)} %get-tuple-element.61), channel_id=1, source_target_pairs={{0,2},{1,3},{2,0},{3,1},{4,6},{5,7},{6,4},{7,5},{8,10},{9,11},{10,... | collective-permute-start | bytes 1179656 | tf_op jit(solution)/shard_map/ppermute | solution.py:644
  79.7 23.2 %collective-permute-start.5 = (bf16[144,256]{1,0:T(8,128)(2,1)S(1)}, bf16[144,256]{1,0:T(8,128)(2,1)S(1)}, u32[]{:S(2)}, u32[]{:S(2)}) collective-permute-start(bf16[144,256]{1,0:T(8,128)(2,1)S(1)} %get-tuple-element.52.own_ref), channel_id=1, source_target_pairs={{0,6},{1,7},{2,4},{3,5},{4,2},{5,3},{6,0},{7,1},{8,14},{9,15},{10,... | collective-permute-start | bytes 221192 | tf_op jit(solution)/shard_map/ppermute | solution.py:644
  82.5 20.3 %collective-permute-start.4 = (bf16[144,256]{1,0:T(8,128)(2,1)S(1)}, bf16[144,256]{1,0:T(8,128)(2,1)S(1)}, u32[]{:S(2)}, u32[]{:S(2)}) collective-permute-start(bf16[144,256]{1,0:T(8,128)(2,1)S(1)} %get-tuple-element.52.own_ref), channel_id=1, source_target_pairs={{0,4},{1,5},{2,6},{3,7},{4,0},{5,1},{6,2},{7,3},{8,12},{9,13},{10,... | collective-permute-start | bytes 221192 | tf_op jit(solution)/shard_map/ppermute | solution.py:644
  85.4 20.6 %collective-permute-start.3 = (bf16[144,256]{1,0:T(8,128)(2,1)S(1)}, bf16[144,256]{1,0:T(8,128)(2,1)S(1)}, u32[]{:S(2)}, u32[]{:S(2)}) collective-permute-start(bf16[144,256]{1,0:T(8,128)(2,1)S(1)} %get-tuple-element.52.own_ref), channel_id=1, source_target_pairs={{0,2},{1,3},{2,0},{3,1},{4,6},{5,7},{6,4},{7,5},{8,10},{9,11},{10,... | collective-permute-start | bytes 221192 | tf_op jit(solution)/shard_map/ppermute | solution.py:644
  106.7 3.7 %collective-permute-start.10 = (f32[8,128]{1,0:T(8,128)S(1)}, f32[8,128]{1,0:T(8,128)S(1)}, u32[]{:S(2)}, u32[]{:S(2)}) collective-permute-start(f32[8,128]{1,0:T(8,128)S(1)} %get-tuple-element.62), channel_id=1, source_target_pairs={{0,96},{32,64},{64,32},{96,0},{128,224},{160,192},{192,160},{224,1... | collective-permute-start | bytes 12296 | tf_op jit(solution)/shard_map/ppermute | solution.py:647
  109.1 4.0 %collective-permute-start.9 = (f32[8,128]{1,0:T(8,128)S(1)}, f32[8,128]{1,0:T(8,128)S(1)}, u32[]{:S(2)}, u32[]{:S(2)}) collective-permute-start(f32[8,128]{1,0:T(8,128)S(1)} %get-tuple-element.62), channel_id=1, source_target_pairs={{0,64},{32,96},{64,0},{96,32},{128,192},{160,224},{192,128},{224,1... | collective-permute-start | bytes 12296 | tf_op jit(solution)/shard_map/ppermute | solution.py:647
  109.4 3.7 %collective-permute-start.8 = (f32[8,128]{1,0:T(8,128)S(1)}, f32[8,128]{1,0:T(8,128)S(1)}, u32[]{:S(2)}, u32[]{:S(2)}) collective-permute-start(f32[8,128]{1,0:T(8,128)S(1)} %get-tuple-element.62), channel_id=1, source_target_pairs={{0,32},{32,0},{64,96},{96,64},{128,160},{160,128},{192,224},{224,1... | collective-permute-start | bytes 12296 | tf_op jit(solution)/shard_map/ppermute | solution.py:647
  113.1 2.5 %collective-permute-start.11 = (f32[8,128]{1,0:T(8,128)S(1)}, f32[8,128]{1,0:T(8,128)S(1)}, u32[]{:S(2)}, u32[]{:S(2)}) collective-permute-start(f32[8,128]{1,0:T(8,128)S(1)} %add_add_fusion.scale_ref), channel_id=1, source_target_pairs={{0,128},{32,160},{64,192},{96,224},{128,0},{160,32},{192,64},{224,... | collective-permute-start | bytes 12296 | tf_op jit(solution)/shard_map/ppermute | solution.py:647
  115.7 0.7 copy-start.8
  116.4 1.0 copy-start.9
  117.4 1.0 copy-start.13
  118.4 1.0 copy-start.15
  119.4 20.4 %copy-start.3 = (bf16[1,256,1024]{2,1,0:T(8,128)(2,1)S(1)}, bf16[1,256,1024]{2,1,0:T(8,128)(2,1)}, u32[]{:S(2)}) copy-start(bf16[1,256,1024]{2,1,0:T(8,128)(2,1)} %param.12) | copy-start | bytes 1572868
  120.9 0.9 copy-start.1
  121.8 21.1 %all-to-all-start.1 = ((bf16[8,400,128]{2,1,0:T(8,128)(2,1)}), bf16[8,400,128]{2,1,0:T(8,128)(2,1)S(1)}, u32[]{:S(2)}, u32[]{:S(2)}) async-start(bf16[8,400,128]{2,1,0:T(8,128)(2,1)} %copy-done.1), calls=%async_computation.1 | async-start | bytes 1638400 | tf_op jit(solution)/shard_map/all_to_all | solution.py:641
  139.8 1.2 copy-start
Sparse Core Ops, SparseCore 0:
  113.7 26.0 all-gather.2

commit v6 on v5

--- a/solution.py
+++ b/solution.py
@@ -70,9 +70,6 @@
 
 def query_slot(plane):
     return lax.shift_right_logical(plane, 1)
-
-
-late_chain = pl.CostEstimate(flops=60_000_000_000, bytes_accessed=0, transcendentals=0)
 
 
 def params(mebibytes):
@@ -128,14 +125,15 @@
 
 
 def all_chunks(work, some_keys, shared, chunks):
-    work(0, some_keys, 0)
+    work(0, some_keys, 0, True)
+    work(some_keys, some_keys, 0, False)
 
     def both(chunk, carry):
-        work(some_keys + chunk * k_tile, k_tile, 0)
+        work(2 * some_keys + chunk * k_tile, k_tile, 0, True)
         return carry
 
     def upper(chunk, carry):
-        work(some_keys + chunk * k_tile, k_tile, 1)
+        work(2 * some_keys + chunk * k_tile, k_tile, 1, True)
         return carry
 
     lax.fori_loop(0, shared, both, 0)
@@ -167,8 +165,9 @@
     block = 2 * rows
     runs = members // 2
     queries = query_ref.shape[0]
-    some_keys = kc_ref.shape[0] // 2
-    fine = key_ref.shape[0] - some_keys
+    coarse = kc_ref.shape[0]
+    some_keys = coarse // 2
+    fine = key_ref.shape[0] - coarse
     first_query = 2 * rows + note_rows
 
     def count(notes):
@@ -190,18 +189,21 @@
     for ref, slot in ((own_ref, own_slot), (kv_ref, 1 - own_slot)):
         for run in range(runs):
             pick = slice(2 * run, 2 * run + 2)
-            spot = pl.ds(pl.multiple_of(some_keys + place_of(run, slot, block), 64), block)
+            spot = pl.ds(pl.multiple_of(coarse + place_of(run, slot, block), 64), block)
             key_ref[spot, :] = unit_rows(ref[pick, 0:rows].reshape(block, width))[0].astype(
                 jnp.bfloat16
             )
             values = ref[pick, rows : 2 * rows].reshape(block, width)
             val_ref[spot, :] = values
             wide_scr[spot, 0:width] = values
-    half = pl.ds(pl.multiple_of(query_slot(plane) * some_keys, some_keys), some_keys)
-    key_ref[0:some_keys, :] = kc_ref[half, :]
-    val_ref[0:some_keys, :] = vc_ref[half, :]
-    wide_scr[0:some_keys, 0:width] = vc_ref[half, :]
-    wide_scr[:, width:] = jnp.ones((some_keys + fine, width), jnp.bfloat16)
+    own_half = query_slot(plane)
+    for index, half in enumerate((own_half, 1 - own_half)):
+        spot = slice(index * some_keys, (index + 1) * some_keys)
+        half = pl.ds(pl.multiple_of(half * some_keys, some_keys), some_keys)
+        key_ref[spot, :] = kc_ref[half, :]
+        val_ref[spot, :] = vc_ref[half, :]
+        wide_scr[spot, 0:width] = vc_ref[half, :]
+    wide_scr[:, width:] = jnp.ones((coarse + fine, width), jnp.bfloat16)
 
     own_slot = query_slot(plane)
     for ref, slot, start in ((own_ref, own_slot, first_query), (qc_ref, 1 - own_slot, note_rows)):
@@ -212,7 +214,7 @@
                 ref[pick, start : start + rows].reshape(block, width)
             )[0].astype(jnp.bfloat16)
             cot_ref[spot, :] = ref[pick, start + rows : start + 2 * rows].reshape(block, width)
-    limit_scr[...] = some_keys + limit_of(
+    limit_scr[...] = coarse + limit_of(
         lax.broadcasted_iota(jnp.int32, (queries, width), 0)
     )
 
@@ -220,7 +222,7 @@
     slope = sharp * log2_e
     sum_scr[...] = jnp.zeros_like(sum_scr)
 
-    def probs(start, size, part):
+    def probs(start, size, part, counts):
         first = part * queries // 2
         spot = key_spot(start, size)
         cosine = dot_nt(query_ref[first:, :], key_ref[spot, :])
@@ -229,7 +231,8 @@
         seen = place < wide_as(limit_scr[first:, :], size)
         prob = jnp.where(seen, prob, 0.0).astype(jnp.bfloat16)
         prob_ref[first:, spot] = prob
-        sum_scr[first:, :] += dot_nn(prob, wide_scr[spot, :])
+        if counts:
+            sum_scr[first:, :] += dot_nn(prob, wide_scr[spot, :])
 
     shared = (limit_of(queries // 2 - 1) + k_tile - 1) // k_tile
     shared_ref[0] = shared
@@ -282,8 +285,8 @@
     runs = members // 2
     queries = query_ref.shape[0]
     first_query = 2 * rows + note_rows
-    some_keys = small_ref.shape[0] - note_rows
-    fine = key_ref.shape[0] - some_keys
+    coarse = small_ref.shape[0] - note_rows
+    fine = key_ref.shape[0] - coarse
     sharp = jnp.exp(jnp.full((1, width), log_ref[head], jnp.float32))[:, 0:1]
 
     row = lax.broadcasted_iota(jnp.int32, (width, width), 0)
@@ -308,20 +311,21 @@
         jnp.bfloat16
     )
 
-    def grads(start, size, part):
+    def grads(start, size, part, counts):
         first = part * queries // 2
         spot = key_spot(start, size)
         prob = prob_ref[first:, spot]
         dprob = dot_nt(cot_ref[first:, :], val_ref[spot, :])
         dscore = prob.astype(jnp.float32) * (dprob - wide_as(mean_scr[first:, :], size))
         dscore = dscore.astype(jnp.bfloat16)
-        grad_scr[first:, :] += dot_nn(dscore, key_ref[spot, :])
+        if counts:
+            grad_scr[first:, :] += dot_nn(dscore, key_ref[spot, :])
         dk = dot_nn(query_turn[:, first:], dscore)
         dv = dot_nn(cot_turn[:, first:], prob)
         turn_scr[spot, 0:width] = jnp.transpose(dk).astype(jnp.bfloat16)
         turn_scr[spot, width:] = jnp.transpose(dv).astype(jnp.bfloat16)
 
-    all_chunks(grads, some_keys, shared_ref[0], fine // k_tile)
+    all_chunks(grads, coarse // 2, shared_ref[0], fine // k_tile)
 
     own_slot = query_slot(plane)
     scale = coarse_scale_ref[pl.ds(pl.multiple_of(head * 8, 8), 8), :]
@@ -345,18 +349,18 @@
     own_slot = key_slot(plane)
     for slot, target in ((own_slot, dkv_ref), (1 - own_slot, dkv_send_ref)):
         for run in range(runs):
-            spot = pl.ds(pl.multiple_of(some_keys + place_of(run, slot, block), 64), block)
+            spot = pl.ds(pl.multiple_of(coarse + place_of(run, slot, block), 64), block)
             target[run * block : (run + 1) * block, :] = turn_scr[spot, :]
-    small_ref[0:some_keys, :] = turn_scr[0:some_keys, :]
-    small_ref[some_keys:, :] = in_pieces(sum_all(scale), 2 * width)
+    small_ref[0:coarse, :] = turn_scr[0:coarse, :]
+    small_ref[coarse:, :] = in_pieces(sum_all(scale), 2 * width)
 
 
 def run_fine(log_scale, own_rows, kv_rows, qc_rows, key_coarse, val_coarse, coarse_scale, swap):
     members, tall, width = own_rows.shape
     rows = (tall - note_rows) // 4
-    some_keys = key_coarse.shape[0] // 2
+    coarse = key_coarse.shape[0]
     queries = 2 * members * rows
-    total = some_keys + queries
+    total = coarse + queries
     vmem = pl.BlockSpec(memory_space=pltpu.VMEM)
     smem = pl.BlockSpec(memory_space=pltpu.SMEM)
 
@@ -397,7 +401,7 @@
     half = low(queries // 2, 2 * width)
     return pl.pallas_call(
         backward_kernel,
-        out_shape=(half, half, half, half, low(some_keys + note_rows, 2 * width)),
+        out_shape=(half, half, half, half, low(coarse + note_rows, 2 * width)),
         in_specs=[smem, smem] + [vmem] * 11,
         out_specs=(vmem,) * 5,
         scratch_shapes=[
@@ -508,35 +512,35 @@
     )(log_scale, levels[:, None], levels[None, :], queries, keys, values, cots)
 
 
-def small_kernel(own_ref, near_ref, across_ref, far_ref, sum_ref, scale_ref):
-    plane, _ = seq_place()
-    some_keys = own_ref.shape[0] - note_rows
-    terms = [ref[...].astype(jnp.float32) for ref in (own_ref, near_ref, across_ref, far_ref)]
-    half = query_slot(plane)
-    for place, pair in ((half, terms[:2]), (1 - half, terms[2:])):
-        spot = pl.ds(pl.multiple_of(place * some_keys, some_keys), some_keys)
-        sum_ref[spot, :] = (pair[0][:some_keys] + pair[1][:some_keys]).astype(jnp.bfloat16)
-    scale = terms[0][some_keys:] + terms[1][some_keys:] + terms[2][some_keys:] + terms[3][some_keys:]
-    scale = jnp.sum(scale[:, : scale_ref.shape[1]], axis=0, keepdims=True)
+def small_kernel(own_ref, near_ref, sum_ref, scale_ref):
+    coarse, both = sum_ref.shape
+    some_keys = coarse // 2
+    summed = own_ref[...].astype(jnp.float32) + near_ref[...].astype(jnp.float32)
+    own_half = query_slot(seq_place()[0])
+    for index, half in enumerate((own_half, 1 - own_half)):
+        spot = pl.ds(pl.multiple_of(half * some_keys, some_keys), some_keys)
+        sum_ref[spot, :] = summed[index * some_keys : (index + 1) * some_keys].astype(jnp.bfloat16)
+    scale = jnp.sum(summed[coarse:, : both // 2], axis=0, keepdims=True)
     scale_ref[...] = jnp.broadcast_to(scale, scale_ref.shape)
 
 
-def run_small(terms):
-    tall, both = terms[0].shape
+def run_small(own, near):
+    tall, both = own.shape
     return pl.pallas_call(
         small_kernel,
         out_shape=(
-            jax.ShapeDtypeStruct((2 * (tall - note_rows), both), jnp.bfloat16),
+            jax.ShapeDtypeStruct((tall - note_rows, both), jnp.bfloat16),
             jax.ShapeDtypeStruct((8, both // 2), jnp.float32),
         ),
         compiler_params=params(2),
         name="sum_coarse_terms",
-    )(*terms)
+    )(own, near)
 
 
 def sum_kernel(
-    od_ref, other_od_ref, dkv_ref, other_dkv_ref, own_ref, scale_ref, other_scale_ref, all_ref
+    od_ref, other_od_ref, dkv_ref, other_dkv_ref, own_ref, *scale_and_all
 ):
+    *scale_refs, all_ref = scale_and_all
     members, tall, width = all_ref.shape
     rows = (tall - note_rows) // 4
     fine = members * rows
@@ -552,19 +556,21 @@
     summed = dkv_ref[...].astype(jnp.float32) + other_dkv_ref[...].astype(jnp.float32)
     put(2, project(own_ref[:, 0:rows].reshape(fine, width), summed[:, :width]))
     put(3, summed[:, width:])
-    note = in_pieces(scale_ref[0:1, 0:1] + other_scale_ref[0:1, 0:1], width)
+    scale = scale_refs[0][0:1, 0:1]
+    for ref in scale_refs[1:]:
+        scale = scale + ref[0:1, 0:1]
+    note = in_pieces(scale, width)
     for member in range(members):
         all_ref[member, 4 * rows :] = note
 
 
-def run_sum(od, other_od, dkv, other_dkv, own_rows, scale, other_scale):
+def run_sum(od, other_od, dkv, other_dkv, own_rows, scales):
     return pl.pallas_call(
         sum_kernel,
         out_shape=jax.ShapeDtypeStruct(own_rows.shape, jnp.bfloat16),
         compiler_params=params(6),
-        cost_estimate=late_chain,
         name="sum_pairs",
-    )(od, other_od, dkv, other_dkv, own_rows, scale, other_scale)
+    )(od, other_od, dkv, other_dkv, own_rows, *scales)
 
 
 def join_kernel(terms_ref, dk_own_ref, dv_own_ref, k_ref, dk_ref, dv_ref, last_ref):
@@ -610,7 +616,6 @@
         in_specs=[vmem, vmem],
         out_specs=(vmem,) * 4 + (pl.BlockSpec(memory_space=pltpu.SMEM),),
         compiler_params=params(3),
-        cost_estimate=late_chain,
         name="unpack_heads",
     )(all_back, after)
 
@@ -646,6 +651,14 @@
     def to_image(array, flip):
         return lax.ppermute(array, "dp", [(i, i ^ flip) for i in range(images)])
 
+    def to_both(array, image_flip, plane_flip):
+        there = [
+            (i ^ image_flip) * seq + (j ^ (2 * plane_flip))
+            for i in range(images)
+            for j in range(seq)
+        ]
+        return lax.ppermute(array, ("dp", "seq"), list(enumerate(there)))
+
     own_rows = exchange(run_pack(heads, fine_ids, k_fine[0], v_fine[0], q_fine[0], cot_fine[0]))
     kv_rows = to_plane(own_rows[:, : 2 * rows + note_rows], 1)
     qc_rows = to_plane(own_rows[:, 2 * rows :], 3)
@@ -657,13 +670,14 @@
         log_scale, own_rows, kv_rows, qc_rows, key_c, val_c, scale_c, lambda stat: to_plane(stat, 3)
     )
 
-    small_sum, scale = run_small([small] + [to_plane(small, flip) for flip in (1, 2, 3)])
+    small_sum, scale = run_small(small, to_plane(small, 1))
     of_image = lax.all_gather(small_sum, "seq", axis=0, axis_index_groups=groups)
 
     other_dkv = to_plane(dkv_send, 1)
     other_od = to_plane(od_send, 3)
     scale = scale + to_image(scale, 1) + to_image(scale, 2) + to_image(scale, 3)
-    all_parts = run_sum(od, other_od, dkv, other_dkv, own_rows, scale, to_image(scale, 4))
+    scales = [scale, to_plane(scale, 3), to_image(scale, 4), to_both(scale, 4, 3)]
+    all_parts = run_sum(od, other_od, dkv, other_dkv, own_rows, scales)
     all_back = exchange(all_parts)
     dk_c, dv_c, after = run_join(of_image, dk_own, dv_own, k_coarse[0])
     factor = 1.0 / math.sqrt(images * (coarse + seq * rows))

time: 152 us -> 138 us (0.908); the launches traced: 151 us -> 138 us
  waiting for transfers between devices: 44.1 us -> 29.4 us
    ppermute x8 -> x7, waiting for transfers between devices: 27.3 us -> 13.7 us  [to_plane(): return lax.ppermute(array, 'seq', [(i, i ^ 2 * flip) for i in range(seq)])]
    all_gather x1, waiting for transfers between devices: 11.4 us -> 0.01 us  [body(): lax.all_gather(small_sum, 'seq', axis=0, axis_index_groups=groups)]
    all_to_all x1, waiting for transfers between devices: 0.01 us -> 9.55 us  [exchange(): lax.all_to_all(parts, 'seq', 0, 0, axis_index_groups=groups, tiled=True)]
    ppermute x0 -> x1, waiting for transfers between devices: none -> 2.87 us  [to_both(): return lax.ppermute(array, ('dp', 'seq'), list(enumerate(there)))]
    ppermute x4, waiting for transfers between devices: 5.25 us -> 3.27 us  [to_image(): return lax.ppermute(array, 'dp', [(i, i ^ flip) for i in range(images)])]
    unnamed x32 -> x34, local copies, waits for them, and re-layouts: 12.9 us -> 13.3 us
    ppermute x8 -> x7, starting transfers between devices: 17.6 us -> 17.4 us  [to_plane(): return lax.ppermute(array, 'seq', [(i, i ^ 2 * flip) for i in range(seq)])]
  transfers between devices with their start and end apart: 14 -> 14, of which waited for: 9 -> 10; matrix products, arithmetic and copies ran while one was open for 1% -> 1% of each run, Pallas kernels for 8% -> 8%
where the time goes in v6:
time: 138 us
  Pallas kernels  31.6 us (23%)
  waiting for transfers between devices  29.4 us (21%)
  starting transfers between devices  27.7 us (20%)
  blocking collectives  19.7 us (14%)
  local copies, waits for them, and re-layouts  15.7 us (11%)
  between operations  14.1 us (10%)
    all_to_all x1, blocking collectives, exchange(): lax.all_to_all(parts, 'seq', 0, 0, axis_index_groups=groups, tiled=True)  19.7 us
    ppermute x7, starting transfers between devices, to_plane(): return lax.ppermute(array, 'seq', [(i, i ^ 2 * flip) for i in range(seq)])  17.4 us
    ppermute x7, waiting for transfers between devices, to_plane(): return lax.ppermute(array, 'seq', [(i, i ^ 2 * flip) for i in range(seq)])  13.7 us
    unnamed x34, local copies, waits for them, and re-layouts  13.3 us
    pallas_call x1, Pallas kernels, run_fine(): pl.pallas_call(backward_kernel, out_shape=(half, half, half, half, low(co...  10.1 us
    all_to_all x1, waiting for transfers between devices, exchange(): lax.all_to_all(parts, 'seq', 0, 0, axis_index_groups=groups, tiled=True)  9.55 us
    pallas_call x1, Pallas kernels, run_coarse(): pl.pallas_call(coarse_kernel, out_shape=(low, low, wide, wide, jax.ShapeD...  7.81 us
    pallas_call x1, Pallas kernels, run_fine(): pl.pallas_call(forward_kernel, out_shape=(low(queries, total), low(total,...  7.24 us
  transfers between devices with their start and end apart: 14, of which 10 were waited for; matrix products, arithmetic and copies ran while one was open for 1% of the time, Pallas kernels for 8%

profile of v6, /device:TPU:1, one launch (start us, length us, event | category | flops | bytes accessed | tf_op | source)
XLA Modules:
  0.0 138.3 jit_solution(1056944579667802382)
XLA Ops:
  7.2 0.0 copy-start.16
  7.2 0.0 all-gather.3.cloned.1.call-start
  7.2 2.3 %pack_heads.1 = bf16[8,400,128]{2,1,0:T(8,128)(2,1)} custom-call(s32[1,96]{1,0:T(1,128)} %ids_ref.1, bf16[96,1024]{1,0:T(8,128)(2,1)} %bitcast.25, bf16[96,1024]{1,0:T(8,128)(2,1)} %bitcast.26, bf16[96,1024]{1,0:T(8,128)(2,1)} %bitcast.27, bf16[96,1024]{1,0:T(8,128)(2,1)} %bitcast.28), custom_call_target="tpu_custom_call" | custom-call | tf_op jit(solution)/shard_map/pack_heads/pallas_call | solution.py:103
  9.5 19.7 %all_to_all.10.own_ref = bf16[8,400,128]{2,1,0:T(8,128)(2,1)S(1)} all-to-all(bf16[8,400,128]{2,1,0:T(8,128)(2,1)} %pack_heads.1), channel_id=1, replica_groups={{0,1,8,9,16,17,24,25},{2,3,10,11,18,19,26,27},{4,5,12,13,20,21,28,29},{..., dimensions={0} | all-to-all | bytes 1638400 | tf_op jit(solution)/shard_map/all_to_all | solution.py:646
  29.2 1.0 fusion
  30.2 5.3 %collective-permute-start.1 = (bf16[8,208,128]{2,1,0:T(8,128)(2,1)}, bf16[8,208,128]{2,1,0:T(8,128)(2,1)}, u32[]{:S(2)}, u32[]{:S(2)}) collective-permute-start(bf16[8,208,128]{2,1,0:T(8,128)(2,1)} %get-tuple-element.69), channel_id=1, source_target_pairs={{0,6},{1,7},{2,4},{3,5},{4,2},{5,3},{6,0},{7,1},{8,14},{9,15},{10,... | collective-permute-start | bytes 1277960 | tf_op jit(solution)/shard_map/ppermute | solution.py:649
  35.5 1.2 collective-permute-start
  36.7 1.5 %copy.20.row_level_ref = s32[256,1]{1,0:T(8,128)} copy(s32[256,1]{0,1:T(1,128)} %bitcast.21) | data formatting | bytes 2048 | tf_op jit(solution)/shard_map/broadcast_in_dim;squeeze | solution.py:512
  38.1 0.0 copy-start.1
  38.1 1.0 copy-done.1
  39.2 0.0 copy-start.8
  39.2 0.9 copy-done.8
  40.1 0.0 copy-start.9
  40.1 0.7 copy-done.9
  40.8 0.0 copy-start.10
  40.8 1.0 copy-done.10
  41.8 0.0 copy-start.11
  41.8 1.0 copy-done.11
  42.9 0.0 copy-start.12
  42.9 1.0 copy-done.12
  43.9 0.7 copy-done.15
  44.6 7.8 %coarse_attention.1 = (bf16[256,1024]{1,0:T(8,128)(2,1)}, bf16[256,1024]{1,0:T(8,128)(2,1)}, f32[256,1024]{1,0:T(8,128)S(1)}, f32[256,1024]{1,0:T(8,128)S(1)}, f...) custom-call(f32[8]{0:T(128)S(1)} %copy-done.15, s32[256,1]{1,0:T(8,128)S(1)} %copy-done.8, ...), custom_call_target="tpu_custom_call" | custom-call | flops 805306368 | bytes 6291456 | tf_op jit(solution)/shard_map/coarse_attention/pallas_call | solution.py:500
  52.4 1.7 %collective-permute-done.1.qc_ref = bf16[8,208,128]{2,1,0:T(8,128)(2,1)} collective-permute-done((bf16[8,208,128]{2,1,0:T(8,128)(2,1)}, bf16[8,208,128]{2,1,0:T(8,128)(2,1)}, u32[]{:S(2)}, u32[]{:S(2)}) %collective-permute-start.1) | collective-permute-done | bytes 426016 | tf_op jit(solution)/shard_map/ppermute | solution.py:649
  54.0 1.5 %collective-permute-done.kv_ref = bf16[8,208,128]{2,1,0:T(8,128)(2,1)} collective-permute-done((bf16[8,208,128]{2,1,0:T(8,128)(2,1)}, bf16[8,208,128]{2,1,0:T(8,128)(2,1)}, u32[]{:S(2)}, u32[]{:S(2)}) %collective-permute-start) | collective-permute-done | bytes 426016 | tf_op jit(solution)/shard_map/ppermute | solution.py:649
  55.6 0.0 copy-done.16
  55.6 7.2 %fine_forward.1 = (bf16[1536,1792]{1,0:T(8,128)(2,1)S(1)}, bf16[1792,128]{1,0:T(8,128)(2,1)S(1)}, bf16[1792,128]{1,0:T(8,128)(2,1)S(1)}, bf16[1536,128]{1,0:T(8,...) custom-call(f32[8]{0:T(128)S(1)} %copy-done.16, ...), custom_call_target="tpu_custom_call" | custom-call | flops 1409286144 | bytes 11010048 | tf_op jit(solution)/shard_map/fine_forward/pallas_call | solution.py:373
  62.8 2.9 %collective-permute-start.2 = (f32[24,128]{1,0:T(8,128)S(1)}, f32[24,128]{1,0:T(8,128)S(1)}, u32[]{:S(2)}, u32[]{:S(2)}) collective-permute-start(f32[24,128]{1,0:T(8,128)S(1)} %get-tuple-element.44.stat_ref), channel_id=1, source_target_pairs={{0,6},{1,7},{2,4},{3,5},{4,2},{5,3},{6,0},{7,1},{8,14},{9,15},{10,... | collective-permute-start | bytes 36872 | tf_op jit(solution)/shard_map/ppermute | solution.py:649
  65.7 1.9 %collective-permute-done.2.other_stat_ref = f32[24,128]{1,0:T(8,128)S(1)} collective-permute-done((f32[24,128]{1,0:T(8,128)S(1)}, f32[24,128]{1,0:T(8,128)S(1)}, u32[]{:S(2)}, u32[]{:S(2)}) %collective-permute-start.2) | collective-permute-done | bytes 12320 | tf_op jit(solution)/shard_map/ppermute | solution.py:649
  67.6 10.1 %fine_backward.1 = (bf16[768,256]{1,0:T(8,128)(2,1)S(1)}, bf16[768,256]{1,0:T(8,128)(2,1)S(1)}, bf16[768,256]{1,0:T(8,128)(2,1)S(1)}, bf16[768,256]{1,0:T(8,128)(2,1)S(1)}, bf16[272,256]{1,0:T(8,128)(2,1)S(1)}) custom-call(f32[8]{0:T(128)S(1)} %copy-done.16, s32[1]{0:T(128)} %get-tuple-element.43.shared_ref, bf16[8,400,128]{2,1,0:T(8,128)(2,1)S(1)} %all_to_all.10.own_ref, ...), custom_call_target="tpu_custom_call" | custom-call | flops 2818572288 | bytes 11010048 | tf_op jit(solution)/shard_map/fine_backward/pallas_call | solution.py:402
  77.7 0.0 copy-start.3
  77.7 0.7 copy-done.3
  78.4 0.7 copy-done.5
  79.2 0.8 copy-done.13
  79.9 0.7 copy-done.14
  80.7 1.9 %collective-permute-start.3 = (bf16[272,256]{1,0:T(8,128)(2,1)S(1)}, bf16[272,256]{1,0:T(8,128)(2,1)S(1)}, u32[]{:S(2)}, u32[]{:S(2)}) collective-permute-start(bf16[272,256]{1,0:T(8,128)(2,1)S(1)} %get-tuple-element.52.own_ref), channel_id=1, source_target_pairs={{0,2},{1,3},{2,0},{3,1},{4,6},{5,7},{6,4},{7,5},{8,10},{9,11},{10,... | collective-permute-start | bytes 417800 | tf_op jit(solution)/shard_map/ppermute | solution.py:649
  82.6 5.5 %collective-permute-done.3.near_ref = bf16[272,256]{1,0:T(8,128)(2,1)S(1)} collective-permute-done((bf16[272,256]{1,0:T(8,128)(2,1)S(1)}, bf16[272,256]{1,0:T(8,128)(2,1)S(1)}, u32[]{:S(2)}, u32[]{:S(2)}) %collective-permute-start.3) | collective-permute-done | bytes 139296 | tf_op jit(solution)/shard_map/ppermute | solution.py:649
  88.1 0.0 copy-start.7
  88.1 0.6 copy-done.7
  88.8 0.0 all-gather.3.cloned.1.call-update
  88.8 0.7 collective-permute-start.4
  89.5 3.2 %collective-permute-start.5 = (bf16[768,256]{1,0:T(8,128)(2,1)}, bf16[768,256]{1,0:T(8,128)(2,1)S(1)}, u32[]{:S(2)}, u32[]{:S(2)}) collective-permute-start(bf16[768,256]{1,0:T(8,128)(2,1)} %copy-done.13), channel_id=1, source_target_pairs={{0,2},{1,3},{2,0},{3,1},{4,6},{5,7},{6,4},{7,5},{8,10},{9,11},{10,... | collective-permute-start | bytes 1179656 | tf_op jit(solution)/shard_map/ppermute | solution.py:649
  92.7 1.9 %collective-permute-start.8 = (f32[8,128]{1,0:T(8,128)S(1)}, f32[8,128]{1,0:T(8,128)S(1)}, u32[]{:S(2)}, u32[]{:S(2)}) collective-permute-start(f32[8,128]{1,0:T(8,128)S(1)} %get-tuple-element.62), channel_id=1, source_target_pairs={{0,96},{32,64},{64,32},{96,0},{128,224},{160,192},{192,160},{224,1... | collective-permute-start | bytes 12296 | tf_op jit(solution)/shard_map/ppermute | solution.py:652
  94.7 0.0 collective-permute-start.7
  94.7 1.3 collective-permute-start.6
  96.0 0.4 collective-permute-done.8
  96.4 2.5 %collective-permute-done.7 = f32[8,128]{1,0:T(8,128)S(1)} collective-permute-done((f32[8,128]{1,0:T(8,128)S(1)}, f32[8,128]{1,0:T(8,128)S(1)}, u32[]{:S(2)}, u32[]{:S(2)}) %collective-permute-start.7) | collective-permute-done | bytes 4128 | tf_op jit(solution)/shard_map/ppermute | solution.py:652
  98.9 0.0 collective-permute-done.6
  98.9 0.1 collective-permute-start.11
  99.0 1.6 %collective-permute-start.10 = (f32[8,128]{1,0:T(8,128)S(1)}, f32[8,128]{1,0:T(8,128)S(1)}, u32[]{:S(2)}, u32[]{:S(2)}) collective-permute-start(f32[8,128]{1,0:T(8,128)S(1)} %add_add_fusion.scale_and_all_0_), channel_id=1, source_target_pairs={{0,128},{32,160},{64,192},{96,224},{128,0},{160,32},{192,64},{224,... | collective-permute-start | bytes 12296 | tf_op jit(solution)/shard_map/ppermute | solution.py:652
  100.7 2.2 %collective-permute-start.9 = (f32[8,128]{1,0:T(8,128)S(1)}, f32[8,128]{1,0:T(8,128)S(1)}, u32[]{:S(2)}, u32[]{:S(2)}) collective-permute-start(f32[8,128]{1,0:T(8,128)S(1)} %add_add_fusion.scale_and_all_0_), channel_id=1, source_target_pairs={{0,6},{1,7},{2,4},{3,5},{4,2},{5,3},{6,0},{7,1},{8,14},{9,15},{10,... | collective-permute-start | bytes 12296 | tf_op jit(solution)/shard_map/ppermute | solution.py:649
  102.9 2.9 %collective-permute-done.11.scale_and_all_3_ = f32[8,128]{1,0:T(8,128)S(1)} collective-permute-done((f32[8,128]{1,0:T(8,128)S(1)}, f32[8,128]{1,0:T(8,128)S(1)}, u32[]{:S(2)}, u32[]{:S(2)}) %collective-permute-start.11) | collective-permute-done | bytes 4128 | tf_op jit(solution)/shard_map/ppermute | solution.py:660
  105.7 0.3 collective-permute-done.10.scale_and_all_2_
  106.1 3.1 %collective-permute-done.9.scale_and_all_1_ = f32[8,128]{1,0:T(8,128)S(1)} collective-permute-done((f32[8,128]{1,0:T(8,128)S(1)}, f32[8,128]{1,0:T(8,128)S(1)}, u32[]{:S(2)}, u32[]{:S(2)}) %collective-permute-start.9) | collective-permute-done | bytes 4128 | tf_op jit(solution)/shard_map/ppermute | solution.py:649
  109.2 0.0 collective-permute-done.4.other_od_ref
  109.2 0.0 collective-permute-done.5.other_dkv_ref
  109.2 1.0 copy-done.4
  110.2 1.0 copy-done.6
  111.2 1.3 sum_pairs.1
  112.6 5.2 %all-to-all-start.1 = ((bf16[8,400,128]{2,1,0:T(8,128)(2,1)}), bf16[8,400,128]{2,1,0:T(8,128)(2,1)S(1)}, u32[]{:S(2)}, u32[]{:S(2)}) async-start(bf16[8,400,128]{2,1,0:T(8,128)(2,1)} %sum_pairs.1), calls=%async_computation.1 | async-start | bytes 1638400 | tf_op jit(solution)/shard_map/all_to_all | solution.py:646
  117.8 0.0 copy-done.2
  117.8 1.2 copy-done
  119.0 1.9 %join_coarse.1 = (bf16[256,1024]{1,0:T(8,128)(2,1)}, bf16[256,1024]{1,0:T(8,128)(2,1)}, f32[8,128]{1,0:T(8,128)S(1)}) custom-call(bf16[8,256,256]{2,1,0:T(8,128)(2,1)S(1)} %bitcast.18, f32[256,1024]{1,0:T(8,128)S(1)} %get-tuple-element.54.dk_own_ref, f32[256,1024]{1,0:T(8,128)S(1)} %get-tuple-element.55.dv_own_ref, bf16[256,1024]{1,0:T(8,128)(2,1)S(1)} %bitcast.20), custom_call_target="tpu_custom_call" | custom-call | tf_op jit(solution)/shard_map/join_coarse/pallas_call | solution.py:590
  120.9 9.5 %all-to-all-done.1.all_ref = bf16[8,400,128]{2,1,0:T(8,128)(2,1)S(1)} async-done(((bf16[8,400,128]{2,1,0:T(8,128)(2,1)}), bf16[8,400,128]{2,1,0:T(8,128)(2,1)S(1)}, u32[]{:S(2)}, u32[]{:S(2)}) %all-to-all-start.1) | async-done | bytes 819232 | tf_op jit(solution)/shard_map/all_to_all | solution.py:646
  130.5 0.9 unpack_heads.1
  (11 shorter events, 0.1 us)
Async XLA Ops:
  7.2 48.4 %copy-start.16 = (f32[8]{0:T(128)S(1)}, f32[8]{0:T(128)}, u32[]{:S(2)}) copy-start(f32[8]{0:T(128)} %log_ref.5) | copy-start | bytes 100
  7.2 110.6 %all-gather.3.cloned.1.call-start = ((), (), s32[]{:S(2)}) async-start(), calls=%async_computation.2 | async-start | bytes 1179648 | tf_op jit(solution)/shard_map/all_gather | solution.py:674
  30.2 23.8 %collective-permute-start.1 = (bf16[8,208,128]{2,1,0:T(8,128)(2,1)}, bf16[8,208,128]{2,1,0:T(8,128)(2,1)}, u32[]{:S(2)}, u32[]{:S(2)}) collective-permute-start(bf16[8,208,128]{2,1,0:T(8,128)(2,1)} %get-tuple-element.69), channel_id=1, source_target_pairs={{0,6},{1,7},{2,4},{3,5},{4,2},{5,3},{6,0},{7,1},{8,14},{9,15},{10,... | collective-permute-start | bytes 1277960 | tf_op jit(solution)/shard_map/ppermute | solution.py:649
  35.5 20.1 %collective-permute-start = (bf16[8,208,128]{2,1,0:T(8,128)(2,1)}, bf16[8,208,128]{2,1,0:T(8,128)(2,1)}, u32[]{:S(2)}, u32[]{:S(2)}) collective-permute-start(bf16[8,208,128]{2,1,0:T(8,128)(2,1)} %get-tuple-element.70), channel_id=1, source_target_pairs={{0,2},{1,3},{2,0},{3,1},{4,6},{5,7},{6,4},{7,5},{8,10},{9,11},{10,... | collective-permute-start | bytes 1277960 | tf_op jit(solution)/shard_map/ppermute | solution.py:649
  38.1 1.0 copy-start.1
  39.2 0.9 copy-start.8
  40.1 0.7 copy-start.9
  40.8 1.0 copy-start.10
  41.8 1.0 copy-start.11
  42.9 1.0 copy-start.12
  43.9 0.7 copy-start.15
  62.8 4.7 %collective-permute-start.2 = (f32[24,128]{1,0:T(8,128)S(1)}, f32[24,128]{1,0:T(8,128)S(1)}, u32[]{:S(2)}, u32[]{:S(2)}) collective-permute-start(f32[24,128]{1,0:T(8,128)S(1)} %get-tuple-element.44.stat_ref), channel_id=1, source_target_pairs={{0,6},{1,7},{2,4},{3,5},{4,2},{5,3},{6,0},{7,1},{8,14},{9,15},{10,... | collective-permute-start | bytes 36872 | tf_op jit(solution)/shard_map/ppermute | solution.py:649
  67.6 50.3 %copy-start.2 = (bf16[1,256,1024]{2,1,0:T(8,128)(2,1)S(1)}, bf16[1,256,1024]{2,1,0:T(8,128)(2,1)}, u32[]{:S(2)}) copy-start(bf16[1,256,1024]{2,1,0:T(8,128)(2,1)} %param.12) | copy-start | bytes 1572868
  77.7 0.7 copy-start.3
  78.4 0.8 copy-start.5
  79.2 0.8 copy-start.13
  79.9 0.7 copy-start.14
  80.7 7.4 %collective-permute-start.3 = (bf16[272,256]{1,0:T(8,128)(2,1)S(1)}, bf16[272,256]{1,0:T(8,128)(2,1)S(1)}, u32[]{:S(2)}, u32[]{:S(2)}) collective-permute-start(bf16[272,256]{1,0:T(8,128)(2,1)S(1)} %get-tuple-element.52.own_ref), channel_id=1, source_target_pairs={{0,2},{1,3},{2,0},{3,1},{4,6},{5,7},{6,4},{7,5},{8,10},{9,11},{10,... | collective-permute-start | bytes 417800 | tf_op jit(solution)/shard_map/ppermute | solution.py:649
  88.1 0.7 copy-start.7
  88.8 20.4 %collective-permute-start.4 = (bf16[768,256]{1,0:T(8,128)(2,1)}, bf16[768,256]{1,0:T(8,128)(2,1)S(1)}, u32[]{:S(2)}, u32[]{:S(2)}) collective-permute-start(bf16[768,256]{1,0:T(8,128)(2,1)} %copy-done.14), channel_id=1, source_target_pairs={{0,6},{1,7},{2,4},{3,5},{4,2},{5,3},{6,0},{7,1},{8,14},{9,15},{10,... | collective-permute-start | bytes 1179656 | tf_op jit(solution)/shard_map/ppermute | solution.py:649
  89.5 19.8 %collective-permute-start.5 = (bf16[768,256]{1,0:T(8,128)(2,1)}, bf16[768,256]{1,0:T(8,128)(2,1)S(1)}, u32[]{:S(2)}, u32[]{:S(2)}) collective-permute-start(bf16[768,256]{1,0:T(8,128)(2,1)} %copy-done.13), channel_id=1, source_target_pairs={{0,2},{1,3},{2,0},{3,1},{4,6},{5,7},{6,4},{7,5},{8,10},{9,11},{10,... | collective-permute-start | bytes 1179656 | tf_op jit(solution)/shard_map/ppermute | solution.py:649
  92.7 3.7 %collective-permute-start.8 = (f32[8,128]{1,0:T(8,128)S(1)}, f32[8,128]{1,0:T(8,128)S(1)}, u32[]{:S(2)}, u32[]{:S(2)}) collective-permute-start(f32[8,128]{1,0:T(8,128)S(1)} %get-tuple-element.62), channel_id=1, source_target_pairs={{0,96},{32,64},{64,32},{96,0},{128,224},{160,192},{192,160},{224,1... | collective-permute-start | bytes 12296 | tf_op jit(solution)/shard_map/ppermute | solution.py:652
  94.7 4.3 %collective-permute-start.7 = (f32[8,128]{1,0:T(8,128)S(1)}, f32[8,128]{1,0:T(8,128)S(1)}, u32[]{:S(2)}, u32[]{:S(2)}) collective-permute-start(f32[8,128]{1,0:T(8,128)S(1)} %get-tuple-element.62), channel_id=1, source_target_pairs={{0,64},{32,96},{64,0},{96,32},{128,192},{160,224},{192,128},{224,1... | collective-permute-start | bytes 12296 | tf_op jit(solution)/shard_map/ppermute | solution.py:652
  94.7 4.3 %collective-permute-start.6 = (f32[8,128]{1,0:T(8,128)S(1)}, f32[8,128]{1,0:T(8,128)S(1)}, u32[]{:S(2)}, u32[]{:S(2)}) collective-permute-start(f32[8,128]{1,0:T(8,128)S(1)} %get-tuple-element.62), channel_id=1, source_target_pairs={{0,32},{32,0},{64,96},{96,64},{128,160},{160,128},{192,224},{224,1... | collective-permute-start | bytes 12296 | tf_op jit(solution)/shard_map/ppermute | solution.py:652
  98.9 6.8 %collective-permute-start.11 = (f32[8,128]{1,0:T(8,128)S(1)}, f32[8,128]{1,0:T(8,128)S(1)}, u32[]{:S(2)}, u32[]{:S(2)}) collective-permute-start(f32[8,128]{1,0:T(8,128)S(1)} %add_add_fusion.scale_and_all_0_), channel_id=1, source_target_pairs={{0,134},{1,135},{2,132},{3,133},{4,130},{5,131},{6,128},{7,129},{8... | collective-permute-start | bytes 12296 | tf_op jit(solution)/shard_map/ppermute | solution.py:660
  99.0 7.0 %collective-permute-start.10 = (f32[8,128]{1,0:T(8,128)S(1)}, f32[8,128]{1,0:T(8,128)S(1)}, u32[]{:S(2)}, u32[]{:S(2)}) collective-permute-start(f32[8,128]{1,0:T(8,128)S(1)} %add_add_fusion.scale_and_all_0_), channel_id=1, source_target_pairs={{0,128},{32,160},{64,192},{96,224},{128,0},{160,32},{192,64},{224,... | collective-permute-start | bytes 12296 | tf_op jit(solution)/shard_map/ppermute | solution.py:652
  100.7 8.5 %collective-permute-start.9 = (f32[8,128]{1,0:T(8,128)S(1)}, f32[8,128]{1,0:T(8,128)S(1)}, u32[]{:S(2)}, u32[]{:S(2)}) collective-permute-start(f32[8,128]{1,0:T(8,128)S(1)} %add_add_fusion.scale_and_all_0_), channel_id=1, source_target_pairs={{0,6},{1,7},{2,4},{3,5},{4,2},{5,3},{6,0},{7,1},{8,14},{9,15},{10,... | collective-permute-start | bytes 12296 | tf_op jit(solution)/shard_map/ppermute | solution.py:649
  109.2 1.0 copy-start.4
  110.2 1.0 copy-start.6
  112.6 17.9 %all-to-all-start.1 = ((bf16[8,400,128]{2,1,0:T(8,128)(2,1)}), bf16[8,400,128]{2,1,0:T(8,128)(2,1)S(1)}, u32[]{:S(2)}, u32[]{:S(2)}) async-start(bf16[8,400,128]{2,1,0:T(8,128)(2,1)} %sum_pairs.1), calls=%async_computation.1 | async-start | bytes 1638400 | tf_op jit(solution)/shard_map/all_to_all | solution.py:646
  117.8 1.2 copy-start
Sparse Core Ops, SparseCore 0:
  88.9 24.0 all-gather.2

commit v7 on v6

--- a/solution.py
+++ b/solution.py
@@ -11,6 +11,7 @@
 norm_eps = 1e-06
 log2_e = 1.4426950408889634
 k_tile = 256
+q_rows = 384
 note_rows = 16
 
 planes = 4
@@ -223,16 +224,17 @@
     sum_scr[...] = jnp.zeros_like(sum_scr)
 
     def probs(start, size, part, counts):
-        first = part * queries // 2
         spot = key_spot(start, size)
-        cosine = dot_nt(query_ref[first:, :], key_ref[spot, :])
-        prob = jnp.exp2(cosine * slope - slope)
         place = start + lax.broadcasted_iota(jnp.int32, (1, size), 1)
-        seen = place < wide_as(limit_scr[first:, :], size)
-        prob = jnp.where(seen, prob, 0.0).astype(jnp.bfloat16)
-        prob_ref[first:, spot] = prob
-        if counts:
-            sum_scr[first:, :] += dot_nn(prob, wide_scr[spot, :])
+        for first in range(part * queries // 2, queries, q_rows):
+            here = slice(first, first + q_rows)
+            cosine = dot_nt(query_ref[here, :], key_ref[spot, :])
+            prob = jnp.exp2(cosine * slope - slope)
+            seen = place < wide_as(limit_scr[here, :], size)
+            prob = jnp.where(seen, prob, 0.0).astype(jnp.bfloat16)
+            prob_ref[here, spot] = prob
+            if counts:
+                sum_scr[here, :] += dot_nn(prob, wide_scr[spot, :])
 
     shared = (limit_of(queries // 2 - 1) + k_tile - 1) // k_tile
     shared_ref[0] = shared
@@ -277,6 +279,7 @@
     query_turn,
     cot_turn,
     turn_scr,
+    score_scr,
 ):
     plane, head = seq_place()
     members, tall, width = own_ref.shape
@@ -312,18 +315,22 @@
     )
 
     def grads(start, size, part, counts):
-        first = part * queries // 2
         spot = key_spot(start, size)
-        prob = prob_ref[first:, spot]
-        dprob = dot_nt(cot_ref[first:, :], val_ref[spot, :])
-        dscore = prob.astype(jnp.float32) * (dprob - wide_as(mean_scr[first:, :], size))
-        dscore = dscore.astype(jnp.bfloat16)
-        if counts:
-            grad_scr[first:, :] += dot_nn(dscore, key_ref[spot, :])
-        dk = dot_nn(query_turn[:, first:], dscore)
-        dv = dot_nn(cot_turn[:, first:], prob)
+        below = part * queries // 2
+        dv = dot_nn(cot_turn[:, below:], prob_ref[below:, spot])
+        turn_scr[spot, width:] = jnp.transpose(dv).astype(jnp.bfloat16)
+        for first in range(below, queries, q_rows):
+            here = slice(first, first + q_rows)
+            dprob = dot_nt(cot_ref[here, :], val_ref[spot, :])
+            dscore = prob_ref[here, spot].astype(jnp.float32) * (
+                dprob - wide_as(mean_scr[here, :], size)
+            )
+            dscore = dscore.astype(jnp.bfloat16)
+            score_scr[here, 0:size] = dscore
+            if counts:
+                grad_scr[here, :] += dot_nn(dscore, key_ref[spot, :])
+        dk = dot_nn(query_turn[:, below:], score_scr[below:, 0:size])
         turn_scr[spot, 0:width] = jnp.transpose(dk).astype(jnp.bfloat16)
-        turn_scr[spot, width:] = jnp.transpose(dv).astype(jnp.bfloat16)
 
     all_chunks(grads, coarse // 2, shared_ref[0], fine // k_tile)
 
@@ -411,6 +418,7 @@
             pltpu.VMEM((width, queries), jnp.bfloat16),
             pltpu.VMEM((width, queries), jnp.bfloat16),
             pltpu.VMEM((total, 2 * width), jnp.bfloat16),
+            pltpu.VMEM((queries, k_tile), jnp.bfloat16),
         ],
         compiler_params=params(16),
         cost_estimate=pl.CostEstimate(

time: 138 us -> 138 us (level)
  starting transfers between devices: 27.7 us -> 30.6 us
  waiting for transfers between devices: 29.4 us -> 26.9 us
    ppermute x4, starting transfers between devices: 4.9 us -> 8.26 us  [to_image(): return lax.ppermute(array, 'dp', [(i, i ^ flip) for i in range(images)])]
    ppermute x7, starting transfers between devices: 17.4 us -> 14.7 us  [to_plane(): return lax.ppermute(array, 'seq', [(i, i ^ 2 * flip) for i in range(seq)])]
    all_to_all x1, starting transfers between devices: 5.24 us -> 6.96 us  [exchange(): lax.all_to_all(parts, 'seq', 0, 0, axis_index_groups=groups, tiled=True)]
    ppermute x7, waiting for transfers between devices: 13.7 us -> 12 us  [to_plane(): return lax.ppermute(array, 'seq', [(i, i ^ 2 * flip) for i in range(seq)])]
  transfers between devices with their start and end apart: 14 -> 14, of which waited for: 10 -> 9; matrix products, arithmetic and copies ran while one was open for 1% -> 1% of each run, Pallas kernels for 8% -> 8%
where the time goes in v7:
time: 138 us; the launch traced here: 137 us
  starting transfers between devices  30.6 us (22%)
  Pallas kernels  30.3 us (22%)
  waiting for transfers between devices  26.9 us (19%)
  blocking collectives  19.7 us (14%)
  local copies, waits for them, and re-layouts  15.7 us (11%)
  between operations  14.1 us (10%)
    all_to_all x1, blocking collectives, exchange(): lax.all_to_all(parts, 'seq', 0, 0, axis_index_groups=groups, tiled=True)  19.7 us
    ppermute x7, starting transfers between devices, to_plane(): return lax.ppermute(array, 'seq', [(i, i ^ 2 * flip) for i in range(seq)])  14.7 us
    unnamed x34, local copies, waits for them, and re-layouts  13.3 us
    ppermute x7, waiting for transfers between devices, to_plane(): return lax.ppermute(array, 'seq', [(i, i ^ 2 * flip) for i in range(seq)])  12 us
    all_to_all x1, waiting for transfers between devices, exchange(): lax.all_to_all(parts, 'seq', 0, 0, axis_index_groups=groups, tiled=True)  9.55 us
    pallas_call x1, Pallas kernels, run_fine(): pl.pallas_call(backward_kernel, out_shape=(half, half, half, half, low(co...  9.23 us
    ppermute x4, starting transfers between devices, to_image(): return lax.ppermute(array, 'dp', [(i, i ^ flip) for i in range(images)])  8.26 us
    pallas_call x1, Pallas kernels, run_coarse(): pl.pallas_call(coarse_kernel, out_shape=(low, low, wide, wide, jax.ShapeD...  7.81 us
  transfers between devices with their start and end apart: 14, of which 9 were waited for; matrix products, arithmetic and copies ran while one was open for 1% of the time, Pallas kernels for 8%

profile of v7, /device:TPU:1, one launch (start us, length us, event | category | flops | bytes accessed | tf_op | source)
XLA Modules:
  0.0 137.3 jit_solution(12313318346906791993)
XLA Ops:
  7.2 0.0 copy-start.16
  7.2 0.0 all-gather.3.cloned.1.call-start
  7.2 2.3 %pack_heads.1 = bf16[8,400,128]{2,1,0:T(8,128)(2,1)} custom-call(s32[1,96]{1,0:T(1,128)} %ids_ref.1, bf16[96,1024]{1,0:T(8,128)(2,1)} %bitcast.25, bf16[96,1024]{1,0:T(8,128)(2,1)} %bitcast.26, bf16[96,1024]{1,0:T(8,128)(2,1)} %bitcast.27, bf16[96,1024]{1,0:T(8,128)(2,1)} %bitcast.28), custom_call_target="tpu_custom_call" | custom-call | tf_op jit(solution)/shard_map/pack_heads/pallas_call | solution.py:104
  9.5 19.7 %all_to_all.10.own_ref = bf16[8,400,128]{2,1,0:T(8,128)(2,1)S(1)} all-to-all(bf16[8,400,128]{2,1,0:T(8,128)(2,1)} %pack_heads.1), channel_id=1, replica_groups={{0,1,8,9,16,17,24,25},{2,3,10,11,18,19,26,27},{4,5,12,13,20,21,28,29},{..., dimensions={0} | all-to-all | bytes 1638400 | tf_op jit(solution)/shard_map/all_to_all | solution.py:654
  29.2 1.0 fusion
  30.2 5.3 %collective-permute-start.1 = (bf16[8,208,128]{2,1,0:T(8,128)(2,1)}, bf16[8,208,128]{2,1,0:T(8,128)(2,1)}, u32[]{:S(2)}, u32[]{:S(2)}) collective-permute-start(bf16[8,208,128]{2,1,0:T(8,128)(2,1)} %get-tuple-element.69), channel_id=1, source_target_pairs={{0,6},{1,7},{2,4},{3,5},{4,2},{5,3},{6,0},{7,1},{8,14},{9,15},{10,... | collective-permute-start | bytes 1277960 | tf_op jit(solution)/shard_map/ppermute | solution.py:657
  35.5 1.2 collective-permute-start
  36.7 1.5 %copy.20.row_level_ref = s32[256,1]{1,0:T(8,128)} copy(s32[256,1]{0,1:T(1,128)} %bitcast.21) | data formatting | bytes 2048 | tf_op jit(solution)/shard_map/broadcast_in_dim;squeeze | solution.py:520
  38.1 0.0 copy-start.1
  38.1 1.0 copy-done.1
  39.2 0.0 copy-start.8
  39.2 0.9 copy-done.8
  40.1 0.0 copy-start.9
  40.1 0.7 copy-done.9
  40.8 0.0 copy-start.10
  40.8 1.0 copy-done.10
  41.8 1.0 copy-done.11
  42.9 0.0 copy-start.12
  42.9 1.0 copy-done.12
  43.9 0.0 copy-start.15
  43.9 0.7 copy-done.15
  44.6 7.8 %coarse_attention.1 = (bf16[256,1024]{1,0:T(8,128)(2,1)}, bf16[256,1024]{1,0:T(8,128)(2,1)}, f32[256,1024]{1,0:T(8,128)S(1)}, f32[256,1024]{1,0:T(8,128)S(1)}, f...) custom-call(f32[8]{0:T(128)S(1)} %copy-done.15, s32[256,1]{1,0:T(8,128)S(1)} %copy-done.8, ...), custom_call_target="tpu_custom_call" | custom-call | flops 805306368 | bytes 6291456 | tf_op jit(solution)/shard_map/coarse_attention/pallas_call | solution.py:508
  52.4 1.7 %collective-permute-done.1.qc_ref = bf16[8,208,128]{2,1,0:T(8,128)(2,1)} collective-permute-done((bf16[8,208,128]{2,1,0:T(8,128)(2,1)}, bf16[8,208,128]{2,1,0:T(8,128)(2,1)}, u32[]{:S(2)}, u32[]{:S(2)}) %collective-permute-start.1) | collective-permute-done | bytes 426016 | tf_op jit(solution)/shard_map/ppermute | solution.py:657
  54.0 1.5 %collective-permute-done.kv_ref = bf16[8,208,128]{2,1,0:T(8,128)(2,1)} collective-permute-done((bf16[8,208,128]{2,1,0:T(8,128)(2,1)}, bf16[8,208,128]{2,1,0:T(8,128)(2,1)}, u32[]{:S(2)}, u32[]{:S(2)}) %collective-permute-start) | collective-permute-done | bytes 426016 | tf_op jit(solution)/shard_map/ppermute | solution.py:657
  55.6 0.0 copy-done.16
  55.6 6.8 %fine_forward.1 = (bf16[1536,1792]{1,0:T(8,128)(2,1)S(1)}, bf16[1792,128]{1,0:T(8,128)(2,1)S(1)}, bf16[1792,128]{1,0:T(8,128)(2,1)S(1)}, bf16[1536,128]{1,0:T(8,...) custom-call(f32[8]{0:T(128)S(1)} %copy-done.16, ...), custom_call_target="tpu_custom_call" | custom-call | flops 1409286144 | bytes 11010048 | tf_op jit(solution)/shard_map/fine_forward/pallas_call | solution.py:380
  62.4 2.6 %collective-permute-start.2 = (f32[24,128]{1,0:T(8,128)S(1)}, f32[24,128]{1,0:T(8,128)S(1)}, u32[]{:S(2)}, u32[]{:S(2)}) collective-permute-start(f32[24,128]{1,0:T(8,128)S(1)} %get-tuple-element.44.stat_ref), channel_id=1, source_target_pairs={{0,6},{1,7},{2,4},{3,5},{4,2},{5,3},{6,0},{7,1},{8,14},{9,15},{10,... | collective-permute-start | bytes 36872 | tf_op jit(solution)/shard_map/ppermute | solution.py:657
  65.0 2.1 %collective-permute-done.2.other_stat_ref = f32[24,128]{1,0:T(8,128)S(1)} collective-permute-done((f32[24,128]{1,0:T(8,128)S(1)}, f32[24,128]{1,0:T(8,128)S(1)}, u32[]{:S(2)}, u32[]{:S(2)}) %collective-permute-start.2) | collective-permute-done | bytes 12320 | tf_op jit(solution)/shard_map/ppermute | solution.py:657
  67.1 9.2 %fine_backward.1 = (bf16[768,256]{1,0:T(8,128)(2,1)S(1)}, bf16[768,256]{1,0:T(8,128)(2,1)S(1)}, bf16[768,256]{1,0:T(8,128)(2,1)S(1)}, bf16[768,256]{1,0:T(8,128)(2,1)S(1)}, bf16[272,256]{1,0:T(8,128)(2,1)S(1)}) custom-call(f32[8]{0:T(128)S(1)} %copy-done.16, s32[1]{0:T(128)} %get-tuple-element.43.shared_ref, bf16[8,400,128]{2,1,0:T(8,128)(2,1)S(1)} %all_to_all.10.own_ref, ...), custom_call_target="tpu_custom_call" | custom-call | flops 2818572288 | bytes 11010048 | tf_op jit(solution)/shard_map/fine_backward/pallas_call | solution.py:409
  76.4 0.0 copy-start.3
  76.4 0.7 copy-done.3
  77.1 0.7 copy-done.5
  77.9 0.8 copy-done.13
  78.6 0.7 copy-done.14
  79.4 1.9 %collective-permute-start.3 = (bf16[272,256]{1,0:T(8,128)(2,1)S(1)}, bf16[272,256]{1,0:T(8,128)(2,1)S(1)}, u32[]{:S(2)}, u32[]{:S(2)}) collective-permute-start(bf16[272,256]{1,0:T(8,128)(2,1)S(1)} %get-tuple-element.52.own_ref), channel_id=1, source_target_pairs={{0,2},{1,3},{2,0},{3,1},{4,6},{5,7},{6,4},{7,5},{8,10},{9,11},{10,... | collective-permute-start | bytes 417800 | tf_op jit(solution)/shard_map/ppermute | solution.py:657
  81.3 4.4 %collective-permute-done.3.near_ref = bf16[272,256]{1,0:T(8,128)(2,1)S(1)} collective-permute-done((bf16[272,256]{1,0:T(8,128)(2,1)S(1)}, bf16[272,256]{1,0:T(8,128)(2,1)S(1)}, u32[]{:S(2)}, u32[]{:S(2)}) %collective-permute-start.3) | collective-permute-done | bytes 139296 | tf_op jit(solution)/shard_map/ppermute | solution.py:657
  85.7 0.0 copy-start.7
  85.7 0.6 copy-done.7
  86.4 0.0 all-gather.3.cloned.1.call-update
  86.4 0.9 collective-permute-start.4
  87.3 0.0 collective-permute-start.5
  87.3 2.5 %collective-permute-start.8 = (f32[8,128]{1,0:T(8,128)S(1)}, f32[8,128]{1,0:T(8,128)S(1)}, u32[]{:S(2)}, u32[]{:S(2)}) collective-permute-start(f32[8,128]{1,0:T(8,128)S(1)} %get-tuple-element.62), channel_id=1, source_target_pairs={{0,96},{32,64},{64,32},{96,0},{128,224},{160,192},{192,160},{224,1... | collective-permute-start | bytes 12296 | tf_op jit(solution)/shard_map/ppermute | solution.py:660
  89.8 4.9 %collective-permute-start.7 = (f32[8,128]{1,0:T(8,128)S(1)}, f32[8,128]{1,0:T(8,128)S(1)}, u32[]{:S(2)}, u32[]{:S(2)}) collective-permute-start(f32[8,128]{1,0:T(8,128)S(1)} %get-tuple-element.62), channel_id=1, source_target_pairs={{0,64},{32,96},{64,0},{96,32},{128,192},{160,224},{192,128},{224,1... | collective-permute-start | bytes 12296 | tf_op jit(solution)/shard_map/ppermute | solution.py:660
  94.7 0.0 collective-permute-start.6
  94.7 0.0 collective-permute-done.8
  94.7 1.0 collective-permute-done.7
  95.7 1.8 %collective-permute-done.6 = f32[8,128]{1,0:T(8,128)S(1)} collective-permute-done((f32[8,128]{1,0:T(8,128)S(1)}, f32[8,128]{1,0:T(8,128)S(1)}, u32[]{:S(2)}, u32[]{:S(2)}) %collective-permute-start.6) | collective-permute-done | bytes 4128 | tf_op jit(solution)/shard_map/ppermute | solution.py:660
  97.5 0.6 collective-permute-start.11
  98.1 0.8 collective-permute-start.10
  99.0 2.7 %collective-permute-start.9 = (f32[8,128]{1,0:T(8,128)S(1)}, f32[8,128]{1,0:T(8,128)S(1)}, u32[]{:S(2)}, u32[]{:S(2)}) collective-permute-start(f32[8,128]{1,0:T(8,128)S(1)} %add_add_fusion.scale_and_all_0_), channel_id=1, source_target_pairs={{0,6},{1,7},{2,4},{3,5},{4,2},{5,3},{6,0},{7,1},{8,14},{9,15},{10,... | collective-permute-start | bytes 12296 | tf_op jit(solution)/shard_map/ppermute | solution.py:657
  101.7 2.5 %collective-permute-done.11.scale_and_all_3_ = f32[8,128]{1,0:T(8,128)S(1)} collective-permute-done((f32[8,128]{1,0:T(8,128)S(1)}, f32[8,128]{1,0:T(8,128)S(1)}, u32[]{:S(2)}, u32[]{:S(2)}) %collective-permute-start.11) | collective-permute-done | bytes 4128 | tf_op jit(solution)/shard_map/ppermute | solution.py:668
  104.2 0.0 collective-permute-done.10.scale_and_all_2_
  104.2 2.4 %collective-permute-done.9.scale_and_all_1_ = f32[8,128]{1,0:T(8,128)S(1)} collective-permute-done((f32[8,128]{1,0:T(8,128)S(1)}, f32[8,128]{1,0:T(8,128)S(1)}, u32[]{:S(2)}, u32[]{:S(2)}) %collective-permute-start.9) | collective-permute-done | bytes 4128 | tf_op jit(solution)/shard_map/ppermute | solution.py:657
  106.5 0.0 collective-permute-done.4.other_od_ref
  106.6 0.0 collective-permute-done.5.other_dkv_ref
  106.6 1.0 copy-done.4
  107.6 1.0 copy-done.6
  108.5 1.3 sum_pairs.1
  109.9 7.0 %all-to-all-start.1 = ((bf16[8,400,128]{2,1,0:T(8,128)(2,1)}), bf16[8,400,128]{2,1,0:T(8,128)(2,1)S(1)}, u32[]{:S(2)}, u32[]{:S(2)}) async-start(bf16[8,400,128]{2,1,0:T(8,128)(2,1)} %sum_pairs.1), calls=%async_computation.1 | async-start | bytes 1638400 | tf_op jit(solution)/shard_map/all_to_all | solution.py:654
  116.8 0.0 copy-done.2
  116.8 1.2 copy-done
  118.1 1.9 %join_coarse.1 = (bf16[256,1024]{1,0:T(8,128)(2,1)}, bf16[256,1024]{1,0:T(8,128)(2,1)}, f32[8,128]{1,0:T(8,128)S(1)}) custom-call(bf16[8,256,256]{2,1,0:T(8,128)(2,1)S(1)} %bitcast.18, f32[256,1024]{1,0:T(8,128)S(1)} %get-tuple-element.54.dk_own_ref, f32[256,1024]{1,0:T(8,128)S(1)} %get-tuple-element.55.dv_own_ref, bf16[256,1024]{1,0:T(8,128)(2,1)S(1)} %bitcast.20), custom_call_target="tpu_custom_call" | custom-call | tf_op jit(solution)/shard_map/join_coarse/pallas_call | solution.py:598
  119.9 9.5 %all-to-all-done.1.all_ref = bf16[8,400,128]{2,1,0:T(8,128)(2,1)S(1)} async-done(((bf16[8,400,128]{2,1,0:T(8,128)(2,1)}), bf16[8,400,128]{2,1,0:T(8,128)(2,1)S(1)}, u32[]{:S(2)}, u32[]{:S(2)}) %all-to-all-start.1) | async-done | bytes 819232 | tf_op jit(solution)/shard_map/all_to_all | solution.py:654
  129.5 0.9 unpack_heads.1
  (11 shorter events, 0.1 us)
Async XLA Ops:
  7.2 48.4 %copy-start.16 = (f32[8]{0:T(128)S(1)}, f32[8]{0:T(128)}, u32[]{:S(2)}) copy-start(f32[8]{0:T(128)} %log_ref.5) | copy-start | bytes 100
  7.2 109.6 %all-gather.3.cloned.1.call-start = ((), (), s32[]{:S(2)}) async-start(), calls=%async_computation.2 | async-start | bytes 1179648 | tf_op jit(solution)/shard_map/all_gather | solution.py:682
  30.2 23.8 %collective-permute-start.1 = (bf16[8,208,128]{2,1,0:T(8,128)(2,1)}, bf16[8,208,128]{2,1,0:T(8,128)(2,1)}, u32[]{:S(2)}, u32[]{:S(2)}) collective-permute-start(bf16[8,208,128]{2,1,0:T(8,128)(2,1)} %get-tuple-element.69), channel_id=1, source_target_pairs={{0,6},{1,7},{2,4},{3,5},{4,2},{5,3},{6,0},{7,1},{8,14},{9,15},{10,... | collective-permute-start | bytes 1277960 | tf_op jit(solution)/shard_map/ppermute | solution.py:657
  35.5 20.1 %collective-permute-start = (bf16[8,208,128]{2,1,0:T(8,128)(2,1)}, bf16[8,208,128]{2,1,0:T(8,128)(2,1)}, u32[]{:S(2)}, u32[]{:S(2)}) collective-permute-start(bf16[8,208,128]{2,1,0:T(8,128)(2,1)} %get-tuple-element.70), channel_id=1, source_target_pairs={{0,2},{1,3},{2,0},{3,1},{4,6},{5,7},{6,4},{7,5},{8,10},{9,11},{10,... | collective-permute-start | bytes 1277960 | tf_op jit(solution)/shard_map/ppermute | solution.py:657
  38.1 1.0 copy-start.1
  39.2 0.9 copy-start.8
  40.1 0.7 copy-start.9
  40.8 1.0 copy-start.10
  41.8 1.0 copy-start.11
  42.9 1.0 copy-start.12
  43.9 0.7 copy-start.15
  62.4 4.7 %collective-permute-start.2 = (f32[24,128]{1,0:T(8,128)S(1)}, f32[24,128]{1,0:T(8,128)S(1)}, u32[]{:S(2)}, u32[]{:S(2)}) collective-permute-start(f32[24,128]{1,0:T(8,128)S(1)} %get-tuple-element.44.stat_ref), channel_id=1, source_target_pairs={{0,6},{1,7},{2,4},{3,5},{4,2},{5,3},{6,0},{7,1},{8,14},{9,15},{10,... | collective-permute-start | bytes 36872 | tf_op jit(solution)/shard_map/ppermute | solution.py:657
  67.1 49.7 %copy-start.2 = (bf16[1,256,1024]{2,1,0:T(8,128)(2,1)S(1)}, bf16[1,256,1024]{2,1,0:T(8,128)(2,1)}, u32[]{:S(2)}) copy-start(bf16[1,256,1024]{2,1,0:T(8,128)(2,1)} %param.12) | copy-start | bytes 1572868
  76.4 0.7 copy-start.3
  77.1 0.8 copy-start.5
  77.9 0.8 copy-start.13
  78.6 0.7 copy-start.14
  79.4 6.3 %collective-permute-start.3 = (bf16[272,256]{1,0:T(8,128)(2,1)S(1)}, bf16[272,256]{1,0:T(8,128)(2,1)S(1)}, u32[]{:S(2)}, u32[]{:S(2)}) collective-permute-start(bf16[272,256]{1,0:T(8,128)(2,1)S(1)} %get-tuple-element.52.own_ref), channel_id=1, source_target_pairs={{0,2},{1,3},{2,0},{3,1},{4,6},{5,7},{6,4},{7,5},{8,10},{9,11},{10,... | collective-permute-start | bytes 417800 | tf_op jit(solution)/shard_map/ppermute | solution.py:657
  85.7 0.7 copy-start.7
  86.4 20.2 %collective-permute-start.4 = (bf16[768,256]{1,0:T(8,128)(2,1)}, bf16[768,256]{1,0:T(8,128)(2,1)S(1)}, u32[]{:S(2)}, u32[]{:S(2)}) collective-permute-start(bf16[768,256]{1,0:T(8,128)(2,1)} %copy-done.14), channel_id=1, source_target_pairs={{0,6},{1,7},{2,4},{3,5},{4,2},{5,3},{6,0},{7,1},{8,14},{9,15},{10,... | collective-permute-start | bytes 1179656 | tf_op jit(solution)/shard_map/ppermute | solution.py:657
  87.3 19.3 %collective-permute-start.5 = (bf16[768,256]{1,0:T(8,128)(2,1)}, bf16[768,256]{1,0:T(8,128)(2,1)S(1)}, u32[]{:S(2)}, u32[]{:S(2)}) collective-permute-start(bf16[768,256]{1,0:T(8,128)(2,1)} %copy-done.13), channel_id=1, source_target_pairs={{0,2},{1,3},{2,0},{3,1},{4,6},{5,7},{6,4},{7,5},{8,10},{9,11},{10,... | collective-permute-start | bytes 1179656 | tf_op jit(solution)/shard_map/ppermute | solution.py:657
  87.3 7.4 %collective-permute-start.8 = (f32[8,128]{1,0:T(8,128)S(1)}, f32[8,128]{1,0:T(8,128)S(1)}, u32[]{:S(2)}, u32[]{:S(2)}) collective-permute-start(f32[8,128]{1,0:T(8,128)S(1)} %get-tuple-element.62), channel_id=1, source_target_pairs={{0,96},{32,64},{64,32},{96,0},{128,224},{160,192},{192,160},{224,1... | collective-permute-start | bytes 12296 | tf_op jit(solution)/shard_map/ppermute | solution.py:660
  89.8 5.9 %collective-permute-start.7 = (f32[8,128]{1,0:T(8,128)S(1)}, f32[8,128]{1,0:T(8,128)S(1)}, u32[]{:S(2)}, u32[]{:S(2)}) collective-permute-start(f32[8,128]{1,0:T(8,128)S(1)} %get-tuple-element.62), channel_id=1, source_target_pairs={{0,64},{32,96},{64,0},{96,32},{128,192},{160,224},{192,128},{224,1... | collective-permute-start | bytes 12296 | tf_op jit(solution)/shard_map/ppermute | solution.py:660
  94.7 2.8 %collective-permute-start.6 = (f32[8,128]{1,0:T(8,128)S(1)}, f32[8,128]{1,0:T(8,128)S(1)}, u32[]{:S(2)}, u32[]{:S(2)}) collective-permute-start(f32[8,128]{1,0:T(8,128)S(1)} %get-tuple-element.62), channel_id=1, source_target_pairs={{0,32},{32,0},{64,96},{96,64},{128,160},{160,128},{192,224},{224,1... | collective-permute-start | bytes 12296 | tf_op jit(solution)/shard_map/ppermute | solution.py:660
  97.5 6.7 %collective-permute-start.11 = (f32[8,128]{1,0:T(8,128)S(1)}, f32[8,128]{1,0:T(8,128)S(1)}, u32[]{:S(2)}, u32[]{:S(2)}) collective-permute-start(f32[8,128]{1,0:T(8,128)S(1)} %add_add_fusion.scale_and_all_0_), channel_id=1, source_target_pairs={{0,134},{1,135},{2,132},{3,133},{4,130},{5,131},{6,128},{7,129},{8... | collective-permute-start | bytes 12296 | tf_op jit(solution)/shard_map/ppermute | solution.py:668
  98.1 6.1 %collective-permute-start.10 = (f32[8,128]{1,0:T(8,128)S(1)}, f32[8,128]{1,0:T(8,128)S(1)}, u32[]{:S(2)}, u32[]{:S(2)}) collective-permute-start(f32[8,128]{1,0:T(8,128)S(1)} %add_add_fusion.scale_and_all_0_), channel_id=1, source_target_pairs={{0,128},{32,160},{64,192},{96,224},{128,0},{160,32},{192,64},{224,... | collective-permute-start | bytes 12296 | tf_op jit(solution)/shard_map/ppermute | solution.py:660
  99.0 7.6 %collective-permute-start.9 = (f32[8,128]{1,0:T(8,128)S(1)}, f32[8,128]{1,0:T(8,128)S(1)}, u32[]{:S(2)}, u32[]{:S(2)}) collective-permute-start(f32[8,128]{1,0:T(8,128)S(1)} %add_add_fusion.scale_and_all_0_), channel_id=1, source_target_pairs={{0,6},{1,7},{2,4},{3,5},{4,2},{5,3},{6,0},{7,1},{8,14},{9,15},{10,... | collective-permute-start | bytes 12296 | tf_op jit(solution)/shard_map/ppermute | solution.py:657
  106.6 1.0 copy-start.4
  107.6 1.0 copy-start.6
  109.9 19.6 %all-to-all-start.1 = ((bf16[8,400,128]{2,1,0:T(8,128)(2,1)}), bf16[8,400,128]{2,1,0:T(8,128)(2,1)S(1)}, u32[]{:S(2)}, u32[]{:S(2)}) async-start(bf16[8,400,128]{2,1,0:T(8,128)(2,1)} %sum_pairs.1), calls=%async_computation.1 | async-start | bytes 1638400 | tf_op jit(solution)/shard_map/all_to_all | solution.py:654
  116.8 1.2 copy-start
Sparse Core Ops, SparseCore 0:
  86.5 26.5 all-gather.2

commit v8 on v6

--- a/solution.py
+++ b/solution.py
@@ -124,16 +124,18 @@
     return pl.ds(first if isinstance(first, int) else pl.multiple_of(first, 128), size)
 
 
-def all_chunks(work, some_keys, shared, chunks):
+def coarse_chunks(work, some_keys):
     work(0, some_keys, 0, True)
     work(some_keys, some_keys, 0, False)
 
+
+def fine_chunks(work, coarse, shared, chunks):
     def both(chunk, carry):
-        work(2 * some_keys + chunk * k_tile, k_tile, 0, True)
+        work(coarse + chunk * k_tile, k_tile, 0, True)
         return carry
 
     def upper(chunk, carry):
-        work(2 * some_keys + chunk * k_tile, k_tile, 1, True)
+        work(coarse + chunk * k_tile, k_tile, 1, True)
         return carry
 
     lax.fori_loop(0, shared, both, 0)
@@ -236,7 +238,8 @@
 
     shared = (limit_of(queries // 2 - 1) + k_tile - 1) // k_tile
     shared_ref[0] = shared
-    all_chunks(probs, some_keys, shared, fine // k_tile)
+    coarse_chunks(probs, some_keys)
+    fine_chunks(probs, coarse, shared, fine // k_tile)
 
     num = sum_scr[:, :width]
     num_ref[...] = num
@@ -252,11 +255,24 @@
             )
 
 
-def backward_kernel(
+def key_grads(refs, targets, start, size, first, counts):
+    prob_ref, key_ref, val_ref, cot_ref, mean_ref, query_turn, cot_turn, grad_ref = refs
+    dk_target, dv_target = targets
+    spot = key_spot(start, size)
+    prob = prob_ref[first:, spot]
+    dprob = dot_nt(cot_ref[first:, :], val_ref[spot, :])
+    dscore = prob.astype(jnp.float32) * (dprob - wide_as(mean_ref[first:, :], size))
+    dscore = dscore.astype(jnp.bfloat16)
+    if counts:
+        grad_ref[first:, :] += dot_nn(dscore, key_ref[spot, :])
+    dk = dot_nn(query_turn[:, first:], dscore)
+    dv = dot_nn(cot_turn[:, first:], prob)
+    dk_target[...] = jnp.transpose(dk).astype(jnp.bfloat16)
+    dv_target[...] = jnp.transpose(dv).astype(jnp.bfloat16)
+
+
+def coarse_back_kernel(
     log_ref,
-    shared_ref,
-    own_ref,
-    qc_ref,
     stat_ref,
     other_stat_ref,
     prob_ref,
@@ -264,18 +280,71 @@
     val_ref,
     query_ref,
     cot_ref,
+    small_ref,
+    den_ref,
+    mean_ref,
+    grad_ref,
+    query_turn,
+    cot_turn,
+):
+    _, head = seq_place()
+    queries, width = query_ref.shape
+    coarse = small_ref.shape[0]
+    sharp = jnp.exp(jnp.full((1, width), log_ref[head], jnp.float32))[:, 0:1]
+    row = lax.broadcasted_iota(jnp.int32, (width, width), 0)
+    lane = lax.broadcasted_iota(jnp.int32, (width, width), 1)
+    parts = queries // width
+
+    def column(index):
+        values = stat_ref[index : index + 1, :] + other_stat_ref[index : index + 1, :]
+        return jnp.sum(jnp.where(row == lane, values, 0.0), axis=1, keepdims=True)
+
+    for part in range(parts):
+        spot = slice(part * width, (part + 1) * width)
+        r_den = 1.0 / column(part)
+        den_ref[spot, :] = jnp.broadcast_to(r_den, (width, width))
+        mean_ref[spot, :] = jnp.broadcast_to(column(parts + part) * r_den, (width, width))
+
+    grad_ref[...] = jnp.zeros_like(grad_ref)
+    query_turn[...] = jnp.transpose(
+        query_ref[...].astype(jnp.float32) * (den_ref[...] * sharp)
+    ).astype(jnp.bfloat16)
+    cot_turn[...] = jnp.transpose(cot_ref[...].astype(jnp.float32) * den_ref[...]).astype(
+        jnp.bfloat16
+    )
+    refs = (prob_ref, key_ref, val_ref, cot_ref, mean_ref, query_turn, cot_turn, grad_ref)
+
+    def work(start, size, part, counts):
+        spot = slice(start, start + size)
+        targets = (small_ref.at[spot, 0:width], small_ref.at[spot, width:])
+        key_grads(refs, targets, start, size, 0, counts)
+
+    coarse_chunks(work, coarse // 2)
+
+
+def fine_back_kernel(
+    log_ref,
+    shared_ref,
+    own_ref,
+    qc_ref,
+    prob_ref,
+    key_ref,
+    val_ref,
+    query_ref,
+    cot_ref,
     num_ref,
+    den_ref,
+    mean_ref,
+    grad_in_ref,
+    query_turn,
+    cot_turn,
     coarse_scale_ref,
     od_ref,
     od_send_ref,
     dkv_ref,
     dkv_send_ref,
-    small_ref,
-    den_scr,
-    mean_scr,
+    scale_ref,
     grad_scr,
-    query_turn,
-    cot_turn,
     turn_scr,
 ):
     plane, head = seq_place()
@@ -285,47 +354,18 @@
     runs = members // 2
     queries = query_ref.shape[0]
     first_query = 2 * rows + note_rows
-    coarse = small_ref.shape[0] - note_rows
-    fine = key_ref.shape[0] - coarse
+    fine = turn_scr.shape[0]
+    coarse = key_ref.shape[0] - fine
     sharp = jnp.exp(jnp.full((1, width), log_ref[head], jnp.float32))[:, 0:1]
-
-    row = lax.broadcasted_iota(jnp.int32, (width, width), 0)
-    lane = lax.broadcasted_iota(jnp.int32, (width, width), 1)
-    parts = queries // width
-
-    def column(index):
-        values = stat_ref[index : index + 1, :] + other_stat_ref[index : index + 1, :]
-        return jnp.sum(jnp.where(row == lane, values, 0.0), axis=1, keepdims=True)
-
-    for part in range(parts):
-        spot = slice(part * width, (part + 1) * width)
-        r_den = 1.0 / column(part)
-        den_scr[spot, :] = jnp.broadcast_to(r_den, (width, width))
-        mean_scr[spot, :] = jnp.broadcast_to(column(parts + part) * r_den, (width, width))
-
-    grad_scr[...] = jnp.zeros_like(grad_scr)
-    query_turn[...] = jnp.transpose(
-        query_ref[...].astype(jnp.float32) * (den_scr[...] * sharp)
-    ).astype(jnp.bfloat16)
-    cot_turn[...] = jnp.transpose(cot_ref[...].astype(jnp.float32) * den_scr[...]).astype(
-        jnp.bfloat16
-    )
-
-    def grads(start, size, part, counts):
-        first = part * queries // 2
-        spot = key_spot(start, size)
-        prob = prob_ref[first:, spot]
-        dprob = dot_nt(cot_ref[first:, :], val_ref[spot, :])
-        dscore = prob.astype(jnp.float32) * (dprob - wide_as(mean_scr[first:, :], size))
-        dscore = dscore.astype(jnp.bfloat16)
-        if counts:
-            grad_scr[first:, :] += dot_nn(dscore, key_ref[spot, :])
-        dk = dot_nn(query_turn[:, first:], dscore)
-        dv = dot_nn(cot_turn[:, first:], prob)
-        turn_scr[spot, 0:width] = jnp.transpose(dk).astype(jnp.bfloat16)
-        turn_scr[spot, width:] = jnp.transpose(dv).astype(jnp.bfloat16)
-
-    all_chunks(grads, coarse // 2, shared_ref[0], fine // k_tile)
+    grad_scr[...] = grad_in_ref[...]
+    refs = (prob_ref, key_ref, val_ref, cot_ref, mean_ref, query_turn, cot_turn, grad_scr)
+
+    def work(start, size, part, counts):
+        spot = key_spot(start - coarse, size)
+        targets = (turn_scr.at[spot, 0:width], turn_scr.at[spot, width:])
+        key_grads(refs, targets, start, size, part * queries // 2, counts)
+
+    fine_chunks(work, coarse, shared_ref[0], fine // k_tile)
 
     own_slot = query_slot(plane)
     scale = coarse_scale_ref[pl.ds(pl.multiple_of(head * 8, 8), 8), :]
@@ -338,7 +378,7 @@
             spot = pl.ds(place_of(run, slot, block), block)
             pick = ref[2 * run : 2 * run + 2, start : start + rows]
             q_dir, q_inv = unit_rows(pick.reshape(block, width))
-            r_den = den_scr[spot, :]
+            r_den = den_ref[spot, :]
             grad = grad_scr[spot, :] * (r_den * sharp)
             along = jnp.sum(q_dir * grad, axis=-1, keepdims=True)
             scale = scale + fold_rows(query_ref[spot, :].astype(jnp.float32) * grad)
@@ -349,10 +389,9 @@
     own_slot = key_slot(plane)
     for slot, target in ((own_slot, dkv_ref), (1 - own_slot, dkv_send_ref)):
         for run in range(runs):
-            spot = pl.ds(pl.multiple_of(coarse + place_of(run, slot, block), 64), block)
+            spot = pl.ds(place_of(run, slot, block), block)
             target[run * block : (run + 1) * block, :] = turn_scr[spot, :]
-    small_ref[0:coarse, :] = turn_scr[0:coarse, :]
-    small_ref[coarse:, :] = in_pieces(sum_all(scale), 2 * width)
+    scale_ref[...] = jnp.broadcast_to(sum_all(scale), scale_ref.shape)
 
 
 def run_fine(log_scale, own_rows, kv_rows, qc_rows, key_coarse, val_coarse, coarse_scale, swap):
@@ -398,24 +437,40 @@
         name="fine_forward",
     )(log_scale, own_rows, kv_rows, qc_rows, key_coarse, val_coarse)
     other_stat = swap(stat)
+    small, den, mean, grad, query_turned, cot_turned = pl.pallas_call(
+        coarse_back_kernel,
+        out_shape=(
+            low(coarse, 2 * width),
+            wide(queries, width),
+            wide(queries, width),
+            wide(queries, width),
+            low(width, queries),
+            low(width, queries),
+        ),
+        in_specs=[smem] + [vmem] * 7,
+        out_specs=(vmem,) * 6,
+        compiler_params=params(12),
+        cost_estimate=pl.CostEstimate(
+            flops=8 * queries * coarse * width,
+            bytes_accessed=4 * queries * coarse,
+            transcendentals=0,
+        ),
+        name="coarse_key_grads",
+    )(log_scale, stat, other_stat, prob, keys, values, query, cot)
     half = low(queries // 2, 2 * width)
-    return pl.pallas_call(
-        backward_kernel,
-        out_shape=(half, half, half, half, low(coarse + note_rows, 2 * width)),
-        in_specs=[smem, smem] + [vmem] * 11,
+    outs = pl.pallas_call(
+        fine_back_kernel,
+        out_shape=(half, half, half, half, wide(8, width)),
+        in_specs=[smem, smem] + [vmem] * 14,
         out_specs=(vmem,) * 5,
         scratch_shapes=[
             pltpu.VMEM((queries, width), jnp.float32),
-            pltpu.VMEM((queries, width), jnp.float32),
-            pltpu.VMEM((queries, width), jnp.float32),
-            pltpu.VMEM((width, queries), jnp.bfloat16),
-            pltpu.VMEM((width, queries), jnp.bfloat16),
-            pltpu.VMEM((total, 2 * width), jnp.bfloat16),
+            pltpu.VMEM((queries, 2 * width), jnp.bfloat16),
         ],
         compiler_params=params(16),
         cost_estimate=pl.CostEstimate(
-            flops=8 * queries * total * width,
-            bytes_accessed=4 * queries * total,
+            flops=8 * queries * queries * width,
+            bytes_accessed=4 * queries * queries,
             transcendentals=0,
         ),
         name="fine_backward",
@@ -424,16 +479,20 @@
         shared,
         own_rows,
         qc_rows,
-        stat,
-        other_stat,
         prob,
         keys,
         values,
         query,
         cot,
         num,
+        den,
+        mean,
+        grad,
+        query_turned,
+        cot_turned,
         coarse_scale,
     )
+    return small, outs
 
 
 def coarse_kernel(
@@ -512,29 +571,22 @@
     )(log_scale, levels[:, None], levels[None, :], queries, keys, values, cots)
 
 
-def small_kernel(own_ref, near_ref, sum_ref, scale_ref):
-    coarse, both = sum_ref.shape
-    some_keys = coarse // 2
+def small_kernel(own_ref, near_ref, _, sum_ref):
+    some_keys = sum_ref.shape[0] // 2
     summed = own_ref[...].astype(jnp.float32) + near_ref[...].astype(jnp.float32)
     own_half = query_slot(seq_place()[0])
     for index, half in enumerate((own_half, 1 - own_half)):
         spot = pl.ds(pl.multiple_of(half * some_keys, some_keys), some_keys)
         sum_ref[spot, :] = summed[index * some_keys : (index + 1) * some_keys].astype(jnp.bfloat16)
-    scale = jnp.sum(summed[coarse:, : both // 2], axis=0, keepdims=True)
-    scale_ref[...] = jnp.broadcast_to(scale, scale_ref.shape)
-
-
-def run_small(own, near):
-    tall, both = own.shape
+
+
+def run_small(own, near, after):
     return pl.pallas_call(
         small_kernel,
-        out_shape=(
-            jax.ShapeDtypeStruct((tall - note_rows, both), jnp.bfloat16),
-            jax.ShapeDtypeStruct((8, both // 2), jnp.float32),
-        ),
+        out_shape=jax.ShapeDtypeStruct(own.shape, jnp.bfloat16),
         compiler_params=params(2),
         name="sum_coarse_terms",
-    )(own, near)
+    )(own, near, after)
 
 
 def sum_kernel(
@@ -666,17 +718,19 @@
     out_c, dq_c, dk_own, dv_own, scale_c, key_c, val_c = run_coarse(
         log_scale, coarse_ids[0], q_coarse[0], k_coarse[0], v_coarse[0], cot_coarse[0]
     )
-    od, od_send, dkv, dkv_send, small = run_fine(
+    small, (od, od_send, dkv, dkv_send, scale) = run_fine(
         log_scale, own_rows, kv_rows, qc_rows, key_c, val_c, scale_c, lambda stat: to_plane(stat, 3)
     )
 
-    small_sum, scale = run_small(small, to_plane(small, 1))
+    small_sum = run_small(small, to_plane(small, 1), scale)
     of_image = lax.all_gather(small_sum, "seq", axis=0, axis_index_groups=groups)
 
     other_dkv = to_plane(dkv_send, 1)
     other_od = to_plane(od_send, 3)
     scale = scale + to_image(scale, 1) + to_image(scale, 2) + to_image(scale, 3)
-    scales = [scale, to_plane(scale, 3), to_image(scale, 4), to_both(scale, 4, 3)]
+    scales = [scale, to_image(scale, 4)]
+    for flip in (1, 2, 3):
+        scales += [to_plane(scale, flip), to_both(scale, 4, flip)]
     all_parts = run_sum(od, other_od, dkv, other_dkv, own_rows, scales)
     all_back = exchange(all_parts)
     dk_c, dv_c, after = run_join(of_image, dk_own, dv_own, k_coarse[0])

time: 138 us -> 144 us (1.043)
  starting transfers between devices: 27.7 us -> 36.1 us
  waiting for transfers between devices: 29.4 us -> 27.5 us
    ppermute x7 -> x9, waiting for transfers between devices: 13.7 us -> 6.07 us  [to_plane(): return lax.ppermute(array, 'seq', [(i, i ^ 2 * flip) for i in range(seq)])]
    ppermute x1 -> x3, starting transfers between devices: 0.09 us -> 5.06 us  [to_both(): return lax.ppermute(array, ('dp', 'seq'), list(enumerate(there)))]
    ppermute x7 -> x9, starting transfers between devices: 17.4 us -> 20.5 us  [to_plane(): return lax.ppermute(array, 'seq', [(i, i ^ 2 * flip) for i in range(seq)])]
    ppermute x1 -> x3, waiting for transfers between devices: 2.87 us -> 5.94 us  [to_both(): return lax.ppermute(array, ('dp', 'seq'), list(enumerate(there)))]
    ppermute x4, waiting for transfers between devices: 3.27 us -> 5.87 us  [to_image(): return lax.ppermute(array, 'dp', [(i, i ^ flip) for i in range(images)])]
    all_to_all x1, starting transfers between devices: 5.24 us -> 7.19 us  [exchange(): lax.all_to_all(parts, 'seq', 0, 0, axis_index_groups=groups, tiled=True)]
    ppermute x4, starting transfers between devices: 4.9 us -> 3.26 us  [to_image(): return lax.ppermute(array, 'dp', [(i, i ^ flip) for i in range(images)])]
    pallas_call x2 -> x3, Pallas kernels: 10.2 us -> 9.43 us  [the longest x1 7.46 us: run_fine(): pl.pallas_call(fine_back_kernel, out_shape=(half, half, half, half, wide(...]
  transfers between devices with their start and end apart: 14 -> 18, of which waited for: 10 -> 9; matrix products, arithmetic and copies ran while one was open for 1% -> 1% of each run, Pallas kernels for 8% -> 13%
where the time goes in v8:
time: 144 us; the launch traced here: 143 us
  starting transfers between devices  36.1 us (25%)
  Pallas kernels  30.2 us (21%)
  waiting for transfers between devices  27.5 us (19%)
  blocking collectives  19.7 us (14%)
  local copies, waits for them, and re-layouts  15.7 us (11%)
  between operations  14.1 us (10%)
    ppermute x9, starting transfers between devices, to_plane(): return lax.ppermute(array, 'seq', [(i, i ^ 2 * flip) for i in range(seq)])  20.5 us
    all_to_all x1, blocking collectives, exchange(): lax.all_to_all(parts, 'seq', 0, 0, axis_index_groups=groups, tiled=True)  19.7 us
    unnamed x34, local copies, waits for them, and re-layouts  13.2 us
    all_to_all x1, waiting for transfers between devices, exchange(): lax.all_to_all(parts, 'seq', 0, 0, axis_index_groups=groups, tiled=True)  9.56 us
    pallas_call x1, Pallas kernels, run_coarse(): pl.pallas_call(coarse_kernel, out_shape=(low, low, wide, wide, jax.ShapeD...  7.79 us
    pallas_call x1, Pallas kernels, run_fine(): pl.pallas_call(fine_back_kernel, out_shape=(half, half, half, half, wide(...  7.46 us
    all_to_all x1, starting transfers between devices, exchange(): lax.all_to_all(parts, 'seq', 0, 0, axis_index_groups=groups, tiled=True)  7.19 us
    pallas_call x1, Pallas kernels, run_fine(): pl.pallas_call(forward_kernel, out_shape=(low(queries, total), low(total,...  6.56 us
  transfers between devices with their start and end apart: 18, of which 9 were waited for; matrix products, arithmetic and copies ran while one was open for 1% of the time, Pallas kernels for 13%

profile of v8, /device:TPU:1, one launch (start us, length us, event | category | flops | bytes accessed | tf_op | source)
XLA Modules:
  0.0 143.3 jit_solution(11447388143117474569)
XLA Ops:
  7.2 0.0 copy-start.10
  7.2 0.0 all-gather.3.cloned.1.call-start
  7.2 2.3 %pack_heads.1 = bf16[8,400,128]{2,1,0:T(8,128)(2,1)} custom-call(s32[1,96]{1,0:T(1,128)} %ids_ref.1, bf16[96,1024]{1,0:T(8,128)(2,1)} %bitcast.25, bf16[96,1024]{1,0:T(8,128)(2,1)} %bitcast.26, bf16[96,1024]{1,0:T(8,128)(2,1)} %bitcast.27, bf16[96,1024]{1,0:T(8,128)(2,1)} %bitcast.28), custom_call_target="tpu_custom_call" | custom-call | tf_op jit(solution)/shard_map/pack_heads/pallas_call | solution.py:103
  9.5 19.7 %all_to_all.10.own_ref = bf16[8,400,128]{2,1,0:T(8,128)(2,1)S(1)} all-to-all(bf16[8,400,128]{2,1,0:T(8,128)(2,1)} %pack_heads.1), channel_id=1, replica_groups={{0,1,8,9,16,17,24,25},{2,3,10,11,18,19,26,27},{4,5,12,13,20,21,28,29},{..., dimensions={0} | all-to-all | bytes 1638400 | tf_op jit(solution)/shard_map/all_to_all | solution.py:698
  29.2 1.0 fusion
  30.2 5.3 %collective-permute-start.1 = (bf16[8,208,128]{2,1,0:T(8,128)(2,1)}, bf16[8,208,128]{2,1,0:T(8,128)(2,1)}, u32[]{:S(2)}, u32[]{:S(2)}) collective-permute-start(bf16[8,208,128]{2,1,0:T(8,128)(2,1)} %get-tuple-element.77), channel_id=1, source_target_pairs={{0,6},{1,7},{2,4},{3,5},{4,2},{5,3},{6,0},{7,1},{8,14},{9,15},{10,... | collective-permute-start | bytes 1277960 | tf_op jit(solution)/shard_map/ppermute | solution.py:701
  35.5 1.2 collective-permute-start
  36.7 1.5 %copy.20.row_level_ref = s32[256,1]{1,0:T(8,128)} copy(s32[256,1]{0,1:T(1,128)} %bitcast.21) | data formatting | bytes 2048 | tf_op jit(solution)/shard_map/broadcast_in_dim;squeeze | solution.py:571
  38.1 1.0 copy-done.1
  39.2 0.9 copy-done.8
  40.1 0.7 copy-done.9
  40.7 0.7 copy-done.11
  41.4 1.0 copy-done.12
  42.5 1.0 copy-done.13
  43.5 1.0 copy-done.14
  44.5 7.8 %coarse_attention.1 = (bf16[256,1024]{1,0:T(8,128)(2,1)}, bf16[256,1024]{1,0:T(8,128)(2,1)}, f32[256,1024]{1,0:T(8,128)S(1)}, f32[256,1024]{1,0:T(8,128)S(1)}, f...) custom-call(f32[8]{0:T(128)S(1)} %copy-done.9, s32[256,1]{1,0:T(8,128)S(1)} %copy-done.8, ...), custom_call_target="tpu_custom_call" | custom-call | flops 805306368 | bytes 6291456 | tf_op jit(solution)/shard_map/coarse_attention/pallas_call | solution.py:559
  52.3 1.7 %collective-permute-done.1.qc_ref = bf16[8,208,128]{2,1,0:T(8,128)(2,1)} collective-permute-done((bf16[8,208,128]{2,1,0:T(8,128)(2,1)}, bf16[8,208,128]{2,1,0:T(8,128)(2,1)}, u32[]{:S(2)}, u32[]{:S(2)}) %collective-permute-start.1) | collective-permute-done | bytes 426016 | tf_op jit(solution)/shard_map/ppermute | solution.py:701
  54.0 1.5 %collective-permute-done.kv_ref = bf16[8,208,128]{2,1,0:T(8,128)(2,1)} collective-permute-done((bf16[8,208,128]{2,1,0:T(8,128)(2,1)}, bf16[8,208,128]{2,1,0:T(8,128)(2,1)}, u32[]{:S(2)}, u32[]{:S(2)}) %collective-permute-start) | collective-permute-done | bytes 426016 | tf_op jit(solution)/shard_map/ppermute | solution.py:701
  55.5 6.6 %fine_forward.1 = (bf16[1536,1792]{1,0:T(8,128)(2,1)S(1)}, bf16[1792,128]{1,0:T(8,128)(2,1)S(1)}, bf16[1792,128]{1,0:T(8,128)(2,1)S(1)}, bf16[1536,128]{1,0:T(8,...) custom-call(f32[8]{0:T(128)S(1)} %copy-done.10, ...), custom_call_target="tpu_custom_call" | custom-call | flops 1409286144 | bytes 11010048 | tf_op jit(solution)/shard_map/fine_forward/pallas_call | solution.py:412
  62.1 2.9 %collective-permute-start.2 = (f32[24,128]{1,0:T(8,128)S(1)}, f32[24,128]{1,0:T(8,128)S(1)}, u32[]{:S(2)}, u32[]{:S(2)}) collective-permute-start(f32[24,128]{1,0:T(8,128)S(1)} %get-tuple-element.47.stat_ref), channel_id=1, source_target_pairs={{0,6},{1,7},{2,4},{3,5},{4,2},{5,3},{6,0},{7,1},{8,14},{9,15},{10,... | collective-permute-start | bytes 36872 | tf_op jit(solution)/shard_map/ppermute | solution.py:701
  65.0 1.9 %collective-permute-done.2.other_stat_ref = f32[24,128]{1,0:T(8,128)S(1)} collective-permute-done((f32[24,128]{1,0:T(8,128)S(1)}, f32[24,128]{1,0:T(8,128)S(1)}, u32[]{:S(2)}, u32[]{:S(2)}) %collective-permute-start.2) | collective-permute-done | bytes 12320 | tf_op jit(solution)/shard_map/ppermute | solution.py:701
  66.9 1.9 %coarse_key_grads.1 = (bf16[256,256]{1,0:T(8,128)(2,1)S(1)}, f32[1536,128]{1,0:T(8,128)S(1)}, f32[1536,128]{1,0:T(8,128)S(1)}, f32[1536,128]{1,0:T(8,128)S(1)}, ...) custom-call(f32[8]{0:T(128)S(1)} %copy-done.10, f32[24,128]{1,0:T(8,128)S(1)} %get-tuple-element.47.stat_ref, ...), custom_call_target="tpu_custom_call" | custom-call | flops 402653184 | bytes 1572864 | tf_op jit(solution)/shard_map/coarse_key_grads/pallas_call | solution.py:440
  68.8 2.2 %collective-permute-start.3 = (bf16[256,256]{1,0:T(8,128)(2,1)S(1)}, bf16[256,256]{1,0:T(8,128)(2,1)S(1)}, u32[]{:S(2)}, u32[]{:S(2)}) collective-permute-start(bf16[256,256]{1,0:T(8,128)(2,1)S(1)} %get-tuple-element.53.own_ref), channel_id=1, source_target_pairs={{0,2},{1,3},{2,0},{3,1},{4,6},{5,7},{6,4},{7,5},{8,10},{9,11},{10,... | collective-permute-start | bytes 393224 | tf_op jit(solution)/shard_map/ppermute | solution.py:701
  71.0 7.5 %fine_backward.1 = (bf16[768,256]{1,0:T(8,128)(2,1)S(1)}, bf16[768,256]{1,0:T(8,128)(2,1)S(1)}, bf16[768,256]{1,0:T(8,128)(2,1)S(1)}, bf16[768,256]{1,0:T(8,128)(2,1)S(1)}, f32[8,128]{1,0:T(8,128)S(1)}) custom-call(f32[8]{0:T(128)S(1)} %copy-done.10, s32[1]{0:T(128)} %get-tuple-element.54.shared_ref, bf16[8,400,128]{2,1,0:T(8,128)(2,1)S(1)} %all_to_all.10.own_ref, ...), custom_call_target="tpu_custom_call" | custom-call | flops 2415919104 | bytes 9437184 | tf_op jit(solution)/shard_map/fine_backward/pallas_call | solution.py:461
  78.5 0.0 copy-start.4
  78.5 0.7 copy-done.4
  79.2 0.7 copy-done.6
  80.0 0.7 copy-done.15
  80.7 0.7 copy-done.16
  81.4 0.0 collective-permute-done.3.near_ref
  81.5 0.0 copy-start.3
  81.5 0.6 copy-done.3
  82.1 0.0 all-gather.3.cloned.1.call-update
  82.2 1.0 collective-permute-start.4
  83.2 2.4 %collective-permute-start.5 = (bf16[768,256]{1,0:T(8,128)(2,1)}, bf16[768,256]{1,0:T(8,128)(2,1)S(1)}, u32[]{:S(2)}, u32[]{:S(2)}) collective-permute-start(bf16[768,256]{1,0:T(8,128)(2,1)} %copy-done.15), channel_id=1, source_target_pairs={{0,2},{1,3},{2,0},{3,1},{4,6},{5,7},{6,4},{7,5},{8,10},{9,11},{10,... | collective-permute-start | bytes 1179656 | tf_op jit(solution)/shard_map/ppermute | solution.py:701
  85.5 2.4 %collective-permute-start.8 = (f32[8,128]{1,0:T(8,128)S(1)}, f32[8,128]{1,0:T(8,128)S(1)}, u32[]{:S(2)}, u32[]{:S(2)}) collective-permute-start(f32[8,128]{1,0:T(8,128)S(1)} %get-tuple-element.62._), channel_id=1, source_target_pairs={{0,96},{32,64},{64,32},{96,0},{128,224},{160,192},{192,160},{224,1... | collective-permute-start | bytes 12296 | tf_op jit(solution)/shard_map/ppermute | solution.py:704
  88.0 0.6 collective-permute-start.7
  88.5 0.3 collective-permute-start.6
  88.8 0.4 collective-permute-done.8
  89.2 3.0 %collective-permute-done.7 = f32[8,128]{1,0:T(8,128)S(1)} collective-permute-done((f32[8,128]{1,0:T(8,128)S(1)}, f32[8,128]{1,0:T(8,128)S(1)}, u32[]{:S(2)}, u32[]{:S(2)}) %collective-permute-start.7) | collective-permute-done | bytes 4128 | tf_op jit(solution)/shard_map/ppermute | solution.py:704
  92.2 0.0 collective-permute-done.6
  92.2 2.0 %collective-permute-start.15 = (f32[8,128]{1,0:T(8,128)S(1)}, f32[8,128]{1,0:T(8,128)S(1)}, u32[]{:S(2)}, u32[]{:S(2)}) collective-permute-start(f32[8,128]{1,0:T(8,128)S(1)} %add_add_fusion.scale_and_all_0_), channel_id=1, source_target_pairs={{0,134},{1,135},{2,132},{3,133},{4,130},{5,131},{6,128},{7,129},{8... | collective-permute-start | bytes 12296 | tf_op jit(solution)/shard_map/ppermute | solution.py:712
  94.3 2.0 %collective-permute-start.14 = (f32[8,128]{1,0:T(8,128)S(1)}, f32[8,128]{1,0:T(8,128)S(1)}, u32[]{:S(2)}, u32[]{:S(2)}) collective-permute-start(f32[8,128]{1,0:T(8,128)S(1)} %add_add_fusion.scale_and_all_0_), channel_id=1, source_target_pairs={{0,6},{1,7},{2,4},{3,5},{4,2},{5,3},{6,0},{7,1},{8,14},{9,15},{10,... | collective-permute-start | bytes 12296 | tf_op jit(solution)/shard_map/ppermute | solution.py:701
  96.3 1.3 collective-permute-start.13
  97.5 5.9 %collective-permute-done.15.scale_and_all_7_ = f32[8,128]{1,0:T(8,128)S(1)} collective-permute-done((f32[8,128]{1,0:T(8,128)S(1)}, f32[8,128]{1,0:T(8,128)S(1)}, u32[]{:S(2)}, u32[]{:S(2)}) %collective-permute-start.15) | collective-permute-done | bytes 4128 | tf_op jit(solution)/shard_map/ppermute | solution.py:712
  103.5 1.2 collective-permute-start.12
  104.6 0.0 collective-permute-done.14.scale_and_all_6_
  104.6 1.8 %collective-permute-start.11 = (f32[8,128]{1,0:T(8,128)S(1)}, f32[8,128]{1,0:T(8,128)S(1)}, u32[]{:S(2)}, u32[]{:S(2)}) collective-permute-start(f32[8,128]{1,0:T(8,128)S(1)} %add_add_fusion.scale_and_all_0_), channel_id=1, source_target_pairs={{0,130},{1,131},{2,128},{3,129},{4,134},{5,135},{6,132},{7,133},{8... | collective-permute-start | bytes 12296 | tf_op jit(solution)/shard_map/ppermute | solution.py:712
  106.4 2.4 %collective-permute-start.10 = (f32[8,128]{1,0:T(8,128)S(1)}, f32[8,128]{1,0:T(8,128)S(1)}, u32[]{:S(2)}, u32[]{:S(2)}) collective-permute-start(f32[8,128]{1,0:T(8,128)S(1)} %add_add_fusion.scale_and_all_0_), channel_id=1, source_target_pairs={{0,2},{1,3},{2,0},{3,1},{4,6},{5,7},{6,4},{7,5},{8,10},{9,11},{10,... | collective-permute-start | bytes 12296 | tf_op jit(solution)/shard_map/ppermute | solution.py:701
  108.8 1.0 collective-permute-done.12.scale_and_all_4_
  109.8 0.0 collective-permute-start.9
  109.8 0.0 collective-permute-done.11.scale_and_all_3_
  109.8 0.0 collective-permute-done.10.scale_and_all_2_
  109.8 2.4 %collective-permute-done.9.scale_and_all_1_ = f32[8,128]{1,0:T(8,128)S(1)} collective-permute-done((f32[8,128]{1,0:T(8,128)S(1)}, f32[8,128]{1,0:T(8,128)S(1)}, u32[]{:S(2)}, u32[]{:S(2)}) %collective-permute-start.9) | collective-permute-done | bytes 4128 | tf_op jit(solution)/shard_map/ppermute | solution.py:704
  112.3 0.0 collective-permute-done.4.other_od_ref
  112.3 0.0 collective-permute-done.5.other_dkv_ref
  112.3 1.0 copy-done.5
  113.3 1.0 copy-done.7
  114.3 1.3 sum_pairs.1
  115.6 7.2 %all-to-all-start.1 = ((bf16[8,400,128]{2,1,0:T(8,128)(2,1)}), bf16[8,400,128]{2,1,0:T(8,128)(2,1)S(1)}, u32[]{:S(2)}, u32[]{:S(2)}) async-start(bf16[8,400,128]{2,1,0:T(8,128)(2,1)} %sum_pairs.1), calls=%async_computation.1 | async-start | bytes 1638400 | tf_op jit(solution)/shard_map/all_to_all | solution.py:698
  122.8 1.2 copy-done
  124.0 1.9 %join_coarse.1 = (bf16[256,1024]{1,0:T(8,128)(2,1)}, bf16[256,1024]{1,0:T(8,128)(2,1)}, f32[8,128]{1,0:T(8,128)S(1)}) custom-call(bf16[8,256,256]{2,1,0:T(8,128)(2,1)S(1)} %bitcast.18, f32[256,1024]{1,0:T(8,128)S(1)} %get-tuple-element.63.dk_own_ref, f32[256,1024]{1,0:T(8,128)S(1)} %get-tuple-element.64.dv_own_ref, bf16[256,1024]{1,0:T(8,128)(2,1)S(1)} %bitcast.20), custom_call_target="tpu_custom_call" | custom-call | tf_op jit(solution)/shard_map/join_coarse/pallas_call | solution.py:642
  125.9 9.6 %all-to-all-done.1.all_ref = bf16[8,400,128]{2,1,0:T(8,128)(2,1)S(1)} async-done(((bf16[8,400,128]{2,1,0:T(8,128)(2,1)}), bf16[8,400,128]{2,1,0:T(8,128)(2,1)S(1)}, u32[]{:S(2)}, u32[]{:S(2)}) %all-to-all-start.1) | async-done | bytes 819232 | tf_op jit(solution)/shard_map/all_to_all | solution.py:698
  135.5 0.9 unpack_heads.1
  (20 shorter events, 0.1 us)
Async XLA Ops:
  7.2 48.4 %copy-start.10 = (f32[8]{0:T(128)S(1)}, f32[8]{0:T(128)}, u32[]{:S(2)}) copy-start(f32[8]{0:T(128)} %log_ref.7) | copy-start | bytes 100
  7.2 115.6 %all-gather.3.cloned.1.call-start = ((), (), s32[]{:S(2)}) async-start(), calls=%async_computation.2 | async-start | bytes 1179648 | tf_op jit(solution)/shard_map/all_gather | solution.py:726
  30.2 23.8 %collective-permute-start.1 = (bf16[8,208,128]{2,1,0:T(8,128)(2,1)}, bf16[8,208,128]{2,1,0:T(8,128)(2,1)}, u32[]{:S(2)}, u32[]{:S(2)}) collective-permute-start(bf16[8,208,128]{2,1,0:T(8,128)(2,1)} %get-tuple-element.77), channel_id=1, source_target_pairs={{0,6},{1,7},{2,4},{3,5},{4,2},{5,3},{6,0},{7,1},{8,14},{9,15},{10,... | collective-permute-start | bytes 1277960 | tf_op jit(solution)/shard_map/ppermute | solution.py:701
  35.5 20.1 %collective-permute-start = (bf16[8,208,128]{2,1,0:T(8,128)(2,1)}, bf16[8,208,128]{2,1,0:T(8,128)(2,1)}, u32[]{:S(2)}, u32[]{:S(2)}) collective-permute-start(bf16[8,208,128]{2,1,0:T(8,128)(2,1)} %get-tuple-element.78), channel_id=1, source_target_pairs={{0,2},{1,3},{2,0},{3,1},{4,6},{5,7},{6,4},{7,5},{8,10},{9,11},{10,... | collective-permute-start | bytes 1277960 | tf_op jit(solution)/shard_map/ppermute | solution.py:701
  38.1 1.0 copy-start.1
  39.2 0.9 copy-start.8
  40.1 0.7 copy-start.9
  40.7 0.7 copy-start.11
  41.4 1.0 copy-start.12
  42.5 1.0 copy-start.13
  43.5 1.0 copy-start.14
  62.1 4.7 %collective-permute-start.2 = (f32[24,128]{1,0:T(8,128)S(1)}, f32[24,128]{1,0:T(8,128)S(1)}, u32[]{:S(2)}, u32[]{:S(2)}) collective-permute-start(f32[24,128]{1,0:T(8,128)S(1)} %get-tuple-element.47.stat_ref), channel_id=1, source_target_pairs={{0,6},{1,7},{2,4},{3,5},{4,2},{5,3},{6,0},{7,1},{8,14},{9,15},{10,... | collective-permute-start | bytes 36872 | tf_op jit(solution)/shard_map/ppermute | solution.py:701
  68.8 12.6 %collective-permute-start.3 = (bf16[256,256]{1,0:T(8,128)(2,1)S(1)}, bf16[256,256]{1,0:T(8,128)(2,1)S(1)}, u32[]{:S(2)}, u32[]{:S(2)}) collective-permute-start(bf16[256,256]{1,0:T(8,128)(2,1)S(1)} %get-tuple-element.53.own_ref), channel_id=1, source_target_pairs={{0,2},{1,3},{2,0},{3,1},{4,6},{5,7},{6,4},{7,5},{8,10},{9,11},{10,... | collective-permute-start | bytes 393224 | tf_op jit(solution)/shard_map/ppermute | solution.py:701
  78.5 0.7 copy-start.4
  79.2 0.7 copy-start.6
  80.0 0.7 copy-start.15
  80.7 0.7 copy-start.16
  81.4 41.4 %copy-start.2 = (bf16[1,256,1024]{2,1,0:T(8,128)(2,1)S(1)}, bf16[1,256,1024]{2,1,0:T(8,128)(2,1)}, u32[]{:S(2)}) copy-start(bf16[1,256,1024]{2,1,0:T(8,128)(2,1)} %param.12) | copy-start | bytes 1572868
  81.5 0.7 copy-start.3
  82.2 30.1 %collective-permute-start.4 = (bf16[768,256]{1,0:T(8,128)(2,1)}, bf16[768,256]{1,0:T(8,128)(2,1)S(1)}, u32[]{:S(2)}, u32[]{:S(2)}) collective-permute-start(bf16[768,256]{1,0:T(8,128)(2,1)} %copy-done.16), channel_id=1, source_target_pairs={{0,6},{1,7},{2,4},{3,5},{4,2},{5,3},{6,0},{7,1},{8,14},{9,15},{10,... | collective-permute-start | bytes 1179656 | tf_op jit(solution)/shard_map/ppermute | solution.py:701
  83.2 29.1 %collective-permute-start.5 = (bf16[768,256]{1,0:T(8,128)(2,1)}, bf16[768,256]{1,0:T(8,128)(2,1)S(1)}, u32[]{:S(2)}, u32[]{:S(2)}) collective-permute-start(bf16[768,256]{1,0:T(8,128)(2,1)} %copy-done.15), channel_id=1, source_target_pairs={{0,2},{1,3},{2,0},{3,1},{4,6},{5,7},{6,4},{7,5},{8,10},{9,11},{10,... | collective-permute-start | bytes 1179656 | tf_op jit(solution)/shard_map/ppermute | solution.py:701
  85.5 3.7 %collective-permute-start.8 = (f32[8,128]{1,0:T(8,128)S(1)}, f32[8,128]{1,0:T(8,128)S(1)}, u32[]{:S(2)}, u32[]{:S(2)}) collective-permute-start(f32[8,128]{1,0:T(8,128)S(1)} %get-tuple-element.62._), channel_id=1, source_target_pairs={{0,96},{32,64},{64,32},{96,0},{128,224},{160,192},{192,160},{224,1... | collective-permute-start | bytes 12296 | tf_op jit(solution)/shard_map/ppermute | solution.py:704
  88.0 4.3 %collective-permute-start.7 = (f32[8,128]{1,0:T(8,128)S(1)}, f32[8,128]{1,0:T(8,128)S(1)}, u32[]{:S(2)}, u32[]{:S(2)}) collective-permute-start(f32[8,128]{1,0:T(8,128)S(1)} %get-tuple-element.62._), channel_id=1, source_target_pairs={{0,64},{32,96},{64,0},{96,32},{128,192},{160,224},{192,128},{224,1... | collective-permute-start | bytes 12296 | tf_op jit(solution)/shard_map/ppermute | solution.py:704
  88.5 3.7 %collective-permute-start.6 = (f32[8,128]{1,0:T(8,128)S(1)}, f32[8,128]{1,0:T(8,128)S(1)}, u32[]{:S(2)}, u32[]{:S(2)}) collective-permute-start(f32[8,128]{1,0:T(8,128)S(1)} %get-tuple-element.62._), channel_id=1, source_target_pairs={{0,32},{32,0},{64,96},{96,64},{128,160},{160,128},{192,224},{224,1... | collective-permute-start | bytes 12296 | tf_op jit(solution)/shard_map/ppermute | solution.py:704
  92.2 11.2 %collective-permute-start.15 = (f32[8,128]{1,0:T(8,128)S(1)}, f32[8,128]{1,0:T(8,128)S(1)}, u32[]{:S(2)}, u32[]{:S(2)}) collective-permute-start(f32[8,128]{1,0:T(8,128)S(1)} %add_add_fusion.scale_and_all_0_), channel_id=1, source_target_pairs={{0,134},{1,135},{2,132},{3,133},{4,130},{5,131},{6,128},{7,129},{8... | collective-permute-start | bytes 12296 | tf_op jit(solution)/shard_map/ppermute | solution.py:712
  94.3 10.4 %collective-permute-start.14 = (f32[8,128]{1,0:T(8,128)S(1)}, f32[8,128]{1,0:T(8,128)S(1)}, u32[]{:S(2)}, u32[]{:S(2)}) collective-permute-start(f32[8,128]{1,0:T(8,128)S(1)} %add_add_fusion.scale_and_all_0_), channel_id=1, source_target_pairs={{0,6},{1,7},{2,4},{3,5},{4,2},{5,3},{6,0},{7,1},{8,14},{9,15},{10,... | collective-permute-start | bytes 12296 | tf_op jit(solution)/shard_map/ppermute | solution.py:701
  96.3 10.1 %collective-permute-start.13 = (f32[8,128]{1,0:T(8,128)S(1)}, f32[8,128]{1,0:T(8,128)S(1)}, u32[]{:S(2)}, u32[]{:S(2)}) collective-permute-start(f32[8,128]{1,0:T(8,128)S(1)} %add_add_fusion.scale_and_all_0_), channel_id=1, source_target_pairs={{0,132},{1,133},{2,134},{3,135},{4,128},{5,129},{6,130},{7,131},{8... | collective-permute-start | bytes 12296 | tf_op jit(solution)/shard_map/ppermute | solution.py:712
  103.5 6.4 %collective-permute-start.12 = (f32[8,128]{1,0:T(8,128)S(1)}, f32[8,128]{1,0:T(8,128)S(1)}, u32[]{:S(2)}, u32[]{:S(2)}) collective-permute-start(f32[8,128]{1,0:T(8,128)S(1)} %add_add_fusion.scale_and_all_0_), channel_id=1, source_target_pairs={{0,4},{1,5},{2,6},{3,7},{4,0},{5,1},{6,2},{7,3},{8,12},{9,13},{10,... | collective-permute-start | bytes 12296 | tf_op jit(solution)/shard_map/ppermute | solution.py:701
  104.6 5.2 %collective-permute-start.11 = (f32[8,128]{1,0:T(8,128)S(1)}, f32[8,128]{1,0:T(8,128)S(1)}, u32[]{:S(2)}, u32[]{:S(2)}) collective-permute-start(f32[8,128]{1,0:T(8,128)S(1)} %add_add_fusion.scale_and_all_0_), channel_id=1, source_target_pairs={{0,130},{1,131},{2,128},{3,129},{4,134},{5,135},{6,132},{7,133},{8... | collective-permute-start | bytes 12296 | tf_op jit(solution)/shard_map/ppermute | solution.py:712
  106.4 3.4 %collective-permute-start.10 = (f32[8,128]{1,0:T(8,128)S(1)}, f32[8,128]{1,0:T(8,128)S(1)}, u32[]{:S(2)}, u32[]{:S(2)}) collective-permute-start(f32[8,128]{1,0:T(8,128)S(1)} %add_add_fusion.scale_and_all_0_), channel_id=1, source_target_pairs={{0,2},{1,3},{2,0},{3,1},{4,6},{5,7},{6,4},{7,5},{8,10},{9,11},{10,... | collective-permute-start | bytes 12296 | tf_op jit(solution)/shard_map/ppermute | solution.py:701
  109.8 2.5 %collective-permute-start.9 = (f32[8,128]{1,0:T(8,128)S(1)}, f32[8,128]{1,0:T(8,128)S(1)}, u32[]{:S(2)}, u32[]{:S(2)}) collective-permute-start(f32[8,128]{1,0:T(8,128)S(1)} %add_add_fusion.scale_and_all_0_), channel_id=1, source_target_pairs={{0,128},{32,160},{64,192},{96,224},{128,0},{160,32},{192,64},{224,... | collective-permute-start | bytes 12296 | tf_op jit(solution)/shard_map/ppermute | solution.py:704
  112.3 1.0 copy-start.5
  113.3 1.0 copy-start.7
  115.6 19.9 %all-to-all-start.1 = ((bf16[8,400,128]{2,1,0:T(8,128)(2,1)}), bf16[8,400,128]{2,1,0:T(8,128)(2,1)S(1)}, u32[]{:S(2)}, u32[]{:S(2)}) async-start(bf16[8,400,128]{2,1,0:T(8,128)(2,1)} %sum_pairs.1), calls=%async_computation.1 | async-start | bytes 1638400 | tf_op jit(solution)/shard_map/all_to_all | solution.py:698
  122.8 1.2 copy-start
Sparse Core Ops, SparseCore 0:
  82.3 25.0 all-gather.2

commit v9 on v8

--- a/solution.py
+++ b/solution.py
@@ -571,7 +571,8 @@
     )(log_scale, levels[:, None], levels[None, :], queries, keys, values, cots)
 
 
-def small_kernel(own_ref, near_ref, _, sum_ref):
+def small_kernel(own_ref, near_ref, scale_ref, near_scale_ref, sum_ref, pair_ref):
+    pair_ref[...] = scale_ref[...] + near_scale_ref[...]
     some_keys = sum_ref.shape[0] // 2
     summed = own_ref[...].astype(jnp.float32) + near_ref[...].astype(jnp.float32)
     own_half = query_slot(seq_place()[0])
@@ -580,13 +581,16 @@
         sum_ref[spot, :] = summed[index * some_keys : (index + 1) * some_keys].astype(jnp.bfloat16)
 
 
-def run_small(own, near, after):
+def run_small(own, near, scale, near_scale):
     return pl.pallas_call(
         small_kernel,
-        out_shape=jax.ShapeDtypeStruct(own.shape, jnp.bfloat16),
+        out_shape=(
+            jax.ShapeDtypeStruct(own.shape, jnp.bfloat16),
+            jax.ShapeDtypeStruct(scale.shape, jnp.float32),
+        ),
         compiler_params=params(2),
         name="sum_coarse_terms",
-    )(own, near, after)
+    )(own, near, scale, near_scale)
 
 
 def sum_kernel(
@@ -722,15 +726,13 @@
         log_scale, own_rows, kv_rows, qc_rows, key_c, val_c, scale_c, lambda stat: to_plane(stat, 3)
     )
 
-    small_sum = run_small(small, to_plane(small, 1), scale)
+    small_sum, scale = run_small(small, to_plane(small, 1), scale, to_plane(scale, 1))
     of_image = lax.all_gather(small_sum, "seq", axis=0, axis_index_groups=groups)
 
     other_dkv = to_plane(dkv_send, 1)
     other_od = to_plane(od_send, 3)
     scale = scale + to_image(scale, 1) + to_image(scale, 2) + to_image(scale, 3)
-    scales = [scale, to_image(scale, 4)]
-    for flip in (1, 2, 3):
-        scales += [to_plane(scale, flip), to_both(scale, 4, flip)]
+    scales = [scale, to_plane(scale, 3), to_image(scale, 4), to_both(scale, 4, 3)]
     all_parts = run_sum(od, other_od, dkv, other_dkv, own_rows, scales)
     all_back = exchange(all_parts)
     dk_c, dv_c, after = run_join(of_image, dk_own, dv_own, k_coarse[0])

time: 144 us -> 138 us (0.958)
  starting transfers between devices: 36.1 us -> 29.3 us
    ppermute x3 -> x1, starting transfers between devices: 5.06 us -> 1.05 us  [to_both(): return lax.ppermute(array, ('dp', 'seq'), list(enumerate(there)))]
    ppermute x9 -> x8, starting transfers between devices: 20.5 us -> 16.9 us  [to_plane(): return lax.ppermute(array, 'seq', [(i, i ^ 2 * flip) for i in range(seq)])]
    ppermute x9 -> x8, waiting for transfers between devices: 6.07 us -> 8.12 us  [to_plane(): return lax.ppermute(array, 'seq', [(i, i ^ 2 * flip) for i in range(seq)])]
    ppermute x4, waiting for transfers between devices: 5.87 us -> 3.89 us  [to_image(): return lax.ppermute(array, 'dp', [(i, i ^ flip) for i in range(images)])]
    ppermute x3 -> x1, waiting for transfers between devices: 5.94 us -> 7.35 us  [to_both(): return lax.ppermute(array, ('dp', 'seq'), list(enumerate(there)))]
  transfers between devices with their start and end apart: 18 -> 15, of which waited for: 9 -> 9; matrix products, arithmetic and copies ran while one was open for 1% -> 1% of each run, Pallas kernels for 13% -> 13%
where the time goes in v9:
time: 138 us; the launch traced here: 137 us
  Pallas kernels  29.6 us (21%)
  starting transfers between devices  29.3 us (21%)
  waiting for transfers between devices  28.9 us (21%)
  blocking collectives  19.7 us (14%)
  local copies, waits for them, and re-layouts  15.7 us (11%)
  between operations  14.2 us (10%)
    all_to_all x1, blocking collectives, exchange(): lax.all_to_all(parts, 'seq', 0, 0, axis_index_groups=groups, tiled=True)  19.7 us
    ppermute x8, starting transfers between devices, to_plane(): return lax.ppermute(array, 'seq', [(i, i ^ 2 * flip) for i in range(seq)])  16.9 us
    unnamed x34, local copies, waits for them, and re-layouts  13.2 us
    all_to_all x1, waiting for transfers between devices, exchange(): lax.all_to_all(parts, 'seq', 0, 0, axis_index_groups=groups, tiled=True)  9.56 us
    ppermute x8, waiting for transfers between devices, to_plane(): return lax.ppermute(array, 'seq', [(i, i ^ 2 * flip) for i in range(seq)])  8.12 us
    pallas_call x1, Pallas kernels, run_coarse(): pl.pallas_call(coarse_kernel, out_shape=(low, low, wide, wide, jax.ShapeD...  7.79 us
    ppermute x1, waiting for transfers between devices, to_both(): return lax.ppermute(array, ('dp', 'seq'), list(enumerate(there)))  7.35 us
    pallas_call x1, Pallas kernels, run_fine(): pl.pallas_call(fine_back_kernel, out_shape=(half, half, half, half, wide(...  6.98 us
  transfers between devices with their start and end apart: 15, of which 9 were waited for; matrix products, arithmetic and copies ran while one was open for 1% of the time, Pallas kernels for 13%

profile of v9, /device:TPU:1, one launch (start us, length us, event | category | flops | bytes accessed | tf_op | source)
XLA Modules:
  0.0 137.4 jit_solution(6355632291820398406)
XLA Ops:
  7.2 0.0 copy-start.10
  7.2 0.0 all-gather.3.cloned.1.call-start
  7.2 2.3 %pack_heads.1 = bf16[8,400,128]{2,1,0:T(8,128)(2,1)} custom-call(s32[1,96]{1,0:T(1,128)} %ids_ref.1, bf16[96,1024]{1,0:T(8,128)(2,1)} %bitcast.25, bf16[96,1024]{1,0:T(8,128)(2,1)} %bitcast.26, bf16[96,1024]{1,0:T(8,128)(2,1)} %bitcast.27, bf16[96,1024]{1,0:T(8,128)(2,1)} %bitcast.28), custom_call_target="tpu_custom_call" | custom-call | tf_op jit(solution)/shard_map/pack_heads/pallas_call | solution.py:103
  9.5 19.7 %all_to_all.10.own_ref = bf16[8,400,128]{2,1,0:T(8,128)(2,1)S(1)} all-to-all(bf16[8,400,128]{2,1,0:T(8,128)(2,1)} %pack_heads.1), channel_id=1, replica_groups={{0,1,8,9,16,17,24,25},{2,3,10,11,18,19,26,27},{4,5,12,13,20,21,28,29},{..., dimensions={0} | all-to-all | bytes 1638400 | tf_op jit(solution)/shard_map/all_to_all | solution.py:702
  29.2 1.0 fusion
  30.2 5.3 %collective-permute-start.1 = (bf16[8,208,128]{2,1,0:T(8,128)(2,1)}, bf16[8,208,128]{2,1,0:T(8,128)(2,1)S(1)}, u32[]{:S(2)}, u32[]{:S(2)}) collective-permute-start(bf16[8,208,128]{2,1,0:T(8,128)(2,1)} %get-tuple-element.81), channel_id=1, source_target_pairs={{0,6},{1,7},{2,4},{3,5},{4,2},{5,3},{6,0},{7,1},{8,14},{9,15},{10,... | collective-permute-start | bytes 1277960 | tf_op jit(solution)/shard_map/ppermute | solution.py:705
  35.5 1.2 collective-permute-start
  36.7 1.5 %copy.20.row_level_ref = s32[256,1]{1,0:T(8,128)} copy(s32[256,1]{0,1:T(1,128)} %bitcast.21) | data formatting | bytes 2048 | tf_op jit(solution)/shard_map/broadcast_in_dim;squeeze | solution.py:571
  38.1 0.0 copy-start.1
  38.1 1.0 copy-done.1
  39.2 0.0 copy-start.8
  39.2 0.9 copy-done.8
  40.1 0.7 copy-done.9
  40.7 0.7 copy-done.11
  41.4 1.0 copy-done.12
  42.5 1.0 copy-done.13
  43.5 1.0 copy-done.14
  44.6 7.8 %coarse_attention.1 = (bf16[256,1024]{1,0:T(8,128)(2,1)}, bf16[256,1024]{1,0:T(8,128)(2,1)}, f32[256,1024]{1,0:T(8,128)S(1)}, f32[256,1024]{1,0:T(8,128)S(1)}, f...) custom-call(f32[8]{0:T(128)S(1)} %copy-done.9, s32[256,1]{1,0:T(8,128)S(1)} %copy-done.8, ...), custom_call_target="tpu_custom_call" | custom-call | flops 805306368 | bytes 6291456 | tf_op jit(solution)/shard_map/coarse_attention/pallas_call | solution.py:559
  52.3 1.7 %collective-permute-done.1.qc_ref = bf16[8,208,128]{2,1,0:T(8,128)(2,1)S(1)} collective-permute-done((bf16[8,208,128]{2,1,0:T(8,128)(2,1)}, bf16[8,208,128]{2,1,0:T(8,128)(2,1)S(1)}, u32[]{:S(2)}, u32[]{:S(2)}) %collective-permute-start.1) | collective-permute-done | bytes 426016 | tf_op jit(solution)/shard_map/ppermute | solution.py:705
  54.0 1.5 %collective-permute-done.kv_ref = bf16[8,208,128]{2,1,0:T(8,128)(2,1)} collective-permute-done((bf16[8,208,128]{2,1,0:T(8,128)(2,1)}, bf16[8,208,128]{2,1,0:T(8,128)(2,1)}, u32[]{:S(2)}, u32[]{:S(2)}) %collective-permute-start) | collective-permute-done | bytes 426016 | tf_op jit(solution)/shard_map/ppermute | solution.py:705
  55.6 0.0 copy-done.10
  55.6 6.4 %fine_forward.1 = (bf16[1536,1792]{1,0:T(8,128)(2,1)S(1)}, bf16[1792,128]{1,0:T(8,128)(2,1)S(1)}, bf16[1792,128]{1,0:T(8,128)(2,1)S(1)}, bf16[1536,128]{1,0:T(8,...) custom-call(f32[8]{0:T(128)S(1)} %copy-done.10, ...), custom_call_target="tpu_custom_call" | custom-call | flops 1409286144 | bytes 11010048 | tf_op jit(solution)/shard_map/fine_forward/pallas_call | solution.py:412
  62.0 2.8 %collective-permute-start.2 = (f32[24,128]{1,0:T(8,128)S(1)}, f32[24,128]{1,0:T(8,128)S(1)}, u32[]{:S(2)}, u32[]{:S(2)}) collective-permute-start(f32[24,128]{1,0:T(8,128)S(1)} %get-tuple-element.49.stat_ref), channel_id=1, source_target_pairs={{0,6},{1,7},{2,4},{3,5},{4,2},{5,3},{6,0},{7,1},{8,14},{9,15},{10,... | collective-permute-start | bytes 36872 | tf_op jit(solution)/shard_map/ppermute | solution.py:705
  64.8 2.0 %collective-permute-done.2.other_stat_ref = f32[24,128]{1,0:T(8,128)S(1)} collective-permute-done((f32[24,128]{1,0:T(8,128)S(1)}, f32[24,128]{1,0:T(8,128)S(1)}, u32[]{:S(2)}, u32[]{:S(2)}) %collective-permute-start.2) | collective-permute-done | bytes 12320 | tf_op jit(solution)/shard_map/ppermute | solution.py:705
  66.7 1.9 %coarse_key_grads.1 = (bf16[256,256]{1,0:T(8,128)(2,1)S(1)}, f32[1536,128]{1,0:T(8,128)S(1)}, f32[1536,128]{1,0:T(8,128)S(1)}, f32[1536,128]{1,0:T(8,128)S(1)}, ...) custom-call(f32[8]{0:T(128)S(1)} %copy-done.10, f32[24,128]{1,0:T(8,128)S(1)} %get-tuple-element.49.stat_ref, ...), custom_call_target="tpu_custom_call" | custom-call | flops 402653184 | bytes 1572864 | tf_op jit(solution)/shard_map/coarse_key_grads/pallas_call | solution.py:440
  68.7 2.2 %collective-permute-start.3 = (bf16[256,256]{1,0:T(8,128)(2,1)S(1)}, bf16[256,256]{1,0:T(8,128)(2,1)S(1)}, u32[]{:S(2)}, u32[]{:S(2)}) collective-permute-start(bf16[256,256]{1,0:T(8,128)(2,1)S(1)} %get-tuple-element.55.own_ref), channel_id=1, source_target_pairs={{0,2},{1,3},{2,0},{3,1},{4,6},{5,7},{6,4},{7,5},{8,10},{9,11},{10,... | collective-permute-start | bytes 393224 | tf_op jit(solution)/shard_map/ppermute | solution.py:705
  70.9 7.0 %fine_backward.1 = (bf16[768,256]{1,0:T(8,128)(2,1)S(1)}, bf16[768,256]{1,0:T(8,128)(2,1)S(1)}, bf16[768,256]{1,0:T(8,128)(2,1)S(1)}, bf16[768,256]{1,0:T(8,128)(2,1)S(1)}, f32[8,128]{1,0:T(8,128)S(1)}) custom-call(f32[8]{0:T(128)S(1)} %copy-done.10, s32[1]{0:T(128)} %get-tuple-element.56.shared_ref, bf16[8,400,128]{2,1,0:T(8,128)(2,1)S(1)} %all_to_all.10.own_ref, ...), custom_call_target="tpu_custom_call" | custom-call | flops 2415919104 | bytes 9437184 | tf_op jit(solution)/shard_map/fine_backward/pallas_call | solution.py:461
  77.9 0.0 copy-start.3
  77.9 0.7 copy-done.3
  78.6 0.7 copy-done.5
  79.4 0.7 copy-done.15
  80.1 0.7 copy-done.16
  80.9 0.4 collective-permute-start.4
  81.3 2.9 %collective-permute-done.4.near_scale_ref = f32[8,128]{1,0:T(8,128)S(1)} collective-permute-done((f32[8,128]{1,0:T(8,128)S(1)}, f32[8,128]{1,0:T(8,128)S(1)}, u32[]{:S(2)}, u32[]{:S(2)}) %collective-permute-start.4) | collective-permute-done | bytes 4128 | tf_op jit(solution)/shard_map/ppermute | solution.py:705
  84.2 0.0 collective-permute-done.3.near_ref
  84.3 0.0 copy-start.7
  84.3 0.6 copy-done.7
  84.9 0.0 all-gather.3.cloned.1.call-update
  84.9 0.8 collective-permute-start.5
  85.8 2.4 %collective-permute-start.6 = (bf16[768,256]{1,0:T(8,128)(2,1)}, bf16[768,256]{1,0:T(8,128)(2,1)S(1)}, u32[]{:S(2)}, u32[]{:S(2)}) collective-permute-start(bf16[768,256]{1,0:T(8,128)(2,1)} %copy-done.15), channel_id=1, source_target_pairs={{0,2},{1,3},{2,0},{3,1},{4,6},{5,7},{6,4},{7,5},{8,10},{9,11},{10,... | collective-permute-start | bytes 1179656 | tf_op jit(solution)/shard_map/ppermute | solution.py:705
  88.1 2.5 %collective-permute-start.9 = (f32[8,128]{1,0:T(8,128)S(1)}, f32[8,128]{1,0:T(8,128)S(1)}, u32[]{:S(2)}, u32[]{:S(2)}) collective-permute-start(f32[8,128]{1,0:T(8,128)S(1)} %get-tuple-element.74), channel_id=1, source_target_pairs={{0,96},{32,64},{64,32},{96,0},{128,224},{160,192},{192,160},{224,1... | collective-permute-start | bytes 12296 | tf_op jit(solution)/shard_map/ppermute | solution.py:708
  90.6 0.5 collective-permute-start.8
  91.1 0.3 collective-permute-start.7
  91.4 0.4 collective-permute-done.9
  91.8 3.1 %collective-permute-done.8 = f32[8,128]{1,0:T(8,128)S(1)} collective-permute-done((f32[8,128]{1,0:T(8,128)S(1)}, f32[8,128]{1,0:T(8,128)S(1)}, u32[]{:S(2)}, u32[]{:S(2)}) %collective-permute-start.8) | collective-permute-done | bytes 4128 | tf_op jit(solution)/shard_map/ppermute | solution.py:708
  94.9 0.0 collective-permute-done.7
  94.9 1.1 collective-permute-start.12
  95.9 1.1 collective-permute-start.11
  97.1 1.8 %collective-permute-start.10 = (f32[8,128]{1,0:T(8,128)S(1)}, f32[8,128]{1,0:T(8,128)S(1)}, u32[]{:S(2)}, u32[]{:S(2)}) collective-permute-start(f32[8,128]{1,0:T(8,128)S(1)} %add_add_fusion.scale_and_all_0_), channel_id=1, source_target_pairs={{0,6},{1,7},{2,4},{3,5},{4,2},{5,3},{6,0},{7,1},{8,14},{9,15},{10,... | collective-permute-start | bytes 12296 | tf_op jit(solution)/shard_map/ppermute | solution.py:705
  98.8 7.4 %collective-permute-done.12.scale_and_all_3_ = f32[8,128]{1,0:T(8,128)S(1)} collective-permute-done((f32[8,128]{1,0:T(8,128)S(1)}, f32[8,128]{1,0:T(8,128)S(1)}, u32[]{:S(2)}, u32[]{:S(2)}) %collective-permute-start.12) | collective-permute-done | bytes 4128 | tf_op jit(solution)/shard_map/ppermute | solution.py:716
  106.2 0.4 collective-permute-done.11.scale_and_all_2_
  106.6 0.0 collective-permute-done.10.scale_and_all_1_
  106.6 0.0 collective-permute-done.5.other_od_ref
  106.6 0.0 collective-permute-done.6.other_dkv_ref
  106.6 0.0 copy-start.4
  106.6 1.0 copy-done.4
  107.6 1.0 copy-done.6
  108.6 1.3 sum_pairs.1
  109.9 7.0 %all-to-all-start.1 = ((bf16[8,400,128]{2,1,0:T(8,128)(2,1)}), bf16[8,400,128]{2,1,0:T(8,128)(2,1)S(1)}, u32[]{:S(2)}, u32[]{:S(2)}) async-start(bf16[8,400,128]{2,1,0:T(8,128)(2,1)} %sum_pairs.1), calls=%async_computation.1 | async-start | bytes 1638400 | tf_op jit(solution)/shard_map/all_to_all | solution.py:702
  116.9 0.0 copy-done.2
  116.9 1.2 copy-done
  118.1 1.9 %join_coarse.1 = (bf16[256,1024]{1,0:T(8,128)(2,1)}, bf16[256,1024]{1,0:T(8,128)(2,1)}, f32[8,128]{1,0:T(8,128)S(1)}) custom-call(bf16[8,256,256]{2,1,0:T(8,128)(2,1)S(1)} %bitcast.18, f32[256,1024]{1,0:T(8,128)S(1)} %get-tuple-element.66.dk_own_ref, f32[256,1024]{1,0:T(8,128)S(1)} %get-tuple-element.67.dv_own_ref, bf16[256,1024]{1,0:T(8,128)(2,1)S(1)} %bitcast.20), custom_call_target="tpu_custom_call" | custom-call | tf_op jit(solution)/shard_map/join_coarse/pallas_call | solution.py:646
  120.0 9.6 %all-to-all-done.1.all_ref = bf16[8,400,128]{2,1,0:T(8,128)(2,1)S(1)} async-done(((bf16[8,400,128]{2,1,0:T(8,128)(2,1)}), bf16[8,400,128]{2,1,0:T(8,128)(2,1)S(1)}, u32[]{:S(2)}, u32[]{:S(2)}) %all-to-all-start.1) | async-done | bytes 819232 | tf_op jit(solution)/shard_map/all_to_all | solution.py:702
  129.6 0.9 unpack_heads.1
  (14 shorter events, 0.1 us)
Async XLA Ops:
  7.2 48.4 %copy-start.10 = (f32[8]{0:T(128)S(1)}, f32[8]{0:T(128)}, u32[]{:S(2)}) copy-start(f32[8]{0:T(128)} %log_ref.7) | copy-start | bytes 100
  7.2 109.7 %all-gather.3.cloned.1.call-start = ((), (), s32[]{:S(2)}) async-start(), calls=%async_computation.2 | async-start | bytes 1179648 | tf_op jit(solution)/shard_map/all_gather | solution.py:730
  30.2 23.8 %collective-permute-start.1 = (bf16[8,208,128]{2,1,0:T(8,128)(2,1)}, bf16[8,208,128]{2,1,0:T(8,128)(2,1)S(1)}, u32[]{:S(2)}, u32[]{:S(2)}) collective-permute-start(bf16[8,208,128]{2,1,0:T(8,128)(2,1)} %get-tuple-element.81), channel_id=1, source_target_pairs={{0,6},{1,7},{2,4},{3,5},{4,2},{5,3},{6,0},{7,1},{8,14},{9,15},{10,... | collective-permute-start | bytes 1277960 | tf_op jit(solution)/shard_map/ppermute | solution.py:705
  35.5 20.1 %collective-permute-start = (bf16[8,208,128]{2,1,0:T(8,128)(2,1)}, bf16[8,208,128]{2,1,0:T(8,128)(2,1)}, u32[]{:S(2)}, u32[]{:S(2)}) collective-permute-start(bf16[8,208,128]{2,1,0:T(8,128)(2,1)} %get-tuple-element.82), channel_id=1, source_target_pairs={{0,2},{1,3},{2,0},{3,1},{4,6},{5,7},{6,4},{7,5},{8,10},{9,11},{10,... | collective-permute-start | bytes 1277960 | tf_op jit(solution)/shard_map/ppermute | solution.py:705
  38.1 1.0 copy-start.1
  39.2 0.9 copy-start.8
  40.1 0.7 copy-start.9
  40.7 0.7 copy-start.11
  41.4 1.0 copy-start.12
  42.5 1.0 copy-start.13
  43.5 1.0 copy-start.14
  62.0 4.7 %collective-permute-start.2 = (f32[24,128]{1,0:T(8,128)S(1)}, f32[24,128]{1,0:T(8,128)S(1)}, u32[]{:S(2)}, u32[]{:S(2)}) collective-permute-start(f32[24,128]{1,0:T(8,128)S(1)} %get-tuple-element.49.stat_ref), channel_id=1, source_target_pairs={{0,6},{1,7},{2,4},{3,5},{4,2},{5,3},{6,0},{7,1},{8,14},{9,15},{10,... | collective-permute-start | bytes 36872 | tf_op jit(solution)/shard_map/ppermute | solution.py:705
  68.7 15.5 %collective-permute-start.3 = (bf16[256,256]{1,0:T(8,128)(2,1)S(1)}, bf16[256,256]{1,0:T(8,128)(2,1)S(1)}, u32[]{:S(2)}, u32[]{:S(2)}) collective-permute-start(bf16[256,256]{1,0:T(8,128)(2,1)S(1)} %get-tuple-element.55.own_ref), channel_id=1, source_target_pairs={{0,2},{1,3},{2,0},{3,1},{4,6},{5,7},{6,4},{7,5},{8,10},{9,11},{10,... | collective-permute-start | bytes 393224 | tf_op jit(solution)/shard_map/ppermute | solution.py:705
  77.9 0.7 copy-start.3
  78.6 0.7 copy-start.5
  79.4 0.7 copy-start.15
  80.1 0.7 copy-start.16
  80.9 36.0 %copy-start.2 = (bf16[1,256,1024]{2,1,0:T(8,128)(2,1)S(1)}, bf16[1,256,1024]{2,1,0:T(8,128)(2,1)}, u32[]{:S(2)}) copy-start(bf16[1,256,1024]{2,1,0:T(8,128)(2,1)} %param.12) | copy-start | bytes 1572868
  80.9 3.4 %collective-permute-start.4 = (f32[8,128]{1,0:T(8,128)S(1)}, f32[8,128]{1,0:T(8,128)S(1)}, u32[]{:S(2)}, u32[]{:S(2)}) collective-permute-start(f32[8,128]{1,0:T(8,128)S(1)} %get-tuple-element.64.scale_ref), channel_id=1, source_target_pairs={{0,2},{1,3},{2,0},{3,1},{4,6},{5,7},{6,4},{7,5},{8,10},{9,11},{10,... | collective-permute-start | bytes 12296 | tf_op jit(solution)/shard_map/ppermute | solution.py:705
  84.3 0.7 copy-start.7
  84.9 21.7 %collective-permute-start.5 = (bf16[768,256]{1,0:T(8,128)(2,1)}, bf16[768,256]{1,0:T(8,128)(2,1)S(1)}, u32[]{:S(2)}, u32[]{:S(2)}) collective-permute-start(bf16[768,256]{1,0:T(8,128)(2,1)} %copy-done.16), channel_id=1, source_target_pairs={{0,6},{1,7},{2,4},{3,5},{4,2},{5,3},{6,0},{7,1},{8,14},{9,15},{10,... | collective-permute-start | bytes 1179656 | tf_op jit(solution)/shard_map/ppermute | solution.py:705
  85.8 20.8 %collective-permute-start.6 = (bf16[768,256]{1,0:T(8,128)(2,1)}, bf16[768,256]{1,0:T(8,128)(2,1)S(1)}, u32[]{:S(2)}, u32[]{:S(2)}) collective-permute-start(bf16[768,256]{1,0:T(8,128)(2,1)} %copy-done.15), channel_id=1, source_target_pairs={{0,2},{1,3},{2,0},{3,1},{4,6},{5,7},{6,4},{7,5},{8,10},{9,11},{10,... | collective-permute-start | bytes 1179656 | tf_op jit(solution)/shard_map/ppermute | solution.py:705
  88.1 3.7 %collective-permute-start.9 = (f32[8,128]{1,0:T(8,128)S(1)}, f32[8,128]{1,0:T(8,128)S(1)}, u32[]{:S(2)}, u32[]{:S(2)}) collective-permute-start(f32[8,128]{1,0:T(8,128)S(1)} %get-tuple-element.74), channel_id=1, source_target_pairs={{0,96},{32,64},{64,32},{96,0},{128,224},{160,192},{192,160},{224,1... | collective-permute-start | bytes 12296 | tf_op jit(solution)/shard_map/ppermute | solution.py:708
  90.6 4.3 %collective-permute-start.8 = (f32[8,128]{1,0:T(8,128)S(1)}, f32[8,128]{1,0:T(8,128)S(1)}, u32[]{:S(2)}, u32[]{:S(2)}) collective-permute-start(f32[8,128]{1,0:T(8,128)S(1)} %get-tuple-element.74), channel_id=1, source_target_pairs={{0,64},{32,96},{64,0},{96,32},{128,192},{160,224},{192,128},{224,1... | collective-permute-start | bytes 12296 | tf_op jit(solution)/shard_map/ppermute | solution.py:708
  91.1 3.7 %collective-permute-start.7 = (f32[8,128]{1,0:T(8,128)S(1)}, f32[8,128]{1,0:T(8,128)S(1)}, u32[]{:S(2)}, u32[]{:S(2)}) collective-permute-start(f32[8,128]{1,0:T(8,128)S(1)} %get-tuple-element.74), channel_id=1, source_target_pairs={{0,32},{32,0},{64,96},{96,64},{128,160},{160,128},{192,224},{224,1... | collective-permute-start | bytes 12296 | tf_op jit(solution)/shard_map/ppermute | solution.py:708
  94.9 11.3 %collective-permute-start.12 = (f32[8,128]{1,0:T(8,128)S(1)}, f32[8,128]{1,0:T(8,128)S(1)}, u32[]{:S(2)}, u32[]{:S(2)}) collective-permute-start(f32[8,128]{1,0:T(8,128)S(1)} %add_add_fusion.scale_and_all_0_), channel_id=1, source_target_pairs={{0,134},{1,135},{2,132},{3,133},{4,130},{5,131},{6,128},{7,129},{8... | collective-permute-start | bytes 12296 | tf_op jit(solution)/shard_map/ppermute | solution.py:716
  95.9 10.7 %collective-permute-start.11 = (f32[8,128]{1,0:T(8,128)S(1)}, f32[8,128]{1,0:T(8,128)S(1)}, u32[]{:S(2)}, u32[]{:S(2)}) collective-permute-start(f32[8,128]{1,0:T(8,128)S(1)} %add_add_fusion.scale_and_all_0_), channel_id=1, source_target_pairs={{0,128},{32,160},{64,192},{96,224},{128,0},{160,32},{192,64},{224,... | collective-permute-start | bytes 12296 | tf_op jit(solution)/shard_map/ppermute | solution.py:708
  97.1 9.6 %collective-permute-start.10 = (f32[8,128]{1,0:T(8,128)S(1)}, f32[8,128]{1,0:T(8,128)S(1)}, u32[]{:S(2)}, u32[]{:S(2)}) collective-permute-start(f32[8,128]{1,0:T(8,128)S(1)} %add_add_fusion.scale_and_all_0_), channel_id=1, source_target_pairs={{0,6},{1,7},{2,4},{3,5},{4,2},{5,3},{6,0},{7,1},{8,14},{9,15},{10,... | collective-permute-start | bytes 12296 | tf_op jit(solution)/shard_map/ppermute | solution.py:705
  106.6 1.0 copy-start.4
  107.6 1.0 copy-start.6
  109.9 19.6 %all-to-all-start.1 = ((bf16[8,400,128]{2,1,0:T(8,128)(2,1)}), bf16[8,400,128]{2,1,0:T(8,128)(2,1)S(1)}, u32[]{:S(2)}, u32[]{:S(2)}) async-start(bf16[8,400,128]{2,1,0:T(8,128)(2,1)} %sum_pairs.1), calls=%async_computation.1 | async-start | bytes 1638400 | tf_op jit(solution)/shard_map/all_to_all | solution.py:702
  116.9 1.2 copy-start
Sparse Core Ops, SparseCore 0:
  85.1 26.0 all-gather.2

commit v10 on v8

--- a/solution.py
+++ b/solution.py
@@ -590,12 +590,15 @@
 
 
 def sum_kernel(
-    od_ref, other_od_ref, dkv_ref, other_dkv_ref, own_ref, *scale_and_all
+    od_ref, other_od_ref, dkv_ref, other_dkv_ref, own_ref, *scale_refs
 ):
-    *scale_refs, all_ref = scale_and_all
+    *scale_refs, all_ref, table_ref = scale_refs
     members, tall, width = all_ref.shape
-    rows = (tall - note_rows) // 4
+    rows = tall // 4
     fine = members * rows
+    _, head = seq_place()
+    for flip, ref in enumerate(scale_refs):
+        table_ref[pl.ds(lax.bitwise_xor(head, flip), 1), :] = ref[0:1, :]
 
     def put(place, value):
         all_ref[:, place * rows : (place + 1) * rows] = value.astype(jnp.bfloat16).reshape(
@@ -608,18 +611,16 @@
     summed = dkv_ref[...].astype(jnp.float32) + other_dkv_ref[...].astype(jnp.float32)
     put(2, project(own_ref[:, 0:rows].reshape(fine, width), summed[:, :width]))
     put(3, summed[:, width:])
-    scale = scale_refs[0][0:1, 0:1]
-    for ref in scale_refs[1:]:
-        scale = scale + ref[0:1, 0:1]
-    note = in_pieces(scale, width)
-    for member in range(members):
-        all_ref[member, 4 * rows :] = note
 
 
 def run_sum(od, other_od, dkv, other_dkv, own_rows, scales):
+    members, tall, width = own_rows.shape
     return pl.pallas_call(
         sum_kernel,
-        out_shape=jax.ShapeDtypeStruct(own_rows.shape, jnp.bfloat16),
+        out_shape=(
+            jax.ShapeDtypeStruct((members, tall - note_rows, width), jnp.bfloat16),
+            jax.ShapeDtypeStruct((members, width), jnp.float32),
+        ),
         compiler_params=params(6),
         name="sum_pairs",
     )(od, other_od, dkv, other_dkv, own_rows, *scales)
@@ -647,29 +648,32 @@
     )(terms, dk_own, dv_own, keys)
 
 
-def unpack_kernel(factor, all_ref, _, out_ref, dq_ref, dk_ref, dv_ref, scale_ref):
+def unpack_kernel(factor, all_ref, _, *refs):
+    *table_refs, out_ref, dq_ref, dk_ref, dv_ref, scale_ref = refs
     heads, tall, width = all_ref.shape
-    rows = (tall - note_rows) // 4
+    rows = tall // 4
+    table = table_refs[0][...]
+    for ref in table_refs[1:]:
+        table = table + ref[...]
     for head in range(heads):
         lanes = slice(head * width, (head + 1) * width)
         for place, ref in enumerate((out_ref, dq_ref, dk_ref, dv_ref)):
             ref[:, lanes] = all_ref[head, place * rows : (place + 1) * rows]
-        note = all_ref[head, 4 * rows :].astype(jnp.float32)
-        scale_ref[head] = jnp.sum(note[:, 0:1]) * factor
-
-
-def run_unpack(factor, all_back, after):
+        scale_ref[head] = jnp.sum(table[head : head + 1, 0:1]) * factor
+
+
+def run_unpack(factor, all_back, after, tables):
     heads, tall, width = all_back.shape
-    flat = jax.ShapeDtypeStruct(((tall - note_rows) // 4, heads * width), jnp.bfloat16)
+    flat = jax.ShapeDtypeStruct((tall // 4, heads * width), jnp.bfloat16)
     vmem = pl.BlockSpec(memory_space=pltpu.VMEM)
     return pl.pallas_call(
         partial(unpack_kernel, factor),
         out_shape=(flat,) * 4 + (jax.ShapeDtypeStruct((heads,), jnp.float32),),
-        in_specs=[vmem, vmem],
+        in_specs=[vmem] * (2 + len(tables)),
         out_specs=(vmem,) * 4 + (pl.BlockSpec(memory_space=pltpu.SMEM),),
         compiler_params=params(3),
         name="unpack_heads",
-    )(all_back, after)
+    )(all_back, after, *tables)
 
 
 def body(
@@ -700,6 +704,10 @@
     def to_plane(array, flip):
         return lax.ppermute(array, "seq", [(i, i ^ (2 * flip)) for i in range(seq)])
 
+    def to_head(array, flip):
+        other = 8 * (flip // 2) + flip % 2
+        return lax.ppermute(array, "seq", [(i, i ^ other) for i in range(seq)])
+
     def to_image(array, flip):
         return lax.ppermute(array, "dp", [(i, i ^ flip) for i in range(images)])
 
@@ -728,14 +736,15 @@
     other_dkv = to_plane(dkv_send, 1)
     other_od = to_plane(od_send, 3)
     scale = scale + to_image(scale, 1) + to_image(scale, 2) + to_image(scale, 3)
-    scales = [scale, to_image(scale, 4)]
+    scales = [scale] + [to_head(scale, flip) for flip in range(1, heads)]
+    all_parts, table = run_sum(od, other_od, dkv, other_dkv, own_rows, scales)
+    tables = [table, to_image(table, 4)]
     for flip in (1, 2, 3):
-        scales += [to_plane(scale, flip), to_both(scale, 4, flip)]
-    all_parts = run_sum(od, other_od, dkv, other_dkv, own_rows, scales)
+        tables += [to_plane(table, flip), to_both(table, 4, flip)]
     all_back = exchange(all_parts)
     dk_c, dv_c, after = run_join(of_image, dk_own, dv_own, k_coarse[0])
     factor = 1.0 / math.sqrt(images * (coarse + seq * rows))
-    fine_out, fine_dq, fine_dk, fine_dv, grad_scale = run_unpack(factor, all_back, after)
+    fine_out, fine_dq, fine_dk, fine_dv, grad_scale = run_unpack(factor, all_back, after, tables)
     return (
         out_c[None],
         dq_c[None],

time: 144 us -> 138 us (0.958)
  waiting for transfers between devices: 27.5 us -> 11 us
  starting transfers between devices: 36.1 us -> 44 us
    ppermute x0 -> x7, starting transfers between devices: none -> 11.4 us  [to_head(): return lax.ppermute(array, 'seq', [(i, i ^ other) for i in range(seq)])]
    all_to_all x1, waiting for transfers between devices: 9.56 us -> 0.01 us  [exchange(): lax.all_to_all(parts, 'seq', 0, 0, axis_index_groups=groups, tiled=True)]
    ppermute x3, waiting for transfers between devices: 5.94 us -> 0.01 us  [to_both(): return lax.ppermute(array, ('dp', 'seq'), list(enumerate(there)))]
    all_to_all x1, starting transfers between devices: 7.19 us -> 3.79 us  [exchange(): lax.all_to_all(parts, 'seq', 0, 0, axis_index_groups=groups, tiled=True)]
    ppermute x4, waiting for transfers between devices: 5.87 us -> 2.8 us  [to_image(): return lax.ppermute(array, 'dp', [(i, i ^ flip) for i in range(images)])]
    ppermute x0 -> x7, waiting for transfers between devices: none -> 3.06 us  [to_head(): return lax.ppermute(array, 'seq', [(i, i ^ other) for i in range(seq)])]
    ppermute x9, starting transfers between devices: 20.5 us -> 18.1 us  [to_plane(): return lax.ppermute(array, 'seq', [(i, i ^ 2 * flip) for i in range(seq)])]
    ppermute x4, starting transfers between devices: 3.26 us -> 5.26 us  [to_image(): return lax.ppermute(array, 'dp', [(i, i ^ flip) for i in range(images)])]
  transfers between devices with their start and end apart: 18 -> 25, of which waited for: 9 -> 9; matrix products, arithmetic and copies ran while one was open for 1% -> 1% of each run, Pallas kernels for 13% -> 14%
where the time goes in v10:
time: 138 us; the launch traced here: 136 us
  starting transfers between devices  44 us (32%)
  Pallas kernels  31 us (22%)
  blocking collectives  19.7 us (14%)
  local copies, waits for them, and re-layouts  16.6 us (12%)
  between operations  14.2 us (10%)
  waiting for transfers between devices  11 us (8%)
    all_to_all x1, blocking collectives, exchange(): lax.all_to_all(parts, 'seq', 0, 0, axis_index_groups=groups, tiled=True)  19.7 us
    ppermute x9, starting transfers between devices, to_plane(): return lax.ppermute(array, 'seq', [(i, i ^ 2 * flip) for i in range(seq)])  18.1 us
    unnamed x36, local copies, waits for them, and re-layouts  14.1 us
    ppermute x7, starting transfers between devices, to_head(): return lax.ppermute(array, 'seq', [(i, i ^ other) for i in range(seq)])  11.4 us
    pallas_call x1, Pallas kernels, run_fine(): pl.pallas_call(fine_back_kernel, out_shape=(half, half, half, half, wide(...  8.46 us
    pallas_call x1, Pallas kernels, run_coarse(): pl.pallas_call(coarse_kernel, out_shape=(low, low, wide, wide, jax.ShapeD...  7.79 us
    pallas_call x1, Pallas kernels, run_fine(): pl.pallas_call(forward_kernel, out_shape=(low(queries, total), low(total,...  7.23 us
    ppermute x3, starting transfers between devices, to_both(): return lax.ppermute(array, ('dp', 'seq'), list(enumerate(there)))  5.4 us
  transfers between devices with their start and end apart: 25, of which 9 were waited for; matrix products, arithmetic and copies ran while one was open for 1% of the time, Pallas kernels for 14%

profile of v10, /device:TPU:1, one launch (start us, length us, event | category | flops | bytes accessed | tf_op | source)
XLA Modules:
  0.0 136.4 jit_solution(8416066201656209691)
XLA Ops:
  7.2 0.0 copy-start.11
  7.2 0.0 all-gather.3.cloned.1.call-start
  7.2 2.3 %pack_heads.1 = bf16[8,400,128]{2,1,0:T(8,128)(2,1)} custom-call(s32[1,96]{1,0:T(1,128)} %ids_ref.1, bf16[96,1024]{1,0:T(8,128)(2,1)} %bitcast.25, bf16[96,1024]{1,0:T(8,128)(2,1)} %bitcast.26, bf16[96,1024]{1,0:T(8,128)(2,1)} %bitcast.27, bf16[96,1024]{1,0:T(8,128)(2,1)} %bitcast.28), custom_call_target="tpu_custom_call" | custom-call | tf_op jit(solution)/shard_map/pack_heads/pallas_call | solution.py:103
  9.5 19.7 %all_to_all.10.own_ref = bf16[8,400,128]{2,1,0:T(8,128)(2,1)S(1)} all-to-all(bf16[8,400,128]{2,1,0:T(8,128)(2,1)} %pack_heads.1), channel_id=1, replica_groups={{0,1,8,9,16,17,24,25},{2,3,10,11,18,19,26,27},{4,5,12,13,20,21,28,29},{..., dimensions={0} | all-to-all | bytes 1638400 | tf_op jit(solution)/shard_map/all_to_all | solution.py:702
  29.2 1.0 fusion
  30.2 5.3 %collective-permute-start.1 = (bf16[8,208,128]{2,1,0:T(8,128)(2,1)}, bf16[8,208,128]{2,1,0:T(8,128)(2,1)}, u32[]{:S(2)}, u32[]{:S(2)}) collective-permute-start(bf16[8,208,128]{2,1,0:T(8,128)(2,1)} %get-tuple-element.81), channel_id=1, source_target_pairs={{0,6},{1,7},{2,4},{3,5},{4,2},{5,3},{6,0},{7,1},{8,14},{9,15},{10,... | collective-permute-start | bytes 1277960 | tf_op jit(solution)/shard_map/ppermute | solution.py:705
  35.5 1.2 collective-permute-start
  36.7 1.5 %copy.20.row_level_ref = s32[256,1]{1,0:T(8,128)} copy(s32[256,1]{0,1:T(1,128)} %bitcast.21) | data formatting | bytes 2048 | tf_op jit(solution)/shard_map/broadcast_in_dim;squeeze | solution.py:571
  38.1 1.0 copy-done.2
  39.2 0.9 copy-done.9
  40.1 0.7 copy-done.10
  40.7 0.7 copy-done.12
  41.4 1.0 copy-done.13
  42.5 1.0 copy-done.14
  43.5 1.0 copy-done.15
  44.6 7.8 %coarse_attention.1 = (bf16[256,1024]{1,0:T(8,128)(2,1)}, bf16[256,1024]{1,0:T(8,128)(2,1)}, f32[256,1024]{1,0:T(8,128)S(1)}, f32[256,1024]{1,0:T(8,128)S(1)}, f...) custom-call(f32[8]{0:T(128)S(1)} %copy-done.10, s32[256,1]{1,0:T(8,128)S(1)} %copy-done.9, ...), custom_call_target="tpu_custom_call" | custom-call | flops 805306368 | bytes 6291456 | tf_op jit(solution)/shard_map/coarse_attention/pallas_call | solution.py:559
  52.3 1.7 %collective-permute-done.1.qc_ref = bf16[8,208,128]{2,1,0:T(8,128)(2,1)} collective-permute-done((bf16[8,208,128]{2,1,0:T(8,128)(2,1)}, bf16[8,208,128]{2,1,0:T(8,128)(2,1)}, u32[]{:S(2)}, u32[]{:S(2)}) %collective-permute-start.1) | collective-permute-done | bytes 426016 | tf_op jit(solution)/shard_map/ppermute | solution.py:705
  54.0 1.5 %collective-permute-done.kv_ref = bf16[8,208,128]{2,1,0:T(8,128)(2,1)} collective-permute-done((bf16[8,208,128]{2,1,0:T(8,128)(2,1)}, bf16[8,208,128]{2,1,0:T(8,128)(2,1)}, u32[]{:S(2)}, u32[]{:S(2)}) %collective-permute-start) | collective-permute-done | bytes 426016 | tf_op jit(solution)/shard_map/ppermute | solution.py:705
  55.6 7.2 %fine_forward.1 = (bf16[1536,1792]{1,0:T(8,128)(2,1)S(1)}, bf16[1792,128]{1,0:T(8,128)(2,1)S(1)}, bf16[1792,128]{1,0:T(8,128)(2,1)S(1)}, bf16[1536,128]{1,0:T(8,...) custom-call(f32[8]{0:T(128)S(1)} %copy-done.11, ...), custom_call_target="tpu_custom_call" | custom-call | flops 1409286144 | bytes 11010048 | tf_op jit(solution)/shard_map/fine_forward/pallas_call | solution.py:412
  62.8 2.9 %collective-permute-start.2 = (f32[24,128]{1,0:T(8,128)S(1)}, f32[24,128]{1,0:T(8,128)S(1)}, u32[]{:S(2)}, u32[]{:S(2)}) collective-permute-start(f32[24,128]{1,0:T(8,128)S(1)} %get-tuple-element.49.stat_ref), channel_id=1, source_target_pairs={{0,6},{1,7},{2,4},{3,5},{4,2},{5,3},{6,0},{7,1},{8,14},{9,15},{10,... | collective-permute-start | bytes 36872 | tf_op jit(solution)/shard_map/ppermute | solution.py:705
  65.7 1.9 %collective-permute-done.2.other_stat_ref = f32[24,128]{1,0:T(8,128)S(1)} collective-permute-done((f32[24,128]{1,0:T(8,128)S(1)}, f32[24,128]{1,0:T(8,128)S(1)}, u32[]{:S(2)}, u32[]{:S(2)}) %collective-permute-start.2) | collective-permute-done | bytes 12320 | tf_op jit(solution)/shard_map/ppermute | solution.py:705
  67.5 1.9 %coarse_key_grads.1 = (bf16[256,256]{1,0:T(8,128)(2,1)S(1)}, f32[1536,128]{1,0:T(8,128)S(1)}, f32[1536,128]{1,0:T(8,128)S(1)}, f32[1536,128]{1,0:T(8,128)S(1)}, ...) custom-call(f32[8]{0:T(128)S(1)} %copy-done.11, f32[24,128]{1,0:T(8,128)S(1)} %get-tuple-element.49.stat_ref, ...), custom_call_target="tpu_custom_call" | custom-call | flops 402653184 | bytes 1572864 | tf_op jit(solution)/shard_map/coarse_key_grads/pallas_call | solution.py:440
  69.5 1.5 %collective-permute-start.3 = (bf16[256,256]{1,0:T(8,128)(2,1)S(1)}, bf16[256,256]{1,0:T(8,128)(2,1)S(1)}, u32[]{:S(2)}, u32[]{:S(2)}) collective-permute-start(bf16[256,256]{1,0:T(8,128)(2,1)S(1)} %get-tuple-element.55.own_ref), channel_id=1, source_target_pairs={{0,2},{1,3},{2,0},{3,1},{4,6},{5,7},{6,4},{7,5},{8,10},{9,11},{10,... | collective-permute-start | bytes 393224 | tf_op jit(solution)/shard_map/ppermute | solution.py:705
  71.0 8.5 %fine_backward.1 = (bf16[768,256]{1,0:T(8,128)(2,1)S(1)}, bf16[768,256]{1,0:T(8,128)(2,1)S(1)}, bf16[768,256]{1,0:T(8,128)(2,1)S(1)}, bf16[768,256]{1,0:T(8,128)(2,1)S(1)}, f32[8,128]{1,0:T(8,128)S(1)}) custom-call(f32[8]{0:T(128)S(1)} %copy-done.11, s32[1]{0:T(128)} %get-tuple-element.56.shared_ref, bf16[8,400,128]{2,1,0:T(8,128)(2,1)S(1)} %all_to_all.10.own_ref, ...), custom_call_target="tpu_custom_call" | custom-call | flops 2415919104 | bytes 9437184 | tf_op jit(solution)/shard_map/fine_backward/pallas_call | solution.py:461
  79.5 0.0 copy-start.5
  79.5 0.7 copy-done.5
  80.2 0.8 copy-done.7
  81.0 0.7 copy-done.16
  81.7 0.7 copy-done.17
  82.5 0.0 copy-start.4
  82.5 0.6 copy-done.4
  83.2 0.0 all-gather.3.cloned.1.call-update
  83.2 1.6 %collective-permute-start.4 = (bf16[768,256]{1,0:T(8,128)(2,1)}, bf16[768,256]{1,0:T(8,128)(2,1)S(1)}, u32[]{:S(2)}, u32[]{:S(2)}) collective-permute-start(bf16[768,256]{1,0:T(8,128)(2,1)} %copy-done.17), channel_id=1, source_target_pairs={{0,6},{1,7},{2,4},{3,5},{4,2},{5,3},{6,0},{7,1},{8,14},{9,15},{10,... | collective-permute-start | bytes 1179656 | tf_op jit(solution)/shard_map/ppermute | solution.py:705
  84.9 1.4 %collective-permute-start.5 = (bf16[768,256]{1,0:T(8,128)(2,1)}, bf16[768,256]{1,0:T(8,128)(2,1)S(1)}, u32[]{:S(2)}, u32[]{:S(2)}) collective-permute-start(bf16[768,256]{1,0:T(8,128)(2,1)} %copy-done.16), channel_id=1, source_target_pairs={{0,2},{1,3},{2,0},{3,1},{4,6},{5,7},{6,4},{7,5},{8,10},{9,11},{10,... | collective-permute-start | bytes 1179656 | tf_op jit(solution)/shard_map/ppermute | solution.py:705
  86.3 1.8 %collective-permute-start.8 = (f32[8,128]{1,0:T(8,128)S(1)}, f32[8,128]{1,0:T(8,128)S(1)}, u32[]{:S(2)}, u32[]{:S(2)}) collective-permute-start(f32[8,128]{1,0:T(8,128)S(1)} %get-tuple-element.64._), channel_id=1, source_target_pairs={{0,96},{32,64},{64,32},{96,0},{128,224},{160,192},{192,160},{224,1... | collective-permute-start | bytes 12296 | tf_op jit(solution)/shard_map/ppermute | solution.py:712
  88.0 0.5 collective-permute-start.7
  88.6 0.9 collective-permute-start.6
  89.5 0.4 collective-permute-done.8
  89.9 2.4 %collective-permute-done.7 = f32[8,128]{1,0:T(8,128)S(1)} collective-permute-done((f32[8,128]{1,0:T(8,128)S(1)}, f32[8,128]{1,0:T(8,128)S(1)}, u32[]{:S(2)}, u32[]{:S(2)}) %collective-permute-start.7) | collective-permute-done | bytes 4128 | tf_op jit(solution)/shard_map/ppermute | solution.py:712
  92.3 4.9 %collective-permute-start.15 = (f32[8,128]{1,0:T(8,128)S(1)}, f32[8,128]{1,0:T(8,128)S(1)}, u32[]{:S(2)}, u32[]{:S(2)}) collective-permute-start(f32[8,128]{1,0:T(8,128)S(1)} %add_add_fusion.scale_refs_0_), channel_id=1, source_target_pairs={{0,25},{1,24},{2,27},{3,26},{4,29},{5,28},{6,31},{7,30},{8,17},{9,... | collective-permute-start | bytes 12296 | tf_op jit(solution)/shard_map/ppermute | solution.py:709
  97.3 1.8 %collective-permute-start.14 = (f32[8,128]{1,0:T(8,128)S(1)}, f32[8,128]{1,0:T(8,128)S(1)}, u32[]{:S(2)}, u32[]{:S(2)}) collective-permute-start(f32[8,128]{1,0:T(8,128)S(1)} %add_add_fusion.scale_refs_0_), channel_id=1, source_target_pairs={{0,24},{1,25},{2,26},{3,27},{4,28},{5,29},{6,30},{7,31},{8,16},{9,... | collective-permute-start | bytes 12296 | tf_op jit(solution)/shard_map/ppermute | solution.py:709
  99.0 0.0 collective-permute-start.13
  99.1 1.6 %collective-permute-start.12 = (f32[8,128]{1,0:T(8,128)S(1)}, f32[8,128]{1,0:T(8,128)S(1)}, u32[]{:S(2)}, u32[]{:S(2)}) collective-permute-start(f32[8,128]{1,0:T(8,128)S(1)} %add_add_fusion.scale_refs_0_), channel_id=1, source_target_pairs={{0,16},{1,17},{2,18},{3,19},{4,20},{5,21},{6,22},{7,23},{8,24},{9,... | collective-permute-start | bytes 12296 | tf_op jit(solution)/shard_map/ppermute | solution.py:709
  100.6 0.7 collective-permute-done.14.scale_refs_6_
  101.3 1.0 collective-permute-start.11
  102.4 1.5 %collective-permute-done.13.scale_refs_5_ = f32[8,128]{1,0:T(8,128)S(1)} collective-permute-done((f32[8,128]{1,0:T(8,128)S(1)}, f32[8,128]{1,0:T(8,128)S(1)}, u32[]{:S(2)}, u32[]{:S(2)}) %collective-permute-start.13) | collective-permute-done | bytes 4128 | tf_op jit(solution)/shard_map/ppermute | solution.py:709
  103.9 0.2 collective-permute-start.10
  104.1 1.9 %collective-permute-start.9 = (f32[8,128]{1,0:T(8,128)S(1)}, f32[8,128]{1,0:T(8,128)S(1)}, u32[]{:S(2)}, u32[]{:S(2)}) collective-permute-start(f32[8,128]{1,0:T(8,128)S(1)} %add_add_fusion.scale_refs_0_), channel_id=1, source_target_pairs={{0,1},{1,0},{2,3},{3,2},{4,5},{5,4},{6,7},{7,6},{8,9},{9,8},{10,11... | collective-permute-start | bytes 12296 | tf_op jit(solution)/shard_map/ppermute | solution.py:709
  105.9 0.4 collective-permute-done.10.scale_refs_2_
  106.3 0.4 collective-permute-done.9.scale_refs_1_
  106.8 1.0 copy-done.6
  107.8 1.0 copy-done.8
  108.8 0.4 sum_pairs.1
  109.2 0.9 copy-done.1
  110.1 3.8 %all-to-all-start.1 = ((bf16[8,384,128]{2,1,0:T(8,128)(2,1)}), bf16[8,384,128]{2,1,0:T(8,128)(2,1)S(1)}, u32[]{:S(2)}, u32[]{:S(2)}) async-start(bf16[8,384,128]{2,1,0:T(8,128)(2,1)} %copy-done.1), calls=%async_computation.1 | async-start | bytes 1572864 | tf_op jit(solution)/shard_map/all_to_all | solution.py:702
  113.9 1.2 collective-permute-start.22
  115.1 1.5 %collective-permute-start.21 = (f32[8,128]{1,0:T(8,128)S(1)}, f32[8,128]{1,0:T(8,128)S(1)}, u32[]{:S(2)}, u32[]{:S(2)}) collective-permute-start(f32[8,128]{1,0:T(8,128)S(1)} %get-tuple-element.75.refs_0_), channel_id=1, source_target_pairs={{0,6},{1,7},{2,4},{3,5},{4,2},{5,3},{6,0},{7,1},{8,14},{9,15},{10,... | collective-permute-start | bytes 12296 | tf_op jit(solution)/shard_map/ppermute | solution.py:705
  116.6 2.7 %collective-permute-start.20 = (f32[8,128]{1,0:T(8,128)S(1)}, f32[8,128]{1,0:T(8,128)S(1)}, u32[]{:S(2)}, u32[]{:S(2)}) collective-permute-start(f32[8,128]{1,0:T(8,128)S(1)} %get-tuple-element.75.refs_0_), channel_id=1, source_target_pairs={{0,132},{1,133},{2,134},{3,135},{4,128},{5,129},{6,130},{7,131},{8... | collective-permute-start | bytes 12296 | tf_op jit(solution)/shard_map/ppermute | solution.py:720
  119.3 2.6 %collective-permute-start.19 = (f32[8,128]{1,0:T(8,128)S(1)}, f32[8,128]{1,0:T(8,128)S(1)}, u32[]{:S(2)}, u32[]{:S(2)}) collective-permute-start(f32[8,128]{1,0:T(8,128)S(1)} %get-tuple-element.75.refs_0_), channel_id=1, source_target_pairs={{0,4},{1,5},{2,6},{3,7},{4,0},{5,1},{6,2},{7,3},{8,12},{9,13},{10,... | collective-permute-start | bytes 12296 | tf_op jit(solution)/shard_map/ppermute | solution.py:705
  121.9 1.5 %collective-permute-start.18 = (f32[8,128]{1,0:T(8,128)S(1)}, f32[8,128]{1,0:T(8,128)S(1)}, u32[]{:S(2)}, u32[]{:S(2)}) collective-permute-start(f32[8,128]{1,0:T(8,128)S(1)} %get-tuple-element.75.refs_0_), channel_id=1, source_target_pairs={{0,130},{1,131},{2,128},{3,129},{4,134},{5,135},{6,132},{7,133},{8... | collective-permute-start | bytes 12296 | tf_op jit(solution)/shard_map/ppermute | solution.py:720
  123.5 2.0 %collective-permute-start.16 = (f32[8,128]{1,0:T(8,128)S(1)}, f32[8,128]{1,0:T(8,128)S(1)}, u32[]{:S(2)}, u32[]{:S(2)}) collective-permute-start(f32[8,128]{1,0:T(8,128)S(1)} %get-tuple-element.75.refs_0_), channel_id=1, source_target_pairs={{0,128},{32,160},{64,192},{96,224},{128,0},{160,32},{192,64},{224,... | collective-permute-start | bytes 12296 | tf_op jit(solution)/shard_map/ppermute | solution.py:712
  125.5 1.2 copy-done
  126.7 1.9 %join_coarse.1 = (bf16[256,1024]{1,0:T(8,128)(2,1)}, bf16[256,1024]{1,0:T(8,128)(2,1)}, f32[8,128]{1,0:T(8,128)S(1)}) custom-call(bf16[8,256,256]{2,1,0:T(8,128)(2,1)S(1)} %bitcast.18, f32[256,1024]{1,0:T(8,128)S(1)} %get-tuple-element.65.dk_own_ref, f32[256,1024]{1,0:T(8,128)S(1)} %get-tuple-element.66.dv_own_ref, bf16[256,1024]{1,0:T(8,128)(2,1)S(1)} %bitcast.20), custom_call_target="tpu_custom_call" | custom-call | tf_op jit(solution)/shard_map/join_coarse/pallas_call | solution.py:643
  128.6 0.9 unpack_heads.1
  (36 shorter events, 0.1 us)
Async XLA Ops:
  7.2 48.4 %copy-start.11 = (f32[8]{0:T(128)S(1)}, f32[8]{0:T(128)}, u32[]{:S(2)}) copy-start(f32[8]{0:T(128)} %log_ref.7) | copy-start | bytes 100
  7.2 118.3 %all-gather.3.cloned.1.call-start = ((), (), s32[]{:S(2)}) async-start(), calls=%async_computation.2 | async-start | bytes 1179648 | tf_op jit(solution)/shard_map/all_gather | solution.py:734
  30.2 23.8 %collective-permute-start.1 = (bf16[8,208,128]{2,1,0:T(8,128)(2,1)}, bf16[8,208,128]{2,1,0:T(8,128)(2,1)}, u32[]{:S(2)}, u32[]{:S(2)}) collective-permute-start(bf16[8,208,128]{2,1,0:T(8,128)(2,1)} %get-tuple-element.81), channel_id=1, source_target_pairs={{0,6},{1,7},{2,4},{3,5},{4,2},{5,3},{6,0},{7,1},{8,14},{9,15},{10,... | collective-permute-start | bytes 1277960 | tf_op jit(solution)/shard_map/ppermute | solution.py:705
  35.5 20.1 %collective-permute-start = (bf16[8,208,128]{2,1,0:T(8,128)(2,1)}, bf16[8,208,128]{2,1,0:T(8,128)(2,1)}, u32[]{:S(2)}, u32[]{:S(2)}) collective-permute-start(bf16[8,208,128]{2,1,0:T(8,128)(2,1)} %get-tuple-element.82), channel_id=1, source_target_pairs={{0,2},{1,3},{2,0},{3,1},{4,6},{5,7},{6,4},{7,5},{8,10},{9,11},{10,... | collective-permute-start | bytes 1277960 | tf_op jit(solution)/shard_map/ppermute | solution.py:705
  38.1 1.0 copy-start.2
  39.2 0.9 copy-start.9
  40.1 0.7 copy-start.10
  40.7 0.7 copy-start.12
  41.4 1.0 copy-start.13
  42.5 1.0 copy-start.14
  43.5 1.0 copy-start.15
  62.8 4.7 %collective-permute-start.2 = (f32[24,128]{1,0:T(8,128)S(1)}, f32[24,128]{1,0:T(8,128)S(1)}, u32[]{:S(2)}, u32[]{:S(2)}) collective-permute-start(f32[24,128]{1,0:T(8,128)S(1)} %get-tuple-element.49.stat_ref), channel_id=1, source_target_pairs={{0,6},{1,7},{2,4},{3,5},{4,2},{5,3},{6,0},{7,1},{8,14},{9,15},{10,... | collective-permute-start | bytes 36872 | tf_op jit(solution)/shard_map/ppermute | solution.py:705
  69.5 13.0 %collective-permute-start.3 = (bf16[256,256]{1,0:T(8,128)(2,1)S(1)}, bf16[256,256]{1,0:T(8,128)(2,1)S(1)}, u32[]{:S(2)}, u32[]{:S(2)}) collective-permute-start(bf16[256,256]{1,0:T(8,128)(2,1)S(1)} %get-tuple-element.55.own_ref), channel_id=1, source_target_pairs={{0,2},{1,3},{2,0},{3,1},{4,6},{5,7},{6,4},{7,5},{8,10},{9,11},{10,... | collective-permute-start | bytes 393224 | tf_op jit(solution)/shard_map/ppermute | solution.py:705
  71.0 54.5 %copy-start.3 = (bf16[1,256,1024]{2,1,0:T(8,128)(2,1)S(1)}, bf16[1,256,1024]{2,1,0:T(8,128)(2,1)}, u32[]{:S(2)}) copy-start(bf16[1,256,1024]{2,1,0:T(8,128)(2,1)} %param.12) | copy-start | bytes 1572868
  79.5 0.7 copy-start.5
  80.2 0.8 copy-start.7
  81.0 0.7 copy-start.16
  81.7 0.7 copy-start.17
  82.5 0.7 copy-start.4
  83.2 23.5 %collective-permute-start.4 = (bf16[768,256]{1,0:T(8,128)(2,1)}, bf16[768,256]{1,0:T(8,128)(2,1)S(1)}, u32[]{:S(2)}, u32[]{:S(2)}) collective-permute-start(bf16[768,256]{1,0:T(8,128)(2,1)} %copy-done.17), channel_id=1, source_target_pairs={{0,6},{1,7},{2,4},{3,5},{4,2},{5,3},{6,0},{7,1},{8,14},{9,15},{10,... | collective-permute-start | bytes 1179656 | tf_op jit(solution)/shard_map/ppermute | solution.py:705
  84.9 21.9 %collective-permute-start.5 = (bf16[768,256]{1,0:T(8,128)(2,1)}, bf16[768,256]{1,0:T(8,128)(2,1)S(1)}, u32[]{:S(2)}, u32[]{:S(2)}) collective-permute-start(bf16[768,256]{1,0:T(8,128)(2,1)} %copy-done.16), channel_id=1, source_target_pairs={{0,2},{1,3},{2,0},{3,1},{4,6},{5,7},{6,4},{7,5},{8,10},{9,11},{10,... | collective-permute-start | bytes 1179656 | tf_op jit(solution)/shard_map/ppermute | solution.py:705
  86.3 3.7 %collective-permute-start.8 = (f32[8,128]{1,0:T(8,128)S(1)}, f32[8,128]{1,0:T(8,128)S(1)}, u32[]{:S(2)}, u32[]{:S(2)}) collective-permute-start(f32[8,128]{1,0:T(8,128)S(1)} %get-tuple-element.64._), channel_id=1, source_target_pairs={{0,96},{32,64},{64,32},{96,0},{128,224},{160,192},{192,160},{224,1... | collective-permute-start | bytes 12296 | tf_op jit(solution)/shard_map/ppermute | solution.py:712
  88.0 4.3 %collective-permute-start.7 = (f32[8,128]{1,0:T(8,128)S(1)}, f32[8,128]{1,0:T(8,128)S(1)}, u32[]{:S(2)}, u32[]{:S(2)}) collective-permute-start(f32[8,128]{1,0:T(8,128)S(1)} %get-tuple-element.64._), channel_id=1, source_target_pairs={{0,64},{32,96},{64,0},{96,32},{128,192},{160,224},{192,128},{224,1... | collective-permute-start | bytes 12296 | tf_op jit(solution)/shard_map/ppermute | solution.py:712
  88.6 3.7 %collective-permute-start.6 = (f32[8,128]{1,0:T(8,128)S(1)}, f32[8,128]{1,0:T(8,128)S(1)}, u32[]{:S(2)}, u32[]{:S(2)}) collective-permute-start(f32[8,128]{1,0:T(8,128)S(1)} %get-tuple-element.64._), channel_id=1, source_target_pairs={{0,32},{32,0},{64,96},{96,64},{128,160},{160,128},{192,224},{224,1... | collective-permute-start | bytes 12296 | tf_op jit(solution)/shard_map/ppermute | solution.py:712
  92.3 6.7 %collective-permute-start.15 = (f32[8,128]{1,0:T(8,128)S(1)}, f32[8,128]{1,0:T(8,128)S(1)}, u32[]{:S(2)}, u32[]{:S(2)}) collective-permute-start(f32[8,128]{1,0:T(8,128)S(1)} %add_add_fusion.scale_refs_0_), channel_id=1, source_target_pairs={{0,25},{1,24},{2,27},{3,26},{4,29},{5,28},{6,31},{7,30},{8,17},{9,... | collective-permute-start | bytes 12296 | tf_op jit(solution)/shard_map/ppermute | solution.py:709
  97.3 4.1 %collective-permute-start.14 = (f32[8,128]{1,0:T(8,128)S(1)}, f32[8,128]{1,0:T(8,128)S(1)}, u32[]{:S(2)}, u32[]{:S(2)}) collective-permute-start(f32[8,128]{1,0:T(8,128)S(1)} %add_add_fusion.scale_refs_0_), channel_id=1, source_target_pairs={{0,24},{1,25},{2,26},{3,27},{4,28},{5,29},{6,30},{7,31},{8,16},{9,... | collective-permute-start | bytes 12296 | tf_op jit(solution)/shard_map/ppermute | solution.py:709
  99.0 4.8 %collective-permute-start.13 = (f32[8,128]{1,0:T(8,128)S(1)}, f32[8,128]{1,0:T(8,128)S(1)}, u32[]{:S(2)}, u32[]{:S(2)}) collective-permute-start(f32[8,128]{1,0:T(8,128)S(1)} %add_add_fusion.scale_refs_0_), channel_id=1, source_target_pairs={{0,17},{1,16},{2,19},{3,18},{4,21},{5,20},{6,23},{7,22},{8,25},{9,... | collective-permute-start | bytes 12296 | tf_op jit(solution)/shard_map/ppermute | solution.py:709
  99.1 5.0 %collective-permute-start.12 = (f32[8,128]{1,0:T(8,128)S(1)}, f32[8,128]{1,0:T(8,128)S(1)}, u32[]{:S(2)}, u32[]{:S(2)}) collective-permute-start(f32[8,128]{1,0:T(8,128)S(1)} %add_add_fusion.scale_refs_0_), channel_id=1, source_target_pairs={{0,16},{1,17},{2,18},{3,19},{4,20},{5,21},{6,22},{7,23},{8,24},{9,... | collective-permute-start | bytes 12296 | tf_op jit(solution)/shard_map/ppermute | solution.py:709
  101.3 4.6 %collective-permute-start.11 = (f32[8,128]{1,0:T(8,128)S(1)}, f32[8,128]{1,0:T(8,128)S(1)}, u32[]{:S(2)}, u32[]{:S(2)}) collective-permute-start(f32[8,128]{1,0:T(8,128)S(1)} %add_add_fusion.scale_refs_0_), channel_id=1, source_target_pairs={{0,9},{1,8},{2,11},{3,10},{4,13},{5,12},{6,15},{7,14},{8,1},{9,0},... | collective-permute-start | bytes 12296 | tf_op jit(solution)/shard_map/ppermute | solution.py:709
  103.9 2.5 %collective-permute-start.10 = (f32[8,128]{1,0:T(8,128)S(1)}, f32[8,128]{1,0:T(8,128)S(1)}, u32[]{:S(2)}, u32[]{:S(2)}) collective-permute-start(f32[8,128]{1,0:T(8,128)S(1)} %add_add_fusion.scale_refs_0_), channel_id=1, source_target_pairs={{0,8},{1,9},{2,10},{3,11},{4,12},{5,13},{6,14},{7,15},{8,0},{9,1},... | collective-permute-start | bytes 12296 | tf_op jit(solution)/shard_map/ppermute | solution.py:709
  104.1 2.7 %collective-permute-start.9 = (f32[8,128]{1,0:T(8,128)S(1)}, f32[8,128]{1,0:T(8,128)S(1)}, u32[]{:S(2)}, u32[]{:S(2)}) collective-permute-start(f32[8,128]{1,0:T(8,128)S(1)} %add_add_fusion.scale_refs_0_), channel_id=1, source_target_pairs={{0,1},{1,0},{2,3},{3,2},{4,5},{5,4},{6,7},{7,6},{8,9},{9,8},{10,11... | collective-permute-start | bytes 12296 | tf_op jit(solution)/shard_map/ppermute | solution.py:709
  106.8 1.0 copy-start.6
  107.8 1.0 copy-start.8
  109.2 0.9 copy-start.1
  110.1 18.5 %all-to-all-start.1 = ((bf16[8,384,128]{2,1,0:T(8,128)(2,1)}), bf16[8,384,128]{2,1,0:T(8,128)(2,1)S(1)}, u32[]{:S(2)}, u32[]{:S(2)}) async-start(bf16[8,384,128]{2,1,0:T(8,128)(2,1)} %copy-done.1), calls=%async_computation.1 | async-start | bytes 1572864 | tf_op jit(solution)/shard_map/all_to_all | solution.py:702
  113.9 9.6 %collective-permute-start.22 = (f32[8,128]{1,0:T(8,128)S(1)}, f32[8,128]{1,0:T(8,128)S(1)}, u32[]{:S(2)}, u32[]{:S(2)}) collective-permute-start(f32[8,128]{1,0:T(8,128)S(1)} %get-tuple-element.75.refs_0_), channel_id=1, source_target_pairs={{0,134},{1,135},{2,132},{3,133},{4,130},{5,131},{6,128},{7,129},{8... | collective-permute-start | bytes 12296 | tf_op jit(solution)/shard_map/ppermute | solution.py:720
  115.1 8.4 %collective-permute-start.21 = (f32[8,128]{1,0:T(8,128)S(1)}, f32[8,128]{1,0:T(8,128)S(1)}, u32[]{:S(2)}, u32[]{:S(2)}) collective-permute-start(f32[8,128]{1,0:T(8,128)S(1)} %get-tuple-element.75.refs_0_), channel_id=1, source_target_pairs={{0,6},{1,7},{2,4},{3,5},{4,2},{5,3},{6,0},{7,1},{8,14},{9,15},{10,... | collective-permute-start | bytes 12296 | tf_op jit(solution)/shard_map/ppermute | solution.py:705
  116.6 12.0 %collective-permute-start.20 = (f32[8,128]{1,0:T(8,128)S(1)}, f32[8,128]{1,0:T(8,128)S(1)}, u32[]{:S(2)}, u32[]{:S(2)}) collective-permute-start(f32[8,128]{1,0:T(8,128)S(1)} %get-tuple-element.75.refs_0_), channel_id=1, source_target_pairs={{0,132},{1,133},{2,134},{3,135},{4,128},{5,129},{6,130},{7,131},{8... | collective-permute-start | bytes 12296 | tf_op jit(solution)/shard_map/ppermute | solution.py:720
  119.3 9.3 %collective-permute-start.19 = (f32[8,128]{1,0:T(8,128)S(1)}, f32[8,128]{1,0:T(8,128)S(1)}, u32[]{:S(2)}, u32[]{:S(2)}) collective-permute-start(f32[8,128]{1,0:T(8,128)S(1)} %get-tuple-element.75.refs_0_), channel_id=1, source_target_pairs={{0,4},{1,5},{2,6},{3,7},{4,0},{5,1},{6,2},{7,3},{8,12},{9,13},{10,... | collective-permute-start | bytes 12296 | tf_op jit(solution)/shard_map/ppermute | solution.py:705
  121.9 6.7 %collective-permute-start.18 = (f32[8,128]{1,0:T(8,128)S(1)}, f32[8,128]{1,0:T(8,128)S(1)}, u32[]{:S(2)}, u32[]{:S(2)}) collective-permute-start(f32[8,128]{1,0:T(8,128)S(1)} %get-tuple-element.75.refs_0_), channel_id=1, source_target_pairs={{0,130},{1,131},{2,128},{3,129},{4,134},{5,135},{6,132},{7,133},{8... | collective-permute-start | bytes 12296 | tf_op jit(solution)/shard_map/ppermute | solution.py:720
  123.5 5.1 %collective-permute-start.17 = (f32[8,128]{1,0:T(8,128)S(1)}, f32[8,128]{1,0:T(8,128)S(1)}, u32[]{:S(2)}, u32[]{:S(2)}) collective-permute-start(f32[8,128]{1,0:T(8,128)S(1)} %get-tuple-element.75.refs_0_), channel_id=1, source_target_pairs={{0,2},{1,3},{2,0},{3,1},{4,6},{5,7},{6,4},{7,5},{8,10},{9,11},{10,... | collective-permute-start | bytes 12296 | tf_op jit(solution)/shard_map/ppermute | solution.py:705
  123.5 5.1 %collective-permute-start.16 = (f32[8,128]{1,0:T(8,128)S(1)}, f32[8,128]{1,0:T(8,128)S(1)}, u32[]{:S(2)}, u32[]{:S(2)}) collective-permute-start(f32[8,128]{1,0:T(8,128)S(1)} %get-tuple-element.75.refs_0_), channel_id=1, source_target_pairs={{0,128},{32,160},{64,192},{96,224},{128,0},{160,32},{192,64},{224,... | collective-permute-start | bytes 12296 | tf_op jit(solution)/shard_map/ppermute | solution.py:712
  125.5 1.2 copy-start
Sparse Core Ops, SparseCore 0:
  83.3 24.0 all-gather.2

commit v11 on v10

--- a/solution.py
+++ b/solution.py
@@ -711,14 +711,6 @@
     def to_image(array, flip):
         return lax.ppermute(array, "dp", [(i, i ^ flip) for i in range(images)])
 
-    def to_both(array, image_flip, plane_flip):
-        there = [
-            (i ^ image_flip) * seq + (j ^ (2 * plane_flip))
-            for i in range(images)
-            for j in range(seq)
-        ]
-        return lax.ppermute(array, ("dp", "seq"), list(enumerate(there)))
-
     own_rows = exchange(run_pack(heads, fine_ids, k_fine[0], v_fine[0], q_fine[0], cot_fine[0]))
     kv_rows = to_plane(own_rows[:, : 2 * rows + note_rows], 1)
     qc_rows = to_plane(own_rows[:, 2 * rows :], 3)
@@ -738,9 +730,8 @@
     scale = scale + to_image(scale, 1) + to_image(scale, 2) + to_image(scale, 3)
     scales = [scale] + [to_head(scale, flip) for flip in range(1, heads)]
     all_parts, table = run_sum(od, other_od, dkv, other_dkv, own_rows, scales)
+    table = table + to_plane(table, 1) + to_plane(table, 2) + to_plane(table, 3)
     tables = [table, to_image(table, 4)]
-    for flip in (1, 2, 3):
-        tables += [to_plane(table, flip), to_both(table, 4, flip)]
     all_back = exchange(all_parts)
     dk_c, dv_c, after = run_join(of_image, dk_own, dv_own, k_coarse[0])
     factor = 1.0 / math.sqrt(images * (coarse + seq * rows))

time: 138 us -> 136 us (0.986)
  starting transfers between devices: 44 us -> 40.1 us
  waiting for transfers between devices: 11 us -> 14.5 us
  Pallas kernels: 31 us -> 29.3 us
    ppermute x3 -> x0, starting transfers between devices: 5.4 us -> none  [to_both(): return lax.ppermute(array, ('dp', 'seq'), list(enumerate(there)))]
    ppermute x9, waiting for transfers between devices: 5.09 us -> 8.06 us  [to_plane(): return lax.ppermute(array, 'seq', [(i, i ^ 2 * flip) for i in range(seq)])]
    ppermute x9, starting transfers between devices: 18.1 us -> 20.5 us  [to_plane(): return lax.ppermute(array, 'seq', [(i, i ^ 2 * flip) for i in range(seq)])]
  transfers between devices with their start and end apart: 25 -> 22, of which waited for: 9 -> 10; matrix products, arithmetic and copies ran while one was open for 1% -> 1% of each run, Pallas kernels for 14% -> 13%
where the time goes in v11:
time: 136 us; the launch traced here: 134 us
  starting transfers between devices  40.1 us (29%)
  Pallas kernels  29.3 us (22%)
  blocking collectives  19.7 us (14%)
  local copies, waits for them, and re-layouts  16.6 us (12%)
  waiting for transfers between devices  14.5 us (11%)
  between operations  14.2 us (10%)
    ppermute x9, starting transfers between devices, to_plane(): return lax.ppermute(array, 'seq', [(i, i ^ 2 * flip) for i in range(seq)])  20.5 us
    all_to_all x1, blocking collectives, exchange(): lax.all_to_all(parts, 'seq', 0, 0, axis_index_groups=groups, tiled=True)  19.7 us
    unnamed x36, local copies, waits for them, and re-layouts  14.2 us
    ppermute x7, starting transfers between devices, to_head(): return lax.ppermute(array, 'seq', [(i, i ^ other) for i in range(seq)])  11.4 us
    ppermute x9, waiting for transfers between devices, to_plane(): return lax.ppermute(array, 'seq', [(i, i ^ 2 * flip) for i in range(seq)])  8.06 us
    pallas_call x1, Pallas kernels, run_coarse(): pl.pallas_call(coarse_kernel, out_shape=(low, low, wide, wide, jax.ShapeD...  7.79 us
    pallas_call x1, Pallas kernels, run_fine(): pl.pallas_call(fine_back_kernel, out_shape=(half, half, half, half, wide(...  7.51 us
    pallas_call x1, Pallas kernels, run_fine(): pl.pallas_call(forward_kernel, out_shape=(low(queries, total), low(total,...  6.56 us
  transfers between devices with their start and end apart: 22, of which 10 were waited for; matrix products, arithmetic and copies ran while one was open for 1% of the time, Pallas kernels for 13%

profile of v11, /device:TPU:1, one launch (start us, length us, event | category | flops | bytes accessed | tf_op | source)
XLA Modules:
  0.0 134.4 jit_solution(10263504109216847271)
XLA Ops:
  7.2 0.0 copy-start.11
  7.2 0.0 all-gather.3.cloned.1.call-start
  7.2 2.3 %pack_heads.1 = bf16[8,400,128]{2,1,0:T(8,128)(2,1)} custom-call(s32[1,96]{1,0:T(1,128)} %ids_ref.1, bf16[96,1024]{1,0:T(8,128)(2,1)} %bitcast.25, bf16[96,1024]{1,0:T(8,128)(2,1)} %bitcast.26, bf16[96,1024]{1,0:T(8,128)(2,1)} %bitcast.27, bf16[96,1024]{1,0:T(8,128)(2,1)} %bitcast.28), custom_call_target="tpu_custom_call" | custom-call | tf_op jit(solution)/shard_map/pack_heads/pallas_call | solution.py:103
  9.5 19.7 %all_to_all.10.own_ref = bf16[8,400,128]{2,1,0:T(8,128)(2,1)S(1)} all-to-all(bf16[8,400,128]{2,1,0:T(8,128)(2,1)} %pack_heads.1), channel_id=1, replica_groups={{0,1,8,9,16,17,24,25},{2,3,10,11,18,19,26,27},{4,5,12,13,20,21,28,29},{..., dimensions={0} | all-to-all | bytes 1638400 | tf_op jit(solution)/shard_map/all_to_all | solution.py:702
  29.2 1.0 fusion
  30.2 5.3 %collective-permute-start.1 = (bf16[8,208,128]{2,1,0:T(8,128)(2,1)}, bf16[8,208,128]{2,1,0:T(8,128)(2,1)}, u32[]{:S(2)}, u32[]{:S(2)}) collective-permute-start(bf16[8,208,128]{2,1,0:T(8,128)(2,1)} %get-tuple-element.81), channel_id=1, source_target_pairs={{0,6},{1,7},{2,4},{3,5},{4,2},{5,3},{6,0},{7,1},{8,14},{9,15},{10,... | collective-permute-start | bytes 1277960 | tf_op jit(solution)/shard_map/ppermute | solution.py:705
  35.5 1.2 collective-permute-start
  36.7 1.5 %copy.20.row_level_ref = s32[256,1]{1,0:T(8,128)} copy(s32[256,1]{0,1:T(1,128)} %bitcast.21) | data formatting | bytes 2048 | tf_op jit(solution)/shard_map/broadcast_in_dim;squeeze | solution.py:571
  38.1 1.0 copy-done.2
  39.2 0.9 copy-done.9
  40.1 0.7 copy-done.10
  40.7 0.7 copy-done.12
  41.4 1.0 copy-done.13
  42.5 1.0 copy-done.14
  43.5 1.0 copy-done.15
  44.5 7.8 %coarse_attention.1 = (bf16[256,1024]{1,0:T(8,128)(2,1)}, bf16[256,1024]{1,0:T(8,128)(2,1)}, f32[256,1024]{1,0:T(8,128)S(1)}, f32[256,1024]{1,0:T(8,128)S(1)}, f...) custom-call(f32[8]{0:T(128)S(1)} %copy-done.10, s32[256,1]{1,0:T(8,128)S(1)} %copy-done.9, ...), custom_call_target="tpu_custom_call" | custom-call | flops 805306368 | bytes 6291456 | tf_op jit(solution)/shard_map/coarse_attention/pallas_call | solution.py:559
  52.3 1.7 %collective-permute-done.1.qc_ref = bf16[8,208,128]{2,1,0:T(8,128)(2,1)} collective-permute-done((bf16[8,208,128]{2,1,0:T(8,128)(2,1)}, bf16[8,208,128]{2,1,0:T(8,128)(2,1)}, u32[]{:S(2)}, u32[]{:S(2)}) %collective-permute-start.1) | collective-permute-done | bytes 426016 | tf_op jit(solution)/shard_map/ppermute | solution.py:705
  54.0 1.5 %collective-permute-done.kv_ref = bf16[8,208,128]{2,1,0:T(8,128)(2,1)} collective-permute-done((bf16[8,208,128]{2,1,0:T(8,128)(2,1)}, bf16[8,208,128]{2,1,0:T(8,128)(2,1)}, u32[]{:S(2)}, u32[]{:S(2)}) %collective-permute-start) | collective-permute-done | bytes 426016 | tf_op jit(solution)/shard_map/ppermute | solution.py:705
  55.6 6.6 %fine_forward.1 = (bf16[1536,1792]{1,0:T(8,128)(2,1)S(1)}, bf16[1792,128]{1,0:T(8,128)(2,1)S(1)}, bf16[1792,128]{1,0:T(8,128)(2,1)S(1)}, bf16[1536,128]{1,0:T(8,...) custom-call(f32[8]{0:T(128)S(1)} %copy-done.11, ...), custom_call_target="tpu_custom_call" | custom-call | flops 1409286144 | bytes 11010048 | tf_op jit(solution)/shard_map/fine_forward/pallas_call | solution.py:412
  62.1 2.9 %collective-permute-start.2 = (f32[24,128]{1,0:T(8,128)S(1)}, f32[24,128]{1,0:T(8,128)S(1)}, u32[]{:S(2)}, u32[]{:S(2)}) collective-permute-start(f32[24,128]{1,0:T(8,128)S(1)} %get-tuple-element.49.stat_ref), channel_id=1, source_target_pairs={{0,6},{1,7},{2,4},{3,5},{4,2},{5,3},{6,0},{7,1},{8,14},{9,15},{10,... | collective-permute-start | bytes 36872 | tf_op jit(solution)/shard_map/ppermute | solution.py:705
  65.0 1.9 %collective-permute-done.2.other_stat_ref = f32[24,128]{1,0:T(8,128)S(1)} collective-permute-done((f32[24,128]{1,0:T(8,128)S(1)}, f32[24,128]{1,0:T(8,128)S(1)}, u32[]{:S(2)}, u32[]{:S(2)}) %collective-permute-start.2) | collective-permute-done | bytes 12320 | tf_op jit(solution)/shard_map/ppermute | solution.py:705
  66.9 1.9 %coarse_key_grads.1 = (bf16[256,256]{1,0:T(8,128)(2,1)S(1)}, f32[1536,128]{1,0:T(8,128)S(1)}, f32[1536,128]{1,0:T(8,128)S(1)}, f32[1536,128]{1,0:T(8,128)S(1)}, ...) custom-call(f32[8]{0:T(128)S(1)} %copy-done.11, f32[24,128]{1,0:T(8,128)S(1)} %get-tuple-element.49.stat_ref, ...), custom_call_target="tpu_custom_call" | custom-call | flops 402653184 | bytes 1572864 | tf_op jit(solution)/shard_map/coarse_key_grads/pallas_call | solution.py:440
  68.8 2.2 %collective-permute-start.3 = (bf16[256,256]{1,0:T(8,128)(2,1)S(1)}, bf16[256,256]{1,0:T(8,128)(2,1)S(1)}, u32[]{:S(2)}, u32[]{:S(2)}) collective-permute-start(bf16[256,256]{1,0:T(8,128)(2,1)S(1)} %get-tuple-element.55.own_ref), channel_id=1, source_target_pairs={{0,2},{1,3},{2,0},{3,1},{4,6},{5,7},{6,4},{7,5},{8,10},{9,11},{10,... | collective-permute-start | bytes 393224 | tf_op jit(solution)/shard_map/ppermute | solution.py:705
  71.0 7.5 %fine_backward.1 = (bf16[768,256]{1,0:T(8,128)(2,1)S(1)}, bf16[768,256]{1,0:T(8,128)(2,1)S(1)}, bf16[768,256]{1,0:T(8,128)(2,1)S(1)}, bf16[768,256]{1,0:T(8,128)(2,1)S(1)}, f32[8,128]{1,0:T(8,128)S(1)}) custom-call(f32[8]{0:T(128)S(1)} %copy-done.11, s32[1]{0:T(128)} %get-tuple-element.56.shared_ref, bf16[8,400,128]{2,1,0:T(8,128)(2,1)S(1)} %all_to_all.10.own_ref, ...), custom_call_target="tpu_custom_call" | custom-call | flops 2415919104 | bytes 9437184 | tf_op jit(solution)/shard_map/fine_backward/pallas_call | solution.py:461
  78.5 0.0 copy-start.5
  78.5 0.7 copy-done.5
  79.3 0.8 copy-done.7
  80.0 0.7 copy-done.16
  80.8 0.7 copy-done.17
  81.5 0.0 collective-permute-done.3.near_ref
  81.6 0.0 copy-start.4
  81.6 0.6 copy-done.4
  82.2 0.0 all-gather.3.cloned.1.call-update
  82.3 1.0 collective-permute-start.4
  83.2 2.3 %collective-permute-start.5 = (bf16[768,256]{1,0:T(8,128)(2,1)}, bf16[768,256]{1,0:T(8,128)(2,1)S(1)}, u32[]{:S(2)}, u32[]{:S(2)}) collective-permute-start(bf16[768,256]{1,0:T(8,128)(2,1)} %copy-done.16), channel_id=1, source_target_pairs={{0,2},{1,3},{2,0},{3,1},{4,6},{5,7},{6,4},{7,5},{8,10},{9,11},{10,... | collective-permute-start | bytes 1179656 | tf_op jit(solution)/shard_map/ppermute | solution.py:705
  85.6 2.5 %collective-permute-start.8 = (f32[8,128]{1,0:T(8,128)S(1)}, f32[8,128]{1,0:T(8,128)S(1)}, u32[]{:S(2)}, u32[]{:S(2)}) collective-permute-start(f32[8,128]{1,0:T(8,128)S(1)} %get-tuple-element.64._), channel_id=1, source_target_pairs={{0,96},{32,64},{64,32},{96,0},{128,224},{160,192},{192,160},{224,1... | collective-permute-start | bytes 12296 | tf_op jit(solution)/shard_map/ppermute | solution.py:712
  88.0 0.5 collective-permute-start.7
  88.6 0.3 collective-permute-start.6
  88.8 0.4 collective-permute-done.8
  89.2 3.1 %collective-permute-done.7 = f32[8,128]{1,0:T(8,128)S(1)} collective-permute-done((f32[8,128]{1,0:T(8,128)S(1)}, f32[8,128]{1,0:T(8,128)S(1)}, u32[]{:S(2)}, u32[]{:S(2)}) %collective-permute-start.7) | collective-permute-done | bytes 4128 | tf_op jit(solution)/shard_map/ppermute | solution.py:712
  92.3 0.0 collective-permute-done.6
  92.3 4.9 %collective-permute-start.15 = (f32[8,128]{1,0:T(8,128)S(1)}, f32[8,128]{1,0:T(8,128)S(1)}, u32[]{:S(2)}, u32[]{:S(2)}) collective-permute-start(f32[8,128]{1,0:T(8,128)S(1)} %add_add_fusion.1.scale_refs_0_), channel_id=1, source_target_pairs={{0,25},{1,24},{2,27},{3,26},{4,29},{5,28},{6,31},{7,30},{8,17},{9,... | collective-permute-start | bytes 12296 | tf_op jit(solution)/shard_map/ppermute | solution.py:709
  97.2 1.8 %collective-permute-start.14 = (f32[8,128]{1,0:T(8,128)S(1)}, f32[8,128]{1,0:T(8,128)S(1)}, u32[]{:S(2)}, u32[]{:S(2)}) collective-permute-start(f32[8,128]{1,0:T(8,128)S(1)} %add_add_fusion.1.scale_refs_0_), channel_id=1, source_target_pairs={{0,24},{1,25},{2,26},{3,27},{4,28},{5,29},{6,30},{7,31},{8,16},{9,... | collective-permute-start | bytes 12296 | tf_op jit(solution)/shard_map/ppermute | solution.py:709
  99.0 1.6 %collective-permute-start.12 = (f32[8,128]{1,0:T(8,128)S(1)}, f32[8,128]{1,0:T(8,128)S(1)}, u32[]{:S(2)}, u32[]{:S(2)}) collective-permute-start(f32[8,128]{1,0:T(8,128)S(1)} %add_add_fusion.1.scale_refs_0_), channel_id=1, source_target_pairs={{0,16},{1,17},{2,18},{3,19},{4,20},{5,21},{6,22},{7,23},{8,24},{9,... | collective-permute-start | bytes 12296 | tf_op jit(solution)/shard_map/ppermute | solution.py:709
  100.6 0.6 collective-permute-done.14.scale_refs_6_
  101.2 1.1 collective-permute-start.11
  102.3 1.5 %collective-permute-done.13.scale_refs_5_ = f32[8,128]{1,0:T(8,128)S(1)} collective-permute-done((f32[8,128]{1,0:T(8,128)S(1)}, f32[8,128]{1,0:T(8,128)S(1)}, u32[]{:S(2)}, u32[]{:S(2)}) %collective-permute-start.13) | collective-permute-done | bytes 4128 | tf_op jit(solution)/shard_map/ppermute | solution.py:709
  103.9 0.2 collective-permute-start.10
  104.0 1.9 %collective-permute-start.9 = (f32[8,128]{1,0:T(8,128)S(1)}, f32[8,128]{1,0:T(8,128)S(1)}, u32[]{:S(2)}, u32[]{:S(2)}) collective-permute-start(f32[8,128]{1,0:T(8,128)S(1)} %add_add_fusion.1.scale_refs_0_), channel_id=1, source_target_pairs={{0,1},{1,0},{2,3},{3,2},{4,5},{5,4},{6,7},{7,6},{8,9},{9,8},{10,11... | collective-permute-start | bytes 12296 | tf_op jit(solution)/shard_map/ppermute | solution.py:709
  105.9 0.4 collective-permute-done.10.scale_refs_2_
  106.3 0.4 collective-permute-done.9.scale_refs_1_
  106.8 1.0 copy-done.6
  107.8 1.0 copy-done.8
  108.8 0.4 sum_pairs.1
  109.2 0.9 copy-done.1
  110.1 3.8 %all-to-all-start.1 = ((bf16[8,384,128]{2,1,0:T(8,128)(2,1)}), bf16[8,384,128]{2,1,0:T(8,128)(2,1)S(1)}, u32[]{:S(2)}, u32[]{:S(2)}) async-start(bf16[8,384,128]{2,1,0:T(8,128)(2,1)} %copy-done.1), calls=%async_computation.1 | async-start | bytes 1572864 | tf_op jit(solution)/shard_map/all_to_all | solution.py:702
  113.9 2.3 %collective-permute-start.18 = (f32[8,128]{1,0:T(8,128)S(1)}, f32[8,128]{1,0:T(8,128)S(1)}, u32[]{:S(2)}, u32[]{:S(2)}) collective-permute-start(f32[8,128]{1,0:T(8,128)S(1)} %get-tuple-element.75), channel_id=1, source_target_pairs={{0,6},{1,7},{2,4},{3,5},{4,2},{5,3},{6,0},{7,1},{8,14},{9,15},{10,... | collective-permute-start | bytes 12296 | tf_op jit(solution)/shard_map/ppermute | solution.py:705
  116.1 1.0 collective-permute-start.17
  117.2 2.4 %collective-permute-start.16 = (f32[8,128]{1,0:T(8,128)S(1)}, f32[8,128]{1,0:T(8,128)S(1)}, u32[]{:S(2)}, u32[]{:S(2)}) collective-permute-start(f32[8,128]{1,0:T(8,128)S(1)} %get-tuple-element.75), channel_id=1, source_target_pairs={{0,2},{1,3},{2,0},{3,1},{4,6},{5,7},{6,4},{7,5},{8,10},{9,11},{10,... | collective-permute-start | bytes 12296 | tf_op jit(solution)/shard_map/ppermute | solution.py:705
  119.5 3.0 %collective-permute-done.17 = f32[8,128]{1,0:T(8,128)S(1)} collective-permute-done((f32[8,128]{1,0:T(8,128)S(1)}, f32[8,128]{1,0:T(8,128)S(1)}, u32[]{:S(2)}, u32[]{:S(2)}) %collective-permute-start.17) | collective-permute-done | bytes 4128 | tf_op jit(solution)/shard_map/ppermute | solution.py:705
  122.5 1.0 collective-permute-start.19
  123.5 1.2 copy-done
  124.8 1.9 %join_coarse.1 = (bf16[256,1024]{1,0:T(8,128)(2,1)}, bf16[256,1024]{1,0:T(8,128)(2,1)}, f32[8,128]{1,0:T(8,128)S(1)}) custom-call(bf16[8,256,256]{2,1,0:T(8,128)(2,1)S(1)} %bitcast.18, f32[256,1024]{1,0:T(8,128)S(1)} %get-tuple-element.65.dk_own_ref, f32[256,1024]{1,0:T(8,128)S(1)} %get-tuple-element.66.dv_own_ref, bf16[256,1024]{1,0:T(8,128)(2,1)S(1)} %bitcast.20), custom_call_target="tpu_custom_call" | custom-call | tf_op jit(solution)/shard_map/join_coarse/pallas_call | solution.py:643
  126.6 0.9 unpack_heads.1
  (31 shorter events, 0.1 us)
Async XLA Ops:
  7.2 48.4 %copy-start.11 = (f32[8]{0:T(128)S(1)}, f32[8]{0:T(128)}, u32[]{:S(2)}) copy-start(f32[8]{0:T(128)} %log_ref.7) | copy-start | bytes 100
  7.2 116.3 %all-gather.3.cloned.1.call-start = ((), (), s32[]{:S(2)}) async-start(), calls=%async_computation.2 | async-start | bytes 1179648 | tf_op jit(solution)/shard_map/all_gather | solution.py:726
  30.2 23.8 %collective-permute-start.1 = (bf16[8,208,128]{2,1,0:T(8,128)(2,1)}, bf16[8,208,128]{2,1,0:T(8,128)(2,1)}, u32[]{:S(2)}, u32[]{:S(2)}) collective-permute-start(bf16[8,208,128]{2,1,0:T(8,128)(2,1)} %get-tuple-element.81), channel_id=1, source_target_pairs={{0,6},{1,7},{2,4},{3,5},{4,2},{5,3},{6,0},{7,1},{8,14},{9,15},{10,... | collective-permute-start | bytes 1277960 | tf_op jit(solution)/shard_map/ppermute | solution.py:705
  35.5 20.1 %collective-permute-start = (bf16[8,208,128]{2,1,0:T(8,128)(2,1)}, bf16[8,208,128]{2,1,0:T(8,128)(2,1)}, u32[]{:S(2)}, u32[]{:S(2)}) collective-permute-start(bf16[8,208,128]{2,1,0:T(8,128)(2,1)} %get-tuple-element.82), channel_id=1, source_target_pairs={{0,2},{1,3},{2,0},{3,1},{4,6},{5,7},{6,4},{7,5},{8,10},{9,11},{10,... | collective-permute-start | bytes 1277960 | tf_op jit(solution)/shard_map/ppermute | solution.py:705
  38.1 1.0 copy-start.2
  39.2 0.9 copy-start.9
  40.1 0.7 copy-start.10
  40.7 0.7 copy-start.12
  41.4 1.0 copy-start.13
  42.5 1.0 copy-start.14
  43.5 1.0 copy-start.15
  62.1 4.7 %collective-permute-start.2 = (f32[24,128]{1,0:T(8,128)S(1)}, f32[24,128]{1,0:T(8,128)S(1)}, u32[]{:S(2)}, u32[]{:S(2)}) collective-permute-start(f32[24,128]{1,0:T(8,128)S(1)} %get-tuple-element.49.stat_ref), channel_id=1, source_target_pairs={{0,6},{1,7},{2,4},{3,5},{4,2},{5,3},{6,0},{7,1},{8,14},{9,15},{10,... | collective-permute-start | bytes 36872 | tf_op jit(solution)/shard_map/ppermute | solution.py:705
  68.8 12.7 %collective-permute-start.3 = (bf16[256,256]{1,0:T(8,128)(2,1)S(1)}, bf16[256,256]{1,0:T(8,128)(2,1)S(1)}, u32[]{:S(2)}, u32[]{:S(2)}) collective-permute-start(bf16[256,256]{1,0:T(8,128)(2,1)S(1)} %get-tuple-element.55.own_ref), channel_id=1, source_target_pairs={{0,2},{1,3},{2,0},{3,1},{4,6},{5,7},{6,4},{7,5},{8,10},{9,11},{10,... | collective-permute-start | bytes 393224 | tf_op jit(solution)/shard_map/ppermute | solution.py:705
  71.0 52.5 %copy-start.3 = (bf16[1,256,1024]{2,1,0:T(8,128)(2,1)S(1)}, bf16[1,256,1024]{2,1,0:T(8,128)(2,1)}, u32[]{:S(2)}) copy-start(bf16[1,256,1024]{2,1,0:T(8,128)(2,1)} %param.12) | copy-start | bytes 1572868
  78.5 0.7 copy-start.5
  79.3 0.8 copy-start.7
  80.0 0.8 copy-start.16
  80.8 0.7 copy-start.17
  81.6 0.7 copy-start.4
  82.3 24.5 %collective-permute-start.4 = (bf16[768,256]{1,0:T(8,128)(2,1)}, bf16[768,256]{1,0:T(8,128)(2,1)S(1)}, u32[]{:S(2)}, u32[]{:S(2)}) collective-permute-start(bf16[768,256]{1,0:T(8,128)(2,1)} %copy-done.17), channel_id=1, source_target_pairs={{0,6},{1,7},{2,4},{3,5},{4,2},{5,3},{6,0},{7,1},{8,14},{9,15},{10,... | collective-permute-start | bytes 1179656 | tf_op jit(solution)/shard_map/ppermute | solution.py:705
  83.2 23.5 %collective-permute-start.5 = (bf16[768,256]{1,0:T(8,128)(2,1)}, bf16[768,256]{1,0:T(8,128)(2,1)S(1)}, u32[]{:S(2)}, u32[]{:S(2)}) collective-permute-start(bf16[768,256]{1,0:T(8,128)(2,1)} %copy-done.16), channel_id=1, source_target_pairs={{0,2},{1,3},{2,0},{3,1},{4,6},{5,7},{6,4},{7,5},{8,10},{9,11},{10,... | collective-permute-start | bytes 1179656 | tf_op jit(solution)/shard_map/ppermute | solution.py:705
  85.6 3.7 %collective-permute-start.8 = (f32[8,128]{1,0:T(8,128)S(1)}, f32[8,128]{1,0:T(8,128)S(1)}, u32[]{:S(2)}, u32[]{:S(2)}) collective-permute-start(f32[8,128]{1,0:T(8,128)S(1)} %get-tuple-element.64._), channel_id=1, source_target_pairs={{0,96},{32,64},{64,32},{96,0},{128,224},{160,192},{192,160},{224,1... | collective-permute-start | bytes 12296 | tf_op jit(solution)/shard_map/ppermute | solution.py:712
  88.0 4.3 %collective-permute-start.7 = (f32[8,128]{1,0:T(8,128)S(1)}, f32[8,128]{1,0:T(8,128)S(1)}, u32[]{:S(2)}, u32[]{:S(2)}) collective-permute-start(f32[8,128]{1,0:T(8,128)S(1)} %get-tuple-element.64._), channel_id=1, source_target_pairs={{0,64},{32,96},{64,0},{96,32},{128,192},{160,224},{192,128},{224,1... | collective-permute-start | bytes 12296 | tf_op jit(solution)/shard_map/ppermute | solution.py:712
  88.6 3.7 %collective-permute-start.6 = (f32[8,128]{1,0:T(8,128)S(1)}, f32[8,128]{1,0:T(8,128)S(1)}, u32[]{:S(2)}, u32[]{:S(2)}) collective-permute-start(f32[8,128]{1,0:T(8,128)S(1)} %get-tuple-element.64._), channel_id=1, source_target_pairs={{0,32},{32,0},{64,96},{96,64},{128,160},{160,128},{192,224},{224,1... | collective-permute-start | bytes 12296 | tf_op jit(solution)/shard_map/ppermute | solution.py:712
  92.3 6.7 %collective-permute-start.15 = (f32[8,128]{1,0:T(8,128)S(1)}, f32[8,128]{1,0:T(8,128)S(1)}, u32[]{:S(2)}, u32[]{:S(2)}) collective-permute-start(f32[8,128]{1,0:T(8,128)S(1)} %add_add_fusion.1.scale_refs_0_), channel_id=1, source_target_pairs={{0,25},{1,24},{2,27},{3,26},{4,29},{5,28},{6,31},{7,30},{8,17},{9,... | collective-permute-start | bytes 12296 | tf_op jit(solution)/shard_map/ppermute | solution.py:709
  97.2 4.0 %collective-permute-start.14 = (f32[8,128]{1,0:T(8,128)S(1)}, f32[8,128]{1,0:T(8,128)S(1)}, u32[]{:S(2)}, u32[]{:S(2)}) collective-permute-start(f32[8,128]{1,0:T(8,128)S(1)} %add_add_fusion.1.scale_refs_0_), channel_id=1, source_target_pairs={{0,24},{1,25},{2,26},{3,27},{4,28},{5,29},{6,30},{7,31},{8,16},{9,... | collective-permute-start | bytes 12296 | tf_op jit(solution)/shard_map/ppermute | solution.py:709
  99.0 4.8 %collective-permute-start.13 = (f32[8,128]{1,0:T(8,128)S(1)}, f32[8,128]{1,0:T(8,128)S(1)}, u32[]{:S(2)}, u32[]{:S(2)}) collective-permute-start(f32[8,128]{1,0:T(8,128)S(1)} %add_add_fusion.1.scale_refs_0_), channel_id=1, source_target_pairs={{0,17},{1,16},{2,19},{3,18},{4,21},{5,20},{6,23},{7,22},{8,25},{9,... | collective-permute-start | bytes 12296 | tf_op jit(solution)/shard_map/ppermute | solution.py:709
  99.0 5.0 %collective-permute-start.12 = (f32[8,128]{1,0:T(8,128)S(1)}, f32[8,128]{1,0:T(8,128)S(1)}, u32[]{:S(2)}, u32[]{:S(2)}) collective-permute-start(f32[8,128]{1,0:T(8,128)S(1)} %add_add_fusion.1.scale_refs_0_), channel_id=1, source_target_pairs={{0,16},{1,17},{2,18},{3,19},{4,20},{5,21},{6,22},{7,23},{8,24},{9,... | collective-permute-start | bytes 12296 | tf_op jit(solution)/shard_map/ppermute | solution.py:709
  101.2 4.7 %collective-permute-start.11 = (f32[8,128]{1,0:T(8,128)S(1)}, f32[8,128]{1,0:T(8,128)S(1)}, u32[]{:S(2)}, u32[]{:S(2)}) collective-permute-start(f32[8,128]{1,0:T(8,128)S(1)} %add_add_fusion.1.scale_refs_0_), channel_id=1, source_target_pairs={{0,9},{1,8},{2,11},{3,10},{4,13},{5,12},{6,15},{7,14},{8,1},{9,0},... | collective-permute-start | bytes 12296 | tf_op jit(solution)/shard_map/ppermute | solution.py:709
  103.9 2.5 %collective-permute-start.10 = (f32[8,128]{1,0:T(8,128)S(1)}, f32[8,128]{1,0:T(8,128)S(1)}, u32[]{:S(2)}, u32[]{:S(2)}) collective-permute-start(f32[8,128]{1,0:T(8,128)S(1)} %add_add_fusion.1.scale_refs_0_), channel_id=1, source_target_pairs={{0,8},{1,9},{2,10},{3,11},{4,12},{5,13},{6,14},{7,15},{8,0},{9,1},... | collective-permute-start | bytes 12296 | tf_op jit(solution)/shard_map/ppermute | solution.py:709
  104.0 2.7 %collective-permute-start.9 = (f32[8,128]{1,0:T(8,128)S(1)}, f32[8,128]{1,0:T(8,128)S(1)}, u32[]{:S(2)}, u32[]{:S(2)}) collective-permute-start(f32[8,128]{1,0:T(8,128)S(1)} %add_add_fusion.1.scale_refs_0_), channel_id=1, source_target_pairs={{0,1},{1,0},{2,3},{3,2},{4,5},{5,4},{6,7},{7,6},{8,9},{9,8},{10,11... | collective-permute-start | bytes 12296 | tf_op jit(solution)/shard_map/ppermute | solution.py:709
  106.8 1.0 copy-start.6
  107.8 1.0 copy-start.8
  109.2 0.9 copy-start.1
  110.1 16.6 %all-to-all-start.1 = ((bf16[8,384,128]{2,1,0:T(8,128)(2,1)}), bf16[8,384,128]{2,1,0:T(8,128)(2,1)S(1)}, u32[]{:S(2)}, u32[]{:S(2)}) async-start(bf16[8,384,128]{2,1,0:T(8,128)(2,1)} %copy-done.1), calls=%async_computation.1 | async-start | bytes 1572864 | tf_op jit(solution)/shard_map/all_to_all | solution.py:702
  113.9 5.7 %collective-permute-start.18 = (f32[8,128]{1,0:T(8,128)S(1)}, f32[8,128]{1,0:T(8,128)S(1)}, u32[]{:S(2)}, u32[]{:S(2)}) collective-permute-start(f32[8,128]{1,0:T(8,128)S(1)} %get-tuple-element.75), channel_id=1, source_target_pairs={{0,6},{1,7},{2,4},{3,5},{4,2},{5,3},{6,0},{7,1},{8,14},{9,15},{10,... | collective-permute-start | bytes 12296 | tf_op jit(solution)/shard_map/ppermute | solution.py:705
  116.1 6.4 %collective-permute-start.17 = (f32[8,128]{1,0:T(8,128)S(1)}, f32[8,128]{1,0:T(8,128)S(1)}, u32[]{:S(2)}, u32[]{:S(2)}) collective-permute-start(f32[8,128]{1,0:T(8,128)S(1)} %get-tuple-element.75), channel_id=1, source_target_pairs={{0,4},{1,5},{2,6},{3,7},{4,0},{5,1},{6,2},{7,3},{8,12},{9,13},{10,... | collective-permute-start | bytes 12296 | tf_op jit(solution)/shard_map/ppermute | solution.py:705
  117.2 5.3 %collective-permute-start.16 = (f32[8,128]{1,0:T(8,128)S(1)}, f32[8,128]{1,0:T(8,128)S(1)}, u32[]{:S(2)}, u32[]{:S(2)}) collective-permute-start(f32[8,128]{1,0:T(8,128)S(1)} %get-tuple-element.75), channel_id=1, source_target_pairs={{0,2},{1,3},{2,0},{3,1},{4,6},{5,7},{6,4},{7,5},{8,10},{9,11},{10,... | collective-permute-start | bytes 12296 | tf_op jit(solution)/shard_map/ppermute | solution.py:705
  122.5 4.1 %collective-permute-start.19 = (f32[8,128]{1,0:T(8,128)S(1)}, f32[8,128]{1,0:T(8,128)S(1)}, u32[]{:S(2)}, u32[]{:S(2)}) collective-permute-start(f32[8,128]{1,0:T(8,128)S(1)} %add_add_fusion.refs_0_), channel_id=1, source_target_pairs={{0,128},{32,160},{64,192},{96,224},{128,0},{160,32},{192,64},{224,... | collective-permute-start | bytes 12296 | tf_op jit(solution)/shard_map/ppermute | solution.py:712
  123.5 1.2 copy-start
Sparse Core Ops, SparseCore 0:
  82.4 25.0 all-gather.2
